TPU v7x, 32 devices: a whole 2x2x4 slice. The times are simulated.
32 devices in a mesh: level: 4 (over z), img: 8 (over y, x, core).
Axes of the slice: x: 2, y: 2, z: 4, core: 2. Of those that a mesh axis runs over, the one named last changes fastest.
Arguments:
- pyramid: bfloat16 [4, 16, 64, 16, 256], P('level', 'img'), may hold values from -6 to 6
- levels: int32 [16, 512, 1], P('img', 'level'), may hold values from 0 to 3; in each aligned block of 128 rows (0 to 127, 128 to 255, ..., all dimensions but the last counted through in order) at most 64 rows name the same one
- region_boxes: int32 [16, 512, 4], P('img', 'level'), may hold values from 0 to 63, as said below
- labels: int32 [16, 512], P('img', 'level'), may hold values from 0 to 80, as said below
- crowd_ignore: int32 [16, 512], P('img', 'level'), may hold values 0 or 1
- targets: float32 [16, 512, 4], P('img', 'level'), may hold values from -6 to 6
- hidden_weight: bfloat16 [12544, 1024], P(('level', 'img')), may hold values from -0.109375 to 0.109375
- hidden_bias: float32 [1024], replicated, may hold values from -3 to 3
- inner_weight: bfloat16 [1024, 1024], P(('level', 'img')), may hold values from -0.25 to 0.25
- inner_bias: float32 [1024], replicated, may hold values from -3 to 3
- class_weight: bfloat16 [1024, 81], P(('level', 'img')), may hold values from -0.75 to 0.75
- class_bias: float32 [81], replicated, may hold values from -3 to 3
- delta_weight: bfloat16 [1024, 320], P(('level', 'img')), may hold values from -0.375 to 0.375
- delta_bias: float32 [320], replicated, may hold values from -3 to 3
Outputs:
- logits: float32 [16, 512, 81], P('img', 'level')
- deltas: float32 [16, 512, 320], P('img', 'level')
- pyramid_grad: float32 [4, 16, 64, 16, 256], P('level', 'img')
- hidden_grad: float32 [12544, 1024], P(('level', 'img'))
- bias_hidden: float32 [1024], replicated
- inner_grad: float32 [1024, 1024], P(('level', 'img'))
- bias_inner: float32 [1024], replicated
- class_grad: float32 [1024, 81], P(('level', 'img'))
- bias_class: float32 [81], replicated
- delta_grad: float32 [1024, 320], P(('level', 'img'))
- bias_delta: float32 [320], replicated
Inputs may be any that keep to these rules, and one draw needn't show every extreme that they name: `levels`: among the 128 regions of one image that one device holds, at most 64 lie on any one level, and some image and level reach 64. `region_boxes`: each row is x0, y0, x1, y1 with 0 <= x0 < x1 <= 15 and 0 <= y0 < y1 <= 63. `labels`: 80 marks background; smaller values are foreground classes.
All inputs are finite; a program needn't handle non-finite values. No bound on the sum of `crowd_ignore` on one device may be relied on, other than what follows from the above.
Results may differ from a plain program's by a relative error of at most 0.011.
Values may be sent and summed in bfloat16 or wider, within the bound.
No kernel may reach another device: no remote copies, remote signals or barrier semaphores. Data moves between devices by JAX's collectives and lax.ppermute only.
A program may use at most 256 MiB of HBM per device.

v0:
```python
import math

import jax
import jax.numpy as jnp
from jax import lax
from jax.sharding import PartitionSpec as P

POOL = 7
SAMPLES = 2
CLS = 81
BOX = 320
RPI = 512
CAPI = 64
MICRO = 2


highest = lax.Precision.HIGHEST


def sample_weights(low_edge, high_edge, extent):
    offsets = (jnp.arange(SAMPLES * POOL, dtype=jnp.float32) + 0.5) / (SAMPLES * POOL)
    box_spans = (high_edge - low_edge).astype(jnp.float32)
    points = low_edge.astype(jnp.float32)[:, None] + offsets[None, :] * box_spans[:, None]
    centres = jnp.arange(extent, dtype=jnp.float32)
    tent_values = jnp.maximum(1.0 - jnp.abs(points[:, :, None] - centres[None, None, :]), 0.0)
    tent_values = tent_values.reshape(points.shape[0], POOL, SAMPLES, extent)
    return jnp.sum(tent_values, axis=2) / SAMPLES


def gelu_exact(values):
    return jax.nn.gelu(values, approximate=False)


def contract_rows(left_side, right_side):
    return lax.dot_general(
        left_side, right_side, (((0,), (0,)), ((), ())), preferred_element_type=jnp.float32
    )


def contract_cols(left_side, right_side):
    return lax.dot_general(
        left_side, right_side, (((1,), (1,)), ((), ())), preferred_element_type=jnp.float32
    )


def crop_slots(feature, slot_boxes):
    count = slot_boxes.shape[0]
    block = math.gcd(16, count)
    groups = slot_boxes.reshape(count // block, block, 4)

    def crop_group(box_group):
        weights_down = sample_weights(box_group[:, 1], box_group[:, 3], feature.shape[0]).astype(
            jnp.bfloat16
        )
        weights_across = sample_weights(box_group[:, 0], box_group[:, 2], feature.shape[1]).astype(
            jnp.bfloat16
        )
        partial_sum = jnp.einsum(
            "spy,yxc->spxc", weights_down, feature, preferred_element_type=jnp.float32
        )
        pooled = jnp.einsum(
            "sqx,spxc->spqc", weights_across.astype(jnp.float32), partial_sum, precision=highest
        )
        return pooled.reshape(block, -1).astype(jnp.bfloat16)

    return lax.map(crop_group, groups).reshape(count, -1)


def spread_slots(extents, slot_boxes, slot_grads):
    height, across, channels = extents
    count = slot_boxes.shape[0]
    block = math.gcd(16, count)
    box_groups = slot_boxes.reshape(count // block, block, 4)
    grad_groups = slot_grads.reshape(count // block, block, POOL, POOL, channels)

    def add_group(total, pieces):
        box_group, grad_group = pieces
        weights_down = sample_weights(box_group[:, 1], box_group[:, 3], height).astype(jnp.bfloat16)
        weights_across = sample_weights(box_group[:, 0], box_group[:, 2], across).astype(
            jnp.bfloat16
        )
        partial_sum = jnp.einsum(
            "sqx,spqc->spxc", weights_across, grad_group, preferred_element_type=jnp.float32
        )
        return (
            total
            + jnp.einsum(
                "spy,spxc->yxc", weights_down.astype(jnp.float32), partial_sum, precision=highest
            ),
            None,
        )

    start = jnp.zeros((height, across, channels), jnp.float32)
    total, unused = lax.scan(add_group, start, (box_groups, grad_groups))
    return total


def slot_table(level_rows, level_count, capacity):
    images_step, regions = level_rows.shape
    member = (
        level_rows[:, :, None] == jnp.arange(level_count, dtype=jnp.int32)[None, None, :]
    ).astype(jnp.int32)
    level_rank = jnp.sum((jnp.cumsum(member, axis=1) - 1) * member, axis=2)
    placed = member[:, :, :, None] * (
        level_rank[:, :, None, None] == jnp.arange(capacity, dtype=jnp.int32)[None, None, None, :]
    ).astype(jnp.int32)
    region_ids = (
        jnp.arange(regions, dtype=jnp.int32)[None, :, None, None]
        + regions * jnp.arange(images_step, dtype=jnp.int32)[:, None, None, None]
    )
    source = jnp.transpose(jnp.sum(placed * region_ids, axis=1), (1, 0, 2))
    filled = jnp.transpose(jnp.sum(placed, axis=1), (1, 0, 2))
    returning = (
        level_rows * (images_step * capacity)
        + jnp.arange(images_step, dtype=jnp.int32)[:, None] * capacity
        + level_rank
    )
    return (source, filled, returning.reshape(-1))


def per_device(
    pyramid,
    levels,
    region_boxes,
    labels,
    crowd_ignore,
    targets,
    hidden_weight,
    hidden_bias,
    inner_weight,
    inner_bias,
    class_weight,
    class_bias,
    delta_weight,
    delta_bias,
):
    level_count = lax.axis_size("level")
    image_count = pyramid.shape[1]
    regions = levels.shape[1]
    images_step = image_count // MICRO
    extents = pyramid.shape[2:]
    hidden_units = inner_weight.shape[1]
    class_count = class_weight.shape[1]
    summed = None
    bias_terms = (
        jnp.zeros_like(hidden_bias),
        jnp.zeros_like(inner_bias),
        jnp.zeros_like(class_bias),
        jnp.zeros_like(delta_bias),
    )
    logit_parts = []
    delta_parts = []
    grad_parts = []
    for step_index in range(MICRO):
        start_image = step_index * images_step
        gathered = (
            lax.all_gather(hidden_weight, ("level", "img"), axis=0, tiled=True),
            lax.all_gather(inner_weight, ("level", "img"), axis=0, tiled=True),
            lax.all_gather(class_weight, ("level", "img"), axis=0, tiled=True),
            lax.all_gather(delta_weight, ("level", "img"), axis=0, tiled=True),
        )
        full_hidden, full_inner, full_class, full_delta = gathered
        level_rows = levels[start_image : start_image + images_step, :, 0]
        boxes_step = region_boxes[start_image : start_image + images_step].reshape(
            images_step * regions, 4
        )
        source, filled, returning = slot_table(level_rows, level_count, CAPI)
        slot_boxes = jnp.take(boxes_step, source.reshape(-1), axis=0).reshape(
            level_count, images_step, CAPI, 4
        )
        arrived = lax.all_to_all(slot_boxes, "level", split_axis=0, concat_axis=0, tiled=True)
        pooled_slots = jnp.stack(
            [
                crop_slots(
                    pyramid[0, start_image], arrived[:, 0].reshape(level_count * CAPI, 4)
                ).reshape(level_count, CAPI, -1)
            ],
            axis=1,
        )
        returned = lax.all_to_all(pooled_slots, "level", split_axis=0, concat_axis=0, tiled=True)
        crop_rows = jnp.take(returned.reshape(-1, returned.shape[-1]), returning, axis=0)
        first_pre = (
            jnp.dot(crop_rows, full_hidden, preferred_element_type=jnp.float32) + hidden_bias
        )
        first_value, first_back = jax.vjp(gelu_exact, first_pre)
        first_act = first_value.astype(jnp.bfloat16)
        second_pre = jnp.dot(first_act, full_inner, preferred_element_type=jnp.float32) + inner_bias
        second_value, second_back = jax.vjp(gelu_exact, second_pre)
        second_act = second_value.astype(jnp.bfloat16)
        logits = jnp.dot(second_act, full_class, preferred_element_type=jnp.float32) + class_bias
        deltas = jnp.dot(second_act, full_delta, preferred_element_type=jnp.float32) + delta_bias
        logit_parts.append(logits.reshape(images_step, regions, -1))
        delta_parts.append(deltas.reshape(images_step, regions, -1))
        label_rows = labels[start_image : start_image + images_step].reshape(-1)
        kept_rows = 1.0 - crowd_ignore[start_image : start_image + images_step].reshape(-1).astype(
            jnp.float32
        )
        target_rows = targets[start_image : start_image + images_step].reshape(-1, 4)
        row_max = jnp.max(logits, axis=1, keepdims=True)
        exponent = jnp.exp(logits - row_max)
        softmax_rows = exponent / jnp.sum(exponent, axis=1, keepdims=True)
        class_hot = (label_rows[:, None] == jnp.arange(CLS, dtype=jnp.int32)[None, :]).astype(
            jnp.float32
        )
        logit_slope = ((softmax_rows - class_hot) * (kept_rows / RPI)[:, None]).astype(jnp.bfloat16)
        foreground = kept_rows * (label_rows < CLS - 1).astype(jnp.float32)
        box_hot = (label_rows[:, None] == jnp.arange(BOX // 4, dtype=jnp.int32)[None, :]).astype(
            jnp.float32
        )
        chosen_box = jnp.sum(deltas.reshape(-1, BOX // 4, 4) * box_hot[:, :, None], axis=1)
        huber_slope = jnp.clip(chosen_box - target_rows, -1.0, 1.0) * (foreground / RPI)[:, None]
        delta_slope = (
            (box_hot[:, :, None] * huber_slope[:, None, :]).reshape(-1, BOX).astype(jnp.bfloat16)
        )
        act_grad = contract_cols(logit_slope, full_class) + contract_cols(delta_slope, full_delta)
        second_grad = second_back(act_grad)[0].astype(jnp.bfloat16)
        first_grad = first_back(contract_cols(second_grad, full_inner))[0].astype(jnp.bfloat16)
        crop_grad = contract_cols(first_grad, full_hidden).astype(jnp.bfloat16)

        def hidden_rows(start, count, crop_rows=crop_rows, first_grad=first_grad):
            return contract_rows(crop_rows, first_grad)

        def rest_rows(
            start,
            count,
            first_act=first_act,
            second_act=second_act,
            second_grad=second_grad,
            logit_slope=logit_slope,
            delta_slope=delta_slope,
        ):
            return jnp.concatenate(
                [
                    contract_rows(first_act, second_grad),
                    contract_rows(second_act, logit_slope),
                    contract_rows(second_act, delta_slope),
                ],
                axis=1,
            )

        hidden_part = lax.psum_scatter(
            hidden_rows(jnp.int32(0), hidden_weight.shape[0] * lax.axis_size(("level", "img"))),
            ("level", "img"),
            scatter_dimension=0,
            tiled=True,
        )
        rest_part = lax.psum_scatter(
            rest_rows(jnp.int32(0), inner_weight.shape[0] * lax.axis_size(("level", "img"))),
            ("level", "img"),
            scatter_dimension=0,
            tiled=True,
        )
        weight_parts = (hidden_part, rest_part)
        summed = weight_parts if step_index == 0 else jax.tree.map(jnp.add, summed, weight_parts)
        bias_terms = (
            bias_terms[0] + jnp.sum(first_grad.astype(jnp.float32), axis=0),
            bias_terms[1] + jnp.sum(second_grad.astype(jnp.float32), axis=0),
            bias_terms[2] + jnp.sum(logit_slope.astype(jnp.float32), axis=0),
            bias_terms[3] + jnp.sum(delta_slope.astype(jnp.float32), axis=0),
        )
        outgoing = jnp.take(crop_grad, source.reshape(-1), axis=0).reshape(
            level_count, images_step, CAPI, -1
        ) * filled[:, :, :, None].astype(jnp.bfloat16)
        landed = lax.all_to_all(outgoing, "level", split_axis=0, concat_axis=0, tiled=True)
        grad_parts.append(
            jnp.stack(
                [
                    spread_slots(
                        extents,
                        arrived[:, 0].reshape(level_count * CAPI, 4),
                        landed[:, 0].reshape(level_count * CAPI, -1),
                    )
                ]
            )[None]
        )
    bias_total = lax.psum(
        (bias_terms[0], bias_terms[1], bias_terms[2], bias_terms[3]), ("level", "img")
    )
    rest_sum = summed[1]
    inner_sum = rest_sum[:, :hidden_units]
    class_sum = rest_sum[:, hidden_units : hidden_units + class_count]
    delta_sum = rest_sum[:, hidden_units + class_count :]
    return (
        jnp.concatenate(logit_parts, axis=0),
        jnp.concatenate(delta_parts, axis=0),
        jnp.concatenate(grad_parts, axis=1),
        summed[0],
        bias_total[0],
        inner_sum,
        bias_total[1],
        class_sum,
        bias_total[2],
        delta_sum,
        bias_total[3],
    )


def solution(mesh):
    return jax.shard_map(
        per_device,
        mesh=mesh,
        in_specs=(
            P("level", "img", None, None, None),
            P("img", "level", None),
            P("img", "level", None),
            P("img", "level"),
            P("img", "level"),
            P("img", "level", None),
            P(("level", "img"), None),
            P(),
            P(("level", "img"), None),
            P(),
            P(("level", "img"), None),
            P(),
            P(("level", "img"), None),
            P(),
        ),
        out_specs=(
            P("img", "level", None),
            P("img", "level", None),
            P("level", "img", None, None, None),
            P(("level", "img"), None),
            P(),
            P(("level", "img"), None),
            P(),
            P(("level", "img"), None),
            P(),
            P(("level", "img"), None),
            P(),
        ),
        check_vma=False,
    )
```

profile of v0, /device:TPU:14, one launch (start us, length us, event | category | flops | bytes accessed | tf_op | source)
XLA Modules:
  0.0 1445.0 jit_solution(10763088198474588370)
XLA Ops:
  13.2 5.3 all-to-all-start
  22.7 4.7 all-to-all-start.2
  29.0 2.4 all-to-all-done.2
  32.4 3.1 broadcast.947.clone
  35.4 64.9 %while.43 = (s32[]{:T(128)}, bf16[16,16,12544]{2,1,0:T(8,128)(2,1)}, s32[16,16,4]{1,2,0:T(4,128)S(1)}, bf16[64,16,256]{2,0,1:T(8,128)(2,1)S(1)}, s32[]{:T(128)}) while((s32[]{:T(128)}, bf16[16,16,12544]{2,1,0:T(8,128)(2,1)}, s32[16,16,4]{1,2,0:T(4,128)S(1)}, bf16[64,16,256]{2,0,1:T(8,128)(2,1)S(1)}, s32[]{:T(128)}) %tuple.156), condition=%wide.region_13.16_spmd, body=%wide.region_10.15_spmd.sunk | while | flops 97555736 | bytes 6285245 | solution.py:66
  101.0 6.6 all-to-all-start.3
  107.6 3.0 broadcast.947.clone.1
  110.6 64.8 %while.42 = (s32[]{:T(128)}, bf16[16,16,12544]{2,1,0:T(8,128)(2,1)}, s32[16,16,4]{1,2,0:T(4,128)S(1)}, bf16[64,16,256]{2,0,1:T(8,128)(2,1)S(1)}, s32[]{:T(128)}) while((s32[]{:T(128)}, bf16[16,16,12544]{2,1,0:T(8,128)(2,1)}, s32[16,16,4]{1,2,0:T(4,128)S(1)}, bf16[64,16,256]{2,0,1:T(8,128)(2,1)S(1)}, s32[]{:T(128)}) %tuple.159), condition=%wide.region_6.8_spmd, body=%wide.region_3.7_spmd.sunk | while | flops 97555736 | bytes 6285245 | solution.py:66
  175.4 122.8 %all-to-all-done.3 = bf16[4,1,64,12544]{3,2,1,0:T(8,128)(2,1)} async-done(((bf16[4,1,64,12544]{3,2,1,0:T(8,128)(2,1)}), bf16[4,1,64,12544]{3,2,1,0:T(8,128)(2,1)}, u32[]{:S(2)}, u32[]{:S(2)}) %all-to-all-start.3) | async-done | bytes 6422560 | tf_op jit(solution)/shard_map/all_to_all | solution.py:180
  298.2 8.8 all-to-all-start.1
  307.8 173.2 %all_gather.18 = bf16[1024,81]{1,0:T(8,128)(2,1)S(1)} all-gather(bf16[32,81]{1,0:T(8,128)(2,1)S(1)} %copy-done.27), channel_id=1, replica_groups=mesh['level'=4,'img'=8] {'level','img'}, dimensions={0}, use_global_device_ids=true | all-gather | bytes 171072 | tf_op jit(solution)/shard_map/all_gather | solution.py:159
  481.1 32.9 %all_gather.19 = bf16[1024,320]{1,0:T(8,128)(2,1)S(1)} all-gather(bf16[32,320]{1,0:T(8,128)(2,1)S(1)} %copy-done.23), channel_id=1, replica_groups=mesh['level'=4,'img'=8] {'level','img'}, dimensions={0}, use_global_device_ids=true | all-gather | bytes 675840 | tf_op jit(solution)/shard_map/all_gather | solution.py:160
  514.0 10.7 gather_fusion.3
  524.8 11.0 gather_fusion.1
  535.8 14.9 %multiply_convert_fusion.9 = (bf16[128,1024]{1,0:T(8,128)(2,1)S(1)}, f32[128,1024]{1,0:T(8,128)}, f32[128,1024]{1,0:T(8,128)}) fusion(f32[1024]{0:T(1024)S(1)} %copy-done.42, bf16[12544,1024]{1,0:T(8,128)(2,1)} %all-gather.3.cloned.1.call-done, bf16[128,12544]{1,0:T(8,128)(2,1)} %gather_fusion.3, pred[128]{0:T(512)(128)(4,1)S(1)} %get-tuple-element.328), kind=kOutput, calls=%fused_computation.160 | convolution fusion | flops 3298590720 | bytes 30216320 | tf_op jit(solution)/shard_map/dot_general | solution.py:183
  550.7 3.2 multiply_convert_fusion.8
  554.2 14.2 multiply_convert_fusion.11
  577.5 2.7 fusion.129
  582.0 2.8 fusion.127
  584.8 14.6 %concatenate.19 = f32[1024,1425]{0,1:T(8,128)} concatenate(f32[1024,1024]{0,1:T(8,128)} %fusion.129, f32[1024,81]{0,1:T(8,128)S(1)} %fusion.130, f32[1024,320]{0,1:T(8,128)S(1)} %fusion.132), dimensions={1} | concatenate | bytes 11673600 | tf_op jit(solution)/shard_map/concatenate | solution.py:232
  599.4 14.7 %concatenate.18 = f32[1024,1425]{0,1:T(8,128)} concatenate(f32[1024,1024]{0,1:T(8,128)} %fusion.127, f32[1024,81]{0,1:T(8,128)S(1)} %fusion.128, f32[1024,320]{0,1:T(8,128)S(1)} %fusion.131), dimensions={1} | concatenate | bytes 11673600 | tf_op jit(solution)/shard_map/concatenate | solution.py:232
  614.1 9.0 add.339
  623.1 6.4 copy.115
  631.2 3.4 convert_reduce_fusion.3
  636.2 23.7 %fusion.66 = f32[12544,1024]{1,0:T(8,128)} fusion(bf16[128,1024]{1,0:T(8,128)(2,1)} %get-tuple-element.275, bf16[128,12544]{1,0:T(8,128)(2,1)} %gather_fusion.1, pred[128]{0:T(512)(128)(4,1)S(1)} %get-tuple-element.280), kind=kOutput, calls=%fused_computation.114 | convolution fusion | flops 3289939968 | bytes 54853760 | tf_op jit(solution)/shard_map/dot_general | solution.py:35
  659.9 36.7 %convolution_add_fusion = f32[12544,1024]{1,0:T(8,128)} fusion(f32[12544,1024]{1,0:T(8,128)} %fusion.66, bf16[128,1024]{1,0:T(8,128)(2,1)S(1)} %get-tuple-element.273, bf16[128,12544]{1,0:T(8,128)(2,1)S(1)} %copy-done.2, pred[128]{0:T(512)(128)(4,1)S(1)} %get-tuple-element.328), kind=kOutput, calls=%fused_computation.104 | convolution fusion | flops 3302785024 | bytes 106233984 | tf_op jit(solution)/shard_map/dot_general | solution.py:35
  697.3 13.7 convolution_convert_fusion.1
  711.0 7.6 gather_fusion.4
  718.7 3.5 broadcast_select_fusion.1
  722.2 3.2 broadcast_multiply_fusion.1
  725.4 7.0 all-to-all-start.4
  733.2 13.3 convolution_convert_fusion
  746.6 7.7 gather_fusion.5
  755.7 252.9 %all-reduce = (f32[1024]{0:T(1024)}, f32[1024]{0:T(1024)}, f32[81]{0:T(128)}, f32[320]{0:T(512)}) all-reduce(f32[1024]{0:T(1024)S(1)} %add.326, f32[1024]{0:T(1024)S(1)} %add.328, f32[81]{0:T(128)S(1)} %add.329, f32[320]{0:T(512)S(1)} %add.331), channel_id=1, replica_groups=mesh['level'=4,'img'=8] {'level','img'}, use_global_device_ids=true, to_apply=%region_34.38 | all-reduce | flops 2449 | bytes 19592 | tf_op jit(solution)/shard_map/psum | solution.py:276
  1009.3 3.5 broadcast_select_fusion
  1012.8 3.2 broadcast_multiply_fusion
  1020.5 8.6 all-to-all-start.5
  1029.1 14.1 reshape_reshape_squeeze.16
  1043.2 77.2 %while.44 = (s32[]{:T(128)}, f32[64,16,256]{2,0,1:T(8,128)S(1)}, s32[16,16,4]{1,2,0:T(4,128)}, bf16[16,16,7,7,256]{4,3,2,1,0:T(8,128)(2,1)}, s32[]{:T(128)}, /*index=5*/s32[]{:T(128)}) while((s32[]{:T(128)}, f32[64,16,256]{2,0,1:T(8,128)S(1)}, s32[16,16,4]{1,2,0:T(4,128)}, bf16[16,16,7,7,256]{4,3,2,1,0:T(8,128)(2,1)}, ...), condition=%wide.region_21.25_spmd.clone, body=%wide.region_18.24_spmd.clone.sunk | while | flops 359367968 | bytes 6309839 | solution.py:94
  1050.5 2.3 fusion.222
  1055.3 2.3 fusion.222
  1060.2 2.3 fusion.222
  1065.0 2.3 fusion.222
  1074.7 2.3 fusion.222
  1079.5 2.3 fusion.222
  1084.3 2.3 fusion.222
  1089.1 2.3 fusion.222
  1094.0 2.3 fusion.222
  1098.8 2.3 fusion.222
  1103.6 2.3 fusion.222
  1108.4 2.3 fusion.222
  1118.1 2.3 fusion.222
  1121.1 86.6 %all-to-all-done.5 = bf16[4,1,64,12544]{3,2,1,0:T(8,128)(2,1)} async-done(((bf16[4,1,64,12544]{3,2,1,0:T(8,128)(2,1)}), bf16[4,1,64,12544]{3,2,1,0:T(8,128)(2,1)}, u32[]{:S(2)}, u32[]{:S(2)}) %all-to-all-start.5) | async-done | bytes 6422560 | tf_op jit(solution)/shard_map/all_to_all | solution.py:264
  1207.7 14.0 reshape_reshape_squeeze.17
  1221.7 77.3 %while.45 = (s32[]{:T(128)}, f32[64,16,256]{2,0,1:T(8,128)S(1)}, s32[16,16,4]{1,2,0:T(4,128)}, bf16[16,16,7,7,256]{4,3,2,1,0:T(8,128)(2,1)}, s32[]{:T(128)}, /*index=5*/s32[]{:T(128)}) while((s32[]{:T(128)}, f32[64,16,256]{2,0,1:T(8,128)S(1)}, s32[16,16,4]{1,2,0:T(4,128)}, bf16[16,16,7,7,256]{4,3,2,1,0:T(8,128)(2,1)}, ...), condition=%wide.region_29.33_spmd.clone, body=%wide.region_26.32_spmd.clone.sunk | while | flops 359367968 | bytes 6309839 | solution.py:94
  1224.2 2.3 fusion.228
  1233.8 2.3 fusion.228
  1248.4 2.3 fusion.228
  1253.2 2.3 fusion.228
  1267.7 2.3 fusion.228
  1272.5 2.3 fusion.228
  1291.8 2.3 fusion.228
  1296.6 2.3 fusion.228
  1301.1 136.9 %reduce-scatter.5.cloned.1.call-done = f32[392,1024]{1,0:T(8,128)} async-done(((f32[12544,1024]{1,0:T(8,128)}), f32[392,1024]{1,0:T(8,128)}) %reduce-scatter.5.cloned.1.call-update) | async-done | bytes 1605648 | tf_op jit(solution)/shard_map/reduce_scatter | solution.py:241
  (815 shorter events, 271.3 us)
Async XLA Ops:
  7.2 12.3 copy-start.10
  7.2 528.6 %all-gather.3.cloned.1.call-start = ((), (), s32[]{:S(2)}) async-start(), calls=%async_computation.8 | async-start | bytes 26492928 | tf_op jit(solution)/shard_map/all_gather | solution.py:157
  10.2 9.3 copy-start.37
  11.0 0.6 copy-start.25
  13.2 9.5 all-to-all-start
  19.4 8.0 copy-start.36
  19.5 7.8 copy-start.24
  22.7 8.8 all-to-all-start.2
  100.3 0.6 copy-start.21
  101.0 197.2 %all-to-all-start.3 = ((bf16[4,1,64,12544]{3,2,1,0:T(8,128)(2,1)}), bf16[4,1,64,12544]{3,2,1,0:T(8,128)(2,1)}, u32[]{:S(2)}, u32[]{:S(2)}) async-start(bf16[4,1,64,12544]{3,2,1,0:T(8,128)(2,1)} %bitcast.272), calls=%async_computation.3 | async-start | bytes 12845056 | tf_op jit(solution)/shard_map/all_to_all | solution.py:180
  175.4 122.8 %copy-start.22 = (s32[16,16,4]{1,2,0:T(4,128)}, s32[16,16,4]{1,2,0:T(4,128)S(1)}, u32[]{:S(2)}) copy-start(s32[16,16,4]{1,2,0:T(4,128)S(1)} %get-tuple-element.587) | copy-start | bytes 12292
  298.2 9.6 copy-start.27
  298.2 182.8 %copy-start.33 = (s32[2,128,1]{1,2,0:T(1,128)S(1)}, s32[2,128,1]{1,2,0:T(1,128)}, u32[]{:S(2)}) copy-start(s32[2,128,1]{1,2,0:T(1,128)} %param.29) | copy-start | bytes 3076
  298.2 182.9 %copy-start.34 = (s32[2,128]{1,0:T(2,128)S(1)}, s32[2,128]{1,0:T(2,128)}, u32[]{:S(2)}) copy-start(s32[2,128]{1,0:T(2,128)} %param.31) | copy-start | bytes 3076
  298.2 182.9 %copy-start.39 = (s32[2,128]{1,0:T(2,128)S(1)}, s32[2,128]{1,0:T(2,128)}, u32[]{:S(2)}) copy-start(s32[2,128]{1,0:T(2,128)} %param.32) | copy-start | bytes 3076
  298.2 182.9 %copy-start.23 = (bf16[32,320]{1,0:T(8,128)(2,1)S(1)}, bf16[32,320]{1,0:T(8,128)(2,1)}, u32[]{:S(2)}) copy-start(bf16[32,320]{1,0:T(8,128)(2,1)} %param.40) | copy-start | bytes 61444
  298.2 226.6 %all-to-all-start.1 = ((bf16[4,1,64,12544]{3,2,1,0:T(8,128)(2,1)}), bf16[4,1,64,12544]{3,2,1,0:T(8,128)(2,1)}, u32[]{:S(2)}, u32[]{:S(2)}) async-start(bf16[4,1,64,12544]{3,2,1,0:T(8,128)(2,1)} %bitcast.271), calls=%async_computation.1 | async-start | bytes 12845056 | tf_op jit(solution)/shard_map/all_to_all | solution.py:180
  307.0 243.7 %all-gather.5.cloned.1.call-start = ((), (), s32[]{:S(2)}) async-start(), calls=%async_computation.9 | async-start | bytes 2162688 | tf_op jit(solution)/shard_map/all_gather | solution.py:158
  307.7 708.3 %reduce-scatter.7.cloned.1.call-start = ((), (), s32[]{:S(2)}) async-start(), calls=%async_computation.11 | async-start | bytes 6488064
  481.0 89.2 %copy-start.4 = (bf16[1024,81]{1,0:T(8,128)(2,1)}, bf16[1024,81]{1,0:T(8,128)(2,1)S(1)}, u32[]{:S(2)}) copy-start(bf16[1024,81]{1,0:T(8,128)(2,1)S(1)} %all_gather.18) | copy-start | bytes 497668
  524.8 11.0 copy-start.42
  535.8 14.9 %copy-start.43 = (f32[1024]{0:T(1024)S(1)}, f32[1024]{0:T(1024)}, u32[]{:S(2)}) copy-start(f32[1024]{0:T(1024)} %param.37) | copy-start | bytes 12292
  550.6 3.2 copy-start.13
  550.6 3.2 copy-start.35
  550.7 3.5 copy-start.3
  554.2 14.2 copy-start.40
  568.4 2.1 copy-start.26
  570.2 1.4 copy-start.32
  570.5 5.1 copy-start.11
  571.0 1.5 copy-start.6
  571.4 1.0 copy-start.8
  572.8 3.7 copy-start.5
  574.0 3.6 copy-start.14
  577.5 3.8 copy-start.15
  581.3 0.7 copy-start.17
  629.5 0.9 copy-start.18
  629.5 1.7 copy-start.41
  629.5 5.1 copy-start.16
  629.6 5.1 copy-start.44
  629.6 808.5 %reduce-scatter.5.cloned.1.call-start = ((), (), s32[]{:S(2)}) async-start(), calls=%async_computation.10 | async-start | bytes 52985856 | tf_op jit(solution)/shard_map/reduce_scatter | solution.py:241
  629.8 4.8 copy-start.45
  636.2 23.7 %copy-start.2 = (bf16[128,12544]{1,0:T(8,128)(2,1)S(1)}, bf16[128,12544]{1,0:T(8,128)(2,1)}, u32[]{:S(2)}) copy-start(bf16[128,12544]{1,0:T(8,128)(2,1)} %gather_fusion.3) | copy-start | bytes 9633796
  696.6 0.7 copy-start.28
  711.0 7.6 copy-start.38
  725.4 7.0 copy-start.29
  725.4 7.0 copy-start.12
  725.4 7.7 copy-start.19
  725.4 7.7 copy-start.20
  725.4 295.0 %all-to-all-start.4 = ((bf16[4,1,64,12544]{3,2,1,0:T(8,128)(2,1)}), bf16[4,1,64,12544]{3,2,1,0:T(8,128)(2,1)}, u32[]{:S(2)}, u32[]{:S(2)}) async-start(bf16[4,1,64,12544]{3,2,1,0:T(8,128)(2,1)} %broadcast_multiply_fusion.1), calls=%async_computation.4 | async-start | bytes 12845056 | tf_op jit(solution)/shard_map/all_to_all | solution.py:264
  746.6 8.4 copy-start.30
  746.6 8.4 copy-start.31
  746.6 261.9 %copy-start.7 = (f32[128,320]{0,1:T(8,128)S(1)}, f32[128,320]{0,1:T(8,128)}, u32[]{:S(2)}) copy-start(f32[128,320]{0,1:T(8,128)} %copy-done.6) | copy-start | bytes 491524
  746.6 261.9 %copy-start.9 = (f32[128,320]{0,1:T(8,128)S(1)}, f32[128,320]{0,1:T(8,128)}, u32[]{:S(2)}) copy-start(f32[128,320]{0,1:T(8,128)} %copy-done.8) | copy-start | bytes 491524
  1020.5 187.2 %all-to-all-start.5 = ((bf16[4,1,64,12544]{3,2,1,0:T(8,128)(2,1)}), bf16[4,1,64,12544]{3,2,1,0:T(8,128)(2,1)}, u32[]{:S(2)}, u32[]{:S(2)}) async-start(bf16[4,1,64,12544]{3,2,1,0:T(8,128)(2,1)} %broadcast_multiply_fusion), calls=%async_computation.5 | async-start | bytes 12845056 | tf_op jit(solution)/shard_map/all_to_all | solution.py:264
  1029.1 14.1 copy-start.1
  1121.1 100.6 %copy-start = (f32[64,16,256]{2,0,1:T(8,128)S(1)}, f32[64,16,256]{2,0,1:T(8,128)}, u32[]{:S(2)}) copy-start(f32[64,16,256]{2,0,1:T(8,128)} %custom-call.1) | copy-start | bytes 3145732
Sparse Core Ops, SparseCore 0:
  10.9 208.4 all-gather.2
  310.7 131.1 all-gather.4
  629.7 150.3 reduce-scatter.6
  782.9 655.0 reduce-scatter.4
where the time goes:
time: 1460 us; the launch traced here: 1450 us
  blocking collectives  459 us (31%)
  waiting for transfers between devices  352 us (24%)
  matrix products  337 us (23%)
  local copies, waits for them, and re-layouts  185 us (13%)
  other arithmetic  52.9 us (4%)
  starting transfers between devices  41.2 us (3%)
  between operations  14.8 us (1%)
    psum x1, blocking collectives, per_device(): lax.psum((bias_terms[0], bias_terms[1], bias_terms[2], bias_terms[3]), ('...  253 us
    all_gather x1, blocking collectives, per_device(): lax.all_gather(class_weight, ('level', 'img'), axis=0, tiled=True)  173 us
    reduce_scatter x1, waiting for transfers between devices, per_device(): lax.psum_scatter(hidden_rows(jnp.int32(0), hidden_weight.shape[0] * lax.a...  137 us
    all_to_all x2, waiting for transfers between devices, per_device(): lax.all_to_all(pooled_slots, 'level', split_axis=0, concat_axis=0, tiled=...  123 us
    all_to_all x2, waiting for transfers between devices, per_device(): lax.all_to_all(outgoing, 'level', split_axis=0, concat_axis=0, tiled=True)  86.6 us
    dot_general x32, matrix products, add_group(): jnp.einsum('spy,spxc->yxc', weights_down.astype(jnp.float32), partial_sum...  74.3 us
    dot_general x8, matrix products, contract_rows(): lax.dot_general(left_side, right_side, (((0,), (0,)), ((), ())), preferre...  67 us
    dot_general x32, matrix products, crop_group(): jnp.einsum('sqx,spxc->spqc', weights_across.astype(jnp.float32), partial_...  66.4 us
  transfers between devices with their start and end apart: 10, of which 5 were waited for; matrix products, arithmetic and copies ran while one was open for 34% of the time, Pallas kernels for 0%

commit v1 on v0

v1 whole, which is shorter than its diff:
```python
import functools

import jax
import jax.numpy as jnp
import numpy as np
from jax import lax
from jax.experimental import pallas as pl
from jax.experimental.pallas import tpu as pltpu
from jax.sharding import PartitionSpec as P

POOL = 7
SAMPLES = 2
CLS = 81
BOX = 320
RPI = 512
BINS = POOL * POOL
LANES = 128
AXES = ("level", "img")
OFFSETS = (np.arange(SAMPLES * POOL, dtype=np.float32) + np.float32(0.5)) / np.float32(
    SAMPLES * POOL
)
SMALL_COST = pl.CostEstimate(flops=10**9, bytes_accessed=1, transcendentals=0)
LARGE_COST = pl.CostEstimate(flops=4 * 10**10, bytes_accessed=1, transcendentals=0)
f32 = jnp.float32
bf16 = jnp.bfloat16
ANY = pl.BlockSpec(memory_space=pl.ANY)
WHOLE = pl.BlockSpec(memory_space=pltpu.VMEM)
SCALAR = pl.BlockSpec(memory_space=pltpu.SMEM)
like = jax.ShapeDtypeStruct


def bin_weights(low, span, centres, at):
    first = jnp.maximum(1.0 - jnp.abs((low + OFFSETS[2 * at] * span) - centres), 0.0)
    second = jnp.maximum(1.0 - jnp.abs((low + OFFSETS[2 * at + 1] * span) - centres), 0.0)
    return ((first + second) * 0.5).astype(bf16)


def fill_weights(box_ref, down_ref, across_ref, height, width, level_count):
    x0, y0, x1, y1, level = [box_ref[k : k + 1, :] for k in range(5)]
    centres = lax.broadcasted_iota(jnp.int32, (width, LANES), 0).astype(f32)
    for q in range(POOL):
        across_ref[q] = bin_weights(x0, x1 - x0, centres, q).astype(f32)
    centres = lax.broadcasted_iota(jnp.int32, (height, LANES), 0).astype(f32)
    for p in range(POOL):
        weights = bin_weights(y0, y1 - y0, centres, p).astype(f32)
        for k in range(level_count):
            down_ref[k * height : (k + 1) * height, p * LANES : (p + 1) * LANES] = jnp.where(
                level == float(k), weights, 0.0
            ).astype(bf16)


def runs_of(order, length, part, group, room):
    place = {chunk: at // group * room + at % group * length for at, chunk in enumerate(order)}
    table = []
    for at in range(BINS):
        row, end, runs = at * part, (at + 1) * part, []
        while row < end:
            chunk = row // length
            stop = min(end, (chunk + 1) * length)
            runs.append((row - at * part, place[chunk] + row - chunk * length, stop - row))
            row = stop
        table.append(runs)
    return table


def gaps_of(table, features):
    held = sorted((kept, kept + count) for runs in table for row, kept, count in runs)
    gaps, last = [], 0
    for first, end in held + [(features, features)]:
        if first > last:
            gaps.append((last, first))
        last = end
    return gaps


def fetch_pieces(seat_ref, piece_refs, kept_ref, sems):
    rows = piece_refs[0].shape[0]
    return [
        pltpu.make_async_copy(
            ref, kept_ref.at[pl.ds(pl.multiple_of((seat_ref[0] ^ k) * rows, 16), rows)], sems.at[k]
        )
        for k, ref in enumerate(piece_refs)
    ]


def crop_kernel(table, sizes, number, at_ref, seat_ref, box_ref, maps_ref, *refs):
    piece_refs, refs = refs[:number], refs[number:]
    if number:
        crop_ref, out_ref, down_ref, across_ref, sums_ref, rows_ref, turned_ref, kept_ref, sems = refs[-9:]
        copies = fetch_pieces(seat_ref, piece_refs, kept_ref, sems)

        @pl.when(pl.program_id(0) == 0)
        def start():
            for copy in copies:
                copy.start()
    else:
        crop_ref, out_ref, down_ref, across_ref, sums_ref, rows_ref = refs[-6:]
    height, width, part, level_count = sizes
    for first, end in gaps_of(table, rows_ref.shape[0]):
        rows_ref[first:end, :] = jnp.zeros((end - first, LANES), f32)
    fill_weights(box_ref, down_ref, across_ref, height, width, level_count)
    sums_ref[...] = jnp.dot(maps_ref[...], down_ref[...], preferred_element_type=f32)
    for p in range(POOL):
        lanes = slice(p * LANES, (p + 1) * LANES)
        for start in range(0, POOL, 2):
            bins = range(start, min(POOL, start + 2))
            totals = [None for q in bins]
            for x in range(width):
                piece = sums_ref[x * part : (x + 1) * part, lanes]
                for at, q in enumerate(bins):
                    term = across_ref[q, x : x + 1, :] * piece
                    totals[at] = term if x == 0 else totals[at] + term
            for at, q in enumerate(bins):
                for row, kept, count in table[p * POOL + q]:
                    rows_ref[kept : kept + count, :] = totals[at][row : row + count]
    crop = rows_ref[...].astype(bf16)
    crop_ref[...] = crop
    if not number:
        out_ref[...] = crop.T
        return
    turned_ref[pl.ds(pl.multiple_of(pl.program_id(0) * LANES, LANES), LANES), :] = crop.T

    @pl.when(pl.program_id(0) == pl.num_programs(0) - 1)
    def multiply():
        for copy in copies:
            copy.wait()
        out_ref[...] = jnp.dot(
            turned_ref[...], kept_ref[...], preferred_element_type=f32
        ).astype(out_ref.dtype)


def spread_kernel(table, sizes, number, seat_ref, box_ref, grad_ref, held_ref, *refs):
    piece_refs = refs[:number]
    total_ref, down_ref, across_ref, sums_ref, rows_ref, crop_ref, kept_ref, sems = refs[-8:]
    height, width, part, level_count = sizes
    images = box_ref.shape[0]
    copies = fetch_pieces(seat_ref, piece_refs, kept_ref, sems)
    for copy in copies:
        copy.start()
    for n in range(images):
        fill_weights(
            box_ref.at[n], down_ref.at[n], across_ref.at[n], height, width, level_count
        )
    for copy in copies:
        copy.wait()
    crop_ref[...] = lax.dot_general(
        kept_ref[...], grad_ref[...], (((1,), (1,)), ((), ())), preferred_element_type=f32
    ).astype(bf16)
    for n in range(images):
        rows_ref[...] = crop_ref[:, n * LANES : (n + 1) * LANES].astype(f32)
        for p in range(POOL):
            lanes = slice(p * LANES, (p + 1) * LANES)
            pieces = []
            for q in range(POOL):
                runs = [rows_ref[kept : kept + count, :] for row, kept, count in table[p * POOL + q]]
                pieces.append(runs[0] if len(runs) == 1 else jnp.concatenate(runs, axis=0))
            for x in range(width):
                total = across_ref[n, 0, x : x + 1, :] * pieces[0]
                for q in range(1, POOL):
                    total = total + across_ref[n, q, x : x + 1, :] * pieces[q]
                sums_ref[x * part : (x + 1) * part, lanes] = total.astype(bf16)
        total_ref[n] = held_ref[n] + lax.dot_general(
            sums_ref[...], down_ref[n], (((1,), (1,)), ((), ())), preferred_element_type=f32
        )


def crop_block(table, sizes, features, boxes, maps, at, count, held, seat, weight=(), out_type=bf16, earlier=()):
    height, width, part, level_count = sizes
    images = boxes.shape[0]
    number = len(weight)
    operands = [boxes, maps, *weight] + ([] if held is None else [held])
    place = len(operands) + 1
    operands += earlier
    rows = images * LANES
    if number:
        units = weight[0].shape[1]
        out_spec = pl.BlockSpec((rows, units), lambda n, *at: (0, 0))
        out_shape = like((rows, units), out_type)
        more = [
            pltpu.VMEM((rows, features), bf16),
            pltpu.VMEM((features, units), bf16),
            pltpu.SemaphoreType.DMA((number,)),
        ]
    else:
        out_spec = pl.BlockSpec((LANES, features), lambda n, *at: (n, 0))
        out_shape = like((rows, features), bf16)
        more = []
    return pl.pallas_call(
        functools.partial(crop_kernel, table, sizes, number),
        grid_spec=pltpu.PrefetchScalarGridSpec(
            num_scalar_prefetch=2,
            grid=(images,),
            in_specs=[
                pl.BlockSpec((None, 8, LANES), lambda n, *at: (n, 0, 0)),
                pl.BlockSpec((None, width * part, level_count * height), lambda n, *at: (n, 0, 0)),
            ]
            + [ANY for one in operands[2:]],
            out_specs=[
                pl.BlockSpec((features, LANES), lambda n, at, seat: (0, at[0] * images + n)),
                out_spec,
            ],
            scratch_shapes=[
                pltpu.VMEM((level_count * height, POOL * LANES), bf16),
                pltpu.VMEM((POOL, width, LANES), f32),
                pltpu.VMEM((width * part, POOL * LANES), f32),
                pltpu.VMEM((features, LANES), f32),
            ]
            + more,
        ),
        out_shape=[like((features, count * images * LANES), bf16), out_shape],
        input_output_aliases={} if held is None else {place: 0},
        compiler_params=pltpu.CompilerParams(vmem_limit_bytes=48 * 2**20),
        cost_estimate=LARGE_COST,
        name="crop_block",
    )(jnp.full((1,), at, jnp.int32), seat, *operands)


def multiply_kernel(number, seat_ref, rows_ref, *refs):
    out_ref, kept_ref, sems = refs[-3:]
    copies = fetch_pieces(seat_ref, refs[:number], kept_ref, sems)
    for copy in copies:
        copy.start()
    for copy in copies:
        copy.wait()
    out_ref[...] = jnp.dot(rows_ref[...], kept_ref[...], preferred_element_type=f32).astype(
        out_ref.dtype
    )


def multiply_block(rows, seat, weight):
    units = weight[0].shape[1]
    return pl.pallas_call(
        functools.partial(multiply_kernel, len(weight)),
        in_specs=[SCALAR, WHOLE] + [ANY for one in weight],
        out_specs=WHOLE,
        out_shape=like((rows.shape[0], units), bf16),
        scratch_shapes=[
            pltpu.VMEM((rows.shape[1], units), bf16),
            pltpu.SemaphoreType.DMA((len(weight),)),
        ],
        compiler_params=pltpu.CompilerParams(vmem_limit_bytes=48 * 2**20),
        cost_estimate=LARGE_COST,
        name="multiply_block",
    )(seat, rows, *weight)


def spread_block(table, sizes, features, boxes, grads, seat, weight, held, earlier=()):
    height, width, part, level_count = sizes
    images = boxes.shape[0]
    units = grads.shape[1]
    return pl.pallas_call(
        functools.partial(spread_kernel, table, sizes, len(weight)),
        in_specs=[SCALAR, WHOLE, WHOLE, WHOLE] + [ANY for one in (*weight, *earlier)],
        out_specs=WHOLE,
        out_shape=like((images, width * part, level_count * height), f32),
        scratch_shapes=[
            pltpu.VMEM((images, level_count * height, POOL * LANES), bf16),
            pltpu.VMEM((images, POOL, width, LANES), f32),
            pltpu.VMEM((width * part, POOL * LANES), bf16),
            pltpu.VMEM((features, LANES), f32),
            pltpu.VMEM((features, images * LANES), bf16),
            pltpu.VMEM((features, units), bf16),
            pltpu.SemaphoreType.DMA((len(weight),)),
        ],
        compiler_params=pltpu.CompilerParams(vmem_limit_bytes=48 * 2**20),
        cost_estimate=LARGE_COST,
        name="spread_block",
    )(seat, boxes, grads, held, *weight, *earlier)


def call(kernel, outs, scalars, arrays, earlier=(), alias=None, name=None):
    arrays = list(arrays)

    def body(*refs):
        at, end = len(scalars), len(scalars) + len(arrays)
        kernel(refs[:at], refs[at:end], refs[end + len(earlier) :])

    result = pl.pallas_call(
        body,
        in_specs=[SCALAR for one in scalars] + [WHOLE for one in arrays] + [ANY for one in earlier],
        out_specs=[WHOLE for one in outs],
        out_shape=outs,
        compiler_params=pltpu.CompilerParams(vmem_limit_bytes=48 * 2**20),
        cost_estimate=SMALL_COST,
        name=name,
    )(*[jnp.full((1,), one, jnp.int32) for one in scalars], *arrays, *earlier)
    return result


def tie_kernel(*refs):
    pass


def tie(array, *earlier):
    return pl.pallas_call(
        tie_kernel,
        in_specs=[ANY for one in (array, *earlier)],
        out_specs=ANY,
        out_shape=like(array.shape, array.dtype),
        input_output_aliases={0: 0},
        cost_estimate=SMALL_COST,
        name="tie",
    )(array, *earlier)


def order_kernel(scalars, arrays, outs):
    for k, ref in enumerate(arrays):
        outs[0][scalars[0][0] ^ k] = ref[...]


def in_order(at, arrays, earlier):
    shape = (len(arrays),) + arrays[0].shape
    return call(order_kernel, [like(shape, arrays[0].dtype)], [at], arrays, earlier, name="in_order")[0]


def full_small_kernel(rows, scalars, arrays, outs):
    units = outs[0].shape[1]
    for k, ref in enumerate(arrays):
        core = scalars[0][0] ^ k
        for y in range(2):
            for x in range(2):
                for level in range(ref.shape[2]):
                    at = pl.multiple_of((((level * 2 + y) * 2 + x) * 2 + core) * rows, rows)
                    outs[0][pl.ds(at, rows), :] = ref[y, x, level, :rows, :]
                    for part in range(2):
                        outs[1][pl.ds(at + part * (rows // 2), rows // 2), :] = ref[
                            y, x, level, rows:, part * (units // 2) : (part + 1) * (units // 2)
                        ]


def split_rows(core, array, rows, sent, kept):
    for at in range(kept.shape[0] // rows):
        mine = pl.multiple_of((2 * at + core) * rows, rows)
        other = pl.multiple_of((2 * at + 1 - core) * rows, rows)
        kept[at * rows : (at + 1) * rows, :] = array[pl.ds(mine, rows), :].astype(bf16)
        sent[at * rows : (at + 1) * rows, :] = array[pl.ds(other, rows), :].astype(bf16)


def small_product_kernel(rows, core_ref, first_ref, second_grad_ref, second_ref, slopes_ref, sent_ref, kept_ref, total_ref):
    turned = (((0,), (0,)), ((), ()))
    units = first_ref.shape[1]
    total_ref[:, :units] = lax.dot_general(
        first_ref[...], second_grad_ref[...], turned, preferred_element_type=f32
    )
    total_ref[:, units:] = lax.dot_general(
        second_ref[...], slopes_ref[...], turned, preferred_element_type=f32
    )
    split_rows(core_ref[0], total_ref, rows, sent_ref, kept_ref)


def small_product(core, rows, first_act, second_grad, second_act, slopes):
    units = first_act.shape[1]
    wide = units + slopes.shape[1]
    half = like((units // 2, wide), bf16)
    return pl.pallas_call(
        functools.partial(small_product_kernel, rows),
        in_specs=[SCALAR] + [WHOLE] * 4,
        out_specs=[WHOLE] * 2,
        out_shape=[half, half],
        scratch_shapes=[pltpu.VMEM((units, wide), f32)],
        compiler_params=pltpu.CompilerParams(vmem_limit_bytes=48 * 2**20),
        cost_estimate=SMALL_COST,
        name="small_product",
    )(jnp.full((1,), core, jnp.int32), first_act, second_grad, second_act, slopes)


def fold_kernel(rows, bit_ref, kept_ref, come_ref, *refs):
    sent_out, kept_out, total_ref = refs[-3:]
    total_ref[...] = kept_ref[...].astype(f32) + come_ref[...].astype(f32)
    split_rows(bit_ref[0], total_ref, rows, sent_out, kept_out)


def fold_rows(bit, rows, kept, come, earlier):
    half = like((kept.shape[0] // 2, kept.shape[1]), bf16)
    return pl.pallas_call(
        functools.partial(fold_kernel, rows),
        in_specs=[SCALAR, WHOLE, WHOLE] + [ANY for one in earlier],
        out_specs=[WHOLE] * 2,
        out_shape=[half, half],
        scratch_shapes=[pltpu.VMEM(kept.shape, f32)],
        compiler_params=pltpu.CompilerParams(vmem_limit_bytes=48 * 2**20),
        cost_estimate=SMALL_COST,
        name="fold_rows",
    )(jnp.full((1,), bit, jnp.int32), kept, come, *earlier)


def last_fold_kernel(rows, scalars, arrays, outs):
    units = outs[0].shape[1]
    for way, out in enumerate(outs):
        at = pl.multiple_of((scalars[0][0] ^ way) * rows, rows)
        total = sum(ref[pl.ds(at, rows), :].astype(f32) for ref in arrays).astype(bf16)
        out[:rows, :] = total[:, :units]
        for part in range(2):
            out[rows:, part * (units // 2) : (part + 1) * (units // 2)] = total[
                part * (rows // 2) : (part + 1) * (rows // 2), units:
            ]


def small_sum_kernel(scalars, arrays, outs):
    total = sum(ref[...].astype(f32) for ref in arrays)
    rows, units = outs[0].shape
    outs[0][...] = total[:rows]
    for part in range(2):
        at = slice(part * (rows // 2), (part + 1) * (rows // 2))
        beside = total[rows:, part * (units // 2) : (part + 1) * (units // 2)]
        outs[1][at, :] = beside[:, :CLS]
        outs[2][at, :] = beside[:, LANES : LANES + BOX]


def gelu_and_slope(values):
    normal = 0.5 * (1.0 + lax.erf(values * np.float32(np.sqrt(0.5))))
    density = jnp.exp(-0.5 * values * values) * np.float32(1.0 / np.sqrt(2.0 * np.pi))
    return values * normal, normal + values * density


def head_kernel(
    own_ref, one_ref, two_ref, three_ref, rows_ref, hidden_bias_ref, inner_ref, inner_bias_ref, heads_ref, heads_bias_ref,
    logits_ref, deltas_ref, first_act_ref, second_act_ref, slopes_ref, second_grad_ref, first_grad_ref, again_ref, bias_ref, first_slope_ref, second_slope_ref,
):
    first_pre = own_ref[...] + hidden_bias_ref[...]
    for come_ref in (one_ref, two_ref, three_ref):
        first_pre = first_pre + come_ref[...].astype(f32)
    act, slope = gelu_and_slope(first_pre)
    first_slope_ref[...] = slope
    act = act.astype(bf16)
    first_act_ref[...] = act
    second_pre = jnp.dot(act, inner_ref[...], preferred_element_type=f32) + inner_bias_ref[...]
    act, slope = gelu_and_slope(second_pre)
    second_slope_ref[...] = slope
    act = act.astype(bf16)
    second_act_ref[...] = act
    heads = jnp.dot(act, heads_ref[...], preferred_element_type=f32) + heads_bias_ref[...]
    logits, deltas = heads[:, :LANES], heads[:, LANES:]
    logits_ref[...] = logits[:, :CLS]
    deltas_ref[...] = deltas[:, :BOX]
    label = rows_ref[:, 0:1]
    kept = 1.0 - rows_ref[:, 1:2]
    column = lax.broadcasted_iota(jnp.int32, logits.shape, 1)
    valid = column < CLS
    row_max = jnp.max(jnp.where(valid, logits, -jnp.inf), axis=1, keepdims=True)
    exponent = jnp.where(valid, jnp.exp(jnp.where(valid, logits - row_max, 0.0)), 0.0)
    softmax_rows = exponent / jnp.sum(exponent, axis=1, keepdims=True)
    hot = (column.astype(f32) == label).astype(f32)
    logit_slope = (softmax_rows - hot) * (kept * np.float32(1.0 / RPI))
    column = lax.broadcasted_iota(jnp.int32, deltas.shape, 1)
    target = rows_ref[:, 2:3]
    for j in range(1, 4):
        target = jnp.where((column & 3) == j, rows_ref[:, 2 + j : 3 + j], target)
    foreground = jnp.where(label < CLS - 1, kept, 0.0)
    hot = ((column >> 2).astype(f32) == label) & (column < BOX)
    delta_slope = jnp.where(
        hot,
        jnp.clip(deltas - target, -1.0, 1.0) * (foreground * np.float32(1.0 / RPI)),
        0.0,
    )
    slopes = jnp.concatenate([logit_slope, delta_slope], axis=1).astype(bf16)
    slopes_ref[...] = slopes
    turned = (((1,), (1,)), ((), ()))
    act_grad = lax.dot_general(slopes, heads_ref[...], turned, preferred_element_type=f32)
    second_grad = (act_grad * second_slope_ref[...]).astype(bf16)
    second_grad_ref[...] = second_grad
    act_grad = lax.dot_general(second_grad, inner_ref[...], turned, preferred_element_type=f32)
    first_grad = (act_grad * first_slope_ref[...]).astype(bf16)
    first_grad_ref[...] = first_grad
    again_ref[...] = first_grad
    units = first_grad.shape[1]
    bias_ref[...] = jnp.zeros_like(bias_ref)
    bias_ref[0:1, :] = jnp.sum(first_grad.astype(f32), axis=0, keepdims=True)
    bias_ref[1:2, :] = jnp.sum(second_grad.astype(f32), axis=0, keepdims=True)
    bias_ref[2:3, : slopes.shape[1]] = jnp.sum(slopes.astype(f32), axis=0, keepdims=True)


def head_block(own, come, rows, hidden_bias, inner, inner_bias, heads, heads_bias):
    count, units = own.shape
    wide = heads.shape[1]
    return pl.pallas_call(
        head_kernel,
        in_specs=[pl.BlockSpec(memory_space=pltpu.VMEM)] * 10,
        out_specs=[pl.BlockSpec(memory_space=pltpu.VMEM)] * 9,
        out_shape=[
            like((count, CLS), f32),
            like((count, BOX), f32),
            like((count, units), bf16),
            like((count, units), bf16),
            like((count, wide), bf16),
            like((count, units), bf16),
            like((count, units), bf16),
            like((count, units), bf16),
            like((8, units), f32),
        ],
        scratch_shapes=[pltpu.VMEM((count, units), f32)] * 2,
        compiler_params=pltpu.CompilerParams(vmem_limit_bytes=48 * 2**20),
        cost_estimate=LARGE_COST,
        name="head_block",
    )(own, *come, rows, hidden_bias, inner, inner_bias, heads, heads_bias)


def arrange_kernel(sizes, came_ref, maps_ref):
    height, width, part, level_count = sizes
    for x in range(width):
        for k in range(level_count):
            maps_ref[x * part : (x + 1) * part, k * height : (k + 1) * height] = came_ref[
                k, :, x * height : (x + 1) * height
            ]


def arrange(sizes, came):
    height, width, part, level_count = sizes
    images = came.shape[1]
    return pl.pallas_call(
        functools.partial(arrange_kernel, sizes),
        grid=(images,),
        in_specs=[
            pl.BlockSpec((level_count, None, part, width * height), lambda n: (0, n, 0, 0))
        ],
        out_specs=pl.BlockSpec((None, width * part, level_count * height), lambda n: (n, 0, 0)),
        out_shape=jax.ShapeDtypeStruct((images, width * part, level_count * height), bf16),
        name="arrange",
    )(came)


def return_kernel(sizes, total_ref, sent_ref):
    height, width, part, level_count = sizes
    for x in range(width):
        for k in range(level_count):
            sent_ref[k, :, x * height : (x + 1) * height] = total_ref[
                x * part : (x + 1) * part, k * height : (k + 1) * height
            ].astype(bf16)


def arrange_back(sizes, total):
    height, width, part, level_count = sizes
    images = total.shape[0]
    return pl.pallas_call(
        functools.partial(return_kernel, sizes),
        grid=(images,),
        in_specs=[pl.BlockSpec((None, width * part, level_count * height), lambda n: (n, 0, 0))],
        out_specs=pl.BlockSpec((level_count, None, part, width * height), lambda n: (0, n, 0, 0)),
        out_shape=jax.ShapeDtypeStruct((level_count, images, part, width * height), bf16),
        name="arrange_back",
    )(total)


def picking(rows, columns, pairs):
    matrix = np.zeros((rows, columns), np.float32)
    for a, b in pairs:
        matrix[a, b] = 1.0
    return jnp.asarray(matrix, bf16)


def reorder(matrix, array, out_type=bf16):
    return jnp.dot(matrix, array, preferred_element_type=f32).astype(out_type)


def swap(array, axis, bit):
    size = lax.axis_size(axis)
    return lax.ppermute(array, axis, [(at, at ^ bit) for at in range(size)])


def exchange(array, axis):
    return lax.all_to_all(array, axis, split_axis=0, concat_axis=0, tiled=True)


def gather_pieces(piece):
    near = [piece] + [swap(piece, "img", bit) for bit in (2, 4, 6)]
    pieces = []
    for one in near:
        pieces += [one, swap(one, "img", 1)]
    return pieces


def product_kernel(number, with_sum, at_ref, grad_ref, *refs):
    crop_refs, refs = refs[:number], refs[number:]
    outs = refs[-number:] if with_sum else [refs[-1].at[n] for n in range(number)]
    for n in range(number):
        total = jnp.dot(crop_refs[n][...], grad_ref[...], preferred_element_type=f32)
        if with_sum:
            total = total + refs[0][n].astype(f32)
        outs[n][...] = total.astype(bf16)


def piece_product(crops, grads, pieces, come, earlier):
    features, count = crops.shape
    units = grads.shape[1]
    rows = features // 8
    number = pieces.shape[0]
    with_sum = come is not None
    crops = crops.reshape(8, rows, count)
    single = pl.BlockSpec((rows, units), lambda n, at: (0, 0))
    stacked = pl.BlockSpec((number, rows, units), lambda n, at: (0, 0, 0))
    return pl.pallas_call(
        functools.partial(product_kernel, number, with_sum),
        grid_spec=pltpu.PrefetchScalarGridSpec(
            num_scalar_prefetch=1,
            grid=(1,),
            in_specs=[pl.BlockSpec((count, units), lambda n, at: (0, 0))]
            + [
                pl.BlockSpec((None, rows, count), lambda n, at, k=k: (at[k], 0, 0))
                for k in range(number)
            ]
            + ([stacked] if with_sum else [])
            + [ANY for one in earlier],
            out_specs=[single] * number if with_sum else stacked,
        ),
        out_shape=[like((rows, units), bf16)] * number
        if with_sum
        else like((number, rows, units), bf16),
        compiler_params=pltpu.CompilerParams(vmem_limit_bytes=48 * 2**20),
        cost_estimate=LARGE_COST,
        name="piece_product",
    )(pieces, grads, *[crops] * number, *([come] if with_sum else []), *earlier)


def scatter_product(crops, grads, place, earlier):
    pairs = ((6, 2), (4, 0))
    others = []
    for bits in pairs:
        pieces = jnp.stack([place ^ bit ^ 1 for bit in bits])
        products = piece_product(crops, grads, pieces, None, earlier)
        earlier = [products]
        others.append(swap(products, "img", 1))
    parts = []
    for bits, other in zip(pairs, others):
        pieces = jnp.stack([place ^ bit for bit in bits])
        sums = piece_product(crops, grads, pieces, other, earlier)
        earlier = sums
        parts += [swap(one, "img", bit) if bit else one for one, bit in zip(sums, bits)]
    return parts, earlier


def butterfly(array):
    for axis in ("img", "level"):
        bit = 1
        while bit < lax.axis_size(axis):
            array = array + swap(array, axis, bit)
            bit *= 2
    return array


def contract_rows(left_side, right_side):
    return lax.dot_general(
        left_side, right_side, (((0,), (0,)), ((), ())), preferred_element_type=f32
    )


def contract_cols(left_side, right_side):
    return lax.dot_general(
        left_side, right_side, (((1,), (1,)), ((), ())), preferred_element_type=f32
    )


def pack_rows(array):
    rows, units = array.shape[-2], array.shape[-1] // 3 * 2
    beside = array[..., units:]
    below = jnp.concatenate([beside[..., : rows // 2, :], beside[..., rows // 2 :, :]], axis=-1)
    return jnp.concatenate([array[..., :units], below], axis=-2)


def per_device(
    pyramid,
    levels,
    region_boxes,
    labels,
    crowd_ignore,
    targets,
    hidden_weight,
    hidden_bias,
    inner_weight,
    inner_bias,
    class_weight,
    class_bias,
    delta_weight,
    delta_bias,
):
    size = lax.axis_size("level")
    planes = lax.axis_size("img")
    z = lax.axis_index("level")
    place = lax.axis_index("img")
    core, x, y = place % 2, place // 2 % 2, place // 4
    images, height, width, channels = pyramid.shape[1:]
    regions = levels.shape[1]
    part = channels // size
    sizes = (height, width, part, size)
    rows, units = hidden_weight.shape
    block_rows = images * regions
    direct = planes == 8 and rows % size == 0

    packed = jnp.concatenate(
        [
            jnp.transpose(region_boxes, (0, 2, 1)),
            jnp.transpose(levels, (0, 2, 1)),
            jnp.zeros((images, 3, regions), jnp.int32),
        ],
        axis=1,
    )
    class_room, delta_room = LANES, units // 2 - LANES
    small = jnp.concatenate(
        [
            inner_weight,
            jnp.pad(class_weight, ((0, 0), (0, class_room - CLS))),
            jnp.pad(delta_weight, ((0, 0), (0, delta_room - BOX))),
        ],
        axis=1,
    )
    heads_bias = jnp.concatenate(
        [
            jnp.pad(class_bias, (0, class_room - CLS)),
            jnp.pad(delta_bias, (0, delta_room - BOX)),
        ]
    )[None]

    if direct:
        length = rows // size
        pad = -(-(length + images) // 8) * 8
        small_rows = small.shape[0] // 2 * 3
        span = pad
        extra = jnp.concatenate(
            [packed.astype(bf16).reshape(images, units), jnp.zeros((16 - images, units), bf16)]
        )
        to_span = picking(
            size * span,
            rows,
            [(k * span + j, j * size + k) for k in range(size) for j in range(length)],
        )
        extra_span = picking(
            size * span,
            16,
            [(k * span + length + n, n) for k in range(size) for n in range(images)],
        )
        room = -(-rows // 16) * 16
        features = planes * room
        from_span = picking(
            room,
            size * span,
            [(k * length + j, k * span + j) for k in range(size) for j in range(length)],
        )
        sent = (
            jnp.dot(to_span, hidden_weight, preferred_element_type=f32)
            + jnp.dot(extra_span, extra, preferred_element_type=f32)
        ).astype(bf16)
        came = exchange(sent.reshape(size, span, units), "level")
        boxes = came[:, length : length + images].reshape(size, images, 8, regions).astype(f32)
        piece = reorder(from_span, came.reshape(size * span, units))
        weight = gather_pieces(piece)
        seat = jnp.full((1,), place, jnp.int32)
        order = [k * planes + at for at in range(planes) for k in range(size)]
        table = runs_of(order, length, part, size, room)
    else:
        boxes = exchange(jnp.broadcast_to(packed[None], (size,) + packed.shape), "level").astype(f32)
        features = BINS * part
        whole = lax.all_gather(hidden_weight, AXES, axis=0, tiled=True)
        weight = [lax.dynamic_index_in_dim(whole.reshape(features, size, units), z, 1, False)]
        seat = jnp.zeros((1,), jnp.int32)
        table = runs_of([0], features, part, 1, features)

    spots = height * width
    by_class = picking(
        channels, channels, [(c % size * part + c // size, c) for c in range(channels)]
    )
    across_first = picking(
        spots, spots, [(y * width + x, x * height + y) for y in range(height) for x in range(width)]
    )
    maps = []
    for n in range(images):
        flat = pyramid[0, n].reshape(spots, channels)
        flat = contract_cols(by_class, flat).astype(bf16)
        maps.append(reorder(flat, across_first).reshape(size, part, spots))
    maps = jnp.stack(maps, axis=1)
    if direct:
        maps = tie(maps, piece)
    maps_came = exchange(maps, "level")
    maps = arrange(sizes, maps_came)

    ways = (2, 3, 1, 0)
    crops, owns, came_sums = None, [], []
    for turn, way in enumerate(ways):
        at = lax.dynamic_index_in_dim(boxes, z ^ way, 0, False)
        if turn == 0:
            crops, crop = crop_block(
                table, sizes, features, at, maps, turn, size, crops, seat
            )
            owns.append(multiply_block(crop, seat, weight))
        else:
            crops, own = crop_block(
                table,
                sizes,
                features,
                at,
                maps,
                turn,
                size,
                crops,
                seat,
                weight,
                bf16 if way else f32,
                owns[-1:],
            )
            owns.append(own)
        if way:
            came_sums.append(swap(owns[-1], "level", way))

    if direct:
        smalls = tie(pack_rows(small), maps_came)
        smalls = [smalls] + [swap(smalls, "level", way) for way in (1, 2, 3)]
        smalls = in_order(z, smalls, owns[:1])
        smalls = in_order(x, [smalls, swap(smalls, "img", 2)], owns[1:2])
        smalls = in_order(y, [smalls, swap(smalls, "img", 4)], owns[2:3])
        full_inner, full_heads = call(
            functools.partial(full_small_kernel, small.shape[0]),
            [like((units, units), bf16), like((units, units // 2), bf16)],
            [core],
            [smalls, swap(smalls, "img", 1)],
            name="full_small",
        )
    else:
        smalls = lax.all_gather(small, AXES, axis=0, tiled=True)
        full_inner, full_heads = smalls[:, :units], smalls[:, units:]

    row_facts = jnp.concatenate(
        [
            labels.reshape(-1, 1).astype(f32),
            crowd_ignore.reshape(-1, 1).astype(f32),
            targets.reshape(-1, 4),
            jnp.zeros((block_rows, 2), f32),
        ],
        axis=1,
    )
    logits, deltas, first_act, second_act, slopes, second_grad, first_grad, first_again, bias_sums = head_block(
        owns[-1],
        came_sums,
        row_facts,
        hidden_bias[None],
        full_inner,
        inner_bias[None],
        full_heads,
        heads_bias,
    )

    near = swap(first_grad, "level", 1)
    far = swap(first_grad, "level", 2)
    farthest = swap(tie(first_again, far), "level", 3)
    grad_of = {0: first_grad, 1: near, 2: far, 3: farthest}
    whole_grads = jnp.concatenate([grad_of[way] for way in ways])

    def take_up(way, held, earlier=()):
        at = lax.dynamic_index_in_dim(boxes, z ^ way, 0, False)
        return spread_block(table, sizes, features, at, grad_of[way], seat, weight, held, earlier)

    held = jnp.zeros((images, width * part, size * height), f32)
    if direct:
        count = small.shape[0]
        sent, kept = small_product(core, count, first_act, second_grad, second_act, slopes)
        held = take_up(0, held, [kept])
        sent, kept = fold_rows(x, count, kept, swap(sent, "img", 1), [held])
        held = take_up(1, held, [kept])
        sent, kept = fold_rows(y, count, kept, swap(sent, "img", 2), [held])
        held = take_up(2, held, [kept])
        smalls = call(
            functools.partial(last_fold_kernel, count),
            [like((small_rows, units), bf16)] * size,
            [z],
            [kept, swap(sent, "img", 4)],
            [held],
            name="last_fold",
        )
        parts, earlier = scatter_product(crops, whole_grads, place, smalls[:1])
        held = take_up(3, held, earlier)
    else:
        for way in range(size):
            held = take_up(way, held)
        small_sum = jnp.concatenate(
            [contract_rows(first_act, second_grad), contract_rows(second_act, slopes)], axis=1
        )
        small_sum = lax.psum_scatter(small_sum, AXES, scatter_dimension=0, tiled=True)
        product = jnp.dot(crops, whole_grads, preferred_element_type=f32)
        own = (jnp.arange(size, dtype=jnp.int32) == z)[None, :, None]
        hidden_sum = lax.psum_scatter(
            jnp.where(own, product[:, None, :], 0.0).reshape(features * size, units),
            AXES,
            scatter_dimension=0,
            tiled=True,
        )

    back = arrange_back(sizes, held)
    if direct:
        smalls = [smalls[0]] + [swap(smalls[way], "level", way) for way in (1, 2, 3)]
        inner_sum, class_sum, delta_sum = call(
            small_sum_kernel,
            [like((count, units), f32), like((count, CLS), f32), like((count, BOX), f32)],
            [],
            smalls,
            [back],
            name="small_sum",
        )
    else:
        inner_sum = small_sum[:, :units]
        class_sum = small_sum[:, units : units + CLS]
        delta_sum = small_sum[:, units + class_room : units + class_room + BOX]
    back = exchange(back, "level").reshape(size, images, part, spots)
    map_grads = []
    for n in range(images):
        flat = contract_cols(across_first, back[:, n].reshape(channels, spots)).astype(bf16)
        map_grads.append(jnp.dot(flat, by_class, preferred_element_type=f32))
    map_grads = jnp.stack(map_grads).reshape(1, images, height, width, channels)

    if direct:
        piece = sum(part.astype(f32) for part in parts).astype(bf16)
        sent = contract_rows(from_span, piece).astype(bf16).reshape(size, span, units)
        bias_sums = tie(bias_sums, sent)
        came = exchange(sent, "level").reshape(size * span, units)
        hidden_sum = contract_rows(to_span, came)

    bias_total = butterfly(bias_sums)
    head_bias = bias_total[2, : class_room + delta_room]
    return (
        logits.reshape(images, regions, -1),
        deltas.reshape(images, regions, -1),
        map_grads,
        hidden_sum,
        bias_total[0],
        inner_sum,
        bias_total[1],
        class_sum,
        head_bias[:CLS],
        delta_sum,
        head_bias[class_room : class_room + BOX],
    )


def solution(mesh):
    return jax.shard_map(
        per_device,
        mesh=mesh,
        in_specs=(
            P("level", "img", None, None, None),
            P("img", "level", None),
            P("img", "level", None),
            P("img", "level"),
            P("img", "level"),
            P("img", "level", None),
            P(AXES, None),
            P(),
            P(AXES, None),
            P(),
            P(AXES, None),
            P(),
            P(AXES, None),
            P(),
        ),
        out_specs=(
            P("img", "level", None),
            P("img", "level", None),
            P("level", "img", None, None, None),
            P(AXES, None),
            P(),
            P(AXES, None),
            P(),
            P(AXES, None),
            P(),
            P(AXES, None),
            P(),
        ),
        check_vma=False,
    )
```

time: 1460 us -> 357 us (0.24)
  the two profiles are of different devices: /device:TPU:14 before, /device:TPU:0 now
where the time goes in v1:
time: 357 us; the launch traced here: 353 us
  Pallas kernels  135 us (38%)
  waiting for transfers between devices  102 us (29%)
  starting transfers between devices  61.8 us (17%)
  local copies, waits for them, and re-layouts  22.6 us (6%)
  matrix products  21.3 us (6%)
  other arithmetic  8.01 us (2%)
    ppermute x35, waiting for transfers between devices, swap(): return lax.ppermute(array, axis, [(at, at ^ bit) for at in range(size)])  80 us
    pallas_call x4, Pallas kernels, spread_block(): pl.pallas_call(functools.partial(spread_kernel, table, sizes, len(weight)...  56.8 us
    ppermute x35, starting transfers between devices, swap(): return lax.ppermute(array, axis, [(at, at ^ bit) for at in range(size)])  40.9 us
    pallas_call x4, Pallas kernels, crop_block(): pl.pallas_call(functools.partial(crop_kernel, table, sizes, number), grid...  39.9 us
    all_to_all x4, waiting for transfers between devices, exchange(): return lax.all_to_all(array, axis, split_axis=0, concat_axis=0, tiled=True)  22.1 us
    all_to_all x4, starting transfers between devices, exchange(): return lax.all_to_all(array, axis, split_axis=0, concat_axis=0, tiled=True)  20.9 us
    pallas_call x4, Pallas kernels, piece_product(): pl.pallas_call(functools.partial(product_kernel, number, with_sum), grid_...  16.7 us
    unnamed x118, local copies, waits for them, and re-layouts  16.1 us
  transfers between devices with their start and end apart: 39, of which 12 were waited for; matrix products, arithmetic and copies ran while one was open for 9% of the time, Pallas kernels for 36%

profile of v1, /device:TPU:0, one launch (start us, length us, event | category | flops | bytes accessed | tf_op | source)
XLA Modules:
  0.0 353.0 jit_solution(15545059566925705725)
XLA Ops:
  2.3 1.6 fusion.12
  3.9 1.3 add_convert_fusion
  5.2 6.4 %all-to-all-start = ((bf16[4,104,1024]{2,1,0:T(8,128)(2,1)}), bf16[4,104,1024]{2,1,0:T(8,128)(2,1)S(1)}, u32[]{:S(2)}, u32[]{:S(2)}) async-start(bf16[4,104,1024]{2,1,0:T(8,128)(2,1)} %bitcast.3), calls=%async_computation | async-start | bytes 1703936 | tf_op jit(solution)/shard_map/all_to_all | solution.py:561
  12.5 2.6 convolution_convert_fusion.6
  15.2 2.5 convolution_convert_fusion.7
  18.8 14.4 %all-to-all-done = bf16[4,104,1024]{2,1,0:T(8,128)(2,1)S(1)} async-done(((bf16[4,104,1024]{2,1,0:T(8,128)(2,1)}), bf16[4,104,1024]{2,1,0:T(8,128)(2,1)S(1)}, u32[]{:S(2)}, u32[]{:S(2)}) %all-to-all-start) | async-done | bytes 852000 | tf_op jit(solution)/shard_map/all_to_all | solution.py:561
  33.2 1.5 fusion.refs_1_.refs_0_
  34.7 3.8 %all-to-all-start.1 = ((bf16[4,2,64,1024]{3,2,1,0:T(8,128)(2,1)}), bf16[4,2,64,1024]{3,2,1,0:T(8,128)(2,1)S(1)}, u32[]{:S(2)}, u32[]{:S(2)}) async-start(bf16[4,2,64,1024]{3,2,1,0:T(8,128)(2,1)} %tie.4), calls=%async_computation.1 | async-start | bytes 2097152 | tf_op jit(solution)/shard_map/all_to_all | solution.py:561
  38.8 1.5 collective-permute-start.1
  40.3 1.5 collective-permute-start.3
  44.2 15.8 %collective-permute-done.1.refs_2_ = bf16[400,1024]{1,0:T(8,128)(2,1)S(1)} collective-permute-done((bf16[400,1024]{1,0:T(8,128)(2,1)S(1)}, bf16[400,1024]{1,0:T(8,128)(2,1)S(1)}, u32[]{:S(2)}, u32[]{:S(2)}) %collective-permute-start.1) | collective-permute-done | bytes 819232 | tf_op jit(solution)/shard_map/ppermute | solution.py:557
  60.0 16.9 %collective-permute-done.3.refs_4_ = bf16[400,1024]{1,0:T(8,128)(2,1)} collective-permute-done((bf16[400,1024]{1,0:T(8,128)(2,1)S(1)}, bf16[400,1024]{1,0:T(8,128)(2,1)}, u32[]{:S(2)}, u32[]{:S(2)}) %collective-permute-start.3) | collective-permute-done | bytes 819232 | tf_op jit(solution)/shard_map/ppermute | solution.py:557
  78.4 1.7 collective-permute-start.10
  80.1 2.6 arrange.1.maps_ref
  83.9 7.1 %crop_block.4 = (bf16[3200,1024]{1,0:T(8,128)(2,1)}, bf16[256,3200]{1,0:T(8,128)(2,1)S(1)}) custom-call(s32[1]{0:T(128)} %constant.92.clone.1.at_ref, s32[1]{0:T(128)} %bitcast.seat_ref, f32[2,8,128]{2,1,0:T(8,128)S(1)} %get-tuple-element.124.box_ref, bf16[2,1024,256]{2,1,0:T(8,128)(2,1)S(1)} %copy-done.5), custom_call_target="tpu_custom_call" | custom-call | flops 40000000000 | bytes 1 | tf_op jit(solution)/shard_map/crop_block/pallas_call | solution.py:188
  92.2 2.4 collective-permute-start.11
  94.9 5.9 %multiply_block.1.refs_9_.refs_5_ = bf16[256,1024]{1,0:T(8,128)(2,1)S(1)} custom-call(s32[1]{0:T(128)} %bitcast.seat_ref, bf16[256,3200]{1,0:T(8,128)(2,1)} %copy-done.37, bf16[400,1024]{1,0:T(8,128)(2,1)S(1)} %copy-done.19, bf16[400,1024]{1,0:T(8,128)(2,1)} %collective-permute-done.refs_1_, bf16[400,1024]{1,0:T(8,128)(2,1)S(1)} %collective-permute-done.1.refs_2_, ...), custom_call_target="tpu_custom_call" | custom-call | flops 40000000000 | bytes 1 | tf_op jit(solution)/shard_map/multiply_block/pallas_call | solution.py:232
  100.8 1.8 collective-permute-start.7
  103.4 10.6 %crop_block.5 = (bf16[3200,1024]{1,0:T(8,128)(2,1)}, bf16[256,1024]{1,0:T(8,128)(2,1)S(1)}) custom-call(s32[1]{0:T(128)} %constant.90.clone.1.at_ref, s32[1]{0:T(128)} %bitcast.seat_ref, f32[2,8,128]{2,1,0:T(8,128)S(1)} %get-tuple-element.125.box_ref, bf16[2,1024,256]{2,1,0:T(8,128)(2,1)} %arrange.1.maps_ref, ...), custom_call_target="tpu_custom_call", output_to_operand_aliasing={{0}: (12, {})} | custom-call | flops 40000000000 | bytes 1 | tf_op jit(solution)/shard_map/crop_block/pallas_call | solution.py:188
  114.1 2.8 collective-permute-start.8
  118.1 10.8 %crop_block.6 = (bf16[3200,1024]{1,0:T(8,128)(2,1)}, bf16[256,1024]{1,0:T(8,128)(2,1)S(1)}) custom-call(s32[1]{0:T(128)} %constant.88.clone.1.at_ref, s32[1]{0:T(128)} %bitcast.seat_ref, f32[2,8,128]{2,1,0:T(8,128)S(1)} %get-tuple-element.126.box_ref, bf16[2,1024,256]{2,1,0:T(8,128)(2,1)} %arrange.1.maps_ref, ...), custom_call_target="tpu_custom_call", output_to_operand_aliasing={{0}: (12, {})} | custom-call | flops 40000000000 | bytes 1 | tf_op jit(solution)/shard_map/crop_block/pallas_call | solution.py:188
  129.8 4.9 %collective-permute-done.14.refs_2_ = bf16[2,4,48,1024]{3,2,1,0:T(8,128)(2,1)S(1)} collective-permute-done((bf16[2,4,48,1024]{3,2,1,0:T(8,128)(2,1)S(1)}, bf16[2,4,48,1024]{3,2,1,0:T(8,128)(2,1)S(1)}, u32[]{:S(2)}, u32[]{:S(2)}) %collective-permute-start.14) | collective-permute-done | bytes 786464 | tf_op jit(solution)/shard_map/ppermute | solution.py:557
  134.8 11.3 %crop_block.7 = (bf16[3200,1024]{1,0:T(8,128)(2,1)}, f32[256,1024]{1,0:T(8,128)}) custom-call(s32[1]{0:T(128)} %constant.82.clone.1.at_ref, s32[1]{0:T(128)} %bitcast.seat_ref, f32[2,8,128]{2,1,0:T(8,128)S(1)} %get-tuple-element.127.box_ref, bf16[2,1024,256]{2,1,0:T(8,128)(2,1)} %arrange.1.maps_ref, ...), custom_call_target="tpu_custom_call", output_to_operand_aliasing={{0}: (12, {})} | custom-call | flops 40000000000 | bytes 1 | tf_op jit(solution)/shard_map/crop_block/pallas_call | solution.py:188
  146.2 1.6 full_small.1
  148.9 4.5 %head_block.1 = (f32[256,81]{1,0:T(8,128)S(1)}, f32[256,320]{1,0:T(8,128)S(1)}, bf16[256,1024]{1,0:T(8,128)(2,1)S(1)}, bf16[256,1024]{1,0:T(8,128)(2,1)S(1)}, bf...) custom-call(f32[256,1024]{1,0:T(8,128)S(1)} %copy-done.38, ...), custom_call_target="tpu_custom_call" | custom-call | flops 40000000000 | bytes 1 | tf_op jit(solution)/shard_map/head_block/pallas_call | solution.py:476
  155.6 2.1 collective-permute-start.16
  158.7 2.5 small_product.1
  162.3 19.7 %collective-permute-done.16.refs_1_.grad_ref = bf16[256,1024]{1,0:T(8,128)(2,1)S(1)} collective-permute-done((bf16[256,1024]{1,0:T(8,128)(2,1)S(1)}, bf16[256,1024]{1,0:T(8,128)(2,1)S(1)}, u32[]{:S(2)}, u32[]{:S(2)}) %collective-permute-start.16) | collective-permute-done | bytes 524320 | tf_op jit(solution)/shard_map/ppermute | solution.py:557
  182.8 1.9 collective-permute-start.17
  184.7 1.5 broadcast_in_dim.48.held_ref
  186.2 14.2 %spread_block.4.refs_0_.held_ref = f32[2,1024,256]{2,1,0:T(8,128)} custom-call(s32[1]{0:T(128)} %bitcast.seat_ref, f32[2,8,128]{2,1,0:T(8,128)S(1)} %get-tuple-element.127.box_ref, bf16[256,1024]{1,0:T(8,128)(2,1)S(1)} %get-tuple-element.59.grad_ref, f32[2,1024,256]{2,1,0:T(8,128)} %broadcast_in_dim.48.held_ref, bf16[400,1024]{1,0:T(8,128)(2,1)S(1)} %copy-done.21, ...), custom_call_target="tpu_custom_call" | custom-call | flops 40000000000 | bytes 1 | tf_op jit(solution)/shard_map/spread_block/pallas_call | solution.py:251
  200.5 1.3 constant_dynamic-update-slice_fusion.1
  204.0 14.3 %spread_block.5.refs_0_.held_ref = f32[2,1024,256]{2,1,0:T(8,128)} custom-call(s32[1]{0:T(128)} %bitcast.seat_ref, f32[2,8,128]{2,1,0:T(8,128)S(1)} %get-tuple-element.126.box_ref, bf16[256,1024]{1,0:T(8,128)(2,1)} %collective-permute-done.18.grad_ref, f32[2,1024,256]{2,1,0:T(8,128)} %spread_block.4.refs_0_.held_ref, bf16[400,1024]{1,0:T(8,128)(2,1)S(1)} %copy-done.21, ...), custom_call_target="tpu_custom_call" | custom-call | flops 40000000000 | bytes 1 | tf_op jit(solution)/shard_map/spread_block/pallas_call | solution.py:251
  218.4 2.8 collective-permute-done.20.come_ref
  221.1 1.6 copy-done.31
  223.0 2.1 collective-permute-start.21
  225.2 14.2 %spread_block.6.refs_3_.held_ref = f32[2,1024,256]{2,1,0:T(8,128)} custom-call(s32[1]{0:T(128)} %bitcast.seat_ref, f32[2,8,128]{2,1,0:T(8,128)S(1)} %copy-done.18, bf16[256,1024]{1,0:T(8,128)(2,1)S(1)} %copy-done.9, f32[2,1024,256]{2,1,0:T(8,128)} %spread_block.5.refs_0_.held_ref, bf16[400,1024]{1,0:T(8,128)(2,1)S(1)} %copy-done.21, ...), custom_call_target="tpu_custom_call" | custom-call | flops 40000000000 | bytes 1 | tf_op jit(solution)/shard_map/spread_block/pallas_call | solution.py:251
  239.4 1.6 copy-done.34
  241.1 3.8 %piece_product.4.refs_2_ = bf16[2,400,1024]{2,1,0:T(8,128)(2,1)S(1)} custom-call(s32[2]{0:T(128)S(1)} %pad_add_fusion.2.at_ref, bf16[1024,1024]{1,0:T(8,128)(2,1)S(1)} %constant_dynamic-update-slice_fusion.grad_ref, bf16[8,400,1024]{2,1,0:T(8,128)(2,1)} %bitcast.99, bf16[8,400,1024]{2,1,0:T(8,128)(2,1)} %bitcast.100, ...), custom_call_target="tpu_custom_call" | custom-call | flops 40000000000 | bytes 1 | tf_op jit(solution)/shard_map/piece_product/pallas_call | solution.py:591
  245.0 3.8 %piece_product.5.refs_3_ = bf16[2,400,1024]{2,1,0:T(8,128)(2,1)S(1)} custom-call(s32[2]{0:T(128)S(1)} %get-tuple-element.128.at_ref, bf16[1024,1024]{1,0:T(8,128)(2,1)S(1)} %constant_dynamic-update-slice_fusion.grad_ref, bf16[8,400,1024]{2,1,0:T(8,128)(2,1)} %bitcast.101, bf16[8,400,1024]{2,1,0:T(8,128)(2,1)} %bitcast.102, ...), custom_call_target="tpu_custom_call" | custom-call | flops 40000000000 | bytes 1 | tf_op jit(solution)/shard_map/piece_product/pallas_call | solution.py:591
  249.4 4.4 %piece_product.6 = (bf16[400,1024]{1,0:T(8,128)(2,1)S(1)}, bf16[400,1024]{1,0:T(8,128)(2,1)S(1)}) custom-call(s32[2]{0:T(128)S(1)} %get-tuple-element.129.at_ref, bf16[1024,1024]{1,0:T(8,128)(2,1)} %copy-done.12, bf16[8,400,1024]{2,1,0:T(8,128)(2,1)} %bitcast.103, bf16[8,400,1024]{2,1,0:T(8,128)(2,1)} %bitcast.104, ...), custom_call_target="tpu_custom_call" | custom-call | flops 40000000000 | bytes 1 | tf_op jit(solution)/shard_map/piece_product/pallas_call | solution.py:591
  254.2 1.3 collective-permute-start.24
  255.4 4.7 %piece_product.7 = (bf16[400,1024]{1,0:T(8,128)(2,1)S(1)}, bf16[400,1024]{1,0:T(8,128)(2,1)S(1)}) custom-call(s32[2]{0:T(128)S(1)} %pad_add_fusion.at_ref, bf16[1024,1024]{1,0:T(8,128)(2,1)} %copy-done.12, bf16[8,400,1024]{2,1,0:T(8,128)(2,1)} %bitcast.105, bf16[8,400,1024]{2,1,0:T(8,128)(2,1)} %bitcast.106, ...), custom_call_target="tpu_custom_call" | custom-call | flops 40000000000 | bytes 1 | tf_op jit(solution)/shard_map/piece_product/pallas_call | solution.py:591
  261.0 2.0 collective-permute-start.26
  263.0 14.1 %spread_block.7.total_ref = f32[2,1024,256]{2,1,0:T(8,128)} custom-call(s32[1]{0:T(128)} %bitcast.seat_ref, f32[2,8,128]{2,1,0:T(8,128)S(1)} %copy-done.16, bf16[256,1024]{1,0:T(8,128)(2,1)S(1)} %copy-done.7, f32[2,1024,256]{2,1,0:T(8,128)} %spread_block.6.refs_3_.held_ref, bf16[400,1024]{1,0:T(8,128)(2,1)S(1)} %copy-done.22, ...), custom_call_target="tpu_custom_call" | custom-call | flops 40000000000 | bytes 1 | tf_op jit(solution)/shard_map/spread_block/pallas_call | solution.py:251
  277.1 2.8 arrange_back.1.refs_4_
  279.9 6.8 %all-to-all-start.2 = ((bf16[4,2,64,1024]{3,2,1,0:T(8,128)(2,1)}), bf16[4,2,64,1024]{3,2,1,0:T(8,128)(2,1)}, u32[]{:S(2)}, u32[]{:S(2)}) async-start(bf16[4,2,64,1024]{3,2,1,0:T(8,128)(2,1)} %arrange_back.1.refs_4_), calls=%async_computation.2 | async-start | bytes 2097152 | tf_op jit(solution)/shard_map/all_to_all | solution.py:561
  286.8 11.8 %collective-permute-done.26 = bf16[400,1024]{1,0:T(8,128)(2,1)} collective-permute-done((bf16[400,1024]{1,0:T(8,128)(2,1)S(1)}, bf16[400,1024]{1,0:T(8,128)(2,1)}, u32[]{:S(2)}, u32[]{:S(2)}) %collective-permute-start.26) | collective-permute-done | bytes 819232 | tf_op jit(solution)/shard_map/ppermute | solution.py:557
  298.6 3.6 %convolution_convert_fusion = bf16[1024,416]{0,1:T(8,128)(2,1)} fusion(bf16[400,416]{1,0:T(8,128)(2,1)S(1)} %copy-done.53, bf16[400,1024]{1,0:T(8,128)(2,1)} %copy-done.32, bf16[400,1024]{1,0:T(8,128)(2,1)} %collective-permute-done.26, bf16[400,1024]{1,0:T(8,128)(2,1)} %collective-permute-done.25, bf16[400,1024]{1,0:T(8,128)(2,1)} %collective-permute-done.24), kind=kOutput, calls=%fused_computation.3 | convolution fusion | flops 344489984 | bytes 4461568 | tf_op jit(solution)/shard_map/dot_general | solution.py:641
  302.2 1.4 collective-permute-done.27
  305.6 5.3 %collective-permute-start.32 = (bf16[48,1024]{1,0:T(8,128)(2,1)S(1)}, bf16[48,1024]{1,0:T(8,128)(2,1)S(1)}, u32[]{:S(2)}, u32[]{:S(2)}) collective-permute-start(bf16[48,1024]{1,0:T(8,128)(2,1)S(1)} %get-tuple-element.77), channel_id=1, source_target_pairs={{0,8},{8,0},{16,24},{24,16},{1,9},{9,1},{17,25},{25,17},{2,10},{10... | collective-permute-start | bytes 294920 | tf_op jit(solution)/shard_map/ppermute | solution.py:557
  311.2 2.0 collective-permute-start.34
  313.2 1.3 collective-permute-start.29
  314.5 2.7 collective-permute-done.29
  320.0 1.3 collective-permute-done.30
  321.3 1.3 collective-permute-start.31
  323.4 2.7 collective-permute-done.31
  327.3 3.8 %all-to-all-start.3 = ((bf16[4,104,1024]{2,1,0:T(8,128)(2,1)}), bf16[4,104,1024]{2,1,0:T(8,128)(2,1)S(1)}, u32[]{:S(2)}, u32[]{:S(2)}) async-start(bf16[4,104,1024]{2,1,0:T(8,128)(2,1)} %bitcast.39.refs_1_), calls=%async_computation.3 | async-start | bytes 1703936 | tf_op jit(solution)/shard_map/all_to_all | solution.py:561
  331.6 2.1 fusion.8
  333.7 2.8 fusion.2
  336.6 3.6 %fusion.1 = f32[1024,256]{1,0:T(8,128)} fusion(bf16[256,256]{1,0:T(8,128)(2,1)S(1)} %copy-done.55, bf16[256,1024]{1,0:T(8,128)(2,1)S(1)} %bitcast.87, bf16[1024,1024]{1,0:T(8,128)(2,1)} %constant.101.clone), kind=kOutput, calls=%fused_computation.12 | convolution fusion | flops 671350784 | bytes 3801088 | tf_op jit(solution)/shard_map/dot_general | solution.py:903
  340.2 2.8 pad_maximum_fusion
  343.0 7.7 %all-to-all-done.3 = bf16[4,104,1024]{2,1,0:T(8,128)(2,1)S(1)} async-done(((bf16[4,104,1024]{2,1,0:T(8,128)(2,1)}), bf16[4,104,1024]{2,1,0:T(8,128)(2,1)S(1)}, u32[]{:S(2)}, u32[]{:S(2)}) %all-to-all-start.3) | async-done | bytes 852000 | tf_op jit(solution)/shard_map/all_to_all | solution.py:561
  350.7 1.8 fusion.13
  (205 shorter events, 31.8 us)
Async XLA Ops:
  3.9 7.7 %copy-start.41 = (bf16[1,2,64,16,256]{4,3,2,1,0:T(8,128)(2,1)S(1)}, bf16[1,2,64,16,256]{4,3,2,1,0:T(8,128)(2,1)}, u32[]{:S(2)}) copy-start(bf16[1,2,64,16,256]{4,3,2,1,0:T(8,128)(2,1)} %param.19) | copy-start | bytes 3145732
  5.2 7.3 %copy-start.54 = (bf16[256,256]{1,0:T(8,128)(2,1)S(1)}, bf16[256,256]{1,0:T(8,128)(2,1)}, u32[]{:S(2)}) copy-start(bf16[256,256]{1,0:T(8,128)(2,1)} %constant.100.clone) | copy-start | bytes 393220
  5.2 28.0 %all-to-all-start = ((bf16[4,104,1024]{2,1,0:T(8,128)(2,1)}), bf16[4,104,1024]{2,1,0:T(8,128)(2,1)S(1)}, u32[]{:S(2)}, u32[]{:S(2)}) async-start(bf16[4,104,1024]{2,1,0:T(8,128)(2,1)} %bitcast.3), calls=%async_computation | async-start | bytes 1703936 | tf_op jit(solution)/shard_map/all_to_all | solution.py:561
  15.2 18.0 %copy-start.52 = (bf16[400,416]{1,0:T(8,128)(2,1)S(1)}, bf16[400,416]{1,0:T(8,128)(2,1)}, u32[]{:S(2)}) copy-start(bf16[400,416]{1,0:T(8,128)(2,1)} %constant.99.clone) | copy-start | bytes 998404
  34.7 7.6 %copy-start.48 = (f32[320]{0:T(512)S(1)}, f32[320]{0:T(512)}, u32[]{:S(2)}) copy-start(f32[320]{0:T(512)} %param.32) | copy-start | bytes 3844
  34.7 7.6 %copy-start.51 = (f32[81]{0:T(128)S(1)}, f32[81]{0:T(128)}, u32[]{:S(2)}) copy-start(f32[81]{0:T(128)} %param.30) | copy-start | bytes 976
  34.7 7.8 %copy-start.45 = (bf16[32,320]{1,0:T(8,128)(2,1)S(1)}, bf16[32,320]{1,0:T(8,128)(2,1)}, u32[]{:S(2)}) copy-start(bf16[32,320]{1,0:T(8,128)(2,1)} %param.31) | copy-start | bytes 61444
  34.7 7.8 %copy-start.46 = (bf16[32,81]{1,0:T(8,128)(2,1)S(1)}, bf16[32,81]{1,0:T(8,128)(2,1)}, u32[]{:S(2)}) copy-start(bf16[32,81]{1,0:T(8,128)(2,1)} %param.29) | copy-start | bytes 15556
  34.7 7.8 %copy-start.44 = (bf16[32,1024]{1,0:T(8,128)(2,1)S(1)}, bf16[32,1024]{1,0:T(8,128)(2,1)}, u32[]{:S(2)}) copy-start(bf16[32,1024]{1,0:T(8,128)(2,1)} %param.27) | copy-start | bytes 196612
  34.7 42.7 %all-to-all-start.1 = ((bf16[4,2,64,1024]{3,2,1,0:T(8,128)(2,1)}), bf16[4,2,64,1024]{3,2,1,0:T(8,128)(2,1)S(1)}, u32[]{:S(2)}, u32[]{:S(2)}) async-start(bf16[4,2,64,1024]{3,2,1,0:T(8,128)(2,1)} %tie.4), calls=%async_computation.1 | async-start | bytes 2097152 | tf_op jit(solution)/shard_map/all_to_all | solution.py:561
  38.8 21.2 %collective-permute-start.1 = (bf16[400,1024]{1,0:T(8,128)(2,1)S(1)}, bf16[400,1024]{1,0:T(8,128)(2,1)S(1)}, u32[]{:S(2)}, u32[]{:S(2)}) collective-permute-start(bf16[400,1024]{1,0:T(8,128)(2,1)S(1)} %copy-done.19), channel_id=1, source_target_pairs={{0,2},{1,3},{2,0},{3,1},{4,6},{5,7},{6,4},{7,5},{8,10},{9,11},{10,... | collective-permute-start | bytes 2457608 | tf_op jit(solution)/shard_map/ppermute | solution.py:557
  40.3 36.6 %collective-permute-start.3 = (bf16[400,1024]{1,0:T(8,128)(2,1)S(1)}, bf16[400,1024]{1,0:T(8,128)(2,1)}, u32[]{:S(2)}, u32[]{:S(2)}) collective-permute-start(bf16[400,1024]{1,0:T(8,128)(2,1)S(1)} %copy-done.19), channel_id=1, source_target_pairs={{0,4},{1,5},{2,6},{3,7},{4,0},{5,1},{6,2},{7,3},{8,12},{9,13},{10,... | collective-permute-start | bytes 2457608 | tf_op jit(solution)/shard_map/ppermute | solution.py:557
  41.8 35.1 %collective-permute-start.5 = (bf16[400,1024]{1,0:T(8,128)(2,1)S(1)}, bf16[400,1024]{1,0:T(8,128)(2,1)}, u32[]{:S(2)}, u32[]{:S(2)}) collective-permute-start(bf16[400,1024]{1,0:T(8,128)(2,1)S(1)} %copy-done.19), channel_id=1, source_target_pairs={{0,6},{1,7},{2,4},{3,5},{4,2},{5,3},{6,0},{7,1},{8,14},{9,15},{10,... | collective-permute-start | bytes 2457608 | tf_op jit(solution)/shard_map/ppermute | solution.py:557
  43.2 49.0 %collective-permute-start = (bf16[400,1024]{1,0:T(8,128)(2,1)S(1)}, bf16[400,1024]{1,0:T(8,128)(2,1)}, u32[]{:S(2)}, u32[]{:S(2)}) collective-permute-start(bf16[400,1024]{1,0:T(8,128)(2,1)S(1)} %copy-done.19), channel_id=1, source_target_pairs={{0,1},{1,0},{2,3},{3,2},{4,5},{5,4},{6,7},{7,6},{8,9},{9,8},{10,11... | collective-permute-start | bytes 2457608 | tf_op jit(solution)/shard_map/ppermute | solution.py:557
  44.1 38.5 %copy-start.17 = (f32[2,8,128]{2,1,0:T(8,128)}, f32[2,8,128]{2,1,0:T(8,128)S(1)}, u32[]{:S(2)}) copy-start(f32[2,8,128]{2,1,0:T(8,128)S(1)} %get-tuple-element.124.box_ref) | copy-start | bytes 24580
  44.2 59.3 %copy-start.15 = (f32[2,8,128]{2,1,0:T(8,128)}, f32[2,8,128]{2,1,0:T(8,128)S(1)}, u32[]{:S(2)}) copy-start(f32[2,8,128]{2,1,0:T(8,128)S(1)} %get-tuple-element.125.box_ref) | copy-start | bytes 24580
  60.0 58.1 %copy-start.23 = (bf16[400,1024]{1,0:T(8,128)(2,1)}, bf16[400,1024]{1,0:T(8,128)(2,1)S(1)}, u32[]{:S(2)}) copy-start(bf16[400,1024]{1,0:T(8,128)(2,1)S(1)} %collective-permute-done.1.refs_2_) | copy-start | bytes 2457604
  60.0 34.6 %collective-permute-start.2 = (bf16[400,1024]{1,0:T(8,128)(2,1)S(1)}, bf16[400,1024]{1,0:T(8,128)(2,1)}, u32[]{:S(2)}, u32[]{:S(2)}) collective-permute-start(bf16[400,1024]{1,0:T(8,128)(2,1)S(1)} %collective-permute-done.1.refs_2_), channel_id=1, source_target_pairs={{0,1},{1,0},{2,3},{3,2},{4,5},{5,4},{6,7},{7,6},{8,9},{9,8},{10,11... | collective-permute-start | bytes 2457608 | tf_op jit(solution)/shard_map/ppermute | solution.py:557
  76.9 18.0 %collective-permute-start.4 = (bf16[400,1024]{1,0:T(8,128)(2,1)}, bf16[400,1024]{1,0:T(8,128)(2,1)}, u32[]{:S(2)}, u32[]{:S(2)}) collective-permute-start(bf16[400,1024]{1,0:T(8,128)(2,1)} %collective-permute-done.3.refs_4_), channel_id=1, source_target_pairs={{0,1},{1,0},{2,3},{3,2},{4,5},{5,4},{6,7},{7,6},{8,9},{9,8},{10,11... | collective-permute-start | bytes 2457608 | tf_op jit(solution)/shard_map/ppermute | solution.py:557
  76.9 18.0 %collective-permute-start.6 = (bf16[400,1024]{1,0:T(8,128)(2,1)}, bf16[400,1024]{1,0:T(8,128)(2,1)}, u32[]{:S(2)}, u32[]{:S(2)}) collective-permute-start(bf16[400,1024]{1,0:T(8,128)(2,1)} %collective-permute-done.5.refs_6_), channel_id=1, source_target_pairs={{0,1},{1,0},{2,3},{3,2},{4,5},{5,4},{6,7},{7,6},{8,9},{9,8},{10,11... | collective-permute-start | bytes 2457608 | tf_op jit(solution)/shard_map/ppermute | solution.py:557
  78.4 24.2 %collective-permute-start.10 = (bf16[48,1024]{1,0:T(8,128)(2,1)}, bf16[48,1024]{1,0:T(8,128)(2,1)S(1)}, u32[]{:S(2)}, u32[]{:S(2)}) collective-permute-start(bf16[48,1024]{1,0:T(8,128)(2,1)} %tie.5.refs_1_), channel_id=1, source_target_pairs={{0,8},{8,0},{16,24},{24,16},{1,9},{9,1},{17,25},{25,17},{2,10},{10... | collective-permute-start | bytes 294920 | tf_op jit(solution)/shard_map/ppermute | solution.py:557
  83.9 8.3 %copy-start.13 = (bf16[48,1024]{1,0:T(8,128)(2,1)S(1)}, bf16[48,1024]{1,0:T(8,128)(2,1)}, u32[]{:S(2)}) copy-start(bf16[48,1024]{1,0:T(8,128)(2,1)} %tie.5.refs_1_) | copy-start | bytes 294916
  92.2 10.4 %collective-permute-start.11 = (bf16[48,1024]{1,0:T(8,128)(2,1)S(1)}, bf16[48,1024]{1,0:T(8,128)(2,1)S(1)}, u32[]{:S(2)}, u32[]{:S(2)}) collective-permute-start(bf16[48,1024]{1,0:T(8,128)(2,1)S(1)} %copy-done.13), channel_id=1, source_target_pairs={{0,16},{8,24},{16,0},{24,8},{1,17},{9,25},{17,1},{25,9},{2,18},{10... | collective-permute-start | bytes 294920 | tf_op jit(solution)/shard_map/ppermute | solution.py:557
  94.6 8.0 %collective-permute-start.12 = (bf16[48,1024]{1,0:T(8,128)(2,1)S(1)}, bf16[48,1024]{1,0:T(8,128)(2,1)S(1)}, u32[]{:S(2)}, u32[]{:S(2)}) collective-permute-start(bf16[48,1024]{1,0:T(8,128)(2,1)S(1)} %copy-done.13), channel_id=1, source_target_pairs={{0,24},{8,16},{16,8},{24,0},{1,25},{9,17},{17,9},{25,1},{2,26},{10... | collective-permute-start | bytes 294920 | tf_op jit(solution)/shard_map/ppermute | solution.py:557
  100.8 48.0 %collective-permute-start.7 = (bf16[256,1024]{1,0:T(8,128)(2,1)S(1)}, bf16[256,1024]{1,0:T(8,128)(2,1)S(1)}, u32[]{:S(2)}, u32[]{:S(2)}) collective-permute-start(bf16[256,1024]{1,0:T(8,128)(2,1)S(1)} %multiply_block.1.refs_9_.refs_5_), channel_id=1, source_target_pairs={{0,16},{8,24},{16,0},{24,8},{1,17},{9,25},{17,1},{25,9},{2,18},{10... | collective-permute-start | bytes 1572872 | tf_op jit(solution)/shard_map/ppermute | solution.py:557
  102.6 14.2 %collective-permute-start.13 = (bf16[4,48,1024]{2,1,0:T(8,128)(2,1)S(1)}, bf16[4,48,1024]{2,1,0:T(8,128)(2,1)S(1)}, u32[]{:S(2)}, u32[]{:S(2)}) collective-permute-start(bf16[4,48,1024]{2,1,0:T(8,128)(2,1)S(1)} %in_order.3.refs_1_), channel_id=1, source_target_pairs={{0,2},{1,3},{2,0},{3,1},{4,6},{5,7},{6,4},{7,5},{8,10},{9,11},{10,... | collective-permute-start | bytes 1179656 | tf_op jit(solution)/shard_map/ppermute | solution.py:557
  114.1 34.8 %collective-permute-start.8 = (bf16[256,1024]{1,0:T(8,128)(2,1)S(1)}, bf16[256,1024]{1,0:T(8,128)(2,1)S(1)}, u32[]{:S(2)}, u32[]{:S(2)}) collective-permute-start(bf16[256,1024]{1,0:T(8,128)(2,1)S(1)} %get-tuple-element.50.refs_9_.refs_3_), channel_id=1, source_target_pairs={{0,24},{8,16},{16,8},{24,0},{1,25},{9,17},{17,9},{25,1},{2,26},{10... | collective-permute-start | bytes 1572872 | tf_op jit(solution)/shard_map/ppermute | solution.py:557
  116.9 17.8 %collective-permute-start.14 = (bf16[2,4,48,1024]{3,2,1,0:T(8,128)(2,1)S(1)}, bf16[2,4,48,1024]{3,2,1,0:T(8,128)(2,1)S(1)}, u32[]{:S(2)}, u32[]{:S(2)}) collective-permute-start(bf16[2,4,48,1024]{3,2,1,0:T(8,128)(2,1)S(1)} %in_order.4.refs_1_), channel_id=1, source_target_pairs={{0,4},{1,5},{2,6},{3,7},{4,0},{5,1},{6,2},{7,3},{8,12},{9,13},{10,... | collective-permute-start | bytes 2359304 | tf_op jit(solution)/shard_map/ppermute | solution.py:557
  129.0 19.9 %collective-permute-start.9 = (bf16[256,1024]{1,0:T(8,128)(2,1)S(1)}, bf16[256,1024]{1,0:T(8,128)(2,1)S(1)}, u32[]{:S(2)}, u32[]{:S(2)}) collective-permute-start(bf16[256,1024]{1,0:T(8,128)(2,1)S(1)} %get-tuple-element.52.refs_9_.refs_3_), channel_id=1, source_target_pairs={{0,8},{8,0},{16,24},{24,16},{1,9},{9,1},{17,25},{25,17},{2,10},{10... | collective-permute-start | bytes 1572872 | tf_op jit(solution)/shard_map/ppermute | solution.py:557
  134.7 11.5 %collective-permute-start.15 = (bf16[2,2,4,48,1024]{4,3,2,1,0:T(8,128)(2,1)S(1)}, bf16[2,2,4,48,1024]{4,3,2,1,0:T(8,128)(2,1)S(1)}, u32[]{:S(2)}, u32[]{:S(2)}) collective-permute-start(bf16[2,2,4,48,1024]{4,3,2,1,0:T(8,128)(2,1)S(1)} %in_order.5.refs_1_), channel_id=1, source_target_pairs={{0,1},{1,0},{2,3},{3,2},{4,5},{5,4},{6,7},{7,6},{8,9},{9,8},{10,11... | collective-permute-start | bytes 4718600 | tf_op jit(solution)/shard_map/ppermute | solution.py:557
  155.6 26.4 %collective-permute-start.16 = (bf16[256,1024]{1,0:T(8,128)(2,1)S(1)}, bf16[256,1024]{1,0:T(8,128)(2,1)S(1)}, u32[]{:S(2)}, u32[]{:S(2)}) collective-permute-start(bf16[256,1024]{1,0:T(8,128)(2,1)S(1)} %get-tuple-element.59.grad_ref), channel_id=1, source_target_pairs={{0,16},{8,24},{16,0},{24,8},{1,17},{9,25},{17,1},{25,9},{2,18},{10... | collective-permute-start | bytes 1572872 | tf_op jit(solution)/shard_map/ppermute | solution.py:557
  157.9 42.6 %collective-permute-start.18 = (bf16[256,1024]{1,0:T(8,128)(2,1)S(1)}, bf16[256,1024]{1,0:T(8,128)(2,1)}, u32[]{:S(2)}, u32[]{:S(2)}) collective-permute-start(bf16[256,1024]{1,0:T(8,128)(2,1)S(1)} %get-tuple-element.59.grad_ref), channel_id=1, source_target_pairs={{0,8},{8,0},{16,24},{24,16},{1,9},{9,1},{17,25},{25,17},{2,10},{10... | collective-permute-start | bytes 1572872 | tf_op jit(solution)/shard_map/ppermute | solution.py:557
  162.3 39.5 %collective-permute-start.19 = (bf16[512,1536]{1,0:T(8,128)(2,1)}, bf16[512,1536]{1,0:T(8,128)(2,1)S(1)}, u32[]{:S(2)}, u32[]{:S(2)}) collective-permute-start(bf16[512,1536]{1,0:T(8,128)(2,1)} %get-tuple-element.65), channel_id=1, source_target_pairs={{0,1},{1,0},{2,3},{3,2},{4,5},{5,4},{6,7},{7,6},{8,9},{9,8},{10,11... | collective-permute-start | bytes 4718600 | tf_op jit(solution)/shard_map/ppermute | solution.py:557
  182.8 17.6 %collective-permute-start.17 = (bf16[256,1024]{1,0:T(8,128)(2,1)}, bf16[256,1024]{1,0:T(8,128)(2,1)S(1)}, u32[]{:S(2)}, u32[]{:S(2)}) collective-permute-start(bf16[256,1024]{1,0:T(8,128)(2,1)} %tie.6), channel_id=1, source_target_pairs={{0,24},{8,16},{16,8},{24,0},{1,25},{9,17},{17,9},{25,1},{2,26},{10... | collective-permute-start | bytes 1572872 | tf_op jit(solution)/shard_map/ppermute | solution.py:557
  186.2 14.2 %copy-start.9 = (bf16[256,1024]{1,0:T(8,128)(2,1)S(1)}, bf16[256,1024]{1,0:T(8,128)(2,1)}, u32[]{:S(2)}) copy-start(bf16[256,1024]{1,0:T(8,128)(2,1)} %copy-done.8) | copy-start | bytes 1572868
  201.9 43.2 %copy-start.12 = (bf16[1024,1024]{1,0:T(8,128)(2,1)}, bf16[1024,1024]{1,0:T(8,128)(2,1)S(1)}, u32[]{:S(2)}) copy-start(bf16[1024,1024]{1,0:T(8,128)(2,1)S(1)} %constant_dynamic-update-slice_fusion.grad_ref) | copy-start | bytes 6291460
  202.8 18.4 %collective-permute-start.20 = (bf16[256,1536]{1,0:T(8,128)(2,1)S(1)}, bf16[256,1536]{1,0:T(8,128)(2,1)S(1)}, u32[]{:S(2)}, u32[]{:S(2)}) collective-permute-start(bf16[256,1536]{1,0:T(8,128)(2,1)S(1)} %get-tuple-element.67), channel_id=1, source_target_pairs={{0,2},{1,3},{2,0},{3,1},{4,6},{5,7},{6,4},{7,5},{8,10},{9,11},{10,... | collective-permute-start | bytes 2359304 | tf_op jit(solution)/shard_map/ppermute | solution.py:557
  223.0 16.4 %collective-permute-start.21 = (bf16[128,1536]{1,0:T(8,128)(2,1)S(1)}, bf16[128,1536]{1,0:T(8,128)(2,1)S(1)}, u32[]{:S(2)}, u32[]{:S(2)}) collective-permute-start(bf16[128,1536]{1,0:T(8,128)(2,1)S(1)} %get-tuple-element.70), channel_id=1, source_target_pairs={{0,4},{1,5},{2,6},{3,7},{4,0},{5,1},{6,2},{7,3},{8,12},{9,13},{10,... | collective-permute-start | bytes 1179656 | tf_op jit(solution)/shard_map/ppermute | solution.py:557
  244.9 4.4 %collective-permute-start.23 = (bf16[2,400,1024]{2,1,0:T(8,128)(2,1)S(1)}, bf16[2,400,1024]{2,1,0:T(8,128)(2,1)S(1)}, u32[]{:S(2)}, u32[]{:S(2)}) collective-permute-start(bf16[2,400,1024]{2,1,0:T(8,128)(2,1)S(1)} %piece_product.4.refs_2_), channel_id=1, source_target_pairs={{0,1},{1,0},{2,3},{3,2},{4,5},{5,4},{6,7},{7,6},{8,9},{9,8},{10,11... | collective-permute-start | bytes 4915208 | tf_op jit(solution)/shard_map/ppermute | solution.py:557
  248.8 6.6 %collective-permute-start.22 = (bf16[2,400,1024]{2,1,0:T(8,128)(2,1)S(1)}, bf16[2,400,1024]{2,1,0:T(8,128)(2,1)S(1)}, u32[]{:S(2)}, u32[]{:S(2)}) collective-permute-start(bf16[2,400,1024]{2,1,0:T(8,128)(2,1)S(1)} %piece_product.5.refs_3_), channel_id=1, source_target_pairs={{0,1},{1,0},{2,3},{3,2},{4,5},{5,4},{6,7},{7,6},{8,9},{9,8},{10,11... | collective-permute-start | bytes 4915208 | tf_op jit(solution)/shard_map/ppermute | solution.py:557
  253.8 44.7 %collective-permute-start.25 = (bf16[400,1024]{1,0:T(8,128)(2,1)S(1)}, bf16[400,1024]{1,0:T(8,128)(2,1)}, u32[]{:S(2)}, u32[]{:S(2)}) collective-permute-start(bf16[400,1024]{1,0:T(8,128)(2,1)S(1)} %get-tuple-element.73.refs_4_), channel_id=1, source_target_pairs={{0,2},{1,3},{2,0},{3,1},{4,6},{5,7},{6,4},{7,5},{8,10},{9,11},{10,... | collective-permute-start | bytes 2457608 | tf_op jit(solution)/shard_map/ppermute | solution.py:557
  254.1 8.9 %copy-start.7 = (bf16[256,1024]{1,0:T(8,128)(2,1)S(1)}, bf16[256,1024]{1,0:T(8,128)(2,1)}, u32[]{:S(2)}) copy-start(bf16[256,1024]{1,0:T(8,128)(2,1)} %copy-done.6) | copy-start | bytes 1572868
  254.2 8.9 %copy-start.16 = (f32[2,8,128]{2,1,0:T(8,128)S(1)}, f32[2,8,128]{2,1,0:T(8,128)}, u32[]{:S(2)}) copy-start(f32[2,8,128]{2,1,0:T(8,128)} %copy-done.15) | copy-start | bytes 24580
  254.2 8.9 %copy-start.22 = (bf16[400,1024]{1,0:T(8,128)(2,1)S(1)}, bf16[400,1024]{1,0:T(8,128)(2,1)}, u32[]{:S(2)}) copy-start(bf16[400,1024]{1,0:T(8,128)(2,1)} %fusion.refs_1_.refs_0_) | copy-start | bytes 2457604
  254.2 8.9 %copy-start.26 = (bf16[400,1024]{1,0:T(8,128)(2,1)S(1)}, bf16[400,1024]{1,0:T(8,128)(2,1)}, u32[]{:S(2)}) copy-start(bf16[400,1024]{1,0:T(8,128)(2,1)} %copy-done.23) | copy-start | bytes 2457604
  254.2 44.4 %collective-permute-start.24 = (bf16[400,1024]{1,0:T(8,128)(2,1)S(1)}, bf16[400,1024]{1,0:T(8,128)(2,1)}, u32[]{:S(2)}, u32[]{:S(2)}) collective-permute-start(bf16[400,1024]{1,0:T(8,128)(2,1)S(1)} %get-tuple-element.72.refs_3_), channel_id=1, source_target_pairs={{0,6},{1,7},{2,4},{3,5},{4,2},{5,3},{6,0},{7,1},{8,14},{9,15},{10,... | collective-permute-start | bytes 2457608 | tf_op jit(solution)/shard_map/ppermute | solution.py:557
  261.0 37.5 %collective-permute-start.26 = (bf16[400,1024]{1,0:T(8,128)(2,1)S(1)}, bf16[400,1024]{1,0:T(8,128)(2,1)}, u32[]{:S(2)}, u32[]{:S(2)}) collective-permute-start(bf16[400,1024]{1,0:T(8,128)(2,1)S(1)} %get-tuple-element.74.refs_8_), channel_id=1, source_target_pairs={{0,4},{1,5},{2,6},{3,7},{4,0},{5,1},{6,2},{7,3},{8,12},{9,13},{10,... | collective-permute-start | bytes 2457608 | tf_op jit(solution)/shard_map/ppermute | solution.py:557
  277.1 21.4 %copy-start.53 = (bf16[400,416]{1,0:T(8,128)(2,1)S(1)}, bf16[400,416]{1,0:T(8,128)(2,1)}, u32[]{:S(2)}) copy-start(bf16[400,416]{1,0:T(8,128)(2,1)} %constant.99.clone) | copy-start | bytes 998404
  279.9 47.4 %all-to-all-start.2 = ((bf16[4,2,64,1024]{3,2,1,0:T(8,128)(2,1)}), bf16[4,2,64,1024]{3,2,1,0:T(8,128)(2,1)}, u32[]{:S(2)}, u32[]{:S(2)}) async-start(bf16[4,2,64,1024]{3,2,1,0:T(8,128)(2,1)} %arrange_back.1.refs_4_), calls=%async_computation.2 | async-start | bytes 2097152 | tf_op jit(solution)/shard_map/all_to_all | solution.py:561
  302.1 17.0 %copy-start.11 = (f32[256,320]{1,0:T(8,128)S(1)}, f32[256,320]{1,0:T(8,128)}, u32[]{:S(2)}) copy-start(f32[256,320]{1,0:T(8,128)} %copy-done.10) | copy-start | bytes 983044
  302.1 20.5 %copy-start.2 = (bf16[4,2,64,1024]{3,2,1,0:T(8,128)(2,1)S(1)}, bf16[4,2,64,1024]{3,2,1,0:T(8,128)(2,1)}, u32[]{:S(2)}) copy-start(bf16[4,2,64,1024]{3,2,1,0:T(8,128)(2,1)} %arrange_back.1.refs_4_) | copy-start | bytes 3145732
  302.1 20.5 %copy-start.36 = (bf16[48,1024]{1,0:T(8,128)(2,1)S(1)}, bf16[48,1024]{1,0:T(8,128)(2,1)}, u32[]{:S(2)}) copy-start(bf16[48,1024]{1,0:T(8,128)(2,1)} %copy-done.35) | copy-start | bytes 294916
  302.1 1.5 collective-permute-start.27
  304.4 8.9 %collective-permute-start.28 = (f32[8,1024]{1,0:T(8,128)S(1)}, f32[8,1024]{1,0:T(8,128)S(1)}, u32[]{:S(2)}, u32[]{:S(2)}) collective-permute-start(f32[8,1024]{1,0:T(8,128)S(1)} %add.73), channel_id=1, source_target_pairs={{0,2},{1,3},{2,0},{3,1},{4,6},{5,7},{6,4},{7,5},{8,10},{9,11},{10,... | collective-permute-start | bytes 98312 | tf_op jit(solution)/shard_map/ppermute | solution.py:557
  305.6 17.0 %collective-permute-start.32 = (bf16[48,1024]{1,0:T(8,128)(2,1)S(1)}, bf16[48,1024]{1,0:T(8,128)(2,1)S(1)}, u32[]{:S(2)}, u32[]{:S(2)}) collective-permute-start(bf16[48,1024]{1,0:T(8,128)(2,1)S(1)} %get-tuple-element.77), channel_id=1, source_target_pairs={{0,8},{8,0},{16,24},{24,16},{1,9},{9,1},{17,25},{25,17},{2,10},{10... | collective-permute-start | bytes 294920 | tf_op jit(solution)/shard_map/ppermute | solution.py:557
  310.9 11.8 %collective-permute-start.33 = (bf16[48,1024]{1,0:T(8,128)(2,1)S(1)}, bf16[48,1024]{1,0:T(8,128)(2,1)S(1)}, u32[]{:S(2)}, u32[]{:S(2)}) collective-permute-start(bf16[48,1024]{1,0:T(8,128)(2,1)S(1)} %get-tuple-element.78), channel_id=1, source_target_pairs={{0,16},{8,24},{16,0},{24,8},{1,17},{9,25},{17,1},{25,9},{2,18},{10... | collective-permute-start | bytes 294920 | tf_op jit(solution)/shard_map/ppermute | solution.py:557
  311.2 11.4 %collective-permute-start.34 = (bf16[48,1024]{1,0:T(8,128)(2,1)S(1)}, bf16[48,1024]{1,0:T(8,128)(2,1)S(1)}, u32[]{:S(2)}, u32[]{:S(2)}) collective-permute-start(bf16[48,1024]{1,0:T(8,128)(2,1)S(1)} %get-tuple-element.79), channel_id=1, source_target_pairs={{0,24},{8,16},{16,8},{24,0},{1,25},{9,17},{17,9},{25,1},{2,26},{10... | collective-permute-start | bytes 294920 | tf_op jit(solution)/shard_map/ppermute | solution.py:557
  313.2 4.0 %collective-permute-start.29 = (f32[8,1024]{1,0:T(8,128)S(1)}, f32[8,1024]{1,0:T(8,128)S(1)}, u32[]{:S(2)}, u32[]{:S(2)}) collective-permute-start(f32[8,1024]{1,0:T(8,128)S(1)} %add.74), channel_id=1, source_target_pairs={{0,4},{1,5},{2,6},{3,7},{4,0},{5,1},{6,2},{7,3},{8,12},{9,13},{10,... | collective-permute-start | bytes 98312 | tf_op jit(solution)/shard_map/ppermute | solution.py:557
  317.2 4.1 %collective-permute-start.30 = (f32[8,1024]{1,0:T(8,128)S(1)}, f32[8,1024]{1,0:T(8,128)S(1)}, u32[]{:S(2)}, u32[]{:S(2)}) collective-permute-start(f32[8,1024]{1,0:T(8,128)S(1)} %add.75), channel_id=1, source_target_pairs={{0,8},{8,0},{16,24},{24,16},{1,9},{9,1},{17,25},{25,17},{2,10},{10... | collective-permute-start | bytes 98312 | tf_op jit(solution)/shard_map/ppermute | solution.py:557
  321.3 4.8 %collective-permute-start.31 = (f32[8,1024]{1,0:T(8,128)S(1)}, f32[8,1024]{1,0:T(8,128)S(1)}, u32[]{:S(2)}, u32[]{:S(2)}) collective-permute-start(f32[8,1024]{1,0:T(8,128)S(1)} %add.76), channel_id=1, source_target_pairs={{0,16},{8,24},{16,0},{24,8},{1,17},{9,25},{17,1},{25,9},{2,18},{10... | collective-permute-start | bytes 98312 | tf_op jit(solution)/shard_map/ppermute | solution.py:557
  323.4 10.4 %copy-start.55 = (bf16[256,256]{1,0:T(8,128)(2,1)S(1)}, bf16[256,256]{1,0:T(8,128)(2,1)}, u32[]{:S(2)}) copy-start(bf16[256,256]{1,0:T(8,128)(2,1)} %constant.100.clone) | copy-start | bytes 393220
  327.3 23.4 %all-to-all-start.3 = ((bf16[4,104,1024]{2,1,0:T(8,128)(2,1)}), bf16[4,104,1024]{2,1,0:T(8,128)(2,1)S(1)}, u32[]{:S(2)}, u32[]{:S(2)}) async-start(bf16[4,104,1024]{2,1,0:T(8,128)(2,1)} %bitcast.39.refs_1_), calls=%async_computation.3 | async-start | bytes 1703936 | tf_op jit(solution)/shard_map/all_to_all | solution.py:561
  340.2 10.5 %copy-start.40 = (bf16[416,392]{1,0:T(8,128)(2,1)S(1)}, bf16[416,392]{1,0:T(8,128)(2,1)}, u32[]{:S(2)}) copy-start(bf16[416,392]{1,0:T(8,128)(2,1)} %constant.97.clone) | copy-start | bytes 978436
  340.2 12.3 %copy-start.1 = (bf16[392,1024]{1,0:T(8,128)(2,1)S(1)}, bf16[392,1024]{1,0:T(8,128)(2,1)}, u32[]{:S(2)}) copy-start(bf16[392,1024]{1,0:T(8,128)(2,1)} %param.25) | copy-start | bytes 2408452
  (31 other events, 78.4 us)

commit v2 on v1

v2 whole, which is shorter than its diff:
```python
import functools

import jax
import jax.numpy as jnp
import numpy as np
from jax import lax
from jax.experimental import pallas as pl
from jax.experimental.pallas import tpu as pltpu
from jax.sharding import PartitionSpec as P

POOL = 7
SAMPLES = 2
CLS = 81
BOX = 320
RPI = 512
BINS = POOL * POOL
LANES = 128
AXES = ("level", "img")
OFFSETS = (np.arange(SAMPLES * POOL, dtype=np.float32) + np.float32(0.5)) / np.float32(
    SAMPLES * POOL
)
SMALL_COST = pl.CostEstimate(flops=10**9, bytes_accessed=1, transcendentals=0)
LARGE_COST = pl.CostEstimate(flops=4 * 10**10, bytes_accessed=1, transcendentals=0)
f32 = jnp.float32
bf16 = jnp.bfloat16
ANY = pl.BlockSpec(memory_space=pl.ANY)
WHOLE = pl.BlockSpec(memory_space=pltpu.VMEM)
SCALAR = pl.BlockSpec(memory_space=pltpu.SMEM)
like = jax.ShapeDtypeStruct


def bin_weights(low, span, centres, at):
    first = jnp.maximum(1.0 - jnp.abs((low + OFFSETS[2 * at] * span) - centres), 0.0)
    second = jnp.maximum(1.0 - jnp.abs((low + OFFSETS[2 * at + 1] * span) - centres), 0.0)
    return ((first + second) * 0.5).astype(bf16)


def fill_weights(box_ref, down_ref, across_ref, height, width, level_count):
    x0, y0, x1, y1, level = [box_ref[k : k + 1, :] for k in range(5)]
    centres = lax.broadcasted_iota(jnp.int32, (width, LANES), 0).astype(f32)
    for q in range(POOL):
        across_ref[q] = bin_weights(x0, x1 - x0, centres, q).astype(f32)
    centres = lax.broadcasted_iota(jnp.int32, (height, LANES), 0).astype(f32)
    for p in range(POOL):
        weights = bin_weights(y0, y1 - y0, centres, p).astype(f32)
        for k in range(level_count):
            down_ref[k * height : (k + 1) * height, p * LANES : (p + 1) * LANES] = jnp.where(
                level == float(k), weights, 0.0
            ).astype(bf16)


def runs_of(order, length, part, group, room):
    place = {chunk: at // group * room + at % group * length for at, chunk in enumerate(order)}
    table = []
    for at in range(BINS):
        row, end, runs = at * part, (at + 1) * part, []
        while row < end:
            chunk = row // length
            stop = min(end, (chunk + 1) * length)
            runs.append((row - at * part, place[chunk] + row - chunk * length, stop - row))
            row = stop
        table.append(runs)
    return table


def gaps_of(table, features):
    held = sorted((kept, kept + count) for runs in table for row, kept, count in runs)
    gaps, last = [], 0
    for first, end in held + [(features, features)]:
        if first > last:
            gaps.append((last, first))
        last = end
    return gaps


def gather_kernel(number, seat_ref, *refs):
    kept_ref, sems = refs[-2:]
    rows = refs[0].shape[0]
    copies = []
    for k, ref in enumerate(refs[:number]):
        at = pl.multiple_of((seat_ref[0] ^ k) * rows, 16)
        copies.append(pltpu.make_async_copy(ref, kept_ref.at[pl.ds(at, rows)], sems.at[k]))
    for copy in copies:
        copy.start()
    for copy in copies:
        copy.wait()


def gather_pieces(seat, pieces):
    rows, units = pieces[0].shape
    number = len(pieces)
    return pl.pallas_call(
        functools.partial(gather_kernel, number),
        in_specs=[SCALAR] + [ANY for one in pieces],
        out_specs=WHOLE,
        out_shape=like((number * rows, units), bf16),
        scratch_shapes=[pltpu.SemaphoreType.DMA((number,))],
        compiler_params=pltpu.CompilerParams(vmem_limit_bytes=24 * 2**20),
        cost_estimate=LARGE_COST,
        name="gather_pieces",
    )(seat, *pieces)


def crop_kernel(table, sizes, product, box_ref, maps_ref, *refs):
    if product:
        weight_ref = refs[0]
        crop_ref, out_ref, down_ref, across_ref, sums_ref, rows_ref, turned_ref = refs[-7:]
    else:
        crop_ref, out_ref, down_ref, across_ref, sums_ref, rows_ref = refs[-6:]
    height, width, part, level_count = sizes
    for first, end in gaps_of(table, rows_ref.shape[0]):
        rows_ref[first:end, :] = jnp.zeros((end - first, LANES), f32)
    fill_weights(box_ref, down_ref, across_ref, height, width, level_count)
    sums_ref[...] = jnp.dot(maps_ref[...], down_ref[...], preferred_element_type=f32)
    for p in range(POOL):
        lanes = slice(p * LANES, (p + 1) * LANES)
        for start in range(0, POOL, 2):
            bins = range(start, min(POOL, start + 2))
            totals = [None for q in bins]
            for x in range(width):
                piece = sums_ref[x * part : (x + 1) * part, lanes]
                for at, q in enumerate(bins):
                    term = across_ref[q, x : x + 1, :] * piece
                    totals[at] = term if x == 0 else totals[at] + term
            for at, q in enumerate(bins):
                for row, kept, count in table[p * POOL + q]:
                    rows_ref[kept : kept + count, :] = totals[at][row : row + count]
    crop = rows_ref[...].astype(bf16)
    crop_ref[...] = crop
    if not product:
        out_ref[...] = crop.T
        return
    turned_ref[pl.ds(pl.multiple_of(pl.program_id(0) * LANES, LANES), LANES), :] = crop.T

    @pl.when(pl.program_id(0) == pl.num_programs(0) - 1)
    def multiply():
        out_ref[...] = jnp.dot(
            turned_ref[...], weight_ref[...], preferred_element_type=f32
        ).astype(out_ref.dtype)


def spread_kernel(table, sizes, more, box_ref, grad_ref, weight_ref, *refs):
    held_ref = refs[0]
    total_ref, down_ref, across_ref, sums_ref, rows_ref, crop_ref = refs[-6:]
    height, width, part, level_count = sizes
    images = box_ref.shape[0]
    for n in range(images):
        fill_weights(
            box_ref.at[n], down_ref.at[n], across_ref.at[n], height, width, level_count
        )
    crop_ref[...] = lax.dot_general(
        weight_ref[...], grad_ref[...], (((1,), (1,)), ((), ())), preferred_element_type=f32
    ).astype(bf16)
    for n in range(images):
        rows_ref[...] = crop_ref[:, n * LANES : (n + 1) * LANES].astype(f32)
        for p in range(POOL):
            lanes = slice(p * LANES, (p + 1) * LANES)
            pieces = []
            for q in range(POOL):
                runs = [rows_ref[kept : kept + count, :] for row, kept, count in table[p * POOL + q]]
                pieces.append(runs[0] if len(runs) == 1 else jnp.concatenate(runs, axis=0))
            for x in range(width):
                total = across_ref[n, 0, x : x + 1, :] * pieces[0]
                for q in range(1, POOL):
                    total = total + across_ref[n, q, x : x + 1, :] * pieces[q]
                sums_ref[x * part : (x + 1) * part, lanes] = total.astype(bf16)
        total = lax.dot_general(
            sums_ref[...], down_ref[n], (((1,), (1,)), ((), ())), preferred_element_type=f32
        )
        total_ref[n] = held_ref[n] + total if more else total


def crop_block(table, sizes, features, boxes, maps, weight=None, out_type=bf16, earlier=()):
    height, width, part, level_count = sizes
    images = boxes.shape[0]
    product = weight is not None
    first = [boxes, maps] + ([weight] if product else [])
    rows = images * LANES
    if product:
        units = weight.shape[1]
        out_spec = pl.BlockSpec((rows, units), lambda n: (0, 0))
        out_shape = like((rows, units), out_type)
        more = [pltpu.VMEM((rows, features), bf16)]
    else:
        out_spec = pl.BlockSpec((LANES, features), lambda n: (n, 0))
        out_shape = like((rows, features), bf16)
        more = []
    return pl.pallas_call(
        functools.partial(crop_kernel, table, sizes, product),
        grid=(images,),
        in_specs=[
            pl.BlockSpec((None, 8, LANES), lambda n: (n, 0, 0)),
            pl.BlockSpec((None, width * part, level_count * height), lambda n: (n, 0, 0)),
        ]
        + [WHOLE for one in first[2:]]
        + [ANY for one in earlier],
        out_specs=[pl.BlockSpec((features, LANES), lambda n: (0, n)), out_spec],
        out_shape=[like((features, rows), bf16), out_shape],
        scratch_shapes=[
            pltpu.VMEM((level_count * height, POOL * LANES), bf16),
            pltpu.VMEM((POOL, width, LANES), f32),
            pltpu.VMEM((width * part, POOL * LANES), f32),
            pltpu.VMEM((features, LANES), f32),
        ]
        + more,
        compiler_params=pltpu.CompilerParams(vmem_limit_bytes=24 * 2**20),
        cost_estimate=LARGE_COST,
        name="crop_block",
    )(*first, *earlier)


def multiply_kernel(scalars, arrays, outs):
    outs[0][...] = jnp.dot(
        arrays[0][...], arrays[1][...], preferred_element_type=f32
    ).astype(outs[0].dtype)


def spread_block(table, sizes, boxes, grads, weight, held, earlier=()):
    height, width, part, level_count = sizes
    images = boxes.shape[0]
    features = weight.shape[0]
    held = [] if held is None else [held]
    return pl.pallas_call(
        functools.partial(spread_kernel, table, sizes, bool(held)),
        in_specs=[WHOLE, WHOLE, WHOLE] + [WHOLE for one in held] + [ANY for one in earlier],
        out_specs=WHOLE,
        out_shape=like((images, width * part, level_count * height), f32),
        scratch_shapes=[
            pltpu.VMEM((images, level_count * height, POOL * LANES), bf16),
            pltpu.VMEM((images, POOL, width, LANES), f32),
            pltpu.VMEM((width * part, POOL * LANES), bf16),
            pltpu.VMEM((features, LANES), f32),
            pltpu.VMEM((features, images * LANES), bf16),
        ],
        compiler_params=pltpu.CompilerParams(vmem_limit_bytes=24 * 2**20),
        cost_estimate=LARGE_COST,
        name="spread_block",
    )(boxes, grads, weight, *held, *earlier)


def call(kernel, outs, scalars, arrays, earlier=(), scratch=(), name=None):
    arrays = list(arrays)

    def body(*refs):
        at, end = len(scalars), len(scalars) + len(arrays)
        kernel(refs[:at], refs[at:end], refs[end + len(earlier) :])

    result = pl.pallas_call(
        body,
        in_specs=[SCALAR for one in scalars] + [WHOLE for one in arrays] + [ANY for one in earlier],
        out_specs=[WHOLE for one in outs],
        out_shape=outs,
        scratch_shapes=scratch,
        compiler_params=pltpu.CompilerParams(vmem_limit_bytes=24 * 2**20),
        cost_estimate=LARGE_COST,
        name=name,
    )(*[jnp.full((1,), one, jnp.int32) for one in scalars], *arrays, *earlier)
    return result


def tie_kernel(*refs):
    pass


def tie(arrays, *earlier):
    return pl.pallas_call(
        tie_kernel,
        in_specs=[ANY for one in (*arrays, *earlier)],
        out_specs=[ANY for one in arrays],
        out_shape=[like(one.shape, one.dtype) for one in arrays],
        input_output_aliases={k: k for k in range(len(arrays))},
        cost_estimate=SMALL_COST,
        name="tie",
    )(*arrays, *earlier)


def order_kernel(first, scalars, arrays, outs):
    for k, ref in enumerate(arrays):
        outs[0][scalars[0][0] ^ k] = ref[first:]


def in_order(at, arrays, first, earlier):
    shape = (len(arrays), arrays[0].shape[0] - first) + arrays[0].shape[1:]
    return call(
        functools.partial(order_kernel, first),
        [like(shape, arrays[0].dtype)],
        [at],
        arrays,
        earlier,
        name="in_order",
    )[0]


def full_small_kernel(rows, scalars, arrays, outs):
    units = outs[0].shape[1]
    for k, ref in enumerate(arrays):
        core = scalars[0][0] ^ k
        for chip in range(ref.shape[0]):
            for level in range(ref.shape[1]):
                at = pl.multiple_of(((level * ref.shape[0] + chip) * 2 + core) * rows, rows)
                outs[0][pl.ds(at, rows), :] = ref[chip, level, :rows, :]
                for part in range(2):
                    outs[1][pl.ds(at + part * (rows // 2), rows // 2), :] = ref[
                        chip, level, rows:, part * (units // 2) : (part + 1) * (units // 2)
                    ]


def split_rows(core, array, rows, sent, kept):
    for at in range(array.shape[0] // rows // 2):
        mine = pl.multiple_of((2 * at + core) * rows, rows)
        other = pl.multiple_of((2 * at + 1 - core) * rows, rows)
        kept[at * rows : (at + 1) * rows, :] = array[pl.ds(mine, rows), :].astype(bf16)
        sent[at * rows : (at + 1) * rows, :] = array[pl.ds(other, rows), :].astype(bf16)


def put_biases(biases, refs):
    high = biases.astype(bf16)
    low = (biases - high.astype(f32)).astype(bf16)
    for ref in refs:
        end = ref.shape[0]
        ref[end - 16 : end - 8, : high.shape[1]] = high
        ref[end - 8 : end, : high.shape[1]] = low


def get_biases(ref, units):
    end = ref.shape[0]
    last = ref[end - 16 :, :units].astype(f32)
    return last[:8] + last[8:]


def small_product_kernel(rows, core_ref, first_ref, second_grad_ref, second_ref, slopes_ref, bias_ref, sent_ref, kept_ref, total_ref):
    turned = (((0,), (0,)), ((), ()))
    units = first_ref.shape[1]
    total_ref[:, :units] = lax.dot_general(
        first_ref[...], second_grad_ref[...], turned, preferred_element_type=f32
    )
    total_ref[:, units:] = lax.dot_general(
        second_ref[...], slopes_ref[...], turned, preferred_element_type=f32
    )
    split_rows(core_ref[0], total_ref, rows, sent_ref, kept_ref)
    put_biases(bias_ref[...], [sent_ref, kept_ref])


def small_product(core, rows, first_act, second_grad, second_act, slopes, biases):
    units = first_act.shape[1]
    wide = units + slopes.shape[1]
    half = like((units // 2 + 16, wide), bf16)
    return pl.pallas_call(
        functools.partial(small_product_kernel, rows),
        in_specs=[SCALAR] + [WHOLE] * 5,
        out_specs=[WHOLE] * 2,
        out_shape=[half, half],
        scratch_shapes=[pltpu.VMEM((units, wide), f32)],
        compiler_params=pltpu.CompilerParams(vmem_limit_bytes=24 * 2**20),
        cost_estimate=LARGE_COST,
        name="small_product",
    )(jnp.full((1,), core, jnp.int32), first_act, second_grad, second_act, slopes, biases)


def fold_kernel(rows, bit_ref, kept_ref, come_ref, *refs):
    sent_out, kept_out, total_ref = refs[-3:]
    count, units = total_ref.shape[0], total_ref.shape[1] // 3 * 2
    total_ref[...] = kept_ref[:count, :].astype(f32) + come_ref[:count, :].astype(f32)
    split_rows(bit_ref[0], total_ref, rows, sent_out, kept_out)
    put_biases(get_biases(kept_ref, units) + get_biases(come_ref, units), [sent_out, kept_out])


def fold_rows(bit, rows, kept, come, earlier):
    count = kept.shape[0] - 16
    half = like((count // 2 + 16, kept.shape[1]), bf16)
    return pl.pallas_call(
        functools.partial(fold_kernel, rows),
        in_specs=[SCALAR, WHOLE, WHOLE] + [ANY for one in earlier],
        out_specs=[WHOLE] * 2,
        out_shape=[half, half],
        scratch_shapes=[pltpu.VMEM((count, kept.shape[1]), f32)],
        compiler_params=pltpu.CompilerParams(vmem_limit_bytes=24 * 2**20),
        cost_estimate=LARGE_COST,
        name="fold_rows",
    )(jnp.full((1,), bit, jnp.int32), kept, come, *earlier)


def last_fold_kernel(rows, scalars, arrays, outs):
    units = outs[0].shape[1]
    biases = get_biases(arrays[0], units) + get_biases(arrays[1], units)
    put_biases(biases, outs)
    for way, out in enumerate(outs):
        at = pl.multiple_of((scalars[0][0] ^ way) * rows, rows)
        total = sum(ref[pl.ds(at, rows), :].astype(f32) for ref in arrays).astype(bf16)
        out[:rows, :] = total[:, :units]
        for part in range(2):
            out[rows : rows // 2 * 3, part * (units // 2) : (part + 1) * (units // 2)] = total[
                part * (rows // 2) : (part + 1) * (rows // 2), units:
            ]


def small_sum_kernel(scalars, arrays, outs):
    total = sum(ref[...].astype(f32) for ref in arrays)
    rows, units = outs[0].shape
    biases = [get_biases(ref, units) for ref in arrays]
    outs[3][...] = (biases[0] + biases[1]) + (biases[2] + biases[3])
    outs[0][...] = total[:rows]
    for part in range(2):
        at = slice(part * (rows // 2), (part + 1) * (rows // 2))
        beside = total[rows : rows // 2 * 3, part * (units // 2) : (part + 1) * (units // 2)]
        outs[1][at, :] = beside[:, :CLS]
        outs[2][at, :] = beside[:, LANES : LANES + BOX]


def gelu_and_slope(values):
    normal = 0.5 * (1.0 + lax.erf(values * np.float32(np.sqrt(0.5))))
    density = jnp.exp(-0.5 * values * values) * np.float32(1.0 / np.sqrt(2.0 * np.pi))
    return values * normal, normal + values * density


def head_kernel(
    own_ref, one_ref, two_ref, three_ref, rows_ref, hidden_bias_ref, inner_ref, inner_bias_ref, heads_ref, heads_bias_ref,
    logits_ref, deltas_ref, first_act_ref, second_act_ref, slopes_ref, second_grad_ref, first_grad_ref, again_ref, bias_ref, first_slope_ref, second_slope_ref,
):
    first_pre = own_ref[...] + hidden_bias_ref[...]
    for come_ref in (one_ref, two_ref, three_ref):
        first_pre = first_pre + come_ref[...].astype(f32)
    act, slope = gelu_and_slope(first_pre)
    first_slope_ref[...] = slope
    act = act.astype(bf16)
    first_act_ref[...] = act
    second_pre = jnp.dot(act, inner_ref[...], preferred_element_type=f32) + inner_bias_ref[...]
    act, slope = gelu_and_slope(second_pre)
    second_slope_ref[...] = slope
    act = act.astype(bf16)
    second_act_ref[...] = act
    heads = jnp.dot(act, heads_ref[...], preferred_element_type=f32) + heads_bias_ref[...]
    logits, deltas = heads[:, :LANES], heads[:, LANES:]
    logits_ref[...] = logits[:, :CLS]
    deltas_ref[...] = deltas[:, :BOX]
    label = rows_ref[:, 0:1]
    kept = 1.0 - rows_ref[:, 1:2]
    column = lax.broadcasted_iota(jnp.int32, logits.shape, 1)
    valid = column < CLS
    row_max = jnp.max(jnp.where(valid, logits, -jnp.inf), axis=1, keepdims=True)
    exponent = jnp.where(valid, jnp.exp(jnp.where(valid, logits - row_max, 0.0)), 0.0)
    softmax_rows = exponent / jnp.sum(exponent, axis=1, keepdims=True)
    hot = (column.astype(f32) == label).astype(f32)
    logit_slope = (softmax_rows - hot) * (kept * np.float32(1.0 / RPI))
    column = lax.broadcasted_iota(jnp.int32, deltas.shape, 1)
    target = rows_ref[:, 2:3]
    for j in range(1, 4):
        target = jnp.where((column & 3) == j, rows_ref[:, 2 + j : 3 + j], target)
    foreground = jnp.where(label < CLS - 1, kept, 0.0)
    hot = ((column >> 2).astype(f32) == label) & (column < BOX)
    delta_slope = jnp.where(
        hot,
        jnp.clip(deltas - target, -1.0, 1.0) * (foreground * np.float32(1.0 / RPI)),
        0.0,
    )
    slopes = jnp.concatenate([logit_slope, delta_slope], axis=1).astype(bf16)
    slopes_ref[...] = slopes
    turned = (((1,), (1,)), ((), ()))
    act_grad = lax.dot_general(slopes, heads_ref[...], turned, preferred_element_type=f32)
    second_grad = (act_grad * second_slope_ref[...]).astype(bf16)
    second_grad_ref[...] = second_grad
    act_grad = lax.dot_general(second_grad, inner_ref[...], turned, preferred_element_type=f32)
    first_grad = (act_grad * first_slope_ref[...]).astype(bf16)
    first_grad_ref[...] = first_grad
    again_ref[...] = first_grad
    units = first_grad.shape[1]
    bias_ref[...] = jnp.zeros_like(bias_ref)
    bias_ref[0:1, :] = jnp.sum(first_grad.astype(f32), axis=0, keepdims=True)
    bias_ref[1:2, :] = jnp.sum(second_grad.astype(f32), axis=0, keepdims=True)
    bias_ref[2:3, : slopes.shape[1]] = jnp.sum(slopes.astype(f32), axis=0, keepdims=True)


def head_block(own, come, rows, hidden_bias, inner, inner_bias, heads, heads_bias):
    count, units = own.shape
    wide = heads.shape[1]
    return pl.pallas_call(
        head_kernel,
        in_specs=[pl.BlockSpec(memory_space=pltpu.VMEM)] * 10,
        out_specs=[pl.BlockSpec(memory_space=pltpu.VMEM)] * 9,
        out_shape=[
            like((count, CLS), f32),
            like((count, BOX), f32),
            like((count, units), bf16),
            like((count, units), bf16),
            like((count, wide), bf16),
            like((count, units), bf16),
            like((count, units), bf16),
            like((count, units), bf16),
            like((8, units), f32),
        ],
        scratch_shapes=[pltpu.VMEM((count, units), f32)] * 2,
        compiler_params=pltpu.CompilerParams(vmem_limit_bytes=24 * 2**20),
        cost_estimate=LARGE_COST,
        name="head_block",
    )(own, *come, rows, hidden_bias, inner, inner_bias, heads, heads_bias)


def maps_kernel(scalars, arrays, outs):
    maps_ref, by_class_ref, across_first_ref = arrays[:3]
    pick_ref = outs[-1]
    size, part = by_class_ref.shape[:2]
    images = maps_ref.shape[0]
    for way in range(size):
        pick_ref[way * part : (way + 1) * part, :] = by_class_ref[scalars[0][0] ^ way]
    for n in range(images):
        flat = lax.dot_general(
            pick_ref[...], maps_ref[n], (((1,), (1,)), ((), ())), preferred_element_type=f32
        ).astype(bf16)
        flat = jnp.dot(flat, across_first_ref[...], preferred_element_type=f32).astype(bf16)
        for way in range(size):
            outs[way][n * part : (n + 1) * part, :] = flat[way * part : (way + 1) * part]
    for out in outs[:size]:
        for below in arrays[3:]:
            out[images * part :, :] = below[...]


def maps_back_kernel(scalars, arrays, outs):
    came_refs, (by_class_ref, across_first_ref) = arrays[:-2], arrays[-2:]
    out_ref, pick_ref, flat_ref = outs
    size, part = by_class_ref.shape[:2]
    for way in range(size):
        pick_ref[way * part : (way + 1) * part, :] = by_class_ref[scalars[0][0] ^ way]
    for n in range(out_ref.shape[0]):
        for way in range(size):
            flat_ref[way * part : (way + 1) * part, :] = came_refs[way][n]
        cells = lax.dot_general(
            across_first_ref[...], flat_ref[...], (((1,), (1,)), ((), ())), preferred_element_type=f32
        ).astype(bf16)
        out_ref[n] = jnp.dot(cells, pick_ref[...], preferred_element_type=f32)


def arrange_kernel(sizes, scalars, arrays, outs):
    height, width, part, level_count = sizes
    for n in range(outs[0].shape[0]):
        for x in range(width):
            for k, ref in enumerate(arrays):
                outs[0][n, x * part : (x + 1) * part, k * height : (k + 1) * height] = ref[
                    n * part : (n + 1) * part, x * height : (x + 1) * height
                ]


def arrange_back_kernel(sizes, scalars, arrays, outs):
    height, width, part, level_count = sizes
    for n in range(arrays[0].shape[0]):
        for x in range(width):
            for k, ref in enumerate(outs):
                ref[n, :, x * height : (x + 1) * height] = arrays[0][
                    n, x * part : (x + 1) * part, k * height : (k + 1) * height
                ].astype(bf16)


def split_span_kernel(scalars, arrays, outs):
    total_ref = outs[-1]
    span = outs[0].shape[0]
    total_ref[...] = sum(
        jnp.dot(arrays[k][...], arrays[k + 1][...], preferred_element_type=f32)
        for k in range(0, len(arrays), 2)
    )
    for way, out in enumerate(outs[:-1]):
        at = pl.multiple_of((scalars[0][0] ^ way) * span, 8)
        out[...] = total_ref[pl.ds(at, span), :].astype(bf16)


def join_span_kernel(scalars, arrays, outs):
    total_ref = outs[-1]
    span = arrays[1].shape[0]
    for way, ref in enumerate(arrays[1:]):
        at = pl.multiple_of((scalars[0][0] ^ way) * span, 8)
        total_ref[pl.ds(at, span), :] = ref[...].astype(f32)
    product = jnp.dot(arrays[0][...], total_ref[...].astype(bf16), preferred_element_type=f32)
    for out in outs[:-1]:
        out[...] = product.astype(out.dtype)


def return_span_kernel(scalars, arrays, outs):
    total_ref = outs[-1]
    span = outs[0].shape[0]
    piece = sum(ref[...].astype(f32) for ref in arrays[1:]).astype(bf16)
    total_ref[...] = jnp.dot(arrays[0][...], piece, preferred_element_type=f32)
    for way, out in enumerate(outs[:-1]):
        at = pl.multiple_of((scalars[0][0] ^ way) * span, 8)
        out[...] = total_ref[pl.ds(at, span), :].astype(bf16)


def picking(rows, columns, pairs):
    matrix = np.zeros((rows, columns), np.float32)
    for a, b in pairs:
        matrix[a, b] = 1.0
    return jnp.asarray(matrix, bf16)


def swap(array, axis, bit):
    size = lax.axis_size(axis)
    return lax.ppermute(array, axis, [(at, at ^ bit) for at in range(size)])


def exchange(array, axis):
    return lax.all_to_all(array, axis, split_axis=0, concat_axis=0, tiled=True)


def exchange_ways(arrays, axis):
    return [arrays[0]] + [swap(one, axis, way) for way, one in enumerate(arrays) if way]


def product_kernel(number, parts, with_sum, at_ref, *refs):
    grad_refs, crop_refs, refs = refs[:parts], refs[parts : parts * (number + 1)], refs[parts * (number + 1) :]
    outs = refs[-number:] if with_sum else [refs[-1].at[n] for n in range(number)]
    for n in range(number):
        total = refs[0][n].astype(f32) if with_sum else 0.0
        for k, grad_ref in enumerate(grad_refs):
            total = total + jnp.dot(
                crop_refs[n * parts + k][...], grad_ref[...], preferred_element_type=f32
            )
        outs[n][...] = total.astype(bf16)


def piece_product(crops, grads, pieces, come, earlier):
    features, count = crops[0].shape
    units = grads[0].shape[1]
    rows = features // 8
    number = len(pieces)
    with_sum = come is not None
    crops = [one.reshape(8, rows, count) for one in crops]
    single = pl.BlockSpec((rows, units), lambda n, at: (0, 0))
    stacked = pl.BlockSpec((number, rows, units), lambda n, at: (0, 0, 0))
    return pl.pallas_call(
        functools.partial(product_kernel, number, len(grads), with_sum),
        grid_spec=pltpu.PrefetchScalarGridSpec(
            num_scalar_prefetch=1,
            grid=(1,),
            in_specs=[pl.BlockSpec(one.shape, lambda n, at: (0, 0)) for one in grads]
            + [
                pl.BlockSpec((None, rows, count), lambda n, at, k=k: (at[k], 0, 0))
                for k in range(number)
                for one in crops
            ]
            + ([stacked] if with_sum else [])
            + [ANY for one in earlier],
            out_specs=[single] * number if with_sum else stacked,
        ),
        out_shape=[like((rows, units), bf16)] * number
        if with_sum
        else like((number, rows, units), bf16),
        compiler_params=pltpu.CompilerParams(vmem_limit_bytes=24 * 2**20),
        cost_estimate=LARGE_COST,
        name="piece_product",
    )(jnp.stack(pieces), *grads, *crops * number, *([come] if with_sum else []), *earlier)


def butterfly(array):
    for axis in ("img", "level"):
        bit = 1
        while bit < lax.axis_size(axis):
            array = array + swap(array, axis, bit)
            bit *= 2
    return array


def contract_rows(left_side, right_side):
    return lax.dot_general(
        left_side, right_side, (((0,), (0,)), ((), ())), preferred_element_type=f32
    )


def pack_rows(array):
    rows, units = array.shape[-2], array.shape[-1] // 3 * 2
    beside = array[..., units:]
    below = jnp.concatenate([beside[..., : rows // 2, :], beside[..., rows // 2 :, :]], axis=-1)
    return jnp.concatenate([array[..., :units], below], axis=-2)


def per_device(
    pyramid,
    levels,
    region_boxes,
    labels,
    crowd_ignore,
    targets,
    hidden_weight,
    hidden_bias,
    inner_weight,
    inner_bias,
    class_weight,
    class_bias,
    delta_weight,
    delta_bias,
):
    size = lax.axis_size("level")
    planes = lax.axis_size("img")
    z = lax.axis_index("level")
    place = lax.axis_index("img")
    core, x, y = place % 2, place // 2 % 2, place // 4
    images, height, width, channels = pyramid.shape[1:]
    regions = levels.shape[1]
    part = channels // size
    sizes = (height, width, part, size)
    rows, units = hidden_weight.shape
    block_rows = images * regions
    direct = planes == 8 and rows % size == 0

    packed = jnp.concatenate(
        [
            jnp.transpose(region_boxes, (0, 2, 1)),
            jnp.transpose(levels, (0, 2, 1)),
            jnp.zeros((images, 3, regions), jnp.int32),
        ],
        axis=1,
    )
    class_room, delta_room = LANES, units // 2 - LANES
    small = jnp.concatenate(
        [
            inner_weight,
            jnp.pad(class_weight, ((0, 0), (0, class_room - CLS))),
            jnp.pad(delta_weight, ((0, 0), (0, delta_room - BOX))),
        ],
        axis=1,
    )
    heads_bias = jnp.concatenate(
        [
            jnp.pad(class_bias, (0, class_room - CLS)),
            jnp.pad(delta_bias, (0, delta_room - BOX)),
        ]
    )[None]

    if direct:
        length = rows // size
        span = -(-(length + images) // 8) * 8
        extra = jnp.concatenate(
            [packed.astype(bf16).reshape(images, units), jnp.zeros((16 - images, units), bf16)]
        )
        to_span = picking(
            size * span,
            rows,
            [(k * span + j, j * size + k) for k in range(size) for j in range(length)],
        )
        extra_span = picking(
            size * span,
            16,
            [(k * span + length + n, n) for k in range(size) for n in range(images)],
        )
        room = -(-rows // 16) * 16
        features = planes * room
        from_span = picking(
            room,
            size * span,
            [(k * length + j, k * span + j) for k in range(size) for j in range(length)],
        )
        total = [pltpu.VMEM((size * span, units), f32)]
        sent = call(
            split_span_kernel,
            [like((span, units), bf16)] * size,
            [z],
            [to_span, hidden_weight, extra_span, extra],
            scratch=total,
            name="split_span",
        )
        came = exchange_ways(sent, "level")
        piece, own_piece = call(
            join_span_kernel,
            [like((room, units), bf16)] * 2,
            [z],
            [from_span, *came],
            scratch=total,
            name="join_span",
        )
        boxes = jnp.stack([one[length : length + images].reshape(images, 8, regions) for one in came])
        pieces = [own_piece] + [swap(piece, "img", bit) for bit in (2, 4, 6)]
        order = [k * planes + at for at in range(planes) for k in range(size)]
        table = runs_of(order, length, part, size, room)
    else:
        boxes = exchange(jnp.broadcast_to(packed[None], (size,) + packed.shape), "level")
        boxes = jnp.stack([lax.dynamic_index_in_dim(boxes, z ^ way, 0, False) for way in range(size)])
        features = BINS * part
        whole = lax.all_gather(hidden_weight, AXES, axis=0, tiled=True)
        weight = lax.dynamic_index_in_dim(whole.reshape(features, size, units), z, 1, False)
        table = runs_of([0], features, part, 1, features)
    row = jnp.arange(8)[:, None]
    boxes = jnp.where(row == 4, boxes.astype(jnp.int32) ^ z, boxes.astype(jnp.int32)).astype(f32)

    spots = height * width
    by_class = picking(
        channels, channels, [(c % size * part + c // size, c) for c in range(channels)]
    ).reshape(size, part, channels)
    across_first = picking(
        spots, spots, [(y * width + x, x * height + y) for y in range(height) for x in range(width)]
    )
    picks = [
        pltpu.VMEM((channels, channels), bf16),
        pltpu.VMEM((channels, spots), bf16),
    ]
    small_rows = small.shape[0] // 2 * 3 if direct else 0
    maps = call(
        maps_kernel,
        [like((images * part + small_rows, spots), bf16)] * size,
        [z],
        [pyramid[0].reshape(images, spots, channels), by_class, across_first]
        + ([pack_rows(small)] if direct else []),
        scratch=picks[:1],
        name="maps",
    )
    if direct:
        maps = [maps[0], *tie(maps[1:], piece)]
    maps_came = exchange_ways(maps[:3], "level")
    maps_came.append(swap(tie([maps[3]], maps_came[1])[0], "level", 3))
    maps = call(
        functools.partial(arrange_kernel, sizes),
        [like((images, width * part, size * height), bf16)],
        [],
        maps_came,
        name="arrange",
    )[0]

    ways = (2, 3, 1, 0)
    crops, owns, came_sums = [], [], []
    for turn, way in enumerate(ways):
        if turn == 0:
            crop, turned = crop_block(table, sizes, features, boxes[way], maps)
            if direct:
                pieces = tie(pieces, crop)
                pieces = sum(([one, swap(one, "img", 1)] for one in pieces), [])
                weight = gather_pieces(jnp.full((1,), place, jnp.int32), pieces)
            owns += call(
                multiply_kernel, [like((block_rows, units), bf16)], [], [turned, weight], name="multiply"
            )
        else:
            crop, own = crop_block(
                table, sizes, features, boxes[way], maps, weight, bf16 if way else f32, owns[-1:]
            )
            owns.append(own)
        crops.append(crop)
        if way:
            came_sums.append(swap(owns[-1], "level", way))

    if direct:
        smalls = in_order(z, maps_came, images * part, owns[:1])
        smalls = in_order(
            place // 2, [smalls] + [swap(smalls, "img", bit) for bit in (2, 4, 6)], 0, owns[2:3]
        )
        full_inner, full_heads = call(
            functools.partial(full_small_kernel, small.shape[0]),
            [like((units, units), bf16), like((units, units // 2), bf16)],
            [core],
            [smalls, swap(smalls, "img", 1)],
            name="full_small",
        )
    else:
        smalls = lax.all_gather(small, AXES, axis=0, tiled=True)
        full_inner, full_heads = smalls[:, :units], smalls[:, units:]

    row_facts = jnp.concatenate(
        [
            labels.reshape(-1, 1).astype(f32),
            crowd_ignore.reshape(-1, 1).astype(f32),
            targets.reshape(-1, 4),
            jnp.zeros((block_rows, 2), f32),
        ],
        axis=1,
    )
    logits, deltas, first_act, second_act, slopes, second_grad, first_grad, first_again, bias_sums = head_block(
        owns[-1],
        came_sums,
        row_facts,
        hidden_bias[None],
        full_inner,
        inner_bias[None],
        full_heads,
        heads_bias,
    )

    near = swap(first_grad, "level", 1)
    far = swap(first_grad, "level", 2)
    grad_of = {0: first_grad, 1: near, 2: far}

    def take_up(way, held, earlier=()):
        return spread_block(table, sizes, boxes[way], grad_of[way], weight, held, earlier)

    if direct:
        count = small.shape[0]
        sent, kept = small_product(
            core, count, first_act, second_grad, second_act, slopes, bias_sums
        )
        held = take_up(0, None, [kept])
        sent, kept = fold_rows(x, count, kept, swap(sent, "img", 1), [held])
        grad_of[3] = swap(tie([first_again], far, kept)[0], "level", 3)
        held = take_up(1, held, [kept])
        sent, kept = fold_rows(y, count, kept, swap(sent, "img", 2), [held])
        held = take_up(2, held, [kept])
        smalls = call(
            functools.partial(last_fold_kernel, count),
            [like((small_rows + 16, units), bf16)] * size,
            [z],
            [kept, swap(sent, "img", 4)],
            [held],
            name="last_fold",
        )

        grads = [grad_of[way] for way in ways]
        parts, others = {}, {}

        def for_other(bits, earlier):
            at = [place ^ bit ^ 1 for bit in bits]
            products = piece_product(crops, grads, at, None, earlier)
            others[bits] = swap(products, "img", 1)
            return [products]

        def for_own(bits, earlier):
            at = [place ^ bit for bit in bits]
            own = piece_product(crops, grads, at, others[bits], earlier)
            for one, bit in zip(own, bits):
                parts[bit] = swap(one, "img", bit) if bit else one
            return own

        earlier = for_other((6,), smalls[:1])
        earlier = for_other((2, 4), earlier)
        earlier = for_own((6,), earlier)
        held = take_up(3, held, earlier)
        back = call(
            functools.partial(arrange_back_kernel, sizes),
            [like((images, part, spots), bf16)] * size,
            [],
            [held],
            name="arrange_back",
        )
        earlier = for_other((0,), back[:1])
        inner_sum, class_sum, delta_sum, bias_total = call(
            small_sum_kernel,
            [
                like((count, units), f32),
                like((count, CLS), f32),
                like((count, BOX), f32),
                like((8, units), f32),
            ],
            [],
            exchange_ways(smalls, "level"),
            earlier,
            name="small_sum",
        )
        earlier = for_own((2, 4), [inner_sum])
        earlier = for_own((0,), earlier)
    else:
        held = None
        grad_of[3] = swap(first_again, "level", 3)
        for way in range(size):
            held = take_up(way, held)
        back = call(
            functools.partial(arrange_back_kernel, sizes),
            [like((images, part, spots), bf16)] * size,
            [],
            [held],
            name="arrange_back",
        )
        bias_total = butterfly(bias_sums)
        small_sum = jnp.concatenate(
            [contract_rows(first_act, second_grad), contract_rows(second_act, slopes)], axis=1
        )
        small_sum = lax.psum_scatter(small_sum, AXES, scatter_dimension=0, tiled=True)
        inner_sum = small_sum[:, :units]
        class_sum = small_sum[:, units : units + CLS]
        delta_sum = small_sum[:, units + class_room : units + class_room + BOX]
        whole_grads = jnp.concatenate([grad_of[way] for way in ways])
        product = jnp.dot(
            jnp.concatenate(crops, axis=1), whole_grads, preferred_element_type=f32
        )
        own = (jnp.arange(size, dtype=jnp.int32) == z)[None, :, None]
        hidden_sum = lax.psum_scatter(
            jnp.where(own, product[:, None, :], 0.0).reshape(features * size, units),
            AXES,
            scatter_dimension=0,
            tiled=True,
        )

    map_grads = call(
        maps_back_kernel,
        [like((images, spots, channels), f32)],
        [z],
        [*exchange_ways(back, "level"), by_class, across_first],
        scratch=picks,
        name="maps_back",
    )[0].reshape(1, images, height, width, channels)

    if direct:
        sent = call(
            return_span_kernel,
            [like((span, units), bf16)] * size,
            [z],
            [from_span.T, *[parts[bit] for bit in (0, 2, 4, 6)]],
            scratch=total,
            name="return_span",
        )
        hidden_sum = call(
            join_span_kernel,
            [like((rows, units), f32)],
            [z],
            [to_span.T, *exchange_ways(sent, "level")],
            scratch=total,
            name="join_span",
        )[0]

    head_bias = bias_total[2, : class_room + delta_room]
    return (
        logits.reshape(images, regions, -1),
        deltas.reshape(images, regions, -1),
        map_grads,
        hidden_sum,
        bias_total[0],
        inner_sum,
        bias_total[1],
        class_sum,
        head_bias[:CLS],
        delta_sum,
        head_bias[class_room : class_room + BOX],
    )


def solution(mesh):
    return jax.shard_map(
        per_device,
        mesh=mesh,
        in_specs=(
            P("level", "img", None, None, None),
            P("img", "level", None),
            P("img", "level", None),
            P("img", "level"),
            P("img", "level"),
            P("img", "level", None),
            P(AXES, None),
            P(),
            P(AXES, None),
            P(),
            P(AXES, None),
            P(),
            P(AXES, None),
            P(),
        ),
        out_specs=(
            P("img", "level", None),
            P("img", "level", None),
            P("level", "img", None, None, None),
            P(AXES, None),
            P(),
            P(AXES, None),
            P(),
            P(AXES, None),
            P(),
            P(AXES, None),
            P(),
        ),
        check_vma=False,
    )
```

time: 357 us -> 302 us (0.85)
  the two profiles are of different devices: /device:TPU:0 before, /device:TPU:8 now
where the time goes in v2:
time: 302 us; the launch traced here: 298 us
  Pallas kernels  123 us (41%)
  waiting for transfers between devices  96.3 us (32%)
  starting transfers between devices  41.2 us (14%)
  local copies, waits for them, and re-layouts  34.1 us (11%)
    ppermute x41, waiting for transfers between devices, swap(): return lax.ppermute(array, axis, [(at, at ^ bit) for at in range(size)])  96.3 us
    ppermute x41, starting transfers between devices, swap(): return lax.ppermute(array, axis, [(at, at ^ bit) for at in range(size)])  41.2 us
    pallas_call x4, Pallas kernels, spread_block(): pl.pallas_call(functools.partial(spread_kernel, table, sizes, bool(held))...  38.4 us
    pallas_call x4, Pallas kernels, crop_block(): pl.pallas_call(functools.partial(crop_kernel, table, sizes, product), gri...  34.4 us
    unnamed x157, local copies, waits for them, and re-layouts  32.1 us
    pallas_call x14, Pallas kernels, call(): pl.pallas_call(body, in_specs=[SCALAR for one in scalars] + [WHOLE for on...  20.7 us
    pallas_call x6, Pallas kernels, piece_product(): pl.pallas_call(functools.partial(product_kernel, number, len(grads), with...  19.3 us
  transfers between devices with their start and end apart: 41, of which 17 were waited for; matrix products, arithmetic and copies ran while one was open for 1% of the time, Pallas kernels for 37%

profile of v2, /device:TPU:8, one launch (start us, length us, event | category | flops | bytes accessed | tf_op | source)
XLA Modules:
  0.0 297.7 jit_solution(17484079277329298443)
XLA Ops:
  6.2 3.0 %collective-permute-start.1 = (bf16[104,1024]{1,0:T(8,128)(2,1)S(1)}, bf16[104,1024]{1,0:T(8,128)(2,1)S(1)}, u32[]{:S(2)}, u32[]{:S(2)}) collective-permute-start(bf16[104,1024]{1,0:T(8,128)(2,1)S(1)} %get-tuple-element.73), channel_id=1, source_target_pairs={{0,16},{8,24},{16,0},{24,8},{1,17},{9,25},{17,1},{25,9},{2,18},{10... | collective-permute-start | bytes 638984 | tf_op jit(solution)/shard_map/ppermute | solution.py:594
  9.8 1.6 maps.1
  12.2 2.7 collective-permute-done.refs_3_
  14.9 9.2 %collective-permute-done.1.refs_4_ = bf16[104,1024]{1,0:T(8,128)(2,1)S(1)} collective-permute-done((bf16[104,1024]{1,0:T(8,128)(2,1)S(1)}, bf16[104,1024]{1,0:T(8,128)(2,1)S(1)}, u32[]{:S(2)}, u32[]{:S(2)}) %collective-permute-start.1) | collective-permute-done | bytes 213024 | tf_op jit(solution)/shard_map/ppermute | solution.py:594
  24.1 4.0 %collective-permute-done.2.refs_5_ = bf16[104,1024]{1,0:T(8,128)(2,1)S(1)} collective-permute-done((bf16[104,1024]{1,0:T(8,128)(2,1)S(1)}, bf16[104,1024]{1,0:T(8,128)(2,1)S(1)}, u32[]{:S(2)}, u32[]{:S(2)}) %collective-permute-start.2) | collective-permute-done | bytes 213024 | tf_op jit(solution)/shard_map/ppermute | solution.py:594
  28.2 1.6 join_span.2
  30.7 2.4 collective-permute-start.8
  34.3 3.1 %collective-permute-start.4 = (bf16[176,1024]{1,0:T(8,128)(2,1)}, bf16[176,1024]{1,0:T(8,128)(2,1)S(1)}, u32[]{:S(2)}, u32[]{:S(2)}) collective-permute-start(bf16[176,1024]{1,0:T(8,128)(2,1)} %get-tuple-element.81), channel_id=1, source_target_pairs={{0,16},{8,24},{16,0},{24,8},{1,17},{9,25},{17,1},{25,9},{2,18},{10... | collective-permute-start | bytes 1081352 | tf_op jit(solution)/shard_map/ppermute | solution.py:594
  37.4 10.6 %collective-permute-done.3.refs_1_.refs_2_ = bf16[176,1024]{1,0:T(8,128)(2,1)S(1)} collective-permute-done((bf16[176,1024]{1,0:T(8,128)(2,1)}, bf16[176,1024]{1,0:T(8,128)(2,1)S(1)}, u32[]{:S(2)}, u32[]{:S(2)}) %collective-permute-start.3) | collective-permute-done | bytes 360480 | tf_op jit(solution)/shard_map/ppermute | solution.py:594
  49.3 10.6 %collective-permute-done.4.refs_2_.refs_3_ = bf16[176,1024]{1,0:T(8,128)(2,1)S(1)} collective-permute-done((bf16[176,1024]{1,0:T(8,128)(2,1)}, bf16[176,1024]{1,0:T(8,128)(2,1)S(1)}, u32[]{:S(2)}, u32[]{:S(2)}) %collective-permute-start.4) | collective-permute-done | bytes 360480 | tf_op jit(solution)/shard_map/ppermute | solution.py:594
  59.9 7.2 %collective-permute-done.5.refs_3_.refs_4_ = bf16[176,1024]{1,0:T(8,128)(2,1)S(1)} collective-permute-done((bf16[176,1024]{1,0:T(8,128)(2,1)}, bf16[176,1024]{1,0:T(8,128)(2,1)S(1)}, u32[]{:S(2)}, u32[]{:S(2)}) %collective-permute-start.5) | collective-permute-done | bytes 360480 | tf_op jit(solution)/shard_map/ppermute | solution.py:594
  69.8 6.9 %crop_block.4 = (bf16[3200,256]{1,0:T(8,128)(2,1)S(1)}, bf16[256,3200]{1,0:T(8,128)(2,1)S(1)}) custom-call(f32[2,8,128]{2,1,0:T(8,128)S(1)} %get-tuple-element.168.box_ref, bf16[2,1024,256]{2,1,0:T(8,128)(2,1)S(1)} %arrange.1.maps_ref), custom_call_target="tpu_custom_call" | custom-call | flops 40000000000 | bytes 1 | tf_op jit(solution)/shard_map/crop_block/pallas_call | solution.py:188
  76.7 1.2 copy-done
  83.1 2.3 collective-permute-done.10.refs_3_
  85.5 1.2 collective-permute-done.11.refs_5_
  91.2 1.9 gather_pieces.1.refs_1_.refs_0_.weight_ref
  93.2 2.9 multiply.1.refs_1_.refs_5_
  96.1 2.5 collective-permute-start.18
  99.7 9.5 %crop_block.5 = (bf16[3200,256]{1,0:T(8,128)(2,1)S(1)}, bf16[256,1024]{1,0:T(8,128)(2,1)}) custom-call(f32[2,8,128]{2,1,0:T(8,128)S(1)} %get-tuple-element.166.box_ref, bf16[2,1024,256]{2,1,0:T(8,128)(2,1)S(1)} %copy-done.53, bf16[3200,1024]{1,0:T(8,128)(2,1)S(1)} %gather_pieces.1.refs_1_.refs_0_.weight_ref, bf16[256,1024]{1,0:T(8,128)(2,1)} %multiply.1.refs_1_.refs_5_), custom_call_target="tpu_custom_call" | custom-call | flops 40000000000 | bytes 1 | tf_op jit(solution)/shard_map/crop_block/pallas_call | solution.py:188
  109.2 1.2 copy-done.27
  110.3 1.6 collective-permute-start.14
  111.9 9.2 %crop_block.6 = (bf16[3200,256]{1,0:T(8,128)(2,1)S(1)}, bf16[256,1024]{1,0:T(8,128)(2,1)S(1)}) custom-call(f32[2,8,128]{2,1,0:T(8,128)S(1)} %get-tuple-element.167.box_ref, bf16[2,1024,256]{2,1,0:T(8,128)(2,1)S(1)} %copy-done.53, bf16[3200,1024]{1,0:T(8,128)(2,1)S(1)} %gather_pieces.1.refs_1_.refs_0_.weight_ref, bf16[256,1024]{1,0:T(8,128)(2,1)} %get-tuple-element.90.refs_1_), custom_call_target="tpu_custom_call" | custom-call | flops 40000000000 | bytes 1 | tf_op jit(solution)/shard_map/crop_block/pallas_call | solution.py:188
  121.1 1.2 copy-done.29
  122.3 2.8 collective-permute-start.15
  125.3 8.9 %crop_block.7 = (bf16[3200,256]{1,0:T(8,128)(2,1)S(1)}, f32[256,1024]{1,0:T(8,128)S(1)}) custom-call(f32[2,8,128]{2,1,0:T(8,128)S(1)} %get-tuple-element.169.box_ref, bf16[2,1024,256]{2,1,0:T(8,128)(2,1)S(1)} %copy-done.53, bf16[3200,1024]{1,0:T(8,128)(2,1)S(1)} %gather_pieces.1.refs_1_.refs_0_.weight_ref, ...), custom_call_target="tpu_custom_call" | custom-call | flops 40000000000 | bytes 1 | tf_op jit(solution)/shard_map/crop_block/pallas_call | solution.py:188
  135.4 11.3 %collective-permute-done.14.two_ref = bf16[256,1024]{1,0:T(8,128)(2,1)} collective-permute-done((bf16[256,1024]{1,0:T(8,128)(2,1)}, bf16[256,1024]{1,0:T(8,128)(2,1)}, u32[]{:S(2)}, u32[]{:S(2)}) %collective-permute-start.14) | collective-permute-done | bytes 524320 | tf_op jit(solution)/shard_map/ppermute | solution.py:594
  146.7 4.0 %head_block.1 = (f32[256,81]{1,0:T(8,128)S(1)}, f32[256,320]{1,0:T(8,128)S(1)}, bf16[256,1024]{1,0:T(8,128)(2,1)S(1)}, bf16[256,1024]{1,0:T(8,128)(2,1)S(1)}, bf...) custom-call(f32[256,1024]{1,0:T(8,128)S(1)} %get-tuple-element.92.ow, ...), custom_call_target="tpu_custom_call" | custom-call | flops 40000000000 | bytes 1 | tf_op jit(solution)/shard_map/head_block/pallas_call | solution.py:476
  150.8 1.4 collective-permute-start.23
  152.8 1.3 small_product.1
  154.2 8.9 %spread_block.4.refs_0_ = f32[2,1024,256]{2,1,0:T(8,128)S(1)} custom-call(f32[2,8,128]{2,1,0:T(8,128)S(1)} %get-tuple-element.169.box_ref, bf16[256,1024]{1,0:T(8,128)(2,1)S(1)} %get-tuple-element.98.grad_ref.refs_3_, bf16[3200,1024]{1,0:T(8,128)(2,1)S(1)} %gather_pieces.1.refs_1_.refs_0_.weight_ref, bf16[528,1536]{1,0:T(8,128)(2,1)S(1)} %get-tuple-element.104.refs_0_.kept_ref), custom_call_target="tpu_custom_call" | custom-call | flops 40000000000 | bytes 1 | tf_op jit(solution)/shard_map/spread_block/pallas_call | solution.py:223
  163.1 1.3 copy-done.45
  166.1 1.6 copy-done.46
  167.7 1.4 copy-done.49
  169.1 2.3 fold_rows.2
  172.3 3.3 %collective-permute-done.20.refs_1_.grad_ref.refs_0_ = bf16[256,1024]{1,0:T(8,128)(2,1)} collective-permute-done((bf16[256,1024]{1,0:T(8,128)(2,1)S(1)}, bf16[256,1024]{1,0:T(8,128)(2,1)}, u32[]{:S(2)}, u32[]{:S(2)}) %collective-permute-start.20) | collective-permute-done | bytes 524320 | tf_op jit(solution)/shard_map/ppermute | solution.py:594
  175.6 1.6 collective-permute-start.22
  177.2 1.5 collective-permute-start.24
  178.7 2.9 copy-done.44
  181.5 1.6 copy-done.47
  183.1 9.0 %spread_block.5.refs_0_ = f32[2,1024,256]{2,1,0:T(8,128)S(1)} custom-call(f32[2,8,128]{2,1,0:T(8,128)S(1)} %get-tuple-element.167.box_ref, bf16[256,1024]{1,0:T(8,128)(2,1)S(1)} %collective-permute-done.23.grad_ref.refs_2_, bf16[3200,1024]{1,0:T(8,128)(2,1)S(1)} %copy-done.44, f32[2,1024,256]{2,1,0:T(8,128)S(1)} %copy-done.47, bf16[272,1536]{1,0:T(8,128)(2,1)S(1)} %copy-done.42), custom_call_target="tpu_custom_call" | custom-call | flops 40000000000 | bytes 1 | tf_op jit(solution)/shard_map/spread_block/pallas_call | solution.py:223
  192.1 3.9 %collective-permute-done.24.come_ref = bf16[272,1536]{1,0:T(8,128)(2,1)S(1)} collective-permute-done((bf16[272,1536]{1,0:T(8,128)(2,1)S(1)}, bf16[272,1536]{1,0:T(8,128)(2,1)S(1)}, u32[]{:S(2)}, u32[]{:S(2)}) %collective-permute-start.24) | collective-permute-done | bytes 835616 | tf_op jit(solution)/shard_map/ppermute | solution.py:594
  196.3 1.6 collective-permute-start.25
  197.9 10.3 %spread_block.6.refs_3_.refs_0_ = f32[2,1024,256]{2,1,0:T(8,128)S(1)} custom-call(f32[2,8,128]{2,1,0:T(8,128)S(1)} %copy-done.11, bf16[256,1024]{1,0:T(8,128)(2,1)} %collective-permute-done.20.refs_1_.grad_ref.refs_0_, bf16[3200,1024]{1,0:T(8,128)(2,1)S(1)} %bitcast.111, f32[2,1024,256]{2,1,0:T(8,128)S(1)} %spread_block.5.refs_0_, ...), custom_call_target="tpu_custom_call" | custom-call | flops 40000000000 | bytes 1 | tf_op jit(solution)/shard_map/spread_block/pallas_call | solution.py:223
  211.0 1.6 collective-permute-start.34
  212.6 2.2 piece_product.6.refs_12_
  215.5 5.0 %piece_product.7.refs_9_ = bf16[2,400,1024]{2,1,0:T(8,128)(2,1)} custom-call(s32[2]{0:T(128)S(1)} %pad_add_fusion.at_ref, bf16[256,1024]{1,0:T(8,128)(2,1)} %collective-permute-done.20.refs_1_.grad_ref.refs_0_, bf16[256,1024]{1,0:T(8,128)(2,1)} %collective-permute-done.22.refs_1_.grad_ref, bf16[256,1024]{1,0:T(8,128)(2,1)S(1)} %collective-permute-done.23.grad_ref.refs_2_, ...), custom_call_target="tpu_custom_call" | custom-call | flops 40000000000 | bytes 1 | tf_op jit(solution)/shard_map/piece_product/pallas_call | solution.py:626
  221.1 3.3 %piece_product.8.refs_1_ = bf16[400,1024]{1,0:T(8,128)(2,1)} custom-call(s32[1]{0:T(128)} %bitcast.21.at_ref, bf16[256,1024]{1,0:T(8,128)(2,1)} %collective-permute-done.20.refs_1_.grad_ref.refs_0_, bf16[256,1024]{1,0:T(8,128)(2,1)} %collective-permute-done.22.refs_1_.grad_ref, bf16[256,1024]{1,0:T(8,128)(2,1)S(1)} %collective-permute-done.23.grad_ref.refs_2_, ...), custom_call_target="tpu_custom_call" | custom-call | flops 40000000000 | bytes 1 | tf_op jit(solution)/shard_map/piece_product/pallas_call | solution.py:626
  224.4 2.2 collective-permute-start.37
  226.6 10.2 %spread_block.7.refs_0_ = f32[2,1024,256]{2,1,0:T(8,128)S(1)} custom-call(f32[2,8,128]{2,1,0:T(8,128)S(1)} %get-tuple-element.166.box_ref, bf16[256,1024]{1,0:T(8,128)(2,1)} %collective-permute-done.22.refs_1_.grad_ref, bf16[3200,1024]{1,0:T(8,128)(2,1)S(1)} %bitcast.113, f32[2,1024,256]{2,1,0:T(8,128)S(1)} %spread_block.6.refs_3_.refs_0_, ...), custom_call_target="tpu_custom_call" | custom-call | flops 40000000000 | bytes 1 | tf_op jit(solution)/shard_map/spread_block/pallas_call | solution.py:223
  236.8 1.4 arrange_back.1
  238.2 2.3 piece_product.9.refs_4_
  240.5 1.8 collective-permute-start.27
  242.5 1.7 small_sum.1
  246.9 4.2 %piece_product.10 = (bf16[400,1024]{1,0:T(8,128)(2,1)S(1)}, bf16[400,1024]{1,0:T(8,128)(2,1)S(1)}) custom-call(s32[2]{0:T(128)S(1)} %pad_add_fusion.1.at_ref, bf16[256,1024]{1,0:T(8,128)(2,1)} %collective-permute-done.20.refs_1_.grad_ref.refs_0_, bf16[256,1024]{1,0:T(8,128)(2,1)} %collective-permute-done.22.refs_1_.grad_ref, ...), custom_call_target="tpu_custom_call" | custom-call | flops 40000000000 | bytes 1 | tf_op jit(solution)/shard_map/piece_product/pallas_call | solution.py:626
  252.5 2.2 piece_product.11.refs_2_
  254.7 1.6 collective-permute-start.29
  256.4 15.4 %collective-permute-done.35.refs_3_ = bf16[400,1024]{1,0:T(8,128)(2,1)S(1)} collective-permute-done((bf16[400,1024]{1,0:T(8,128)(2,1)S(1)}, bf16[400,1024]{1,0:T(8,128)(2,1)S(1)}, u32[]{:S(2)}, u32[]{:S(2)}) %collective-permute-start.35) | collective-permute-done | bytes 819232 | tf_op jit(solution)/shard_map/ppermute | solution.py:594
  272.1 2.0 return_span.1
  274.0 1.8 collective-permute-start.38
  275.8 1.3 collective-permute-start.39
  277.6 4.9 %maps_back.1 = f32[2,1024,256]{2,1,0:T(8,128)} custom-call(s32[1]{0:T(128)} %bitcast.refs_0_, bf16[2,64,1024]{2,1,0:T(8,128)(2,1)S(1)} %copy-done.58, bf16[2,64,1024]{2,1,0:T(8,128)(2,1)} %collective-permute-done.27.refs_2_, bf16[2,64,1024]{2,1,0:T(8,128)(2,1)} %collective-permute-done.28.refs_3_, bf16[2,64,1024]{2,1,0:T(8,128)(2,1)S(1)} %collective-permute-done.29.refs_4_, ...), custom_call_target="tpu_custom_call" | custom-call | flops 40000000000 | bytes 1 | tf_op jit(solution)/shard_map/maps_back/pallas_call | solution.py:248
  283.5 8.4 %collective-permute-done.39.refs_4_ = bf16[104,1024]{1,0:T(8,128)(2,1)S(1)} collective-permute-done((bf16[104,1024]{1,0:T(8,128)(2,1)S(1)}, bf16[104,1024]{1,0:T(8,128)(2,1)S(1)}, u32[]{:S(2)}, u32[]{:S(2)}) %collective-permute-start.39) | collective-permute-done | bytes 213024 | tf_op jit(solution)/shard_map/ppermute | solution.py:594
  291.9 3.8 %collective-permute-done.40.refs_5_ = bf16[104,1024]{1,0:T(8,128)(2,1)S(1)} collective-permute-done((bf16[104,1024]{1,0:T(8,128)(2,1)S(1)}, bf16[104,1024]{1,0:T(8,128)(2,1)S(1)}, u32[]{:S(2)}, u32[]{:S(2)}) %collective-permute-start.40) | collective-permute-done | bytes 213024 | tf_op jit(solution)/shard_map/ppermute | solution.py:594
  295.7 1.9 join_span.3
  (238 shorter events, 38.2 us)
Async XLA Ops:
  5.2 4.5 %copy-start.61 = (bf16[32,1024]{1,0:T(8,128)(2,1)S(1)}, bf16[32,1024]{1,0:T(8,128)(2,1)}, u32[]{:S(2)}) copy-start(bf16[32,1024]{1,0:T(8,128)(2,1)} %param.27) | copy-start | bytes 196612
  5.3 4.5 %copy-start.12 = (bf16[1,2,64,16,256]{4,3,2,1,0:T(8,128)(2,1)S(1)}, bf16[1,2,64,16,256]{4,3,2,1,0:T(8,128)(2,1)}, u32[]{:S(2)}) copy-start(bf16[1,2,64,16,256]{4,3,2,1,0:T(8,128)(2,1)} %param.19) | copy-start | bytes 3145732
  5.3 4.5 %copy-start.25 = (bf16[1024,1024]{1,0:T(8,128)(2,1)S(1)}, bf16[1024,1024]{1,0:T(8,128)(2,1)}, u32[]{:S(2)}) copy-start(bf16[1024,1024]{1,0:T(8,128)(2,1)} %constant.76.clone.refs_3_.refs_6_) | copy-start | bytes 6291460
  5.3 4.5 %copy-start.37 = (bf16[4,64,256]{2,1,0:T(8,128)(2,1)S(1)}, bf16[4,64,256]{2,1,0:T(8,128)(2,1)}, u32[]{:S(2)}) copy-start(bf16[4,64,256]{2,1,0:T(8,128)(2,1)} %constant.94.refs_2_.refs_5_) | copy-start | bytes 393220
  6.2 8.7 %collective-permute-start = (bf16[104,1024]{1,0:T(8,128)(2,1)S(1)}, bf16[104,1024]{1,0:T(8,128)(2,1)S(1)}, u32[]{:S(2)}, u32[]{:S(2)}) collective-permute-start(bf16[104,1024]{1,0:T(8,128)(2,1)S(1)} %get-tuple-element.72), channel_id=1, source_target_pairs={{0,8},{8,0},{16,24},{24,16},{1,9},{9,1},{17,25},{25,17},{2,10},{10... | collective-permute-start | bytes 638984 | tf_op jit(solution)/shard_map/ppermute | solution.py:594
  6.2 17.9 %collective-permute-start.1 = (bf16[104,1024]{1,0:T(8,128)(2,1)S(1)}, bf16[104,1024]{1,0:T(8,128)(2,1)S(1)}, u32[]{:S(2)}, u32[]{:S(2)}) collective-permute-start(bf16[104,1024]{1,0:T(8,128)(2,1)S(1)} %get-tuple-element.73), channel_id=1, source_target_pairs={{0,16},{8,24},{16,0},{24,8},{1,17},{9,25},{17,1},{25,9},{2,18},{10... | collective-permute-start | bytes 638984 | tf_op jit(solution)/shard_map/ppermute | solution.py:594
  9.3 18.9 %collective-permute-start.2 = (bf16[104,1024]{1,0:T(8,128)(2,1)S(1)}, bf16[104,1024]{1,0:T(8,128)(2,1)S(1)}, u32[]{:S(2)}, u32[]{:S(2)}) collective-permute-start(bf16[104,1024]{1,0:T(8,128)(2,1)S(1)} %get-tuple-element.74), channel_id=1, source_target_pairs={{0,24},{8,16},{16,8},{24,0},{1,25},{9,17},{17,9},{25,1},{2,26},{10... | collective-permute-start | bytes 638984 | tf_op jit(solution)/shard_map/ppermute | solution.py:594
  9.8 18.3 %copy-start.35 = (bf16[400,416]{1,0:T(8,128)(2,1)S(1)}, bf16[400,416]{1,0:T(8,128)(2,1)}, u32[]{:S(2)}) copy-start(bf16[400,416]{1,0:T(8,128)(2,1)} %constant.74.clone.refs_1_) | copy-start | bytes 998404
  12.2 17.6 %copy-start.20 = (bf16[176,1024]{1,0:T(8,128)(2,1)}, bf16[176,1024]{1,0:T(8,128)(2,1)S(1)}, u32[]{:S(2)}) copy-start(bf16[176,1024]{1,0:T(8,128)(2,1)S(1)} %get-tuple-element.76.refs_0_) | copy-start | bytes 1081348
  12.2 17.6 %copy-start.21 = (bf16[176,1024]{1,0:T(8,128)(2,1)}, bf16[176,1024]{1,0:T(8,128)(2,1)S(1)}, u32[]{:S(2)}) copy-start(bf16[176,1024]{1,0:T(8,128)(2,1)S(1)} %get-tuple-element.77.refs_1_) | copy-start | bytes 1081348
  12.2 17.6 %copy-start.22 = (bf16[176,1024]{1,0:T(8,128)(2,1)}, bf16[176,1024]{1,0:T(8,128)(2,1)S(1)}, u32[]{:S(2)}) copy-start(bf16[176,1024]{1,0:T(8,128)(2,1)S(1)} %get-tuple-element.78.refs_2_) | copy-start | bytes 1081348
  30.7 48.4 %collective-permute-start.8 = (bf16[400,1024]{1,0:T(8,128)(2,1)}, bf16[400,1024]{1,0:T(8,128)(2,1)S(1)}, u32[]{:S(2)}, u32[]{:S(2)}) collective-permute-start(bf16[400,1024]{1,0:T(8,128)(2,1)} %get-tuple-element.79.refs_3_), channel_id=1, source_target_pairs={{0,6},{1,7},{2,4},{3,5},{4,2},{5,3},{6,0},{7,1},{8,14},{9,15},{10,... | collective-permute-start | bytes 2457608 | tf_op jit(solution)/shard_map/ppermute | solution.py:594
  33.1 45.9 %collective-permute-start.7 = (bf16[400,1024]{1,0:T(8,128)(2,1)}, bf16[400,1024]{1,0:T(8,128)(2,1)S(1)}, u32[]{:S(2)}, u32[]{:S(2)}) collective-permute-start(bf16[400,1024]{1,0:T(8,128)(2,1)} %get-tuple-element.79.refs_3_), channel_id=1, source_target_pairs={{0,4},{1,5},{2,6},{3,7},{4,0},{5,1},{6,2},{7,3},{8,12},{9,13},{10,... | collective-permute-start | bytes 2457608 | tf_op jit(solution)/shard_map/ppermute | solution.py:594
  33.6 45.5 %collective-permute-start.6 = (bf16[400,1024]{1,0:T(8,128)(2,1)}, bf16[400,1024]{1,0:T(8,128)(2,1)S(1)}, u32[]{:S(2)}, u32[]{:S(2)}) collective-permute-start(bf16[400,1024]{1,0:T(8,128)(2,1)} %get-tuple-element.79.refs_3_), channel_id=1, source_target_pairs={{0,2},{1,3},{2,0},{3,1},{4,6},{5,7},{6,4},{7,5},{8,10},{9,11},{10,... | collective-permute-start | bytes 2457608 | tf_op jit(solution)/shard_map/ppermute | solution.py:594
  34.2 13.8 %collective-permute-start.3 = (bf16[176,1024]{1,0:T(8,128)(2,1)}, bf16[176,1024]{1,0:T(8,128)(2,1)S(1)}, u32[]{:S(2)}, u32[]{:S(2)}) collective-permute-start(bf16[176,1024]{1,0:T(8,128)(2,1)} %get-tuple-element.80), channel_id=1, source_target_pairs={{0,8},{8,0},{16,24},{24,16},{1,9},{9,1},{17,25},{25,17},{2,10},{10... | collective-permute-start | bytes 1081352 | tf_op jit(solution)/shard_map/ppermute | solution.py:594
  34.3 25.6 %collective-permute-start.4 = (bf16[176,1024]{1,0:T(8,128)(2,1)}, bf16[176,1024]{1,0:T(8,128)(2,1)S(1)}, u32[]{:S(2)}, u32[]{:S(2)}) collective-permute-start(bf16[176,1024]{1,0:T(8,128)(2,1)} %get-tuple-element.81), channel_id=1, source_target_pairs={{0,16},{8,24},{16,0},{24,8},{1,17},{9,25},{17,1},{25,9},{2,18},{10... | collective-permute-start | bytes 1081352 | tf_op jit(solution)/shard_map/ppermute | solution.py:594
  48.8 18.4 %collective-permute-start.5 = (bf16[176,1024]{1,0:T(8,128)(2,1)}, bf16[176,1024]{1,0:T(8,128)(2,1)S(1)}, u32[]{:S(2)}, u32[]{:S(2)}) collective-permute-start(bf16[176,1024]{1,0:T(8,128)(2,1)} %tie.5), channel_id=1, source_target_pairs={{0,24},{8,16},{16,8},{24,0},{1,25},{9,17},{17,9},{25,1},{2,26},{10... | collective-permute-start | bytes 1081352 | tf_op jit(solution)/shard_map/ppermute | solution.py:594
  49.3 20.5 %copy-start.10 = (f32[2,8,128]{2,1,0:T(8,128)}, f32[2,8,128]{2,1,0:T(8,128)S(1)}, u32[]{:S(2)}) copy-start(f32[2,8,128]{2,1,0:T(8,128)S(1)} %get-tuple-element.168.box_ref) | copy-start | bytes 24580
  59.9 9.8 %copy-start.18 = (bf16[176,1024]{1,0:T(8,128)(2,1)}, bf16[176,1024]{1,0:T(8,128)(2,1)S(1)}, u32[]{:S(2)}) copy-start(bf16[176,1024]{1,0:T(8,128)(2,1)S(1)} %collective-permute-done.4.refs_2_.refs_3_) | copy-start | bytes 1081348
  69.7 6.9 %copy-start.52 = (bf16[2,1024,256]{2,1,0:T(8,128)(2,1)}, bf16[2,1024,256]{2,1,0:T(8,128)(2,1)S(1)}, u32[]{:S(2)}) copy-start(bf16[2,1024,256]{2,1,0:T(8,128)(2,1)S(1)} %arrange.1.maps_ref) | copy-start | bytes 3145732
  80.5 2.6 collective-permute-start.9
  80.6 4.9 %collective-permute-start.10 = (bf16[400,1024]{1,0:T(8,128)(2,1)}, bf16[400,1024]{1,0:T(8,128)(2,1)S(1)}, u32[]{:S(2)}, u32[]{:S(2)}) collective-permute-start(bf16[400,1024]{1,0:T(8,128)(2,1)} %get-tuple-element.86.refs_2_), channel_id=1, source_target_pairs={{0,1},{1,0},{2,3},{3,2},{4,5},{5,4},{6,7},{7,6},{8,9},{9,8},{10,11... | collective-permute-start | bytes 2457608 | tf_op jit(solution)/shard_map/ppermute | solution.py:594
  81.1 5.5 %collective-permute-start.11 = (bf16[400,1024]{1,0:T(8,128)(2,1)}, bf16[400,1024]{1,0:T(8,128)(2,1)S(1)}, u32[]{:S(2)}, u32[]{:S(2)}) collective-permute-start(bf16[400,1024]{1,0:T(8,128)(2,1)} %get-tuple-element.87.refs_4_), channel_id=1, source_target_pairs={{0,1},{1,0},{2,3},{3,2},{4,5},{5,4},{6,7},{7,6},{8,9},{9,8},{10,11... | collective-permute-start | bytes 2457608 | tf_op jit(solution)/shard_map/ppermute | solution.py:594
  81.2 5.5 %collective-permute-start.12 = (bf16[400,1024]{1,0:T(8,128)(2,1)}, bf16[400,1024]{1,0:T(8,128)(2,1)}, u32[]{:S(2)}, u32[]{:S(2)}) collective-permute-start(bf16[400,1024]{1,0:T(8,128)(2,1)} %get-tuple-element.88.refs_6_), channel_id=1, source_target_pairs={{0,1},{1,0},{2,3},{3,2},{4,5},{5,4},{6,7},{7,6},{8,9},{9,8},{10,11... | collective-permute-start | bytes 2457608 | tf_op jit(solution)/shard_map/ppermute | solution.py:594
  93.1 61.1 %copy-start.43 = (bf16[3200,1024]{1,0:T(8,128)(2,1)}, bf16[3200,1024]{1,0:T(8,128)(2,1)S(1)}, u32[]{:S(2)}) copy-start(bf16[3200,1024]{1,0:T(8,128)(2,1)S(1)} %gather_pieces.1.refs_1_.refs_0_.weight_ref) | copy-start | bytes 19660804
  96.1 26.2 %collective-permute-start.18 = (bf16[4,48,1024]{2,1,0:T(8,128)(2,1)S(1)}, bf16[4,48,1024]{2,1,0:T(8,128)(2,1)S(1)}, u32[]{:S(2)}, u32[]{:S(2)}) collective-permute-start(bf16[4,48,1024]{2,1,0:T(8,128)(2,1)S(1)} %in_order.2.refs_1_), channel_id=1, source_target_pairs={{0,6},{1,7},{2,4},{3,5},{4,2},{5,3},{6,0},{7,1},{8,14},{9,15},{10,... | collective-permute-start | bytes 1179656 | tf_op jit(solution)/shard_map/ppermute | solution.py:594
  98.6 26.5 %collective-permute-start.17 = (bf16[4,48,1024]{2,1,0:T(8,128)(2,1)S(1)}, bf16[4,48,1024]{2,1,0:T(8,128)(2,1)S(1)}, u32[]{:S(2)}, u32[]{:S(2)}) collective-permute-start(bf16[4,48,1024]{2,1,0:T(8,128)(2,1)S(1)} %in_order.2.refs_1_), channel_id=1, source_target_pairs={{0,4},{1,5},{2,6},{3,7},{4,0},{5,1},{6,2},{7,3},{8,12},{9,13},{10,... | collective-permute-start | bytes 1179656 | tf_op jit(solution)/shard_map/ppermute | solution.py:594
  99.1 26.0 %collective-permute-start.16 = (bf16[4,48,1024]{2,1,0:T(8,128)(2,1)S(1)}, bf16[4,48,1024]{2,1,0:T(8,128)(2,1)S(1)}, u32[]{:S(2)}, u32[]{:S(2)}) collective-permute-start(bf16[4,48,1024]{2,1,0:T(8,128)(2,1)S(1)} %in_order.2.refs_1_), channel_id=1, source_target_pairs={{0,2},{1,3},{2,0},{3,1},{4,6},{5,7},{6,4},{7,5},{8,10},{9,11},{10,... | collective-permute-start | bytes 1179656 | tf_op jit(solution)/shard_map/ppermute | solution.py:594
  99.7 35.7 %collective-permute-start.13 = (bf16[256,1024]{1,0:T(8,128)(2,1)}, bf16[256,1024]{1,0:T(8,128)(2,1)}, u32[]{:S(2)}, u32[]{:S(2)}) collective-permute-start(bf16[256,1024]{1,0:T(8,128)(2,1)} %multiply.1.refs_1_.refs_5_), channel_id=1, source_target_pairs={{0,16},{8,24},{16,0},{24,8},{1,17},{9,25},{17,1},{25,9},{2,18},{10... | collective-permute-start | bytes 1572872 | tf_op jit(solution)/shard_map/ppermute | solution.py:594
  110.3 36.4 %collective-permute-start.14 = (bf16[256,1024]{1,0:T(8,128)(2,1)}, bf16[256,1024]{1,0:T(8,128)(2,1)}, u32[]{:S(2)}, u32[]{:S(2)}) collective-permute-start(bf16[256,1024]{1,0:T(8,128)(2,1)} %get-tuple-element.90.refs_1_), channel_id=1, source_target_pairs={{0,24},{8,16},{16,8},{24,0},{1,25},{9,17},{17,9},{25,1},{2,26},{10... | collective-permute-start | bytes 1572872 | tf_op jit(solution)/shard_map/ppermute | solution.py:594
  122.3 24.4 %collective-permute-start.15 = (bf16[256,1024]{1,0:T(8,128)(2,1)S(1)}, bf16[256,1024]{1,0:T(8,128)(2,1)S(1)}, u32[]{:S(2)}, u32[]{:S(2)}) collective-permute-start(bf16[256,1024]{1,0:T(8,128)(2,1)S(1)} %get-tuple-element.91.refs_1_.refs_5_), channel_id=1, source_target_pairs={{0,8},{8,0},{16,24},{24,16},{1,9},{9,1},{17,25},{25,17},{2,10},{10... | collective-permute-start | bytes 1572872 | tf_op jit(solution)/shard_map/ppermute | solution.py:594
  125.3 9.0 %collective-permute-start.19 = (bf16[4,4,48,1024]{3,2,1,0:T(8,128)(2,1)S(1)}, bf16[4,4,48,1024]{3,2,1,0:T(8,128)(2,1)S(1)}, u32[]{:S(2)}, u32[]{:S(2)}) collective-permute-start(bf16[4,4,48,1024]{3,2,1,0:T(8,128)(2,1)S(1)} %in_order.3.refs_1_), channel_id=1, source_target_pairs={{0,1},{1,0},{2,3},{3,2},{4,5},{5,4},{6,7},{7,6},{8,9},{9,8},{10,11... | collective-permute-start | bytes 4718600 | tf_op jit(solution)/shard_map/ppermute | solution.py:594
  134.3 12.5 %copy-start.23 = (f32[1024]{0:T(1024)S(1)}, f32[1024]{0:T(1024)}, u32[]{:S(2)}) copy-start(f32[1024]{0:T(1024)} %param.26) | copy-start | bytes 12292
  134.3 12.4 %copy-start.24 = (f32[1024]{0:T(1024)S(1)}, f32[1024]{0:T(1024)}, u32[]{:S(2)}) copy-start(f32[1024]{0:T(1024)} %param.28) | copy-start | bytes 12292
  150.8 27.9 %collective-permute-start.23 = (bf16[256,1024]{1,0:T(8,128)(2,1)S(1)}, bf16[256,1024]{1,0:T(8,128)(2,1)S(1)}, u32[]{:S(2)}, u32[]{:S(2)}) collective-permute-start(bf16[256,1024]{1,0:T(8,128)(2,1)S(1)} %get-tuple-element.98.grad_ref.refs_3_), channel_id=1, source_target_pairs={{0,8},{8,0},{16,24},{24,16},{1,9},{9,1},{17,25},{25,17},{2,10},{10... | collective-permute-start | bytes 1572872 | tf_op jit(solution)/shard_map/ppermute | solution.py:594
  152.1 23.4 %collective-permute-start.20 = (bf16[256,1024]{1,0:T(8,128)(2,1)S(1)}, bf16[256,1024]{1,0:T(8,128)(2,1)}, u32[]{:S(2)}, u32[]{:S(2)}) collective-permute-start(bf16[256,1024]{1,0:T(8,128)(2,1)S(1)} %get-tuple-element.98.grad_ref.refs_3_), channel_id=1, source_target_pairs={{0,16},{8,24},{16,0},{24,8},{1,17},{9,25},{17,1},{25,9},{2,18},{10... | collective-permute-start | bytes 1572872 | tf_op jit(solution)/shard_map/ppermute | solution.py:594
  154.1 9.0 %copy-start.48 = (bf16[528,1536]{1,0:T(8,128)(2,1)}, bf16[528,1536]{1,0:T(8,128)(2,1)S(1)}, u32[]{:S(2)}) copy-start(bf16[528,1536]{1,0:T(8,128)(2,1)S(1)} %get-tuple-element.104.refs_0_.kept_ref) | copy-start | bytes 4866052
  154.1 12.0 %collective-permute-start.21 = (bf16[528,1536]{1,0:T(8,128)(2,1)S(1)}, bf16[528,1536]{1,0:T(8,128)(2,1)}, u32[]{:S(2)}, u32[]{:S(2)}) collective-permute-start(bf16[528,1536]{1,0:T(8,128)(2,1)S(1)} %get-tuple-element.105), channel_id=1, source_target_pairs={{0,1},{1,0},{2,3},{3,2},{4,5},{5,4},{6,7},{7,6},{8,9},{9,8},{10,11... | collective-permute-start | bytes 4866056 | tf_op jit(solution)/shard_map/ppermute | solution.py:594
  175.6 37.0 %collective-permute-start.22 = (bf16[256,1024]{1,0:T(8,128)(2,1)}, bf16[256,1024]{1,0:T(8,128)(2,1)}, u32[]{:S(2)}, u32[]{:S(2)}) collective-permute-start(bf16[256,1024]{1,0:T(8,128)(2,1)} %tie.7), channel_id=1, source_target_pairs={{0,24},{8,16},{16,8},{24,0},{1,25},{9,17},{17,9},{25,1},{2,26},{10... | collective-permute-start | bytes 1572872 | tf_op jit(solution)/shard_map/ppermute | solution.py:594
  177.2 18.8 %collective-permute-start.24 = (bf16[272,1536]{1,0:T(8,128)(2,1)S(1)}, bf16[272,1536]{1,0:T(8,128)(2,1)S(1)}, u32[]{:S(2)}, u32[]{:S(2)}) collective-permute-start(bf16[272,1536]{1,0:T(8,128)(2,1)S(1)} %get-tuple-element.107), channel_id=1, source_target_pairs={{0,2},{1,3},{2,0},{3,1},{4,6},{5,7},{6,4},{7,5},{8,10},{9,11},{10,... | collective-permute-start | bytes 2506760 | tf_op jit(solution)/shard_map/ppermute | solution.py:594
  183.1 14.8 %slice-start = ((s8[6553600]{0:T(1024)(128)(4,1)}), s8[4194304]{0:T(1024)(128)(4,1)S(1)}, s32[]{:S(2)}) async-start(s8[6553600]{0:T(1024)(128)(4,1)} %bitcast.110), calls=%async_computation | async-start | bytes 8388608
  196.3 12.0 %collective-permute-start.25 = (bf16[144,1536]{1,0:T(8,128)(2,1)S(1)}, bf16[144,1536]{1,0:T(8,128)(2,1)S(1)}, u32[]{:S(2)}, u32[]{:S(2)}) collective-permute-start(bf16[144,1536]{1,0:T(8,128)(2,1)S(1)} %get-tuple-element.112), channel_id=1, source_target_pairs={{0,4},{1,5},{2,6},{3,7},{4,0},{5,1},{6,2},{7,3},{8,12},{9,13},{10,... | collective-permute-start | bytes 1327112 | tf_op jit(solution)/shard_map/ppermute | solution.py:594
  209.1 31.4 %collective-permute-start.32 = (bf16[64,1024]{1,0:T(8,128)(2,1)}, bf16[64,1024]{1,0:T(8,128)(2,1)}, u32[]{:S(2)}, u32[]{:S(2)}) collective-permute-start(bf16[64,1024]{1,0:T(8,128)(2,1)} %get-tuple-element.118), channel_id=1, source_target_pairs={{0,8},{8,0},{16,24},{24,16},{1,9},{9,1},{17,25},{25,17},{2,10},{10... | collective-permute-start | bytes 393224 | tf_op jit(solution)/shard_map/ppermute | solution.py:594
  209.9 32.4 %collective-permute-start.33 = (bf16[64,1024]{1,0:T(8,128)(2,1)}, bf16[64,1024]{1,0:T(8,128)(2,1)}, u32[]{:S(2)}, u32[]{:S(2)}) collective-permute-start(bf16[64,1024]{1,0:T(8,128)(2,1)} %get-tuple-element.119), channel_id=1, source_target_pairs={{0,16},{8,24},{16,0},{24,8},{1,17},{9,25},{17,1},{25,9},{2,18},{10... | collective-permute-start | bytes 393224 | tf_op jit(solution)/shard_map/ppermute | solution.py:594
  211.0 31.5 %collective-permute-start.34 = (bf16[64,1024]{1,0:T(8,128)(2,1)}, bf16[64,1024]{1,0:T(8,128)(2,1)}, u32[]{:S(2)}, u32[]{:S(2)}) collective-permute-start(bf16[64,1024]{1,0:T(8,128)(2,1)} %get-tuple-element.120), channel_id=1, source_target_pairs={{0,24},{8,16},{16,8},{24,0},{1,25},{9,17},{17,9},{25,1},{2,26},{10... | collective-permute-start | bytes 393224 | tf_op jit(solution)/shard_map/ppermute | solution.py:594
  215.5 5.6 %collective-permute-start.26 = (bf16[1,400,1024]{2,1,0:T(8,128)(2,1)S(1)}, bf16[1,400,1024]{2,1,0:T(8,128)(2,1)S(1)}, u32[]{:S(2)}, u32[]{:S(2)}) collective-permute-start(bf16[1,400,1024]{2,1,0:T(8,128)(2,1)S(1)} %piece_product.6.refs_12_), channel_id=1, source_target_pairs={{0,1},{1,0},{2,3},{3,2},{4,5},{5,4},{6,7},{7,6},{8,9},{9,8},{10,11... | collective-permute-start | bytes 2457608 | tf_op jit(solution)/shard_map/ppermute | solution.py:594
  215.5 11.0 %slice-start.2 = ((s8[6553600]{0:T(1024)(128)(4,1)}), s8[4194304]{0:T(1024)(128)(4,1)S(1)}, s32[]{:S(2)}) async-start(s8[6553600]{0:T(1024)(128)(4,1)} %bitcast.112), calls=%async_computation.2 | async-start | bytes 8388608
  220.5 6.0 %slice-start.3 = ((s8[6553600]{0:T(1024)(128)(4,1)}), s8[2359296]{0:T(1024)(128)(4,1)S(1)}, s32[]{:S(2)}) async-start(s8[6553600]{0:T(1024)(128)(4,1)} %bitcast.112), calls=%async_computation.3 | async-start | bytes 4718592
  220.5 25.4 %collective-permute-start.31 = (bf16[2,400,1024]{2,1,0:T(8,128)(2,1)}, bf16[2,400,1024]{2,1,0:T(8,128)(2,1)}, u32[]{:S(2)}, u32[]{:S(2)}) collective-permute-start(bf16[2,400,1024]{2,1,0:T(8,128)(2,1)} %piece_product.7.refs_9_), channel_id=1, source_target_pairs={{0,1},{1,0},{2,3},{3,2},{4,5},{5,4},{6,7},{7,6},{8,9},{9,8},{10,11... | collective-permute-start | bytes 4915208 | tf_op jit(solution)/shard_map/ppermute | solution.py:594
  224.4 30.3 %collective-permute-start.37 = (bf16[400,1024]{1,0:T(8,128)(2,1)}, bf16[400,1024]{1,0:T(8,128)(2,1)}, u32[]{:S(2)}, u32[]{:S(2)}) collective-permute-start(bf16[400,1024]{1,0:T(8,128)(2,1)} %piece_product.8.refs_1_), channel_id=1, source_target_pairs={{0,6},{1,7},{2,4},{3,5},{4,2},{5,3},{6,0},{7,1},{8,14},{9,15},{10,... | collective-permute-start | bytes 2457608 | tf_op jit(solution)/shard_map/ppermute | solution.py:594
  240.5 36.6 %collective-permute-start.27 = (bf16[2,64,1024]{2,1,0:T(8,128)(2,1)}, bf16[2,64,1024]{2,1,0:T(8,128)(2,1)}, u32[]{:S(2)}, u32[]{:S(2)}) collective-permute-start(bf16[2,64,1024]{2,1,0:T(8,128)(2,1)} %get-tuple-element.115), channel_id=1, source_target_pairs={{0,8},{8,0},{16,24},{24,16},{1,9},{9,1},{17,25},{25,17},{2,10},{10... | collective-permute-start | bytes 786440 | tf_op jit(solution)/shard_map/ppermute | solution.py:594
  242.3 35.3 %collective-permute-start.28 = (bf16[2,64,1024]{2,1,0:T(8,128)(2,1)}, bf16[2,64,1024]{2,1,0:T(8,128)(2,1)}, u32[]{:S(2)}, u32[]{:S(2)}) collective-permute-start(bf16[2,64,1024]{2,1,0:T(8,128)(2,1)} %get-tuple-element.116), channel_id=1, source_target_pairs={{0,16},{8,24},{16,0},{24,8},{1,17},{9,25},{17,1},{25,9},{2,18},{10... | collective-permute-start | bytes 786440 | tf_op jit(solution)/shard_map/ppermute | solution.py:594
  242.5 9.2 %collective-permute-start.30 = (bf16[1,400,1024]{2,1,0:T(8,128)(2,1)S(1)}, bf16[1,400,1024]{2,1,0:T(8,128)(2,1)S(1)}, u32[]{:S(2)}, u32[]{:S(2)}) collective-permute-start(bf16[1,400,1024]{2,1,0:T(8,128)(2,1)S(1)} %piece_product.9.refs_4_), channel_id=1, source_target_pairs={{0,1},{1,0},{2,3},{3,2},{4,5},{5,4},{6,7},{7,6},{8,9},{9,8},{10,11... | collective-permute-start | bytes 2457608 | tf_op jit(solution)/shard_map/ppermute | solution.py:594
  251.1 20.7 %collective-permute-start.35 = (bf16[400,1024]{1,0:T(8,128)(2,1)S(1)}, bf16[400,1024]{1,0:T(8,128)(2,1)S(1)}, u32[]{:S(2)}, u32[]{:S(2)}) collective-permute-start(bf16[400,1024]{1,0:T(8,128)(2,1)S(1)} %get-tuple-element.122.refs_9_), channel_id=1, source_target_pairs={{0,2},{1,3},{2,0},{3,1},{4,6},{5,7},{6,4},{7,5},{8,10},{9,11},{10,... | collective-permute-start | bytes 2457608 | tf_op jit(solution)/shard_map/ppermute | solution.py:594
  251.7 20.4 %copy-start.33 = (bf16[416,400]{1,0:T(8,128)(2,1)S(1)}, bf16[416,400]{1,0:T(8,128)(2,1)}, u32[]{:S(2)}) copy-start(bf16[416,400]{1,0:T(8,128)(2,1)} %constant.96.refs_1_) | copy-start | bytes 998404
  251.7 20.3 %collective-permute-start.36 = (bf16[400,1024]{1,0:T(8,128)(2,1)S(1)}, bf16[400,1024]{1,0:T(8,128)(2,1)S(1)}, u32[]{:S(2)}, u32[]{:S(2)}) collective-permute-start(bf16[400,1024]{1,0:T(8,128)(2,1)S(1)} %get-tuple-element.123.refs_10_), channel_id=1, source_target_pairs={{0,4},{1,5},{2,6},{3,7},{4,0},{5,1},{6,2},{7,3},{8,12},{9,13},{10,... | collective-permute-start | bytes 2457608 | tf_op jit(solution)/shard_map/ppermute | solution.py:594
  254.7 22.9 %copy-start.26 = (bf16[1024,1024]{1,0:T(8,128)(2,1)S(1)}, bf16[1024,1024]{1,0:T(8,128)(2,1)}, u32[]{:S(2)}) copy-start(bf16[1024,1024]{1,0:T(8,128)(2,1)} %constant.76.clone.refs_3_.refs_6_) | copy-start | bytes 6291460
  254.7 22.9 %copy-start.38 = (bf16[4,64,256]{2,1,0:T(8,128)(2,1)S(1)}, bf16[4,64,256]{2,1,0:T(8,128)(2,1)}, u32[]{:S(2)}) copy-start(bf16[4,64,256]{2,1,0:T(8,128)(2,1)} %constant.94.refs_2_.refs_5_) | copy-start | bytes 393220
  254.7 22.9 %copy-start.58 = (bf16[2,64,1024]{2,1,0:T(8,128)(2,1)S(1)}, bf16[2,64,1024]{2,1,0:T(8,128)(2,1)}, u32[]{:S(2)}) copy-start(bf16[2,64,1024]{2,1,0:T(8,128)(2,1)} %copy-done.57) | copy-start | bytes 786436
  254.7 22.9 %collective-permute-start.29 = (bf16[2,64,1024]{2,1,0:T(8,128)(2,1)S(1)}, bf16[2,64,1024]{2,1,0:T(8,128)(2,1)S(1)}, u32[]{:S(2)}, u32[]{:S(2)}) collective-permute-start(bf16[2,64,1024]{2,1,0:T(8,128)(2,1)S(1)} %get-tuple-element.117), channel_id=1, source_target_pairs={{0,24},{8,16},{16,8},{24,0},{1,25},{9,17},{17,9},{25,1},{2,26},{10... | collective-permute-start | bytes 786440 | tf_op jit(solution)/shard_map/ppermute | solution.py:594
  274.0 9.5 %collective-permute-start.38 = (bf16[104,1024]{1,0:T(8,128)(2,1)S(1)}, bf16[104,1024]{1,0:T(8,128)(2,1)S(1)}, u32[]{:S(2)}, u32[]{:S(2)}) collective-permute-start(bf16[104,1024]{1,0:T(8,128)(2,1)S(1)} %get-tuple-element.125), channel_id=1, source_target_pairs={{0,8},{8,0},{16,24},{24,16},{1,9},{9,1},{17,25},{25,17},{2,10},{10... | collective-permute-start | bytes 638984 | tf_op jit(solution)/shard_map/ppermute | solution.py:594
  275.8 16.1 %collective-permute-start.39 = (bf16[104,1024]{1,0:T(8,128)(2,1)S(1)}, bf16[104,1024]{1,0:T(8,128)(2,1)S(1)}, u32[]{:S(2)}, u32[]{:S(2)}) collective-permute-start(bf16[104,1024]{1,0:T(8,128)(2,1)S(1)} %get-tuple-element.126), channel_id=1, source_target_pairs={{0,16},{8,24},{16,0},{24,8},{1,17},{9,25},{17,1},{25,9},{2,18},{10... | collective-permute-start | bytes 638984 | tf_op jit(solution)/shard_map/ppermute | solution.py:594
  277.2 18.5 %copy-start.36 = (bf16[392,416]{1,0:T(8,128)(2,1)S(1)}, bf16[392,416]{1,0:T(8,128)(2,1)}, u32[]{:S(2)}) copy-start(bf16[392,416]{1,0:T(8,128)(2,1)} %constant.95.refs_1_) | copy-start | bytes 978436
  277.2 18.5 %collective-permute-start.40 = (bf16[104,1024]{1,0:T(8,128)(2,1)S(1)}, bf16[104,1024]{1,0:T(8,128)(2,1)S(1)}, u32[]{:S(2)}, u32[]{:S(2)}) collective-permute-start(bf16[104,1024]{1,0:T(8,128)(2,1)S(1)} %get-tuple-element.127), channel_id=1, source_target_pairs={{0,24},{8,16},{16,8},{24,0},{1,25},{9,17},{17,9},{25,1},{2,26},{10... | collective-permute-start | bytes 638984 | tf_op jit(solution)/shard_map/ppermute | solution.py:594
  (50 other events, 96.8 us)

commit v3 on v2

--- a/solution.py
+++ b/solution.py
@@ -23,10 +23,11 @@
 LARGE_COST = pl.CostEstimate(flops=4 * 10**10, bytes_accessed=1, transcendentals=0)
 f32 = jnp.float32
 bf16 = jnp.bfloat16
-ANY = pl.BlockSpec(memory_space=pl.ANY)
+FAR = pl.BlockSpec(memory_space=pl.ANY)
 WHOLE = pl.BlockSpec(memory_space=pltpu.VMEM)
 SCALAR = pl.BlockSpec(memory_space=pltpu.SMEM)
 like = jax.ShapeDtypeStruct
+SIGN = jax.ShapeDtypeStruct((8, LANES), jnp.float32)
 
 
 def bin_weights(low, span, centres, at):
@@ -91,9 +92,9 @@
     number = len(pieces)
     return pl.pallas_call(
         functools.partial(gather_kernel, number),
-        in_specs=[SCALAR] + [ANY for one in pieces],
+        in_specs=[SCALAR] + [FAR for one in pieces],
         out_specs=WHOLE,
-        out_shape=like((number * rows, units), bf16),
+        out_shape=pltpu.VMEM((number * rows, units), bf16),
         scratch_shapes=[pltpu.SemaphoreType.DMA((number,))],
         compiler_params=pltpu.CompilerParams(vmem_limit_bytes=24 * 2**20),
         cost_estimate=LARGE_COST,
@@ -104,9 +105,10 @@
 def crop_kernel(table, sizes, product, box_ref, maps_ref, *refs):
     if product:
         weight_ref = refs[0]
-        crop_ref, out_ref, down_ref, across_ref, sums_ref, rows_ref, turned_ref = refs[-7:]
+        crop_ref, out_ref, sign_ref, down_ref, across_ref, sums_ref, rows_ref, turned_ref = refs[-8:]
     else:
-        crop_ref, out_ref, down_ref, across_ref, sums_ref, rows_ref = refs[-6:]
+        crop_ref, out_ref, sign_ref, down_ref, across_ref, sums_ref, rows_ref = refs[-7:]
+    sign_ref[...] = jnp.zeros_like(sign_ref)
     height, width, part, level_count = sizes
     for first, end in gaps_of(table, rows_ref.shape[0]):
         rows_ref[first:end, :] = jnp.zeros((end - first, LANES), f32)
@@ -139,9 +141,9 @@
         ).astype(out_ref.dtype)
 
 
-def spread_kernel(table, sizes, more, box_ref, grad_ref, weight_ref, *refs):
-    held_ref = refs[0]
-    total_ref, down_ref, across_ref, sums_ref, rows_ref, crop_ref = refs[-6:]
+def spread_kernel(table, sizes, box_ref, grad_ref, weight_ref, *refs):
+    total_ref, sign_ref, down_ref, across_ref, sums_ref, rows_ref, crop_ref = refs[-7:]
+    sign_ref[...] = jnp.zeros_like(sign_ref)
     height, width, part, level_count = sizes
     images = box_ref.shape[0]
     for n in range(images):
@@ -164,13 +166,12 @@
                 for q in range(1, POOL):
                     total = total + across_ref[n, q, x : x + 1, :] * pieces[q]
                 sums_ref[x * part : (x + 1) * part, lanes] = total.astype(bf16)
-        total = lax.dot_general(
+        total_ref[n] = lax.dot_general(
             sums_ref[...], down_ref[n], (((1,), (1,)), ((), ())), preferred_element_type=f32
-        )
-        total_ref[n] = held_ref[n] + total if more else total
-
-
-def crop_block(table, sizes, features, boxes, maps, weight=None, out_type=bf16, earlier=()):
+        ).astype(bf16)
+
+
+def crop_block(table, sizes, features, boxes, maps, weight=None, out_type=bf16, earlier=(), kept_in=like):
     height, width, part, level_count = sizes
     images = boxes.shape[0]
     product = weight is not None
@@ -183,7 +184,7 @@
         more = [pltpu.VMEM((rows, features), bf16)]
     else:
         out_spec = pl.BlockSpec((LANES, features), lambda n: (n, 0))
-        out_shape = like((rows, features), bf16)
+        out_shape = kept_in((rows, features), bf16)
         more = []
     return pl.pallas_call(
         functools.partial(crop_kernel, table, sizes, product),
@@ -193,9 +194,13 @@
             pl.BlockSpec((None, width * part, level_count * height), lambda n: (n, 0, 0)),
         ]
         + [WHOLE for one in first[2:]]
-        + [ANY for one in earlier],
-        out_specs=[pl.BlockSpec((features, LANES), lambda n: (0, n)), out_spec],
-        out_shape=[like((features, rows), bf16), out_shape],
+        + [FAR for one in earlier],
+        out_specs=[
+            pl.BlockSpec((features, LANES), lambda n: (0, n)),
+            out_spec,
+            pl.BlockSpec((8, LANES), lambda n: (0, 0)),
+        ],
+        out_shape=[kept_in((features, rows), bf16), out_shape, SIGN],
         scratch_shapes=[
             pltpu.VMEM((level_count * height, POOL * LANES), bf16),
             pltpu.VMEM((POOL, width, LANES), f32),
@@ -209,22 +214,32 @@
     )(*first, *earlier)
 
 
-def multiply_kernel(scalars, arrays, outs):
-    outs[0][...] = jnp.dot(
-        arrays[0][...], arrays[1][...], preferred_element_type=f32
-    ).astype(outs[0].dtype)
-
-
-def spread_block(table, sizes, boxes, grads, weight, held, earlier=()):
+def multiply_kernel(rows_ref, weight_ref, out_ref, sign_ref):
+    out_ref[...] = jnp.dot(rows_ref[...], weight_ref[...], preferred_element_type=f32).astype(bf16)
+    sign_ref[...] = jnp.zeros_like(sign_ref)
+
+
+def multiply(rows, weight):
+    return pl.pallas_call(
+        multiply_kernel,
+        in_specs=[WHOLE, WHOLE],
+        out_specs=[WHOLE, WHOLE],
+        out_shape=[like((rows.shape[0], weight.shape[1]), bf16), SIGN],
+        compiler_params=pltpu.CompilerParams(vmem_limit_bytes=24 * 2**20),
+        cost_estimate=LARGE_COST,
+        name="multiply",
+    )(rows, weight)
+
+
+def spread_block(table, sizes, boxes, grads, weight, earlier=()):
     height, width, part, level_count = sizes
     images = boxes.shape[0]
     features = weight.shape[0]
-    held = [] if held is None else [held]
     return pl.pallas_call(
-        functools.partial(spread_kernel, table, sizes, bool(held)),
-        in_specs=[WHOLE, WHOLE, WHOLE] + [WHOLE for one in held] + [ANY for one in earlier],
-        out_specs=WHOLE,
-        out_shape=like((images, width * part, level_count * height), f32),
+        functools.partial(spread_kernel, table, sizes),
+        in_specs=[WHOLE, WHOLE, WHOLE] + [FAR for one in earlier],
+        out_specs=[WHOLE, WHOLE],
+        out_shape=[like((images, width * part, level_count * height), bf16), SIGN],
         scratch_shapes=[
             pltpu.VMEM((images, level_count * height, POOL * LANES), bf16),
             pltpu.VMEM((images, POOL, width, LANES), f32),
@@ -235,7 +250,7 @@
         compiler_params=pltpu.CompilerParams(vmem_limit_bytes=24 * 2**20),
         cost_estimate=LARGE_COST,
         name="spread_block",
-    )(boxes, grads, weight, *held, *earlier)
+    )(boxes, grads, weight, *earlier)
 
 
 def call(kernel, outs, scalars, arrays, earlier=(), scratch=(), name=None):
@@ -243,19 +258,20 @@
 
     def body(*refs):
         at, end = len(scalars), len(scalars) + len(arrays)
-        kernel(refs[:at], refs[at:end], refs[end + len(earlier) :])
-
-    result = pl.pallas_call(
+        later = refs[end + len(earlier) :]
+        later[len(outs)][...] = jnp.zeros(SIGN.shape, SIGN.dtype)
+        kernel(refs[:at], refs[at:end], (*later[: len(outs)], *later[len(outs) + 1 :]))
+
+    return pl.pallas_call(
         body,
-        in_specs=[SCALAR for one in scalars] + [WHOLE for one in arrays] + [ANY for one in earlier],
-        out_specs=[WHOLE for one in outs],
-        out_shape=outs,
+        in_specs=[SCALAR for one in scalars] + [WHOLE for one in arrays] + [FAR for one in earlier],
+        out_specs=[WHOLE for one in (*outs, SIGN)],
+        out_shape=[*outs, SIGN],
         scratch_shapes=scratch,
         compiler_params=pltpu.CompilerParams(vmem_limit_bytes=24 * 2**20),
         cost_estimate=LARGE_COST,
         name=name,
     )(*[jnp.full((1,), one, jnp.int32) for one in scalars], *arrays, *earlier)
-    return result
 
 
 def tie_kernel(*refs):
@@ -265,43 +281,37 @@
 def tie(arrays, *earlier):
     return pl.pallas_call(
         tie_kernel,
-        in_specs=[ANY for one in (*arrays, *earlier)],
-        out_specs=[ANY for one in arrays],
+        in_specs=[FAR for one in (*arrays, *earlier)],
+        out_specs=[FAR for one in arrays],
         out_shape=[like(one.shape, one.dtype) for one in arrays],
         input_output_aliases={k: k for k in range(len(arrays))},
+        compiler_params=pltpu.CompilerParams(vmem_limit_bytes=2**20),
         cost_estimate=SMALL_COST,
         name="tie",
     )(*arrays, *earlier)
 
 
-def order_kernel(first, scalars, arrays, outs):
+def order_kernel(scalars, arrays, outs):
     for k, ref in enumerate(arrays):
-        outs[0][scalars[0][0] ^ k] = ref[first:]
-
-
-def in_order(at, arrays, first, earlier):
-    shape = (len(arrays), arrays[0].shape[0] - first) + arrays[0].shape[1:]
-    return call(
-        functools.partial(order_kernel, first),
-        [like(shape, arrays[0].dtype)],
-        [at],
-        arrays,
-        earlier,
-        name="in_order",
-    )[0]
+        outs[0][scalars[0][0] ^ k] = ref[...]
+
+
+def in_order(at, arrays, earlier):
+    shape = (len(arrays),) + arrays[0].shape
+    return call(order_kernel, [like(shape, arrays[0].dtype)], [at], arrays, earlier, name="in_order")[0]
 
 
 def full_small_kernel(rows, scalars, arrays, outs):
     units = outs[0].shape[1]
     for k, ref in enumerate(arrays):
         core = scalars[0][0] ^ k
-        for chip in range(ref.shape[0]):
-            for level in range(ref.shape[1]):
-                at = pl.multiple_of(((level * ref.shape[0] + chip) * 2 + core) * rows, rows)
-                outs[0][pl.ds(at, rows), :] = ref[chip, level, :rows, :]
+        for chip in range(4):
+            for level in range(ref.shape[2]):
+                at = pl.multiple_of(((level * 4 + chip) * 2 + core) * rows, rows)
+                outs[0][pl.ds(at, rows), :] = ref[chip // 2, chip % 2, level, :rows, :]
                 for part in range(2):
                     outs[1][pl.ds(at + part * (rows // 2), rows // 2), :] = ref[
-                        chip, level, rows:, part * (units // 2) : (part + 1) * (units // 2)
+                        chip // 2, chip % 2, level, rows:, part * (units // 2) : (part + 1) * (units // 2)
                     ]
 
 
@@ -328,7 +338,7 @@
     return last[:8] + last[8:]
 
 
-def small_product_kernel(rows, core_ref, first_ref, second_grad_ref, second_ref, slopes_ref, bias_ref, sent_ref, kept_ref, total_ref):
+def small_product_kernel(rows, core_ref, first_ref, second_grad_ref, second_ref, slopes_ref, bias_ref, sent_ref, kept_ref, sign_ref, total_ref):
     turned = (((0,), (0,)), ((), ()))
     units = first_ref.shape[1]
     total_ref[:, :units] = lax.dot_general(
@@ -339,6 +349,7 @@
     )
     split_rows(core_ref[0], total_ref, rows, sent_ref, kept_ref)
     put_biases(bias_ref[...], [sent_ref, kept_ref])
+    sign_ref[...] = jnp.zeros_like(sign_ref)
 
 
 def small_product(core, rows, first_act, second_grad, second_act, slopes, biases):
@@ -348,8 +359,8 @@
     return pl.pallas_call(
         functools.partial(small_product_kernel, rows),
         in_specs=[SCALAR] + [WHOLE] * 5,
-        out_specs=[WHOLE] * 2,
-        out_shape=[half, half],
+        out_specs=[WHOLE] * 3,
+        out_shape=[half, half, SIGN],
         scratch_shapes=[pltpu.VMEM((units, wide), f32)],
         compiler_params=pltpu.CompilerParams(vmem_limit_bytes=24 * 2**20),
         cost_estimate=LARGE_COST,
@@ -357,49 +368,56 @@
     )(jnp.full((1,), core, jnp.int32), first_act, second_grad, second_act, slopes, biases)
 
 
-def fold_kernel(rows, bit_ref, kept_ref, come_ref, *refs):
-    sent_out, kept_out, total_ref = refs[-3:]
+def fold_kernel(rows, chip_ref, kept_ref, come_ref, *refs):
+    outs, sign_ref, total_ref = refs[-6:-2], refs[-2], refs[-1]
+    sign_ref[...] = jnp.zeros_like(sign_ref)
     count, units = total_ref.shape[0], total_ref.shape[1] // 3 * 2
     total_ref[...] = kept_ref[:count, :].astype(f32) + come_ref[:count, :].astype(f32)
-    split_rows(bit_ref[0], total_ref, rows, sent_out, kept_out)
-    put_biases(get_biases(kept_ref, units) + get_biases(come_ref, units), [sent_out, kept_out])
-
-
-def fold_rows(bit, rows, kept, come, earlier):
+    for k, out in enumerate(outs):
+        for at in range(count // rows // 4):
+            first = pl.multiple_of((4 * at + (chip_ref[0] ^ k)) * rows, rows)
+            out[at * rows : (at + 1) * rows, :] = total_ref[pl.ds(first, rows), :].astype(bf16)
+    put_biases(get_biases(kept_ref, units) + get_biases(come_ref, units), outs)
+
+
+def fold_rows(chip, rows, kept, come, earlier):
     count = kept.shape[0] - 16
-    half = like((count // 2 + 16, kept.shape[1]), bf16)
+    quarter = like((count // 4 + 16, kept.shape[1]), bf16)
     return pl.pallas_call(
         functools.partial(fold_kernel, rows),
-        in_specs=[SCALAR, WHOLE, WHOLE] + [ANY for one in earlier],
-        out_specs=[WHOLE] * 2,
-        out_shape=[half, half],
+        in_specs=[SCALAR, WHOLE, WHOLE] + [FAR for one in earlier],
+        out_specs=[WHOLE] * 5,
+        out_shape=[quarter] * 4 + [SIGN],
         scratch_shapes=[pltpu.VMEM((count, kept.shape[1]), f32)],
         compiler_params=pltpu.CompilerParams(vmem_limit_bytes=24 * 2**20),
         cost_estimate=LARGE_COST,
         name="fold_rows",
-    )(jnp.full((1,), bit, jnp.int32), kept, come, *earlier)
+    )(jnp.full((1,), chip, jnp.int32), kept, come, *earlier)
 
 
 def last_fold_kernel(rows, scalars, arrays, outs):
-    units = outs[0].shape[1]
-    biases = get_biases(arrays[0], units) + get_biases(arrays[1], units)
-    put_biases(biases, outs)
-    for way, out in enumerate(outs):
-        at = pl.multiple_of((scalars[0][0] ^ way) * rows, rows)
-        total = sum(ref[pl.ds(at, rows), :].astype(f32) for ref in arrays).astype(bf16)
+    units = outs[0].shape[2]
+    biases = [get_biases(ref, units) for ref in arrays]
+    biases = (biases[0] + biases[1]) + (biases[2] + biases[3])
+    for place in range(outs[0].shape[0]):
+        at = slice(place * rows, (place + 1) * rows)
+        total = sum(ref[at, :].astype(f32) for ref in arrays).astype(bf16)
+        out = outs[0].at[place]
         out[:rows, :] = total[:, :units]
         for part in range(2):
             out[rows : rows // 2 * 3, part * (units // 2) : (part + 1) * (units // 2)] = total[
                 part * (rows // 2) : (part + 1) * (rows // 2), units:
             ]
+        put_biases(biases, [out])
 
 
 def small_sum_kernel(scalars, arrays, outs):
-    total = sum(ref[...].astype(f32) for ref in arrays)
+    came_ref = arrays[0]
+    count = came_ref.shape[0]
+    total = sum(came_ref[place].astype(f32) for place in range(count))
     rows, units = outs[0].shape
-    biases = [get_biases(ref, units) for ref in arrays]
-    outs[3][...] = (biases[0] + biases[1]) + (biases[2] + biases[3])
     outs[0][...] = total[:rows]
+    outs[3][...] = sum(get_biases(came_ref.at[place], units) for place in range(count))
     for part in range(2):
         at = slice(part * (rows // 2), (part + 1) * (rows // 2))
         beside = total[rows : rows // 2 * 3, part * (units // 2) : (part + 1) * (units // 2)]
@@ -414,7 +432,7 @@
 
 
 def head_kernel(
-    own_ref, one_ref, two_ref, three_ref, rows_ref, hidden_bias_ref, inner_ref, inner_bias_ref, heads_ref, heads_bias_ref,
+    own_ref, one_ref, two_ref, three_ref, labels_ref, ignore_ref, targets_ref, hidden_bias_ref, inner_ref, inner_bias_ref, heads_ref, heads_bias_ref,
     logits_ref, deltas_ref, first_act_ref, second_act_ref, slopes_ref, second_grad_ref, first_grad_ref, again_ref, bias_ref, first_slope_ref, second_slope_ref,
 ):
     first_pre = own_ref[...] + hidden_bias_ref[...]
@@ -431,10 +449,17 @@
     second_act_ref[...] = act
     heads = jnp.dot(act, heads_ref[...], preferred_element_type=f32) + heads_bias_ref[...]
     logits, deltas = heads[:, :LANES], heads[:, LANES:]
-    logits_ref[...] = logits[:, :CLS]
-    deltas_ref[...] = deltas[:, :BOX]
-    label = rows_ref[:, 0:1]
-    kept = 1.0 - rows_ref[:, 1:2]
+    facts = []
+    for n in range(labels_ref.shape[0]):
+        rows = slice(n * LANES, (n + 1) * LANES)
+        logits_ref[:, n, :] = logits[rows].T[:CLS]
+        deltas_ref[n] = deltas[rows].T[:BOX]
+        fact = [labels_ref[n : n + 1, :].astype(f32), ignore_ref[n : n + 1, :].astype(f32)]
+        fact += [targets_ref[n], jnp.zeros((2, LANES), f32)]
+        facts.append(jnp.concatenate(fact, axis=0).T)
+    facts = jnp.concatenate(facts, axis=0)
+    label = facts[:, 0:1]
+    kept = 1.0 - facts[:, 1:2]
     column = lax.broadcasted_iota(jnp.int32, logits.shape, 1)
     valid = column < CLS
     row_max = jnp.max(jnp.where(valid, logits, -jnp.inf), axis=1, keepdims=True)
@@ -443,9 +468,9 @@
     hot = (column.astype(f32) == label).astype(f32)
     logit_slope = (softmax_rows - hot) * (kept * np.float32(1.0 / RPI))
     column = lax.broadcasted_iota(jnp.int32, deltas.shape, 1)
-    target = rows_ref[:, 2:3]
+    target = facts[:, 2:3]
     for j in range(1, 4):
-        target = jnp.where((column & 3) == j, rows_ref[:, 2 + j : 3 + j], target)
+        target = jnp.where((column & 3) == j, facts[:, 2 + j : 3 + j], target)
     foreground = jnp.where(label < CLS - 1, kept, 0.0)
     hot = ((column >> 2).astype(f32) == label) & (column < BOX)
     delta_slope = jnp.where(
@@ -470,16 +495,17 @@
     bias_ref[2:3, : slopes.shape[1]] = jnp.sum(slopes.astype(f32), axis=0, keepdims=True)
 
 
-def head_block(own, come, rows, hidden_bias, inner, inner_bias, heads, heads_bias):
+def head_block(own, come, labels, ignore, targets, hidden_bias, inner, inner_bias, heads, heads_bias):
     count, units = own.shape
     wide = heads.shape[1]
+    images = labels.shape[0]
     return pl.pallas_call(
         head_kernel,
-        in_specs=[pl.BlockSpec(memory_space=pltpu.VMEM)] * 10,
+        in_specs=[pl.BlockSpec(memory_space=pltpu.VMEM)] * 12,
         out_specs=[pl.BlockSpec(memory_space=pltpu.VMEM)] * 9,
         out_shape=[
-            like((count, CLS), f32),
-            like((count, BOX), f32),
+            like((CLS, images, LANES), f32),
+            like((images, BOX, LANES), f32),
             like((count, units), bf16),
             like((count, units), bf16),
             like((count, wide), bf16),
@@ -492,11 +518,11 @@
         compiler_params=pltpu.CompilerParams(vmem_limit_bytes=24 * 2**20),
         cost_estimate=LARGE_COST,
         name="head_block",
-    )(own, *come, rows, hidden_bias, inner, inner_bias, heads, heads_bias)
+    )(own, *come, labels, ignore, targets, hidden_bias, inner, inner_bias, heads, heads_bias)
 
 
 def maps_kernel(scalars, arrays, outs):
-    maps_ref, by_class_ref, across_first_ref = arrays[:3]
+    maps_ref, by_class_ref, across_first_ref = arrays
     pick_ref = outs[-1]
     size, part = by_class_ref.shape[:2]
     images = maps_ref.shape[0]
@@ -509,20 +535,17 @@
         flat = jnp.dot(flat, across_first_ref[...], preferred_element_type=f32).astype(bf16)
         for way in range(size):
             outs[way][n * part : (n + 1) * part, :] = flat[way * part : (way + 1) * part]
-    for out in outs[:size]:
-        for below in arrays[3:]:
-            out[images * part :, :] = below[...]
 
 
 def maps_back_kernel(scalars, arrays, outs):
-    came_refs, (by_class_ref, across_first_ref) = arrays[:-2], arrays[-2:]
+    came_ref, by_class_ref, across_first_ref = arrays
     out_ref, pick_ref, flat_ref = outs
     size, part = by_class_ref.shape[:2]
     for way in range(size):
         pick_ref[way * part : (way + 1) * part, :] = by_class_ref[scalars[0][0] ^ way]
     for n in range(out_ref.shape[0]):
         for way in range(size):
-            flat_ref[way * part : (way + 1) * part, :] = came_refs[way][n]
+            flat_ref[way * part : (way + 1) * part, :] = came_ref[scalars[0][0] ^ way, n]
         cells = lax.dot_general(
             across_first_ref[...], flat_ref[...], (((1,), (1,)), ((), ())), preferred_element_type=f32
         ).astype(bf16)
@@ -543,10 +566,11 @@
     height, width, part, level_count = sizes
     for n in range(arrays[0].shape[0]):
         for x in range(width):
-            for k, ref in enumerate(outs):
-                ref[n, :, x * height : (x + 1) * height] = arrays[0][
-                    n, x * part : (x + 1) * part, k * height : (k + 1) * height
-                ].astype(bf16)
+            for k in range(level_count):
+                outs[0][scalars[0][0] ^ k, n, :, x * height : (x + 1) * height] = sum(
+                    ref[n, x * part : (x + 1) * part, k * height : (k + 1) * height].astype(f32)
+                    for ref in arrays
+                ).astype(bf16)
 
 
 def split_span_kernel(scalars, arrays, outs):
@@ -603,48 +627,42 @@
 
 
 def product_kernel(number, parts, with_sum, at_ref, *refs):
-    grad_refs, crop_refs, refs = refs[:parts], refs[parts : parts * (number + 1)], refs[parts * (number + 1) :]
+    grad_refs, crop_refs, refs = refs[:parts], refs[parts : 2 * parts], refs[2 * parts :]
+    sign_ref, refs = refs[-1], refs[:-1]
+    sign_ref[...] = jnp.zeros_like(sign_ref)
     outs = refs[-number:] if with_sum else [refs[-1].at[n] for n in range(number)]
+    rows = crop_refs[0].shape[0] // 8
     for n in range(number):
         total = refs[0][n].astype(f32) if with_sum else 0.0
-        for k, grad_ref in enumerate(grad_refs):
+        at = pl.multiple_of(at_ref[n] * rows, 16)
+        for grad_ref, crop_ref in zip(grad_refs, crop_refs):
             total = total + jnp.dot(
-                crop_refs[n * parts + k][...], grad_ref[...], preferred_element_type=f32
+                crop_ref[pl.ds(at, rows), :], grad_ref[...], preferred_element_type=f32
             )
         outs[n][...] = total.astype(bf16)
 
 
 def piece_product(crops, grads, pieces, come, earlier):
-    features, count = crops[0].shape
+    features = crops[0].shape[0]
     units = grads[0].shape[1]
     rows = features // 8
     number = len(pieces)
     with_sum = come is not None
-    crops = [one.reshape(8, rows, count) for one in crops]
-    single = pl.BlockSpec((rows, units), lambda n, at: (0, 0))
-    stacked = pl.BlockSpec((number, rows, units), lambda n, at: (0, 0, 0))
+    come = [come] if with_sum else []
+    outs = (
+        [like((rows, units), bf16)] * number if with_sum else [like((number, rows, units), bf16)]
+    )
     return pl.pallas_call(
         functools.partial(product_kernel, number, len(grads), with_sum),
-        grid_spec=pltpu.PrefetchScalarGridSpec(
-            num_scalar_prefetch=1,
-            grid=(1,),
-            in_specs=[pl.BlockSpec(one.shape, lambda n, at: (0, 0)) for one in grads]
-            + [
-                pl.BlockSpec((None, rows, count), lambda n, at, k=k: (at[k], 0, 0))
-                for k in range(number)
-                for one in crops
-            ]
-            + ([stacked] if with_sum else [])
-            + [ANY for one in earlier],
-            out_specs=[single] * number if with_sum else stacked,
-        ),
-        out_shape=[like((rows, units), bf16)] * number
-        if with_sum
-        else like((number, rows, units), bf16),
+        in_specs=[SCALAR]
+        + [WHOLE for one in (*grads, *crops, *come)]
+        + [FAR for one in earlier],
+        out_specs=[WHOLE for one in (*outs, SIGN)],
+        out_shape=[*outs, SIGN],
         compiler_params=pltpu.CompilerParams(vmem_limit_bytes=24 * 2**20),
         cost_estimate=LARGE_COST,
         name="piece_product",
-    )(jnp.stack(pieces), *grads, *crops * number, *([come] if with_sum else []), *earlier)
+    )(jnp.stack(pieces), *grads, *crops, *come, *earlier)
 
 
 def butterfly(array):
@@ -746,7 +764,7 @@
             [(k * length + j, k * span + j) for k in range(size) for j in range(length)],
         )
         total = [pltpu.VMEM((size * span, units), f32)]
-        sent = call(
+        *sent, sign = call(
             split_span_kernel,
             [like((span, units), bf16)] * size,
             [z],
@@ -755,7 +773,7 @@
             name="split_span",
         )
         came = exchange_ways(sent, "level")
-        piece, own_piece = call(
+        piece, own_piece, sign = call(
             join_span_kernel,
             [like((room, units), bf16)] * 2,
             [z],
@@ -788,57 +806,59 @@
         pltpu.VMEM((channels, channels), bf16),
         pltpu.VMEM((channels, spots), bf16),
     ]
-    small_rows = small.shape[0] // 2 * 3 if direct else 0
+    small_rows = small.shape[0] // 2 * 3
     maps = call(
         maps_kernel,
-        [like((images * part + small_rows, spots), bf16)] * size,
+        [like((images * part, spots), bf16)] * size,
         [z],
-        [pyramid[0].reshape(images, spots, channels), by_class, across_first]
-        + ([pack_rows(small)] if direct else []),
+        [pyramid[0].reshape(images, spots, channels), by_class, across_first],
         scratch=picks[:1],
         name="maps",
-    )
+    )[:size]
     if direct:
-        maps = [maps[0], *tie(maps[1:], piece)]
+        maps = [maps[0], *tie(maps[1:], sign)]
     maps_came = exchange_ways(maps[:3], "level")
     maps_came.append(swap(tie([maps[3]], maps_came[1])[0], "level", 3))
-    maps = call(
+    maps, sign = call(
         functools.partial(arrange_kernel, sizes),
-        [like((images, width * part, size * height), bf16)],
+        [pltpu.VMEM((images, width * part, size * height), bf16)],
         [],
         maps_came,
         name="arrange",
-    )[0]
+    )
 
     ways = (2, 3, 1, 0)
-    crops, owns, came_sums = [], [], []
+    crops, owns, signs, came_sums = [], [], [], []
+    crops_in = pltpu.VMEM if direct else like
     for turn, way in enumerate(ways):
         if turn == 0:
-            crop, turned = crop_block(table, sizes, features, boxes[way], maps)
+            crop, turned, sign = crop_block(
+                table, sizes, features, boxes[way], maps, kept_in=crops_in
+            )
             if direct:
-                pieces = tie(pieces, crop)
+                own_piece, smalls = tie([own_piece, pack_rows(small)], sign)
+                smalls = exchange_ways([smalls] * size, "level")
+                pieces = [own_piece, *pieces[1:]]
                 pieces = sum(([one, swap(one, "img", 1)] for one in pieces), [])
                 weight = gather_pieces(jnp.full((1,), place, jnp.int32), pieces)
-            owns += call(
-                multiply_kernel, [like((block_rows, units), bf16)], [], [turned, weight], name="multiply"
+            own, sign = multiply(turned, weight)
+        else:
+            crop, own, sign = crop_block(
+                table, sizes, features, boxes[way], maps, weight, bf16 if way else f32, signs[-1:], crops_in
             )
-        else:
-            crop, own = crop_block(
-                table, sizes, features, boxes[way], maps, weight, bf16 if way else f32, owns[-1:]
-            )
-            owns.append(own)
+        owns.append(own)
+        signs.append(sign)
         crops.append(crop)
         if way:
             came_sums.append(swap(owns[-1], "level", way))
 
     if direct:
-        smalls = in_order(z, maps_came, images * part, owns[:1])
-        smalls = in_order(
-            place // 2, [smalls] + [swap(smalls, "img", bit) for bit in (2, 4, 6)], 0, owns[2:3]
-        )
-        full_inner, full_heads = call(
+        smalls = in_order(z, smalls, signs[:1])
+        smalls = in_order(x, [smalls, swap(smalls, "img", 2)], signs[1:2])
+        smalls = in_order(y, [smalls, swap(smalls, "img", 4)], signs[2:3])
+        full_inner, full_heads, sign = call(
             functools.partial(full_small_kernel, small.shape[0]),
-            [like((units, units), bf16), like((units, units // 2), bf16)],
+            [pltpu.VMEM((units, units), bf16), pltpu.VMEM((units, units // 2), bf16)],
             [core],
             [smalls, swap(smalls, "img", 1)],
             name="full_small",
@@ -847,19 +867,12 @@
         smalls = lax.all_gather(small, AXES, axis=0, tiled=True)
         full_inner, full_heads = smalls[:, :units], smalls[:, units:]
 
-    row_facts = jnp.concatenate(
-        [
-            labels.reshape(-1, 1).astype(f32),
-            crowd_ignore.reshape(-1, 1).astype(f32),
-            targets.reshape(-1, 4),
-            jnp.zeros((block_rows, 2), f32),
-        ],
-        axis=1,
-    )
     logits, deltas, first_act, second_act, slopes, second_grad, first_grad, first_again, bias_sums = head_block(
         owns[-1],
         came_sums,
-        row_facts,
+        labels,
+        crowd_ignore,
+        jnp.transpose(targets, (0, 2, 1)),
         hidden_bias[None],
         full_inner,
         inner_bias[None],
@@ -871,58 +884,57 @@
     far = swap(first_grad, "level", 2)
     grad_of = {0: first_grad, 1: near, 2: far}
 
-    def take_up(way, held, earlier=()):
-        return spread_block(table, sizes, boxes[way], grad_of[way], weight, held, earlier)
+    shares = []
+
+    def take_up(way, earlier=()):
+        share, sign = spread_block(table, sizes, boxes[way], grad_of[way], weight, earlier)
+        shares.append(share)
+        return sign
 
     if direct:
         count = small.shape[0]
-        sent, kept = small_product(
+        sent, kept, sign = small_product(
             core, count, first_act, second_grad, second_act, slopes, bias_sums
         )
-        held = take_up(0, None, [kept])
-        sent, kept = fold_rows(x, count, kept, swap(sent, "img", 1), [held])
-        grad_of[3] = swap(tie([first_again], far, kept)[0], "level", 3)
-        held = take_up(1, held, [kept])
-        sent, kept = fold_rows(y, count, kept, swap(sent, "img", 2), [held])
-        held = take_up(2, held, [kept])
-        smalls = call(
-            functools.partial(last_fold_kernel, count),
-            [like((small_rows + 16, units), bf16)] * size,
-            [z],
-            [kept, swap(sent, "img", 4)],
-            [held],
-            name="last_fold",
-        )
+        sign = take_up(0, [sign])
+        *quarters, sign = fold_rows(place // 2, count, kept, swap(sent, "img", 1), [sign])
+        quarters = [
+            swap(one, "img", bit) if bit else one for one, bit in zip(quarters, (0, 2, 4, 6))
+        ]
+        grad_of[3] = swap(tie([first_again], far, sign)[0], "level", 3)
+        sign = take_up(1, [sign])
+        sign = take_up(2, [sign])
 
         grads = [grad_of[way] for way in ways]
         parts, others = {}, {}
 
-        def for_other(bits, earlier):
+        def for_other(bits, sign):
             at = [place ^ bit ^ 1 for bit in bits]
-            products = piece_product(crops, grads, at, None, earlier)
+            products, sign = piece_product(crops, grads, at, None, [sign])
             others[bits] = swap(products, "img", 1)
-            return [products]
-
-        def for_own(bits, earlier):
+            return sign
+
+        def for_own(bits, sign):
             at = [place ^ bit for bit in bits]
-            own = piece_product(crops, grads, at, others[bits], earlier)
+            *own, sign = piece_product(crops, grads, at, others[bits], [sign])
             for one, bit in zip(own, bits):
                 parts[bit] = swap(one, "img", bit) if bit else one
-            return own
-
-        earlier = for_other((6,), smalls[:1])
-        earlier = for_other((2, 4), earlier)
-        earlier = for_own((6,), earlier)
-        held = take_up(3, held, earlier)
-        back = call(
-            functools.partial(arrange_back_kernel, sizes),
-            [like((images, part, spots), bf16)] * size,
-            [],
-            [held],
-            name="arrange_back",
-        )
-        earlier = for_other((0,), back[:1])
-        inner_sum, class_sum, delta_sum, bias_total = call(
+            return sign
+
+        sign = for_other((6,), sign)
+        sign = for_other((2, 4, 0), sign)
+        sign = for_own((6,), sign)
+        sign = for_own((2, 4, 0), sign)
+        smalls, sign = call(
+            functools.partial(last_fold_kernel, count),
+            [like((size, small_rows + 16, units), bf16)],
+            [z],
+            quarters,
+            [sign],
+            name="last_fold",
+        )
+        sign = take_up(3, [sign])
+        inner_sum, class_sum, delta_sum, bias_total, sign = call(
             small_sum_kernel,
             [
                 like((count, units), f32),
@@ -931,22 +943,36 @@
                 like((8, units), f32),
             ],
             [],
-            exchange_ways(smalls, "level"),
-            earlier,
+            [exchange(smalls, "level")],
+            [sign],
             name="small_sum",
         )
-        earlier = for_own((2, 4), [inner_sum])
-        earlier = for_own((0,), earlier)
+        back, sign = call(
+            functools.partial(arrange_back_kernel, sizes),
+            [like((size, images, part, spots), bf16)],
+            [z],
+            shares,
+            [sign],
+            name="arrange_back",
+        )
+        *sent, sign = call(
+            return_span_kernel,
+            [like((span, units), bf16)] * size,
+            [z],
+            [from_span.T, *[parts[bit] for bit in (0, 2, 4, 6)]],
+            [sign],
+            scratch=total,
+            name="return_span",
+        )
     else:
-        held = None
         grad_of[3] = swap(first_again, "level", 3)
         for way in range(size):
-            held = take_up(way, held)
-        back = call(
+            take_up(way)
+        back, sign = call(
             functools.partial(arrange_back_kernel, sizes),
-            [like((images, part, spots), bf16)] * size,
-            [],
-            [held],
+            [like((size, images, part, spots), bf16)],
+            [z],
+            shares,
             name="arrange_back",
         )
         bias_total = butterfly(bias_sums)
@@ -969,37 +995,32 @@
             tiled=True,
         )
 
-    map_grads = call(
+    map_grads, sign = call(
         maps_back_kernel,
         [like((images, spots, channels), f32)],
         [z],
-        [*exchange_ways(back, "level"), by_class, across_first],
+        [exchange(back, "level"), by_class, across_first],
+        [sign],
         scratch=picks,
         name="maps_back",
-    )[0].reshape(1, images, height, width, channels)
+    )
+    map_grads = map_grads.reshape(1, images, height, width, channels)
 
     if direct:
-        sent = call(
-            return_span_kernel,
-            [like((span, units), bf16)] * size,
-            [z],
-            [from_span.T, *[parts[bit] for bit in (0, 2, 4, 6)]],
-            scratch=total,
-            name="return_span",
-        )
         hidden_sum = call(
             join_span_kernel,
             [like((rows, units), f32)],
             [z],
             [to_span.T, *exchange_ways(sent, "level")],
+            [sign],
             scratch=total,
             name="join_span",
         )[0]
 
     head_bias = bias_total[2, : class_room + delta_room]
     return (
-        logits.reshape(images, regions, -1),
-        deltas.reshape(images, regions, -1),
+        jnp.transpose(logits, (1, 2, 0)),
+        jnp.transpose(deltas, (0, 2, 1)),
         map_grads,
         hidden_sum,
         bias_total[0],

time: 302 us -> 276 us (0.914)
  local copies, waits for them, and re-layouts: 34.1 us -> 18.4 us
  waiting for transfers between devices: 96.3 us -> 84.7 us
  starting transfers between devices: 41.2 us -> 50 us
  Pallas kernels: 123 us -> 115 us
    ppermute x41 -> x37, waiting for transfers between devices: 96.3 us -> 62 us  [swap(): return lax.ppermute(array, axis, [(at, at ^ bit) for at in range(size)])]
    all_to_all x0 -> x2, waiting for transfers between devices: none -> 22.7 us  [exchange(): return lax.all_to_all(array, axis, split_axis=0, concat_axis=0, tiled=True)]
    unnamed x157 -> x103, local copies, waits for them, and re-layouts: 32.1 us -> 16.6 us
    all_to_all x0 -> x2, starting transfers between devices: none -> 9.85 us  [exchange(): return lax.all_to_all(array, axis, split_axis=0, concat_axis=0, tiled=True)]
    pallas_call x6 -> x4, Pallas kernels: 19.3 us -> 9.48 us  [piece_product(): pl.pallas_call(functools.partial(product_kernel, number, len(grads), with...]
    ppermute x41 -> x37, starting transfers between devices: 41.2 us -> 40.1 us  [swap(): return lax.ppermute(array, axis, [(at, at ^ bit) for at in range(size)])]
    pallas_call x8 -> x9, Pallas kernels: 38.4 us -> 38.6 us  [the longest x4 35.7 us: spread_block(): pl.pallas_call(functools.partial(spread_kernel, table, sizes), in_specs=[...]
  transfers between devices with their start and end apart: 41 -> 39, of which waited for: 17 -> 14; matrix products, arithmetic and copies ran while one was open for 1% -> 1% of each run, Pallas kernels for 37% -> 39%
where the time goes in v3:
time: 276 us; the launch traced here: 272 us
  Pallas kernels  115 us (42%)
  waiting for transfers between devices  84.7 us (31%)
  starting transfers between devices  50 us (18%)
  local copies, waits for them, and re-layouts  18.4 us (7%)
    ppermute x37, waiting for transfers between devices, swap(): return lax.ppermute(array, axis, [(at, at ^ bit) for at in range(size)])  62 us
    ppermute x37, starting transfers between devices, swap(): return lax.ppermute(array, axis, [(at, at ^ bit) for at in range(size)])  40.1 us
    pallas_call x4, Pallas kernels, spread_block(): pl.pallas_call(functools.partial(spread_kernel, table, sizes), in_specs=[...  35.7 us
    pallas_call x4, Pallas kernels, crop_block(): pl.pallas_call(functools.partial(crop_kernel, table, sizes, product), gri...  34.8 us
    all_to_all x2, waiting for transfers between devices, exchange(): return lax.all_to_all(array, axis, split_axis=0, concat_axis=0, tiled=True)  22.7 us
    pallas_call x14, Pallas kernels, call(): pl.pallas_call(body, in_specs=[SCALAR for one in scalars] + [WHOLE for on...  22.5 us
    unnamed x103, local copies, waits for them, and re-layouts  16.6 us
    all_to_all x2, starting transfers between devices, exchange(): return lax.all_to_all(array, axis, split_axis=0, concat_axis=0, tiled=True)  9.85 us
  transfers between devices with their start and end apart: 39, of which 14 were waited for; matrix products, arithmetic and copies ran while one was open for 1% of the time, Pallas kernels for 39%

profile of v3, /device:TPU:8, one launch (start us, length us, event | category | flops | bytes accessed | tf_op | source)
XLA Modules:
  0.0 271.8 jit_solution(7588242520738265)
XLA Ops:
  2.2 1.1 copy-done.5
  3.3 1.0 copy-done.16
  5.3 1.4 split_span.1
  6.7 3.0 %collective-permute-start.1 = (bf16[104,1024]{1,0:T(8,128)(2,1)S(1)}, bf16[104,1024]{1,0:T(8,128)(2,1)S(1)}, u32[]{:S(2)}, u32[]{:S(2)}) collective-permute-start(bf16[104,1024]{1,0:T(8,128)(2,1)S(1)} %get-tuple-element.100), channel_id=1, source_target_pairs={{0,16},{8,24},{16,0},{24,8},{1,17},{9,25},{17,1},{25,9},{2,18},{10... | collective-permute-start | bytes 638984 | tf_op jit(solution)/shard_map/ppermute | solution.py:618
  10.3 2.0 maps.1
  12.2 3.0 %collective-permute-done.refs_3_ = bf16[104,1024]{1,0:T(8,128)(2,1)S(1)} collective-permute-done((bf16[104,1024]{1,0:T(8,128)(2,1)S(1)}, bf16[104,1024]{1,0:T(8,128)(2,1)S(1)}, u32[]{:S(2)}, u32[]{:S(2)}) %collective-permute-start) | collective-permute-done | bytes 213024 | tf_op jit(solution)/shard_map/ppermute | solution.py:618
  15.3 9.2 %collective-permute-done.1.refs_4_ = bf16[104,1024]{1,0:T(8,128)(2,1)S(1)} collective-permute-done((bf16[104,1024]{1,0:T(8,128)(2,1)S(1)}, bf16[104,1024]{1,0:T(8,128)(2,1)S(1)}, u32[]{:S(2)}, u32[]{:S(2)}) %collective-permute-start.1) | collective-permute-done | bytes 213024 | tf_op jit(solution)/shard_map/ppermute | solution.py:618
  24.5 4.0 %collective-permute-done.2.refs_5_ = bf16[104,1024]{1,0:T(8,128)(2,1)S(1)} collective-permute-done((bf16[104,1024]{1,0:T(8,128)(2,1)S(1)}, bf16[104,1024]{1,0:T(8,128)(2,1)S(1)}, u32[]{:S(2)}, u32[]{:S(2)}) %collective-permute-start.2) | collective-permute-done | bytes 213024 | tf_op jit(solution)/shard_map/ppermute | solution.py:618
  28.6 1.6 join_span.2
  30.2 2.5 collective-permute-start.11
  33.8 3.1 %collective-permute-start.4 = (bf16[128,1024]{1,0:T(8,128)(2,1)S(1)}, bf16[128,1024]{1,0:T(8,128)(2,1)S(1)}, u32[]{:S(2)}, u32[]{:S(2)}) collective-permute-start(bf16[128,1024]{1,0:T(8,128)(2,1)S(1)} %get-tuple-element.108), channel_id=1, source_target_pairs={{0,16},{8,24},{16,0},{24,8},{1,17},{9,25},{17,1},{25,9},{2,18},{10... | collective-permute-start | bytes 786440 | tf_op jit(solution)/shard_map/ppermute | solution.py:618
  36.9 6.1 %collective-permute-done.3.refs_1_ = bf16[128,1024]{1,0:T(8,128)(2,1)S(1)} collective-permute-done((bf16[128,1024]{1,0:T(8,128)(2,1)S(1)}, bf16[128,1024]{1,0:T(8,128)(2,1)S(1)}, u32[]{:S(2)}, u32[]{:S(2)}) %collective-permute-start.3) | collective-permute-done | bytes 262176 | tf_op jit(solution)/shard_map/ppermute | solution.py:618
  42.9 1.6 collective-permute-start.5
  44.6 9.1 %collective-permute-done.4.refs_2_ = bf16[128,1024]{1,0:T(8,128)(2,1)S(1)} collective-permute-done((bf16[128,1024]{1,0:T(8,128)(2,1)S(1)}, bf16[128,1024]{1,0:T(8,128)(2,1)S(1)}, u32[]{:S(2)}, u32[]{:S(2)}) %collective-permute-start.4) | collective-permute-done | bytes 262176 | tf_op jit(solution)/shard_map/ppermute | solution.py:618
  53.7 4.3 %collective-permute-done.5.refs_3_ = bf16[128,1024]{1,0:T(8,128)(2,1)S(1)} collective-permute-done((bf16[128,1024]{1,0:T(8,128)(2,1)S(1)}, bf16[128,1024]{1,0:T(8,128)(2,1)S(1)}, u32[]{:S(2)}, u32[]{:S(2)}) %collective-permute-start.5) | collective-permute-done | bytes 262176 | tf_op jit(solution)/shard_map/ppermute | solution.py:618
  58.0 1.1 arrange.1
  59.1 6.9 %crop_block.4 = (bf16[3200,256]{1,0:T(8,128)(2,1)S(1)}, bf16[256,3200]{1,0:T(8,128)(2,1)S(1)}, f32[8,128]{1,0:T(8,128)S(1)}) custom-call(f32[2,8,128]{2,1,0:T(8,128)S(1)} %get-tuple-element.189.box_ref, bf16[2,1024,256]{2,1,0:T(8,128)(2,1)S(1)} %get-tuple-element.110.maps_ref), custom_call_target="tpu_custom_call" | custom-call | flops 40000000000 | bytes 1 | tf_op jit(solution)/shard_map/crop_block/pallas_call | solution.py:189
  66.0 1.1 copy-done.24
  68.9 1.7 collective-permute-start.18
  71.3 3.0 %collective-permute-start.16 = (bf16[48,1024]{1,0:T(8,128)(2,1)S(1)}, bf16[48,1024]{1,0:T(8,128)(2,1)S(1)}, u32[]{:S(2)}, u32[]{:S(2)}) collective-permute-start(bf16[48,1024]{1,0:T(8,128)(2,1)S(1)} %get-tuple-element.123.refs_1_), channel_id=1, source_target_pairs={{0,8},{8,0},{16,24},{24,16},{1,9},{9,1},{17,25},{25,17},{2,10},{10... | collective-permute-start | bytes 294920 | tf_op jit(solution)/shard_map/ppermute | solution.py:618
  74.4 2.0 gather_pieces.1.weight_ref.refs_0_
  76.4 2.9 %multiply.1 = (bf16[256,1024]{1,0:T(8,128)(2,1)}, f32[8,128]{1,0:T(8,128)S(1)}) custom-call(bf16[256,3200]{1,0:T(8,128)(2,1)S(1)} %copy-done.27, bf16[3200,1024]{1,0:T(8,128)(2,1)S(1)} %gather_pieces.1.weight_ref.refs_0_), custom_call_target="tpu_custom_call" | custom-call | flops 40000000000 | bytes 1 | tf_op jit(solution)/shard_map/multiply/pallas_call | solution.py:223
  80.0 1.5 collective-permute-start.19
  81.5 1.5 collective-permute-start.13
  83.0 9.4 %crop_block.5 = (bf16[3200,256]{1,0:T(8,128)(2,1)S(1)}, bf16[256,1024]{1,0:T(8,128)(2,1)}, f32[8,128]{1,0:T(8,128)S(1)}) custom-call(f32[2,8,128]{2,1,0:T(8,128)S(1)} %get-tuple-element.187.box_ref, bf16[2,1024,256]{2,1,0:T(8,128)(2,1)S(1)} %copy-done.29, bf16[3200,1024]{1,0:T(8,128)(2,1)S(1)} %gather_pieces.1.weight_ref.refs_0_, ...), custom_call_target="tpu_custom_call" | custom-call | flops 40000000000 | bytes 1 | tf_op jit(solution)/shard_map/crop_block/pallas_call | solution.py:189
  92.5 1.1 collective-permute-start.14
  94.2 1.5 collective-permute-start.20
  95.7 8.9 %crop_block.6 = (bf16[3200,256]{1,0:T(8,128)(2,1)S(1)}, bf16[256,1024]{1,0:T(8,128)(2,1)S(1)}, f32[8,128]{1,0:T(8,128)S(1)}) custom-call(f32[2,8,128]{2,1,0:T(8,128)S(1)} %get-tuple-element.188.box_ref, bf16[2,1024,256]{2,1,0:T(8,128)(2,1)S(1)} %copy-done.29, bf16[3200,1024]{1,0:T(8,128)(2,1)S(1)} %gather_pieces.1.weight_ref.refs_0_, ...), custom_call_target="tpu_custom_call" | custom-call | flops 40000000000 | bytes 1 | tf_op jit(solution)/shard_map/crop_block/pallas_call | solution.py:189
  104.6 1.8 collective-permute-start.15
  106.4 6.1 %collective-permute-done.20.refs_2_ = bf16[2,4,48,1024]{3,2,1,0:T(8,128)(2,1)S(1)} collective-permute-done((bf16[2,4,48,1024]{3,2,1,0:T(8,128)(2,1)S(1)}, bf16[2,4,48,1024]{3,2,1,0:T(8,128)(2,1)S(1)}, u32[]{:S(2)}, u32[]{:S(2)}) %collective-permute-start.20) | collective-permute-done | bytes 786464 | tf_op jit(solution)/shard_map/ppermute | solution.py:618
  113.2 9.6 %crop_block.7 = (bf16[3200,256]{1,0:T(8,128)(2,1)S(1)}, f32[256,1024]{1,0:T(8,128)S(1)}, f32[8,128]{1,0:T(8,128)}) custom-call(f32[2,8,128]{2,1,0:T(8,128)S(1)} %get-tuple-element.190.box_ref, bf16[2,1024,256]{2,1,0:T(8,128)(2,1)S(1)} %copy-done.29, bf16[3200,1024]{1,0:T(8,128)(2,1)S(1)} %gather_pieces.1.weight_ref.refs_0_, ...), custom_call_target="tpu_custom_call" | custom-call | flops 40000000000 | bytes 1 | tf_op jit(solution)/shard_map/crop_block/pallas_call | solution.py:189
  123.7 5.7 %collective-permute-done.14.two_ref = bf16[256,1024]{1,0:T(8,128)(2,1)} collective-permute-done((bf16[256,1024]{1,0:T(8,128)(2,1)}, bf16[256,1024]{1,0:T(8,128)(2,1)}, u32[]{:S(2)}, u32[]{:S(2)}) %collective-permute-start.14) | collective-permute-done | bytes 524320 | tf_op jit(solution)/shard_map/ppermute | solution.py:618
  129.4 4.7 %head_block.1 = (f32[81,2,128]{2,1,0:T(2,128)}, f32[2,320,128]{2,1,0:T(8,128)}, bf16[256,1024]{1,0:T(8,128)(2,1)S(1)}, bf16[256,1024]{1,0:T(8,128)(2,1)S(1)}, bf...) custom-call(f32[256,1024]{1,0:T(8,128)S(1)} %get-tuple-element.119.o, ...), custom_call_target="tpu_custom_call" | custom-call | flops 40000000000 | bytes 1 | tf_op jit(solution)/shard_map/head_block/pallas_call | solution.py:502
  134.1 1.7 collective-permute-start.24
  136.5 1.3 small_product.1
  137.9 8.9 %spread_block.4 = (bf16[2,1024,256]{2,1,0:T(8,128)(2,1)S(1)}, f32[8,128]{1,0:T(8,128)S(1)}) custom-call(f32[2,8,128]{2,1,0:T(8,128)S(1)} %get-tuple-element.190.box_ref, bf16[256,1024]{1,0:T(8,128)(2,1)S(1)} %get-tuple-element.131.grad_ref.refs_3_, bf16[3200,1024]{1,0:T(8,128)(2,1)S(1)} %gather_pieces.1.weight_ref.refs_0_, ...), custom_call_target="tpu_custom_call" | custom-call | flops 40000000000 | bytes 1 | tf_op jit(solution)/shard_map/spread_block/pallas_call | solution.py:238
  146.9 1.8 fold_rows.1
  149.2 1.5 collective-permute-start.27
  150.8 1.4 collective-permute-start.28
  152.2 5.8 %collective-permute-done.24.grad_ref.refs_1_.refs_0_ = bf16[256,1024]{1,0:T(8,128)(2,1)S(1)} collective-permute-done((bf16[256,1024]{1,0:T(8,128)(2,1)S(1)}, bf16[256,1024]{1,0:T(8,128)(2,1)S(1)}, u32[]{:S(2)}, u32[]{:S(2)}) %collective-permute-start.24) | collective-permute-done | bytes 524320 | tf_op jit(solution)/shard_map/ppermute | solution.py:618
  157.9 1.5 collective-permute-start.25
  159.4 8.9 %spread_block.5 = (bf16[2,1024,256]{2,1,0:T(8,128)(2,1)S(1)}, f32[8,128]{1,0:T(8,128)S(1)}) custom-call(f32[2,8,128]{2,1,0:T(8,128)S(1)} %get-tuple-element.188.box_ref, bf16[256,1024]{1,0:T(8,128)(2,1)S(1)} %collective-permute-done.22.grad_ref.refs_2_, bf16[3200,1024]{1,0:T(8,128)(2,1)S(1)} %gather_pieces.1.weight_ref.refs_0_, ...), custom_call_target="tpu_custom_call" | custom-call | flops 40000000000 | bytes 1 | tf_op jit(solution)/shard_map/spread_block/pallas_call | solution.py:238
  169.3 9.1 %spread_block.6 = (bf16[2,1024,256]{2,1,0:T(8,128)(2,1)S(1)}, f32[8,128]{1,0:T(8,128)S(1)}) custom-call(f32[2,8,128]{2,1,0:T(8,128)S(1)} %copy-done.3, bf16[256,1024]{1,0:T(8,128)(2,1)S(1)} %collective-permute-done.24.grad_ref.refs_1_.refs_0_, bf16[3200,1024]{1,0:T(8,128)(2,1)S(1)} %gather_pieces.1.weight_ref.refs_0_, f32[8,128]{1,0:T(8,128)S(1)} %get-tuple-element.144.refs_0_), custom_call_target="tpu_custom_call" | custom-call | flops 40000000000 | bytes 1 | tf_op jit(solution)/shard_map/spread_block/pallas_call | solution.py:238
  179.3 3.7 %collective-permute-done.25.refs_1_.grad_ref = bf16[256,1024]{1,0:T(8,128)(2,1)S(1)} collective-permute-done((bf16[256,1024]{1,0:T(8,128)(2,1)S(1)}, bf16[256,1024]{1,0:T(8,128)(2,1)S(1)}, u32[]{:S(2)}, u32[]{:S(2)}) %collective-permute-start.25) | collective-permute-done | bytes 524320 | tf_op jit(solution)/shard_map/ppermute | solution.py:618
  183.0 1.0 piece_product.4
  184.1 3.3 %piece_product.5 = (bf16[3,400,1024]{2,1,0:T(8,128)(2,1)S(1)}, f32[8,128]{1,0:T(8,128)S(1)}) custom-call(s32[3]{0:T(128)S(1)} %pad_add_fusion.1.at_ref, bf16[256,1024]{1,0:T(8,128)(2,1)S(1)} %collective-permute-done.24.grad_ref.refs_1_.refs_0_, bf16[256,1024]{1,0:T(8,128)(2,1)S(1)} %collective-permute-done.25.refs_1_.grad_ref, ...), custom_call_target="tpu_custom_call" | custom-call | flops 40000000000 | bytes 1 | tf_op jit(solution)/shard_map/piece_product/pallas_call | solution.py:655
  188.0 1.9 piece_product.6
  189.9 1.5 collective-permute-start.33
  192.3 3.3 %piece_product.7 = (bf16[400,1024]{1,0:T(8,128)(2,1)S(1)}, bf16[400,1024]{1,0:T(8,128)(2,1)S(1)}, bf16[400,1024]{1,0:T(8,128)(2,1)S(1)}, f32[8,128]{1,0:T(8,128)S(1)}) custom-call(s32[3]{0:T(128)S(1)} %pad_add_fusion.at_ref, bf16[256,1024]{1,0:T(8,128)(2,1)S(1)} %collective-permute-done.24.grad_ref.refs_1_.refs_0_, ...), custom_call_target="tpu_custom_call" | custom-call | flops 40000000000 | bytes 1 | tf_op jit(solution)/shard_map/piece_product/pallas_call | solution.py:655
  195.6 2.6 last_fold.1
  198.2 4.5 %all-to-all-start = ((bf16[4,64,1024]{2,1,0:T(8,128)(2,1)}), bf16[4,64,1024]{2,1,0:T(8,128)(2,1)S(1)}, u32[]{:S(2)}, u32[]{:S(2)}) async-start(bf16[4,64,1024]{2,1,0:T(8,128)(2,1)} %get-tuple-element.164), calls=%async_computation | async-start | bytes 1048576 | tf_op jit(solution)/shard_map/all_to_all | solution.py:622
  203.4 1.5 collective-permute-start.32
  204.9 2.9 %copy-done.23 = bf16[3200,1024]{1,0:T(8,128)(2,1)S(1)} copy-done((bf16[3200,1024]{1,0:T(8,128)(2,1)S(1)}, bf16[3200,1024]{1,0:T(8,128)(2,1)}, u32[]{:S(2)}) %copy-start.23) | copy-done | bytes 6553624
  207.7 8.9 %spread_block.7 = (bf16[2,1024,256]{2,1,0:T(8,128)(2,1)S(1)}, f32[8,128]{1,0:T(8,128)S(1)}) custom-call(f32[2,8,128]{2,1,0:T(8,128)S(1)} %copy-done.1, bf16[256,1024]{1,0:T(8,128)(2,1)S(1)} %copy-done.7, bf16[3200,1024]{1,0:T(8,128)(2,1)S(1)} %copy-done.23, f32[8,128]{1,0:T(8,128)S(1)} %get-tuple-element.162.refs_0_), custom_call_target="tpu_custom_call" | custom-call | flops 40000000000 | bytes 1 | tf_op jit(solution)/shard_map/spread_block/pallas_call | solution.py:238
  219.8 2.3 arrange_back.1
  222.1 5.4 %all-to-all-start.1 = ((bf16[4,2,64,1024]{3,2,1,0:T(8,128)(2,1)}), bf16[4,2,64,1024]{3,2,1,0:T(8,128)(2,1)S(1)}, u32[]{:S(2)}, u32[]{:S(2)}) async-start(bf16[4,2,64,1024]{3,2,1,0:T(8,128)(2,1)} %get-tuple-element.167), calls=%async_computation.1 | async-start | bytes 2097152 | tf_op jit(solution)/shard_map/all_to_all | solution.py:622
  230.3 1.1 copy-done.39
  231.4 2.2 return_span.1
  234.4 2.9 %collective-permute-start.35 = (bf16[104,1024]{1,0:T(8,128)(2,1)S(1)}, bf16[104,1024]{1,0:T(8,128)(2,1)S(1)}, u32[]{:S(2)}, u32[]{:S(2)}) collective-permute-start(bf16[104,1024]{1,0:T(8,128)(2,1)S(1)} %get-tuple-element.177), channel_id=1, source_target_pairs={{0,16},{8,24},{16,0},{24,8},{1,17},{9,25},{17,1},{25,9},{2,18},{10... | collective-permute-start | bytes 638984 | tf_op jit(solution)/shard_map/ppermute | solution.py:618
  237.8 22.7 %all-to-all-done.1.refs_1_ = bf16[4,2,64,1024]{3,2,1,0:T(8,128)(2,1)S(1)} async-done(((bf16[4,2,64,1024]{3,2,1,0:T(8,128)(2,1)}), bf16[4,2,64,1024]{3,2,1,0:T(8,128)(2,1)S(1)}, u32[]{:S(2)}, u32[]{:S(2)}) %all-to-all-start.1) | async-done | bytes 1048608 | tf_op jit(solution)/shard_map/all_to_all | solution.py:622
  260.6 1.6 copy-done.14
  262.2 3.9 %maps_back.1 = (f32[2,1024,256]{2,1,0:T(8,128)}, f32[8,128]{1,0:T(8,128)S(1)}) custom-call(s32[1]{0:T(128)} %bitcast.refs_0_, bf16[4,2,64,1024]{3,2,1,0:T(8,128)(2,1)S(1)} %all-to-all-done.1.refs_1_, bf16[4,64,256]{2,1,0:T(8,128)(2,1)S(1)} %copy-done.20, bf16[1024,1024]{1,0:T(8,128)(2,1)S(1)} %copy-done.14, f32[8,128]{1,0:T(8,128)S(1)} %get-tuple-element.173.refs_4_), custom_call_target="tpu_custom_call" | custom-call | flops 40000000000 | bytes 1 | tf_op jit(solution)/shard_map/maps_back/pallas_call | solution.py:265
  266.1 3.4 %collective-permute-done.36.refs_5_ = bf16[104,1024]{1,0:T(8,128)(2,1)S(1)} collective-permute-done((bf16[104,1024]{1,0:T(8,128)(2,1)S(1)}, bf16[104,1024]{1,0:T(8,128)(2,1)S(1)}, u32[]{:S(2)}, u32[]{:S(2)}) %collective-permute-start.36) | collective-permute-done | bytes 213024 | tf_op jit(solution)/shard_map/ppermute | solution.py:618
  269.5 1.9 join_span.3
  (170 shorter events, 22.2 us)
Async XLA Ops:
  5.2 4.9 %copy-start.43 = (bf16[32,320]{1,0:T(8,128)(2,1)S(1)}, bf16[32,320]{1,0:T(8,128)(2,1)}, u32[]{:S(2)}) copy-start(bf16[32,320]{1,0:T(8,128)(2,1)} %param.31) | copy-start | bytes 61444
  5.2 4.9 %copy-start.44 = (bf16[32,81]{1,0:T(8,128)(2,1)S(1)}, bf16[32,81]{1,0:T(8,128)(2,1)}, u32[]{:S(2)}) copy-start(bf16[32,81]{1,0:T(8,128)(2,1)} %param.29) | copy-start | bytes 15556
  5.2 5.0 %copy-start.4 = (bf16[1,2,64,16,256]{4,3,2,1,0:T(8,128)(2,1)S(1)}, bf16[1,2,64,16,256]{4,3,2,1,0:T(8,128)(2,1)}, u32[]{:S(2)}) copy-start(bf16[1,2,64,16,256]{4,3,2,1,0:T(8,128)(2,1)} %param.19) | copy-start | bytes 3145732
  5.3 5.0 %copy-start.13 = (bf16[1024,1024]{1,0:T(8,128)(2,1)S(1)}, bf16[1024,1024]{1,0:T(8,128)(2,1)}, u32[]{:S(2)}) copy-start(bf16[1024,1024]{1,0:T(8,128)(2,1)} %constant.75.clone.refs_3_) | copy-start | bytes 6291460
  5.3 5.0 %copy-start.19 = (bf16[4,64,256]{2,1,0:T(8,128)(2,1)S(1)}, bf16[4,64,256]{2,1,0:T(8,128)(2,1)}, u32[]{:S(2)}) copy-start(bf16[4,64,256]{2,1,0:T(8,128)(2,1)} %constant.93.refs_2_) | copy-start | bytes 393220
  6.7 8.6 %collective-permute-start = (bf16[104,1024]{1,0:T(8,128)(2,1)S(1)}, bf16[104,1024]{1,0:T(8,128)(2,1)S(1)}, u32[]{:S(2)}, u32[]{:S(2)}) collective-permute-start(bf16[104,1024]{1,0:T(8,128)(2,1)S(1)} %get-tuple-element.99), channel_id=1, source_target_pairs={{0,8},{8,0},{16,24},{24,16},{1,9},{9,1},{17,25},{25,17},{2,10},{10... | collective-permute-start | bytes 638984 | tf_op jit(solution)/shard_map/ppermute | solution.py:618
  6.7 17.9 %collective-permute-start.1 = (bf16[104,1024]{1,0:T(8,128)(2,1)S(1)}, bf16[104,1024]{1,0:T(8,128)(2,1)S(1)}, u32[]{:S(2)}, u32[]{:S(2)}) collective-permute-start(bf16[104,1024]{1,0:T(8,128)(2,1)S(1)} %get-tuple-element.100), channel_id=1, source_target_pairs={{0,16},{8,24},{16,0},{24,8},{1,17},{9,25},{17,1},{25,9},{2,18},{10... | collective-permute-start | bytes 638984 | tf_op jit(solution)/shard_map/ppermute | solution.py:618
  9.7 18.9 %collective-permute-start.2 = (bf16[104,1024]{1,0:T(8,128)(2,1)S(1)}, bf16[104,1024]{1,0:T(8,128)(2,1)S(1)}, u32[]{:S(2)}, u32[]{:S(2)}) collective-permute-start(bf16[104,1024]{1,0:T(8,128)(2,1)S(1)} %get-tuple-element.101), channel_id=1, source_target_pairs={{0,24},{8,16},{16,8},{24,0},{1,25},{9,17},{17,9},{25,1},{2,26},{10... | collective-permute-start | bytes 638984 | tf_op jit(solution)/shard_map/ppermute | solution.py:618
  10.2 18.3 %copy-start.17 = (bf16[400,416]{1,0:T(8,128)(2,1)S(1)}, bf16[400,416]{1,0:T(8,128)(2,1)}, u32[]{:S(2)}) copy-start(bf16[400,416]{1,0:T(8,128)(2,1)} %constant.73.clone.refs_1_) | copy-start | bytes 998404
  30.2 37.5 %collective-permute-start.11 = (bf16[400,1024]{1,0:T(8,128)(2,1)S(1)}, bf16[400,1024]{1,0:T(8,128)(2,1)S(1)}, u32[]{:S(2)}, u32[]{:S(2)}) collective-permute-start(bf16[400,1024]{1,0:T(8,128)(2,1)S(1)} %get-tuple-element.114), channel_id=1, source_target_pairs={{0,6},{1,7},{2,4},{3,5},{4,2},{5,3},{6,0},{7,1},{8,14},{9,15},{10,... | collective-permute-start | bytes 2457608 | tf_op jit(solution)/shard_map/ppermute | solution.py:618
  32.6 35.5 %collective-permute-start.9 = (bf16[400,1024]{1,0:T(8,128)(2,1)S(1)}, bf16[400,1024]{1,0:T(8,128)(2,1)S(1)}, u32[]{:S(2)}, u32[]{:S(2)}) collective-permute-start(bf16[400,1024]{1,0:T(8,128)(2,1)S(1)} %get-tuple-element.114), channel_id=1, source_target_pairs={{0,4},{1,5},{2,6},{3,7},{4,0},{5,1},{6,2},{7,3},{8,12},{9,13},{10,... | collective-permute-start | bytes 2457608 | tf_op jit(solution)/shard_map/ppermute | solution.py:618
  33.1 35.1 %collective-permute-start.7 = (bf16[400,1024]{1,0:T(8,128)(2,1)S(1)}, bf16[400,1024]{1,0:T(8,128)(2,1)S(1)}, u32[]{:S(2)}, u32[]{:S(2)}) collective-permute-start(bf16[400,1024]{1,0:T(8,128)(2,1)S(1)} %get-tuple-element.114), channel_id=1, source_target_pairs={{0,2},{1,3},{2,0},{3,1},{4,6},{5,7},{6,4},{7,5},{8,10},{9,11},{10,... | collective-permute-start | bytes 2457608 | tf_op jit(solution)/shard_map/ppermute | solution.py:618
  33.7 9.2 %collective-permute-start.3 = (bf16[128,1024]{1,0:T(8,128)(2,1)S(1)}, bf16[128,1024]{1,0:T(8,128)(2,1)S(1)}, u32[]{:S(2)}, u32[]{:S(2)}) collective-permute-start(bf16[128,1024]{1,0:T(8,128)(2,1)S(1)} %get-tuple-element.107), channel_id=1, source_target_pairs={{0,8},{8,0},{16,24},{24,16},{1,9},{9,1},{17,25},{25,17},{2,10},{10... | collective-permute-start | bytes 786440 | tf_op jit(solution)/shard_map/ppermute | solution.py:618
  33.8 19.9 %collective-permute-start.4 = (bf16[128,1024]{1,0:T(8,128)(2,1)S(1)}, bf16[128,1024]{1,0:T(8,128)(2,1)S(1)}, u32[]{:S(2)}, u32[]{:S(2)}) collective-permute-start(bf16[128,1024]{1,0:T(8,128)(2,1)S(1)} %get-tuple-element.108), channel_id=1, source_target_pairs={{0,16},{8,24},{16,0},{24,8},{1,17},{9,25},{17,1},{25,9},{2,18},{10... | collective-permute-start | bytes 786440 | tf_op jit(solution)/shard_map/ppermute | solution.py:618
  42.9 15.0 %collective-permute-start.5 = (bf16[128,1024]{1,0:T(8,128)(2,1)S(1)}, bf16[128,1024]{1,0:T(8,128)(2,1)S(1)}, u32[]{:S(2)}, u32[]{:S(2)}) collective-permute-start(bf16[128,1024]{1,0:T(8,128)(2,1)S(1)} %tie.5), channel_id=1, source_target_pairs={{0,24},{8,16},{16,8},{24,0},{1,25},{9,17},{17,9},{25,1},{2,26},{10... | collective-permute-start | bytes 786440 | tf_op jit(solution)/shard_map/ppermute | solution.py:618
  44.6 14.5 %copy-start.2 = (f32[2,8,128]{2,1,0:T(8,128)}, f32[2,8,128]{2,1,0:T(8,128)S(1)}, u32[]{:S(2)}) copy-start(f32[2,8,128]{2,1,0:T(8,128)S(1)} %get-tuple-element.189.box_ref) | copy-start | bytes 24580
  44.6 38.4 %copy-start = (f32[2,8,128]{2,1,0:T(8,128)}, f32[2,8,128]{2,1,0:T(8,128)S(1)}, u32[]{:S(2)}) copy-start(f32[2,8,128]{2,1,0:T(8,128)S(1)} %get-tuple-element.187.box_ref) | copy-start | bytes 24580
  59.1 6.9 %copy-start.28 = (bf16[2,1024,256]{2,1,0:T(8,128)(2,1)}, bf16[2,1024,256]{2,1,0:T(8,128)(2,1)S(1)}, u32[]{:S(2)}) copy-start(bf16[2,1024,256]{2,1,0:T(8,128)(2,1)S(1)} %get-tuple-element.110.maps_ref) | copy-start | bytes 3145732
  67.7 3.6 %collective-permute-start.6 = (bf16[400,1024]{1,0:T(8,128)(2,1)}, bf16[400,1024]{1,0:T(8,128)(2,1)S(1)}, u32[]{:S(2)}, u32[]{:S(2)}) collective-permute-start(bf16[400,1024]{1,0:T(8,128)(2,1)} %get-tuple-element.113.refs_0_), channel_id=1, source_target_pairs={{0,1},{1,0},{2,3},{3,2},{4,5},{5,4},{6,7},{7,6},{8,9},{9,8},{10,11... | collective-permute-start | bytes 2457608 | tf_op jit(solution)/shard_map/ppermute | solution.py:618
  67.7 3.6 %collective-permute-start.12 = (bf16[400,1024]{1,0:T(8,128)(2,1)S(1)}, bf16[400,1024]{1,0:T(8,128)(2,1)}, u32[]{:S(2)}, u32[]{:S(2)}) collective-permute-start(bf16[400,1024]{1,0:T(8,128)(2,1)S(1)} %collective-permute-done.11.refs_6_), channel_id=1, source_target_pairs={{0,1},{1,0},{2,3},{3,2},{4,5},{5,4},{6,7},{7,6},{8,9},{9,8},{10,11... | collective-permute-start | bytes 2457608 | tf_op jit(solution)/shard_map/ppermute | solution.py:618
  68.2 6.2 %collective-permute-start.10 = (bf16[400,1024]{1,0:T(8,128)(2,1)S(1)}, bf16[400,1024]{1,0:T(8,128)(2,1)}, u32[]{:S(2)}, u32[]{:S(2)}) collective-permute-start(bf16[400,1024]{1,0:T(8,128)(2,1)S(1)} %collective-permute-done.9.refs_4_), channel_id=1, source_target_pairs={{0,1},{1,0},{2,3},{3,2},{4,5},{5,4},{6,7},{7,6},{8,9},{9,8},{10,11... | collective-permute-start | bytes 2457608 | tf_op jit(solution)/shard_map/ppermute | solution.py:618
  68.3 6.1 %collective-permute-start.8 = (bf16[400,1024]{1,0:T(8,128)(2,1)S(1)}, bf16[400,1024]{1,0:T(8,128)(2,1)}, u32[]{:S(2)}, u32[]{:S(2)}) collective-permute-start(bf16[400,1024]{1,0:T(8,128)(2,1)S(1)} %collective-permute-done.7.refs_2_), channel_id=1, source_target_pairs={{0,1},{1,0},{2,3},{3,2},{4,5},{5,4},{6,7},{7,6},{8,9},{9,8},{10,11... | collective-permute-start | bytes 2457608 | tf_op jit(solution)/shard_map/ppermute | solution.py:618
  68.9 7.6 %copy-start.27 = (bf16[256,3200]{1,0:T(8,128)(2,1)S(1)}, bf16[256,3200]{1,0:T(8,128)(2,1)}, u32[]{:S(2)}) copy-start(bf16[256,3200]{1,0:T(8,128)(2,1)} %copy-done.26) | copy-start | bytes 4915204
  68.9 10.5 %collective-permute-start.18 = (bf16[48,1024]{1,0:T(8,128)(2,1)S(1)}, bf16[48,1024]{1,0:T(8,128)(2,1)S(1)}, u32[]{:S(2)}, u32[]{:S(2)}) collective-permute-start(bf16[48,1024]{1,0:T(8,128)(2,1)S(1)} %get-tuple-element.123.refs_1_), channel_id=1, source_target_pairs={{0,24},{8,16},{16,8},{24,0},{1,25},{9,17},{17,9},{25,1},{2,26},{10... | collective-permute-start | bytes 294920 | tf_op jit(solution)/shard_map/ppermute | solution.py:618
  71.3 8.1 %collective-permute-start.17 = (bf16[48,1024]{1,0:T(8,128)(2,1)S(1)}, bf16[48,1024]{1,0:T(8,128)(2,1)S(1)}, u32[]{:S(2)}, u32[]{:S(2)}) collective-permute-start(bf16[48,1024]{1,0:T(8,128)(2,1)S(1)} %get-tuple-element.123.refs_1_), channel_id=1, source_target_pairs={{0,16},{8,24},{16,0},{24,8},{1,17},{9,25},{17,1},{25,9},{2,18},{10... | collective-permute-start | bytes 294920 | tf_op jit(solution)/shard_map/ppermute | solution.py:618
  71.3 8.1 %collective-permute-start.16 = (bf16[48,1024]{1,0:T(8,128)(2,1)S(1)}, bf16[48,1024]{1,0:T(8,128)(2,1)S(1)}, u32[]{:S(2)}, u32[]{:S(2)}) collective-permute-start(bf16[48,1024]{1,0:T(8,128)(2,1)S(1)} %get-tuple-element.123.refs_1_), channel_id=1, source_target_pairs={{0,8},{8,0},{16,24},{24,16},{1,9},{9,1},{17,25},{25,17},{2,10},{10... | collective-permute-start | bytes 294920 | tf_op jit(solution)/shard_map/ppermute | solution.py:618
  76.4 92.8 %copy-start.22 = (bf16[3200,1024]{1,0:T(8,128)(2,1)}, bf16[3200,1024]{1,0:T(8,128)(2,1)S(1)}, u32[]{:S(2)}) copy-start(bf16[3200,1024]{1,0:T(8,128)(2,1)S(1)} %gather_pieces.1.weight_ref.refs_0_) | copy-start | bytes 19660804
  79.4 3.6 %copy-start.29 = (bf16[2,1024,256]{2,1,0:T(8,128)(2,1)S(1)}, bf16[2,1024,256]{2,1,0:T(8,128)(2,1)}, u32[]{:S(2)}) copy-start(bf16[2,1024,256]{2,1,0:T(8,128)(2,1)} %copy-done.28) | copy-start | bytes 3145732
  80.0 13.5 %collective-permute-start.19 = (bf16[4,48,1024]{2,1,0:T(8,128)(2,1)S(1)}, bf16[4,48,1024]{2,1,0:T(8,128)(2,1)S(1)}, u32[]{:S(2)}, u32[]{:S(2)}) collective-permute-start(bf16[4,48,1024]{2,1,0:T(8,128)(2,1)S(1)} %get-tuple-element.124.refs_1_), channel_id=1, source_target_pairs={{0,2},{1,3},{2,0},{3,1},{4,6},{5,7},{6,4},{7,5},{8,10},{9,11},{10,... | collective-permute-start | bytes 1179656 | tf_op jit(solution)/shard_map/ppermute | solution.py:618
  81.5 42.2 %collective-permute-start.13 = (bf16[256,1024]{1,0:T(8,128)(2,1)}, bf16[256,1024]{1,0:T(8,128)(2,1)}, u32[]{:S(2)}, u32[]{:S(2)}) collective-permute-start(bf16[256,1024]{1,0:T(8,128)(2,1)} %get-tuple-element.120), channel_id=1, source_target_pairs={{0,16},{8,24},{16,0},{24,8},{1,17},{9,25},{17,1},{25,9},{2,18},{10... | collective-permute-start | bytes 1572872 | tf_op jit(solution)/shard_map/ppermute | solution.py:618
  92.5 36.9 %collective-permute-start.14 = (bf16[256,1024]{1,0:T(8,128)(2,1)}, bf16[256,1024]{1,0:T(8,128)(2,1)}, u32[]{:S(2)}, u32[]{:S(2)}) collective-permute-start(bf16[256,1024]{1,0:T(8,128)(2,1)} %get-tuple-element.121), channel_id=1, source_target_pairs={{0,24},{8,16},{16,8},{24,0},{1,25},{9,17},{17,9},{25,1},{2,26},{10... | collective-permute-start | bytes 1572872 | tf_op jit(solution)/shard_map/ppermute | solution.py:618
  94.2 18.3 %collective-permute-start.20 = (bf16[2,4,48,1024]{3,2,1,0:T(8,128)(2,1)S(1)}, bf16[2,4,48,1024]{3,2,1,0:T(8,128)(2,1)S(1)}, u32[]{:S(2)}, u32[]{:S(2)}) collective-permute-start(bf16[2,4,48,1024]{3,2,1,0:T(8,128)(2,1)S(1)} %get-tuple-element.125.refs_1_), channel_id=1, source_target_pairs={{0,4},{1,5},{2,6},{3,7},{4,0},{5,1},{6,2},{7,3},{8,12},{9,13},{10,... | collective-permute-start | bytes 2359304 | tf_op jit(solution)/shard_map/ppermute | solution.py:618
  104.6 24.8 %collective-permute-start.15 = (bf16[256,1024]{1,0:T(8,128)(2,1)S(1)}, bf16[256,1024]{1,0:T(8,128)(2,1)S(1)}, u32[]{:S(2)}, u32[]{:S(2)}) collective-permute-start(bf16[256,1024]{1,0:T(8,128)(2,1)S(1)} %get-tuple-element.122), channel_id=1, source_target_pairs={{0,8},{8,0},{16,24},{24,16},{1,9},{9,1},{17,25},{25,17},{2,10},{10... | collective-permute-start | bytes 1572872 | tf_op jit(solution)/shard_map/ppermute | solution.py:618
  113.2 9.6 %collective-permute-start.21 = (bf16[2,2,4,48,1024]{4,3,2,1,0:T(8,128)(2,1)S(1)}, bf16[2,2,4,48,1024]{4,3,2,1,0:T(8,128)(2,1)S(1)}, u32[]{:S(2)}, u32[]{:S(2)}) collective-permute-start(bf16[2,2,4,48,1024]{4,3,2,1,0:T(8,128)(2,1)S(1)} %get-tuple-element.126.refs_1_), channel_id=1, source_target_pairs={{0,1},{1,0},{2,3},{3,2},{4,5},{5,4},{6,7},{7,6},{8,9},{9,8},{10,11... | collective-permute-start | bytes 4718600 | tf_op jit(solution)/shard_map/ppermute | solution.py:618
  122.8 6.6 %copy-start.8 = (f32[2,128,4]{1,2,0:T(4,128)S(1)}, f32[2,128,4]{1,2,0:T(4,128)}, u32[]{:S(2)}) copy-start(f32[2,128,4]{1,2,0:T(4,128)} %param.24) | copy-start | bytes 12292
  122.8 6.6 %copy-start.9 = (f32[1024]{0:T(1024)S(1)}, f32[1024]{0:T(1024)}, u32[]{:S(2)}) copy-start(f32[1024]{0:T(1024)} %param.26) | copy-start | bytes 12292
  122.8 6.6 %copy-start.10 = (f32[1024]{0:T(1024)S(1)}, f32[1024]{0:T(1024)}, u32[]{:S(2)}) copy-start(f32[1024]{0:T(1024)} %param.28) | copy-start | bytes 12292
  122.8 6.6 %copy-start.11 = (s32[2,128]{1,0:T(2,128)S(1)}, s32[2,128]{1,0:T(2,128)}, u32[]{:S(2)}) copy-start(s32[2,128]{1,0:T(2,128)} %labels_ref.1) | copy-start | bytes 3076
  122.8 6.6 %copy-start.12 = (s32[2,128]{1,0:T(2,128)S(1)}, s32[2,128]{1,0:T(2,128)}, u32[]{:S(2)}) copy-start(s32[2,128]{1,0:T(2,128)} %ignore_ref.1) | copy-start | bytes 3076
  134.1 23.9 %collective-permute-start.24 = (bf16[256,1024]{1,0:T(8,128)(2,1)S(1)}, bf16[256,1024]{1,0:T(8,128)(2,1)S(1)}, u32[]{:S(2)}, u32[]{:S(2)}) collective-permute-start(bf16[256,1024]{1,0:T(8,128)(2,1)S(1)} %get-tuple-element.131.grad_ref.refs_3_), channel_id=1, source_target_pairs={{0,16},{8,24},{16,0},{24,8},{1,17},{9,25},{17,1},{25,9},{2,18},{10... | collective-permute-start | bytes 1572872 | tf_op jit(solution)/shard_map/ppermute | solution.py:618
  135.8 23.6 %collective-permute-start.22 = (bf16[256,1024]{1,0:T(8,128)(2,1)S(1)}, bf16[256,1024]{1,0:T(8,128)(2,1)S(1)}, u32[]{:S(2)}, u32[]{:S(2)}) collective-permute-start(bf16[256,1024]{1,0:T(8,128)(2,1)S(1)} %get-tuple-element.131.grad_ref.refs_3_), channel_id=1, source_target_pairs={{0,8},{8,0},{16,24},{24,16},{1,9},{9,1},{17,25},{25,17},{2,10},{10... | collective-permute-start | bytes 1572872 | tf_op jit(solution)/shard_map/ppermute | solution.py:618
  137.9 9.0 %collective-permute-start.23 = (bf16[528,1536]{1,0:T(8,128)(2,1)S(1)}, bf16[528,1536]{1,0:T(8,128)(2,1)S(1)}, u32[]{:S(2)}, u32[]{:S(2)}) collective-permute-start(bf16[528,1536]{1,0:T(8,128)(2,1)S(1)} %get-tuple-element.140), channel_id=1, source_target_pairs={{0,1},{1,0},{2,3},{3,2},{4,5},{5,4},{6,7},{7,6},{8,9},{9,8},{10,11... | collective-permute-start | bytes 4866056 | tf_op jit(solution)/shard_map/ppermute | solution.py:618
  148.7 46.9 %collective-permute-start.26 = (bf16[144,1536]{1,0:T(8,128)(2,1)}, bf16[144,1536]{1,0:T(8,128)(2,1)}, u32[]{:S(2)}, u32[]{:S(2)}) collective-permute-start(bf16[144,1536]{1,0:T(8,128)(2,1)} %get-tuple-element.148), channel_id=1, source_target_pairs={{0,2},{1,3},{2,0},{3,1},{4,6},{5,7},{6,4},{7,5},{8,10},{9,11},{10,... | collective-permute-start | bytes 1327112 | tf_op jit(solution)/shard_map/ppermute | solution.py:618
  149.2 46.3 %collective-permute-start.27 = (bf16[144,1536]{1,0:T(8,128)(2,1)}, bf16[144,1536]{1,0:T(8,128)(2,1)}, u32[]{:S(2)}, u32[]{:S(2)}) collective-permute-start(bf16[144,1536]{1,0:T(8,128)(2,1)} %get-tuple-element.149), channel_id=1, source_target_pairs={{0,4},{1,5},{2,6},{3,7},{4,0},{5,1},{6,2},{7,3},{8,12},{9,13},{10,... | collective-permute-start | bytes 1327112 | tf_op jit(solution)/shard_map/ppermute | solution.py:618
  150.8 44.8 %collective-permute-start.28 = (bf16[144,1536]{1,0:T(8,128)(2,1)}, bf16[144,1536]{1,0:T(8,128)(2,1)}, u32[]{:S(2)}, u32[]{:S(2)}) collective-permute-start(bf16[144,1536]{1,0:T(8,128)(2,1)} %get-tuple-element.150), channel_id=1, source_target_pairs={{0,6},{1,7},{2,4},{3,5},{4,2},{5,3},{6,0},{7,1},{8,14},{9,15},{10,... | collective-permute-start | bytes 1327112 | tf_op jit(solution)/shard_map/ppermute | solution.py:618
  157.9 11.3 %copy-start.3 = (f32[2,8,128]{2,1,0:T(8,128)S(1)}, f32[2,8,128]{2,1,0:T(8,128)}, u32[]{:S(2)}) copy-start(f32[2,8,128]{2,1,0:T(8,128)} %copy-done.2) | copy-start | bytes 24580
  157.9 25.1 %collective-permute-start.25 = (bf16[256,1024]{1,0:T(8,128)(2,1)S(1)}, bf16[256,1024]{1,0:T(8,128)(2,1)S(1)}, u32[]{:S(2)}, u32[]{:S(2)}) collective-permute-start(bf16[256,1024]{1,0:T(8,128)(2,1)S(1)} %tie.7), channel_id=1, source_target_pairs={{0,24},{8,16},{16,8},{24,0},{1,25},{9,17},{17,9},{25,1},{2,26},{10... | collective-permute-start | bytes 1572872 | tf_op jit(solution)/shard_map/ppermute | solution.py:618
  169.3 13.8 %copy-start.25 = (bf16[3200,256]{1,0:T(8,128)(2,1)S(1)}, bf16[3200,256]{1,0:T(8,128)(2,1)}, u32[]{:S(2)}) copy-start(bf16[3200,256]{1,0:T(8,128)(2,1)} %copy-done.24) | copy-start | bytes 4915204
  183.0 9.2 %copy-start.6 = (bf16[256,1024]{1,0:T(8,128)(2,1)}, bf16[256,1024]{1,0:T(8,128)(2,1)S(1)}, u32[]{:S(2)}) copy-start(bf16[256,1024]{1,0:T(8,128)(2,1)S(1)} %collective-permute-done.25.refs_1_.grad_ref) | copy-start | bytes 1572868
  184.0 3.9 %collective-permute-start.30 = (bf16[1,400,1024]{2,1,0:T(8,128)(2,1)S(1)}, bf16[1,400,1024]{2,1,0:T(8,128)(2,1)S(1)}, u32[]{:S(2)}, u32[]{:S(2)}) collective-permute-start(bf16[1,400,1024]{2,1,0:T(8,128)(2,1)S(1)} %get-tuple-element.158), channel_id=1, source_target_pairs={{0,1},{1,0},{2,3},{3,2},{4,5},{5,4},{6,7},{7,6},{8,9},{9,8},{10,11... | collective-permute-start | bytes 2457608 | tf_op jit(solution)/shard_map/ppermute | solution.py:618
  187.4 4.9 %collective-permute-start.29 = (bf16[3,400,1024]{2,1,0:T(8,128)(2,1)S(1)}, bf16[3,400,1024]{2,1,0:T(8,128)(2,1)S(1)}, u32[]{:S(2)}, u32[]{:S(2)}) collective-permute-start(bf16[3,400,1024]{2,1,0:T(8,128)(2,1)S(1)} %get-tuple-element.157), channel_id=1, source_target_pairs={{0,1},{1,0},{2,3},{3,2},{4,5},{5,4},{6,7},{7,6},{8,9},{9,8},{10,11... | collective-permute-start | bytes 7372808 | tf_op jit(solution)/shard_map/ppermute | solution.py:618
  189.9 39.4 %collective-permute-start.33 = (bf16[400,1024]{1,0:T(8,128)(2,1)}, bf16[400,1024]{1,0:T(8,128)(2,1)}, u32[]{:S(2)}, u32[]{:S(2)}) collective-permute-start(bf16[400,1024]{1,0:T(8,128)(2,1)} %get-tuple-element.171), channel_id=1, source_target_pairs={{0,6},{1,7},{2,4},{3,5},{4,2},{5,3},{6,0},{7,1},{8,14},{9,15},{10,... | collective-permute-start | bytes 2457608 | tf_op jit(solution)/shard_map/ppermute | solution.py:618
  195.6 9.3 %copy-start.1 = (f32[2,8,128]{2,1,0:T(8,128)S(1)}, f32[2,8,128]{2,1,0:T(8,128)}, u32[]{:S(2)}) copy-start(f32[2,8,128]{2,1,0:T(8,128)} %copy-done) | copy-start | bytes 24580
  195.6 9.3 %copy-start.7 = (bf16[256,1024]{1,0:T(8,128)(2,1)S(1)}, bf16[256,1024]{1,0:T(8,128)(2,1)}, u32[]{:S(2)}) copy-start(bf16[256,1024]{1,0:T(8,128)(2,1)} %copy-done.6) | copy-start | bytes 1572868
  198.2 19.4 %all-to-all-start = ((bf16[4,64,1024]{2,1,0:T(8,128)(2,1)}), bf16[4,64,1024]{2,1,0:T(8,128)(2,1)S(1)}, u32[]{:S(2)}, u32[]{:S(2)}) async-start(bf16[4,64,1024]{2,1,0:T(8,128)(2,1)} %get-tuple-element.164), calls=%async_computation | async-start | bytes 1048576 | tf_op jit(solution)/shard_map/all_to_all | solution.py:622
  202.7 26.6 %collective-permute-start.31 = (bf16[400,1024]{1,0:T(8,128)(2,1)S(1)}, bf16[400,1024]{1,0:T(8,128)(2,1)S(1)}, u32[]{:S(2)}, u32[]{:S(2)}) collective-permute-start(bf16[400,1024]{1,0:T(8,128)(2,1)S(1)} %get-tuple-element.169), channel_id=1, source_target_pairs={{0,2},{1,3},{2,0},{3,1},{4,6},{5,7},{6,4},{7,5},{8,10},{9,11},{10,... | collective-permute-start | bytes 2457608 | tf_op jit(solution)/shard_map/ppermute | solution.py:618
  203.4 25.9 %collective-permute-start.32 = (bf16[400,1024]{1,0:T(8,128)(2,1)S(1)}, bf16[400,1024]{1,0:T(8,128)(2,1)}, u32[]{:S(2)}, u32[]{:S(2)}) collective-permute-start(bf16[400,1024]{1,0:T(8,128)(2,1)S(1)} %get-tuple-element.170), channel_id=1, source_target_pairs={{0,4},{1,5},{2,6},{3,7},{4,0},{5,1},{6,2},{7,3},{8,12},{9,13},{10,... | collective-permute-start | bytes 2457608 | tf_op jit(solution)/shard_map/ppermute | solution.py:618
  222.1 38.4 %all-to-all-start.1 = ((bf16[4,2,64,1024]{3,2,1,0:T(8,128)(2,1)}), bf16[4,2,64,1024]{3,2,1,0:T(8,128)(2,1)S(1)}, u32[]{:S(2)}, u32[]{:S(2)}) async-start(bf16[4,2,64,1024]{3,2,1,0:T(8,128)(2,1)} %get-tuple-element.167), calls=%async_computation.1 | async-start | bytes 2097152 | tf_op jit(solution)/shard_map/all_to_all | solution.py:622
  231.4 29.2 %copy-start.20 = (bf16[4,64,256]{2,1,0:T(8,128)(2,1)S(1)}, bf16[4,64,256]{2,1,0:T(8,128)(2,1)}, u32[]{:S(2)}) copy-start(bf16[4,64,256]{2,1,0:T(8,128)(2,1)} %constant.93.refs_2_) | copy-start | bytes 393220
  234.4 31.7 %collective-permute-start.34 = (bf16[104,1024]{1,0:T(8,128)(2,1)S(1)}, bf16[104,1024]{1,0:T(8,128)(2,1)S(1)}, u32[]{:S(2)}, u32[]{:S(2)}) collective-permute-start(bf16[104,1024]{1,0:T(8,128)(2,1)S(1)} %get-tuple-element.176), channel_id=1, source_target_pairs={{0,8},{8,0},{16,24},{24,16},{1,9},{9,1},{17,25},{25,17},{2,10},{10... | collective-permute-start | bytes 638984 | tf_op jit(solution)/shard_map/ppermute | solution.py:618
  234.4 31.7 %collective-permute-start.35 = (bf16[104,1024]{1,0:T(8,128)(2,1)S(1)}, bf16[104,1024]{1,0:T(8,128)(2,1)S(1)}, u32[]{:S(2)}, u32[]{:S(2)}) collective-permute-start(bf16[104,1024]{1,0:T(8,128)(2,1)S(1)} %get-tuple-element.177), channel_id=1, source_target_pairs={{0,16},{8,24},{16,0},{24,8},{1,17},{9,25},{17,1},{25,9},{2,18},{10... | collective-permute-start | bytes 638984 | tf_op jit(solution)/shard_map/ppermute | solution.py:618
  237.3 32.2 %collective-permute-start.36 = (bf16[104,1024]{1,0:T(8,128)(2,1)S(1)}, bf16[104,1024]{1,0:T(8,128)(2,1)S(1)}, u32[]{:S(2)}, u32[]{:S(2)}) collective-permute-start(bf16[104,1024]{1,0:T(8,128)(2,1)S(1)} %get-tuple-element.178), channel_id=1, source_target_pairs={{0,24},{8,16},{16,8},{24,0},{1,25},{9,17},{17,9},{25,1},{2,26},{10... | collective-permute-start | bytes 638984 | tf_op jit(solution)/shard_map/ppermute | solution.py:618
  262.2 7.3 %copy-start.18 = (bf16[392,416]{1,0:T(8,128)(2,1)S(1)}, bf16[392,416]{1,0:T(8,128)(2,1)}, u32[]{:S(2)}) copy-start(bf16[392,416]{1,0:T(8,128)(2,1)} %constant.95.refs_1_) | copy-start | bytes 978436
  262.2 7.3 %copy-start.41 = (bf16[104,1024]{1,0:T(8,128)(2,1)S(1)}, bf16[104,1024]{1,0:T(8,128)(2,1)}, u32[]{:S(2)}) copy-start(bf16[104,1024]{1,0:T(8,128)(2,1)} %copy-done.40) | copy-start | bytes 638980
  (22 other events, 35.4 us)

commit v4 on v3

--- a/solution.py
+++ b/solution.py
@@ -40,7 +40,7 @@
     x0, y0, x1, y1, level = [box_ref[k : k + 1, :] for k in range(5)]
     centres = lax.broadcasted_iota(jnp.int32, (width, LANES), 0).astype(f32)
     for q in range(POOL):
-        across_ref[q] = bin_weights(x0, x1 - x0, centres, q).astype(f32)
+        across_ref[q] = bin_weights(x0, x1 - x0, centres, q)
     centres = lax.broadcasted_iota(jnp.int32, (height, LANES), 0).astype(f32)
     for p in range(POOL):
         weights = bin_weights(y0, y1 - y0, centres, p).astype(f32)
@@ -74,12 +74,12 @@
     return gaps
 
 
-def gather_kernel(number, seat_ref, *refs):
+def gather_kernel(number, where_ref, *refs):
     kept_ref, sems = refs[-2:]
     rows = refs[0].shape[0]
     copies = []
     for k, ref in enumerate(refs[:number]):
-        at = pl.multiple_of((seat_ref[0] ^ k) * rows, 16)
+        at = pl.multiple_of((where_ref[1] ^ k) * rows, 16)
         copies.append(pltpu.make_async_copy(ref, kept_ref.at[pl.ds(at, rows)], sems.at[k]))
     for copy in copies:
         copy.start()
@@ -87,7 +87,7 @@
         copy.wait()
 
 
-def gather_pieces(seat, pieces):
+def gather_pieces(where, pieces):
     rows, units = pieces[0].shape
     number = len(pieces)
     return pl.pallas_call(
@@ -99,7 +99,7 @@
         compiler_params=pltpu.CompilerParams(vmem_limit_bytes=24 * 2**20),
         cost_estimate=LARGE_COST,
         name="gather_pieces",
-    )(seat, *pieces)
+    )(where, *pieces)
 
 
 def crop_kernel(table, sizes, product, box_ref, maps_ref, *refs):
@@ -113,7 +113,7 @@
     for first, end in gaps_of(table, rows_ref.shape[0]):
         rows_ref[first:end, :] = jnp.zeros((end - first, LANES), f32)
     fill_weights(box_ref, down_ref, across_ref, height, width, level_count)
-    sums_ref[...] = jnp.dot(maps_ref[...], down_ref[...], preferred_element_type=f32)
+    sums_ref[...] = jnp.dot(maps_ref[...], down_ref[...], preferred_element_type=f32).astype(bf16)
     for p in range(POOL):
         lanes = slice(p * LANES, (p + 1) * LANES)
         for start in range(0, POOL, 2):
@@ -126,7 +126,7 @@
                     totals[at] = term if x == 0 else totals[at] + term
             for at, q in enumerate(bins):
                 for row, kept, count in table[p * POOL + q]:
-                    rows_ref[kept : kept + count, :] = totals[at][row : row + count]
+                    rows_ref[kept : kept + count, :] = totals[at][row : row + count].astype(f32)
     crop = rows_ref[...].astype(bf16)
     crop_ref[...] = crop
     if not product:
@@ -160,12 +160,13 @@
             pieces = []
             for q in range(POOL):
                 runs = [rows_ref[kept : kept + count, :] for row, kept, count in table[p * POOL + q]]
-                pieces.append(runs[0] if len(runs) == 1 else jnp.concatenate(runs, axis=0))
+                runs = runs[0] if len(runs) == 1 else jnp.concatenate(runs, axis=0)
+                pieces.append(runs.astype(bf16))
             for x in range(width):
                 total = across_ref[n, 0, x : x + 1, :] * pieces[0]
                 for q in range(1, POOL):
                     total = total + across_ref[n, q, x : x + 1, :] * pieces[q]
-                sums_ref[x * part : (x + 1) * part, lanes] = total.astype(bf16)
+                sums_ref[x * part : (x + 1) * part, lanes] = total
         total_ref[n] = lax.dot_general(
             sums_ref[...], down_ref[n], (((1,), (1,)), ((), ())), preferred_element_type=f32
         ).astype(bf16)
@@ -203,8 +204,8 @@
         out_shape=[kept_in((features, rows), bf16), out_shape, SIGN],
         scratch_shapes=[
             pltpu.VMEM((level_count * height, POOL * LANES), bf16),
-            pltpu.VMEM((POOL, width, LANES), f32),
-            pltpu.VMEM((width * part, POOL * LANES), f32),
+            pltpu.VMEM((POOL, width, LANES), bf16),
+            pltpu.VMEM((width * part, POOL * LANES), bf16),
             pltpu.VMEM((features, LANES), f32),
         ]
         + more,
@@ -242,7 +243,7 @@
         out_shape=[like((images, width * part, level_count * height), bf16), SIGN],
         scratch_shapes=[
             pltpu.VMEM((images, level_count * height, POOL * LANES), bf16),
-            pltpu.VMEM((images, POOL, width, LANES), f32),
+            pltpu.VMEM((images, POOL, width, LANES), bf16),
             pltpu.VMEM((width * part, POOL * LANES), bf16),
             pltpu.VMEM((features, LANES), f32),
             pltpu.VMEM((features, images * LANES), bf16),
@@ -253,25 +254,25 @@
     )(boxes, grads, weight, *earlier)
 
 
-def call(kernel, outs, scalars, arrays, earlier=(), scratch=(), name=None):
+def call(kernel, outs, where, arrays, earlier=(), scratch=(), name=None):
     arrays = list(arrays)
 
     def body(*refs):
-        at, end = len(scalars), len(scalars) + len(arrays)
+        end = 1 + len(arrays)
         later = refs[end + len(earlier) :]
         later[len(outs)][...] = jnp.zeros(SIGN.shape, SIGN.dtype)
-        kernel(refs[:at], refs[at:end], (*later[: len(outs)], *later[len(outs) + 1 :]))
+        kernel(refs[0], refs[1:end], (*later[: len(outs)], *later[len(outs) + 1 :]))
 
     return pl.pallas_call(
         body,
-        in_specs=[SCALAR for one in scalars] + [WHOLE for one in arrays] + [FAR for one in earlier],
+        in_specs=[SCALAR] + [WHOLE for one in arrays] + [FAR for one in earlier],
         out_specs=[WHOLE for one in (*outs, SIGN)],
         out_shape=[*outs, SIGN],
         scratch_shapes=scratch,
         compiler_params=pltpu.CompilerParams(vmem_limit_bytes=24 * 2**20),
         cost_estimate=LARGE_COST,
         name=name,
-    )(*[jnp.full((1,), one, jnp.int32) for one in scalars], *arrays, *earlier)
+    )(where, *arrays, *earlier)
 
 
 def tie_kernel(*refs):
@@ -291,36 +292,48 @@
     )(*arrays, *earlier)
 
 
-def order_kernel(scalars, arrays, outs):
+def add_kernel(where, arrays, outs):
+    outs[0][...] = sum(ref[...].astype(f32) for ref in arrays).astype(outs[0].dtype)
+
+
+def pair_kernel(bit, where, arrays, outs):
+    own = (where[bit[0]] >> bit[1]) & 1
+    outs[0][own] = arrays[0][...]
+    outs[0][1 - own] = arrays[1][...]
+
+
+def pair_up(bit, where, own, earlier):
+    come = swap(own, AXES[bit[0]], 1 << bit[1])
+    out = like((2,) + own.shape, own.dtype)
+    return call(functools.partial(pair_kernel, bit), [out], where, [own, come], earlier, name="pair_up")
+
+
+def order_kernel(where, arrays, outs):
     for k, ref in enumerate(arrays):
-        outs[0][scalars[0][0] ^ k] = ref[...]
-
-
-def in_order(at, arrays, earlier):
-    shape = (len(arrays),) + arrays[0].shape
-    return call(order_kernel, [like(shape, arrays[0].dtype)], [at], arrays, earlier, name="in_order")[0]
-
-
-def full_small_kernel(rows, scalars, arrays, outs):
+        outs[0][(where[1] >> 1) ^ k] = ref[...]
+
+
+def full_small_kernel(rows, where, arrays, outs):
     units = outs[0].shape[1]
     for k, ref in enumerate(arrays):
-        core = scalars[0][0] ^ k
+        core = (where[1] & 1) ^ k
         for chip in range(4):
-            for level in range(ref.shape[2]):
+            for level in range(ref.shape[1]):
                 at = pl.multiple_of(((level * 4 + chip) * 2 + core) * rows, rows)
-                outs[0][pl.ds(at, rows), :] = ref[chip // 2, chip % 2, level, :rows, :]
+                outs[0][pl.ds(at, rows), :] = ref[chip, level, :rows, :]
                 for part in range(2):
                     outs[1][pl.ds(at + part * (rows // 2), rows // 2), :] = ref[
-                        chip // 2, chip % 2, level, rows:, part * (units // 2) : (part + 1) * (units // 2)
+                        chip, level, rows:, part * (units // 2) : (part + 1) * (units // 2)
                     ]
 
 
-def split_rows(core, array, rows, sent, kept):
-    for at in range(array.shape[0] // rows // 2):
-        mine = pl.multiple_of((2 * at + core) * rows, rows)
-        other = pl.multiple_of((2 * at + 1 - core) * rows, rows)
-        kept[at * rows : (at + 1) * rows, :] = array[pl.ds(mine, rows), :].astype(bf16)
-        sent[at * rows : (at + 1) * rows, :] = array[pl.ds(other, rows), :].astype(bf16)
+def split_rows(own, inner, array, rows, sent, kept):
+    step = inner * rows
+    for at in range((kept.shape[0] - 16) // step):
+        mine = pl.multiple_of((2 * at + own) * step, rows)
+        other = pl.multiple_of((2 * at + 1 - own) * step, rows)
+        kept[at * step : (at + 1) * step, :] = array[pl.ds(mine, step), :].astype(bf16)
+        sent[at * step : (at + 1) * step, :] = array[pl.ds(other, step), :].astype(bf16)
 
 
 def put_biases(biases, refs):
@@ -338,7 +351,7 @@
     return last[:8] + last[8:]
 
 
-def small_product_kernel(rows, core_ref, first_ref, second_grad_ref, second_ref, slopes_ref, bias_ref, sent_ref, kept_ref, sign_ref, total_ref):
+def small_product_kernel(rows, where_ref, first_ref, second_grad_ref, second_ref, slopes_ref, bias_ref, sent_ref, kept_ref, sign_ref, total_ref):
     turned = (((0,), (0,)), ((), ()))
     units = first_ref.shape[1]
     total_ref[:, :units] = lax.dot_general(
@@ -347,12 +360,12 @@
     total_ref[:, units:] = lax.dot_general(
         second_ref[...], slopes_ref[...], turned, preferred_element_type=f32
     )
-    split_rows(core_ref[0], total_ref, rows, sent_ref, kept_ref)
+    split_rows(where_ref[1] & 1, 1, total_ref, rows, sent_ref, kept_ref)
     put_biases(bias_ref[...], [sent_ref, kept_ref])
     sign_ref[...] = jnp.zeros_like(sign_ref)
 
 
-def small_product(core, rows, first_act, second_grad, second_act, slopes, biases):
+def small_product(where, rows, first_act, second_grad, second_act, slopes, biases):
     units = first_act.shape[1]
     wide = units + slopes.shape[1]
     half = like((units // 2 + 16, wide), bf16)
@@ -365,64 +378,67 @@
         compiler_params=pltpu.CompilerParams(vmem_limit_bytes=24 * 2**20),
         cost_estimate=LARGE_COST,
         name="small_product",
-    )(jnp.full((1,), core, jnp.int32), first_act, second_grad, second_act, slopes, biases)
-
-
-def fold_kernel(rows, chip_ref, kept_ref, come_ref, *refs):
+    )(where, first_act, second_grad, second_act, slopes, biases)
+
+
+def quarter_kernel(rows, where_ref, kept_ref, come_ref, *refs):
     outs, sign_ref, total_ref = refs[-6:-2], refs[-2], refs[-1]
     sign_ref[...] = jnp.zeros_like(sign_ref)
     count, units = total_ref.shape[0], total_ref.shape[1] // 3 * 2
     total_ref[...] = kept_ref[:count, :].astype(f32) + come_ref[:count, :].astype(f32)
     for k, out in enumerate(outs):
         for at in range(count // rows // 4):
-            first = pl.multiple_of((4 * at + (chip_ref[0] ^ k)) * rows, rows)
+            first = pl.multiple_of((4 * at + ((where_ref[1] >> 1) ^ k)) * rows, rows)
             out[at * rows : (at + 1) * rows, :] = total_ref[pl.ds(first, rows), :].astype(bf16)
     put_biases(get_biases(kept_ref, units) + get_biases(come_ref, units), outs)
 
 
-def fold_rows(chip, rows, kept, come, earlier):
+def quarter_rows(rows, where, kept, come, earlier):
     count = kept.shape[0] - 16
     quarter = like((count // 4 + 16, kept.shape[1]), bf16)
     return pl.pallas_call(
-        functools.partial(fold_kernel, rows),
+        functools.partial(quarter_kernel, rows),
         in_specs=[SCALAR, WHOLE, WHOLE] + [FAR for one in earlier],
         out_specs=[WHOLE] * 5,
         out_shape=[quarter] * 4 + [SIGN],
         scratch_shapes=[pltpu.VMEM((count, kept.shape[1]), f32)],
         compiler_params=pltpu.CompilerParams(vmem_limit_bytes=24 * 2**20),
         cost_estimate=LARGE_COST,
-        name="fold_rows",
-    )(jnp.full((1,), chip, jnp.int32), kept, come, *earlier)
-
-
-def last_fold_kernel(rows, scalars, arrays, outs):
-    units = outs[0].shape[2]
+        name="quarter_rows",
+    )(where, kept, come, *earlier)
+
+
+def halve_kernel(bit, inner, rows, where, arrays, outs):
+    sent_out, kept_out, total_ref = outs
+    count, units = total_ref.shape[0], total_ref.shape[1] // 3 * 2
+    total_ref[...] = sum(ref[:count, :].astype(f32) for ref in arrays)
+    split_rows((where[bit[0]] >> bit[1]) & 1, inner, total_ref, rows, sent_out, kept_out)
     biases = [get_biases(ref, units) for ref in arrays]
-    biases = (biases[0] + biases[1]) + (biases[2] + biases[3])
-    for place in range(outs[0].shape[0]):
-        at = slice(place * rows, (place + 1) * rows)
-        total = sum(ref[at, :].astype(f32) for ref in arrays).astype(bf16)
-        out = outs[0].at[place]
-        out[:rows, :] = total[:, :units]
-        for part in range(2):
-            out[rows : rows // 2 * 3, part * (units // 2) : (part + 1) * (units // 2)] = total[
-                part * (rows // 2) : (part + 1) * (rows // 2), units:
-            ]
-        put_biases(biases, [out])
-
-
-def small_sum_kernel(scalars, arrays, outs):
-    came_ref = arrays[0]
-    count = came_ref.shape[0]
-    total = sum(came_ref[place].astype(f32) for place in range(count))
+    while len(biases) > 1:
+        biases = [biases[k] + biases[k + 1] for k in range(0, len(biases), 2)]
+    put_biases(biases[0], [sent_out, kept_out])
+
+
+def halve_rows(bit, inner, rows, where, arrays, earlier):
+    count, wide = arrays[0].shape[0] - 16, arrays[0].shape[1]
+    return call(
+        functools.partial(halve_kernel, bit, inner, rows),
+        [like((count // 2 + 16, wide), bf16)] * 2,
+        where,
+        arrays,
+        earlier,
+        [pltpu.VMEM((count, wide), f32)],
+        name="halve_rows",
+    )
+
+
+def small_sum_kernel(where, arrays, outs):
     rows, units = outs[0].shape
-    outs[0][...] = total[:rows]
-    outs[3][...] = sum(get_biases(came_ref.at[place], units) for place in range(count))
-    for part in range(2):
-        at = slice(part * (rows // 2), (part + 1) * (rows // 2))
-        beside = total[rows : rows // 2 * 3, part * (units // 2) : (part + 1) * (units // 2)]
-        outs[1][at, :] = beside[:, :CLS]
-        outs[2][at, :] = beside[:, LANES : LANES + BOX]
+    total = sum(ref[:rows, :].astype(f32) for ref in arrays)
+    outs[0][...] = total[:, :units]
+    outs[1][...] = total[:, units : units + CLS]
+    outs[2][...] = total[:, units + LANES : units + LANES + BOX]
+    outs[3][...] = sum(get_biases(ref, units) for ref in arrays)
 
 
 def gelu_and_slope(values):
@@ -432,11 +448,11 @@
 
 
 def head_kernel(
-    own_ref, one_ref, two_ref, three_ref, labels_ref, ignore_ref, targets_ref, hidden_bias_ref, inner_ref, inner_bias_ref, heads_ref, heads_bias_ref,
-    logits_ref, deltas_ref, first_act_ref, second_act_ref, slopes_ref, second_grad_ref, first_grad_ref, again_ref, bias_ref, first_slope_ref, second_slope_ref,
+    own_ref, one_ref, two_ref, labels_ref, ignore_ref, targets_ref, hidden_bias_ref, inner_ref, inner_bias_ref, heads_ref, heads_bias_ref,
+    logits_ref, deltas_ref, first_act_ref, second_act_ref, slopes_ref, second_grad_ref, first_grad_ref, bias_ref, first_slope_ref, second_slope_ref,
 ):
     first_pre = own_ref[...] + hidden_bias_ref[...]
-    for come_ref in (one_ref, two_ref, three_ref):
+    for come_ref in (one_ref, two_ref):
         first_pre = first_pre + come_ref[...].astype(f32)
     act, slope = gelu_and_slope(first_pre)
     first_slope_ref[...] = slope
@@ -487,7 +503,6 @@
     act_grad = lax.dot_general(second_grad, inner_ref[...], turned, preferred_element_type=f32)
     first_grad = (act_grad * first_slope_ref[...]).astype(bf16)
     first_grad_ref[...] = first_grad
-    again_ref[...] = first_grad
     units = first_grad.shape[1]
     bias_ref[...] = jnp.zeros_like(bias_ref)
     bias_ref[0:1, :] = jnp.sum(first_grad.astype(f32), axis=0, keepdims=True)
@@ -501,15 +516,14 @@
     images = labels.shape[0]
     return pl.pallas_call(
         head_kernel,
-        in_specs=[pl.BlockSpec(memory_space=pltpu.VMEM)] * 12,
-        out_specs=[pl.BlockSpec(memory_space=pltpu.VMEM)] * 9,
+        in_specs=[pl.BlockSpec(memory_space=pltpu.VMEM)] * 11,
+        out_specs=[pl.BlockSpec(memory_space=pltpu.VMEM)] * 8,
         out_shape=[
             like((CLS, images, LANES), f32),
             like((images, BOX, LANES), f32),
             like((count, units), bf16),
             like((count, units), bf16),
             like((count, wide), bf16),
-            like((count, units), bf16),
             like((count, units), bf16),
             like((count, units), bf16),
             like((8, units), f32),
@@ -521,13 +535,13 @@
     )(own, *come, labels, ignore, targets, hidden_bias, inner, inner_bias, heads, heads_bias)
 
 
-def maps_kernel(scalars, arrays, outs):
+def maps_kernel(where, arrays, outs):
     maps_ref, by_class_ref, across_first_ref = arrays
     pick_ref = outs[-1]
     size, part = by_class_ref.shape[:2]
     images = maps_ref.shape[0]
     for way in range(size):
-        pick_ref[way * part : (way + 1) * part, :] = by_class_ref[scalars[0][0] ^ way]
+        pick_ref[way * part : (way + 1) * part, :] = by_class_ref[where[0] ^ way]
     for n in range(images):
         flat = lax.dot_general(
             pick_ref[...], maps_ref[n], (((1,), (1,)), ((), ())), preferred_element_type=f32
@@ -537,22 +551,22 @@
             outs[way][n * part : (n + 1) * part, :] = flat[way * part : (way + 1) * part]
 
 
-def maps_back_kernel(scalars, arrays, outs):
-    came_ref, by_class_ref, across_first_ref = arrays
+def maps_back_kernel(where, arrays, outs):
+    came_refs, (by_class_ref, across_first_ref) = arrays[:-2], arrays[-2:]
     out_ref, pick_ref, flat_ref = outs
     size, part = by_class_ref.shape[:2]
     for way in range(size):
-        pick_ref[way * part : (way + 1) * part, :] = by_class_ref[scalars[0][0] ^ way]
+        pick_ref[way * part : (way + 1) * part, :] = by_class_ref[where[0] ^ way]
     for n in range(out_ref.shape[0]):
         for way in range(size):
-            flat_ref[way * part : (way + 1) * part, :] = came_ref[scalars[0][0] ^ way, n]
+            flat_ref[way * part : (way + 1) * part, :] = came_refs[way][n]
         cells = lax.dot_general(
             across_first_ref[...], flat_ref[...], (((1,), (1,)), ((), ())), preferred_element_type=f32
         ).astype(bf16)
         out_ref[n] = jnp.dot(cells, pick_ref[...], preferred_element_type=f32)
 
 
-def arrange_kernel(sizes, scalars, arrays, outs):
+def arrange_kernel(sizes, where, arrays, outs):
     height, width, part, level_count = sizes
     for n in range(outs[0].shape[0]):
         for x in range(width):
@@ -562,47 +576,53 @@
                 ]
 
 
-def arrange_back_kernel(sizes, scalars, arrays, outs):
+def arrange_back_kernel(sizes, where, arrays, outs):
     height, width, part, level_count = sizes
     for n in range(arrays[0].shape[0]):
         for x in range(width):
-            for k in range(level_count):
-                outs[0][scalars[0][0] ^ k, n, :, x * height : (x + 1) * height] = sum(
+            for k, out in enumerate(outs):
+                out[n, :, x * height : (x + 1) * height] = sum(
                     ref[n, x * part : (x + 1) * part, k * height : (k + 1) * height].astype(f32)
                     for ref in arrays
                 ).astype(bf16)
 
 
-def split_span_kernel(scalars, arrays, outs):
+def split_span_kernel(length, where, arrays, outs):
+    weight_ref, extra_ref = arrays
     total_ref = outs[-1]
-    span = outs[0].shape[0]
-    total_ref[...] = sum(
-        jnp.dot(arrays[k][...], arrays[k + 1][...], preferred_element_type=f32)
-        for k in range(0, len(arrays), 2)
-    )
+    span, size = outs[0].shape[0], len(outs) - 1
+    shape = (total_ref.shape[0], weight_ref.shape[0])
+    row = lax.broadcasted_iota(jnp.int32, shape, 0)
+    column = lax.broadcasted_iota(jnp.int32, shape, 1)
+    kind = sum((row >= k * span).astype(jnp.int32) for k in range(1, size))
+    matrix = jnp.where(column == (row - kind * span) * size + kind, 1.0, 0.0).astype(bf16)
+    total_ref[...] = jnp.dot(matrix, weight_ref[...], preferred_element_type=f32)
+    for k in range(size):
+        at = k * span + length
+        total_ref[at : at + extra_ref.shape[0], :] = extra_ref[...]
     for way, out in enumerate(outs[:-1]):
-        at = pl.multiple_of((scalars[0][0] ^ way) * span, 8)
+        at = pl.multiple_of((where[0] ^ way) * span, 8)
         out[...] = total_ref[pl.ds(at, span), :].astype(bf16)
 
 
-def join_span_kernel(scalars, arrays, outs):
+def join_span_kernel(where, arrays, outs):
     total_ref = outs[-1]
     span = arrays[1].shape[0]
     for way, ref in enumerate(arrays[1:]):
-        at = pl.multiple_of((scalars[0][0] ^ way) * span, 8)
+        at = pl.multiple_of((where[0] ^ way) * span, 8)
         total_ref[pl.ds(at, span), :] = ref[...].astype(f32)
     product = jnp.dot(arrays[0][...], total_ref[...].astype(bf16), preferred_element_type=f32)
     for out in outs[:-1]:
         out[...] = product.astype(out.dtype)
 
 
-def return_span_kernel(scalars, arrays, outs):
+def return_span_kernel(where, arrays, outs):
     total_ref = outs[-1]
     span = outs[0].shape[0]
     piece = sum(ref[...].astype(f32) for ref in arrays[1:]).astype(bf16)
     total_ref[...] = jnp.dot(arrays[0][...], piece, preferred_element_type=f32)
     for way, out in enumerate(outs[:-1]):
-        at = pl.multiple_of((scalars[0][0] ^ way) * span, 8)
+        at = pl.multiple_of((where[0] ^ way) * span, 8)
         out[...] = total_ref[pl.ds(at, span), :].astype(bf16)
 
 
@@ -626,7 +646,8 @@
     return [arrays[0]] + [swap(one, axis, way) for way, one in enumerate(arrays) if way]
 
 
-def product_kernel(number, parts, with_sum, at_ref, *refs):
+def product_kernel(bits, parts, with_sum, where_ref, *refs):
+    number = len(bits)
     grad_refs, crop_refs, refs = refs[:parts], refs[parts : 2 * parts], refs[2 * parts :]
     sign_ref, refs = refs[-1], refs[:-1]
     sign_ref[...] = jnp.zeros_like(sign_ref)
@@ -634,7 +655,7 @@
     rows = crop_refs[0].shape[0] // 8
     for n in range(number):
         total = refs[0][n].astype(f32) if with_sum else 0.0
-        at = pl.multiple_of(at_ref[n] * rows, 16)
+        at = pl.multiple_of((where_ref[1] ^ bits[n]) * rows, 16)
         for grad_ref, crop_ref in zip(grad_refs, crop_refs):
             total = total + jnp.dot(
                 crop_ref[pl.ds(at, rows), :], grad_ref[...], preferred_element_type=f32
@@ -642,18 +663,18 @@
         outs[n][...] = total.astype(bf16)
 
 
-def piece_product(crops, grads, pieces, come, earlier):
+def piece_product(crops, grads, where, bits, come, earlier):
     features = crops[0].shape[0]
     units = grads[0].shape[1]
     rows = features // 8
-    number = len(pieces)
+    number = len(bits)
     with_sum = come is not None
     come = [come] if with_sum else []
     outs = (
         [like((rows, units), bf16)] * number if with_sum else [like((number, rows, units), bf16)]
     )
     return pl.pallas_call(
-        functools.partial(product_kernel, number, len(grads), with_sum),
+        functools.partial(product_kernel, bits, len(grads), with_sum),
         in_specs=[SCALAR]
         + [WHOLE for one in (*grads, *crops, *come)]
         + [FAR for one in earlier],
@@ -662,7 +683,7 @@
         compiler_params=pltpu.CompilerParams(vmem_limit_bytes=24 * 2**20),
         cost_estimate=LARGE_COST,
         name="piece_product",
-    )(jnp.stack(pieces), *grads, *crops, *come, *earlier)
+    )(where, *grads, *crops, *come, *earlier)
 
 
 def butterfly(array):
@@ -706,8 +727,7 @@
     size = lax.axis_size("level")
     planes = lax.axis_size("img")
     z = lax.axis_index("level")
-    place = lax.axis_index("img")
-    core, x, y = place % 2, place // 2 % 2, place // 4
+    where = jnp.stack([z, lax.axis_index("img")]).astype(jnp.int32)
     images, height, width, channels = pyramid.shape[1:]
     regions = levels.shape[1]
     part = channels // size
@@ -743,18 +763,10 @@
     if direct:
         length = rows // size
         span = -(-(length + images) // 8) * 8
-        extra = jnp.concatenate(
-            [packed.astype(bf16).reshape(images, units), jnp.zeros((16 - images, units), bf16)]
-        )
         to_span = picking(
             size * span,
             rows,
             [(k * span + j, j * size + k) for k in range(size) for j in range(length)],
-        )
-        extra_span = picking(
-            size * span,
-            16,
-            [(k * span + length + n, n) for k in range(size) for n in range(images)],
         )
         room = -(-rows // 16) * 16
         features = planes * room
@@ -765,10 +777,10 @@
         )
         total = [pltpu.VMEM((size * span, units), f32)]
         *sent, sign = call(
-            split_span_kernel,
+            functools.partial(split_span_kernel, length),
             [like((span, units), bf16)] * size,
-            [z],
-            [to_span, hidden_weight, extra_span, extra],
+            where,
+            [hidden_weight, packed.astype(f32).reshape(images, units)],
             scratch=total,
             name="split_span",
         )
@@ -776,7 +788,7 @@
         piece, own_piece, sign = call(
             join_span_kernel,
             [like((room, units), bf16)] * 2,
-            [z],
+            where,
             [from_span, *came],
             scratch=total,
             name="join_span",
@@ -810,7 +822,7 @@
     maps = call(
         maps_kernel,
         [like((images * part, spots), bf16)] * size,
-        [z],
+        where,
         [pyramid[0].reshape(images, spots, channels), by_class, across_first],
         scratch=picks[:1],
         name="maps",
@@ -819,47 +831,57 @@
         maps = [maps[0], *tie(maps[1:], sign)]
     maps_came = exchange_ways(maps[:3], "level")
     maps_came.append(swap(tie([maps[3]], maps_came[1])[0], "level", 3))
+    if direct:
+        smalls = tie([pack_rows(small)], maps_came[3])[0]
     maps, sign = call(
         functools.partial(arrange_kernel, sizes),
         [pltpu.VMEM((images, width * part, size * height), bf16)],
-        [],
+        where,
         maps_came,
         name="arrange",
     )
 
-    ways = (2, 3, 1, 0)
-    crops, owns, signs, came_sums = [], [], [], []
-    crops_in = pltpu.VMEM if direct else like
+    ways = (3, 2, 1, 0)
+    crops, signs, came_sums = [], [], []
     for turn, way in enumerate(ways):
         if turn == 0:
-            crop, turned, sign = crop_block(
-                table, sizes, features, boxes[way], maps, kept_in=crops_in
-            )
+            crop, turned, sign = crop_block(table, sizes, features, boxes[way], maps)
             if direct:
-                own_piece, smalls = tie([own_piece, pack_rows(small)], sign)
-                smalls = exchange_ways([smalls] * size, "level")
+                smalls, unused = pair_up((0, 0), where, smalls, [sign])
+                own_piece = tie([own_piece], sign)[0]
                 pieces = [own_piece, *pieces[1:]]
                 pieces = sum(([one, swap(one, "img", 1)] for one in pieces), [])
-                weight = gather_pieces(jnp.full((1,), place, jnp.int32), pieces)
+                weight = gather_pieces(where, pieces)
             own, sign = multiply(turned, weight)
+            relayed = swap(own, "level", 1)
         else:
             crop, own, sign = crop_block(
-                table, sizes, features, boxes[way], maps, weight, bf16 if way else f32, signs[-1:], crops_in
+                table, sizes, features, boxes[way], maps, weight, bf16 if way == 1 else f32, signs[-1:]
             )
-        owns.append(own)
+        if way == 2 and direct:
+            smalls, sign = pair_up((0, 1), where, smalls, [sign])
+            smalls = smalls.reshape(size, small_rows, units)
+            smalls = [swap(smalls, "img", bit) if bit else smalls for bit in (0, 2, 4, 6)]
+        if way == 2:
+            own, sign = call(add_kernel, [like(own.shape, bf16)], where, [own, relayed], [sign], name="add")
+        if way in (1, 2):
+            came_sums.append(swap(own, "level", way))
+        crops.append(crop)
         signs.append(sign)
-        crops.append(crop)
-        if way:
-            came_sums.append(swap(owns[-1], "level", way))
 
     if direct:
-        smalls = in_order(z, smalls, signs[:1])
-        smalls = in_order(x, [smalls, swap(smalls, "img", 2)], signs[1:2])
-        smalls = in_order(y, [smalls, swap(smalls, "img", 4)], signs[2:3])
+        smalls, unused = call(
+            order_kernel,
+            [like((4, size, small_rows, units), bf16)],
+            where,
+            smalls,
+            signs[2:3],
+            name="in_order",
+        )
         full_inner, full_heads, sign = call(
             functools.partial(full_small_kernel, small.shape[0]),
             [pltpu.VMEM((units, units), bf16), pltpu.VMEM((units, units // 2), bf16)],
-            [core],
+            where,
             [smalls, swap(smalls, "img", 1)],
             name="full_small",
         )
@@ -867,8 +889,8 @@
         smalls = lax.all_gather(small, AXES, axis=0, tiled=True)
         full_inner, full_heads = smalls[:, :units], smalls[:, units:]
 
-    logits, deltas, first_act, second_act, slopes, second_grad, first_grad, first_again, bias_sums = head_block(
-        owns[-1],
+    logits, deltas, first_act, second_act, slopes, second_grad, first_grad, bias_sums = head_block(
+        own,
         came_sums,
         labels,
         crowd_ignore,
@@ -882,7 +904,7 @@
 
     near = swap(first_grad, "level", 1)
     far = swap(first_grad, "level", 2)
-    grad_of = {0: first_grad, 1: near, 2: far}
+    grad_of = {0: first_grad, 1: near}
 
     shares = []
 
@@ -894,14 +916,15 @@
     if direct:
         count = small.shape[0]
         sent, kept, sign = small_product(
-            core, count, first_act, second_grad, second_act, slopes, bias_sums
+            where, count, first_act, second_grad, second_act, slopes, bias_sums
         )
         sign = take_up(0, [sign])
-        *quarters, sign = fold_rows(place // 2, count, kept, swap(sent, "img", 1), [sign])
+        *quarters, sign = quarter_rows(count, where, kept, swap(sent, "img", 1), [sign])
         quarters = [
             swap(one, "img", bit) if bit else one for one, bit in zip(quarters, (0, 2, 4, 6))
         ]
-        grad_of[3] = swap(tie([first_again], far, sign)[0], "level", 3)
+        grad_of[2] = tie([far], sign)[0]
+        grad_of[3] = swap(grad_of[2], "level", 1)
         sign = take_up(1, [sign])
         sign = take_up(2, [sign])
 
@@ -909,31 +932,28 @@
         parts, others = {}, {}
 
         def for_other(bits, sign):
-            at = [place ^ bit ^ 1 for bit in bits]
-            products, sign = piece_product(crops, grads, at, None, [sign])
+            theirs = tuple(bit ^ 1 for bit in bits)
+            products, sign = piece_product(crops, grads, where, theirs, None, [sign])
             others[bits] = swap(products, "img", 1)
             return sign
 
         def for_own(bits, sign):
-            at = [place ^ bit for bit in bits]
-            *own, sign = piece_product(crops, grads, at, others[bits], [sign])
+            *own, sign = piece_product(crops, grads, where, bits, others[bits], [sign])
             for one, bit in zip(own, bits):
                 parts[bit] = swap(one, "img", bit) if bit else one
             return sign
 
         sign = for_other((6,), sign)
-        sign = for_other((2, 4, 0), sign)
+        sign = for_other((2, 4), sign)
         sign = for_own((6,), sign)
-        sign = for_own((2, 4, 0), sign)
-        smalls, sign = call(
-            functools.partial(last_fold_kernel, count),
-            [like((size, small_rows + 16, units), bf16)],
-            [z],
-            quarters,
-            [sign],
-            name="last_fold",
-        )
+        sent, kept, sign = halve_rows((0, 1), 2, count, where, quarters, [sign])
+        sign = for_own((2, 4), sign)
+        sign = for_other((0,), sign)
         sign = take_up(3, [sign])
+        sent, kept, sign = halve_rows(
+            (0, 0), 1, count, where, [kept, swap(sent, "level", 2)], [sign]
+        )
+        sign = for_own((0,), sign)
         inner_sum, class_sum, delta_sum, bias_total, sign = call(
             small_sum_kernel,
             [
@@ -942,36 +962,39 @@
                 like((count, BOX), f32),
                 like((8, units), f32),
             ],
-            [],
-            [exchange(smalls, "level")],
+            where,
+            [kept, swap(sent, "level", 1)],
             [sign],
             name="small_sum",
         )
-        back, sign = call(
+        half, sign = call(
+            add_kernel, [like(parts[0].shape, f32)], where, [parts[0], parts[6]], [sign], name="add"
+        )
+        *back, sign = call(
             functools.partial(arrange_back_kernel, sizes),
-            [like((size, images, part, spots), bf16)],
-            [z],
+            [like((images, part, spots), bf16)] * size,
+            where,
             shares,
             [sign],
             name="arrange_back",
         )
-        *sent, sign = call(
+        *out, sign = call(
             return_span_kernel,
             [like((span, units), bf16)] * size,
-            [z],
-            [from_span.T, *[parts[bit] for bit in (0, 2, 4, 6)]],
+            where,
+            [from_span.T, half, parts[2], parts[4]],
             [sign],
             scratch=total,
             name="return_span",
         )
     else:
-        grad_of[3] = swap(first_again, "level", 3)
+        grad_of[2], grad_of[3] = far, swap(far, "level", 1)
         for way in range(size):
             take_up(way)
-        back, sign = call(
+        *back, sign = call(
             functools.partial(arrange_back_kernel, sizes),
-            [like((size, images, part, spots), bf16)],
-            [z],
+            [like((images, part, spots), bf16)] * size,
+            where,
             shares,
             name="arrange_back",
         )
@@ -998,20 +1021,19 @@
     map_grads, sign = call(
         maps_back_kernel,
         [like((images, spots, channels), f32)],
-        [z],
-        [exchange(back, "level"), by_class, across_first],
+        where,
+        [*exchange_ways(back, "level"), by_class, across_first],
         [sign],
         scratch=picks,
         name="maps_back",
     )
     map_grads = map_grads.reshape(1, images, height, width, channels)
-
     if direct:
         hidden_sum = call(
             join_span_kernel,
             [like((rows, units), f32)],
-            [z],
-            [to_span.T, *exchange_ways(sent, "level")],
+            where,
+            [to_span.T, *exchange_ways(out, "level")],
             [sign],
             scratch=total,
             name="join_span",

time: 276 us -> 253 us (0.917)
  local copies, waits for them, and re-layouts: 18.4 us -> 3.09 us
  Pallas kernels: 115 us -> 107 us
  waiting for transfers between devices: 84.7 us -> 92.5 us
  starting transfers between devices: 50 us -> 44.3 us
    ppermute x37 -> x43, waiting for transfers between devices: 62 us -> 92.5 us  [swap(): return lax.ppermute(array, axis, [(at, at ^ bit) for at in range(size)])]
    all_to_all x2 -> x0, waiting for transfers between devices: 22.7 us -> none  [exchange(): return lax.all_to_all(array, axis, split_axis=0, concat_axis=0, tiled=True)]
    unnamed x103 -> x51, local copies, waits for them, and re-layouts: 16.6 us -> 1.29 us
    pallas_call x4, Pallas kernels: 34.8 us -> 24.6 us  [crop_block(): pl.pallas_call(functools.partial(crop_kernel, table, sizes, product), gri...]
    all_to_all x2 -> x0, starting transfers between devices: 9.85 us -> none  [exchange(): return lax.all_to_all(array, axis, split_axis=0, concat_axis=0, tiled=True)]
    pallas_call x19 -> x24, Pallas kernels: 33.8 us -> 43.2 us  [the longest x17 28 us: call(): pl.pallas_call(body, in_specs=[SCALAR] + [WHOLE for one in arrays] + [FAR...]
    pallas_call x4, Pallas kernels: 35.7 us -> 28.6 us  [spread_block(): pl.pallas_call(functools.partial(spread_kernel, table, sizes), in_specs=[...]
    ppermute x37 -> x43, starting transfers between devices: 40.1 us -> 44.3 us  [swap(): return lax.ppermute(array, axis, [(at, at ^ bit) for at in range(size)])]
  transfers between devices with their start and end apart: 39 -> 43, of which waited for: 14 -> 21; matrix products, arithmetic and copies ran while one was open for 1% -> 1% of each run, Pallas kernels for 39% -> 39%
where the time goes in v4:
time: 253 us; the launch traced here: 249 us
  Pallas kernels  107 us (42%)
  waiting for transfers between devices  92.5 us (37%)
  starting transfers between devices  44.3 us (18%)
  local copies, waits for them, and re-layouts  3.09 us (1%)
    ppermute x43, waiting for transfers between devices, swap(): return lax.ppermute(array, axis, [(at, at ^ bit) for at in range(size)])  92.5 us
    ppermute x43, starting transfers between devices, swap(): return lax.ppermute(array, axis, [(at, at ^ bit) for at in range(size)])  44.3 us
    pallas_call x4, Pallas kernels, spread_block(): pl.pallas_call(functools.partial(spread_kernel, table, sizes), in_specs=[...  28.6 us
    pallas_call x17, Pallas kernels, call(): pl.pallas_call(body, in_specs=[SCALAR] + [WHOLE for one in arrays] + [FAR...  28 us
    pallas_call x4, Pallas kernels, crop_block(): pl.pallas_call(functools.partial(crop_kernel, table, sizes, product), gri...  24.6 us
    pallas_call x6, Pallas kernels, piece_product(): pl.pallas_call(functools.partial(product_kernel, bits, len(grads), with_s...  13.1 us
  transfers between devices with their start and end apart: 43, of which 21 were waited for; matrix products, arithmetic and copies ran while one was open for 1% of the time, Pallas kernels for 39%

profile of v4, /device:TPU:8, one launch (start us, length us, event | category | flops | bytes accessed | tf_op | source)
XLA Modules:
  0.0 248.9 jit_solution(12039368392631048304)
XLA Ops:
  2.8 1.2 split_span.1
  4.1 3.0 %collective-permute-start.1 = (bf16[104,1024]{1,0:T(8,128)(2,1)S(1)}, bf16[104,1024]{1,0:T(8,128)(2,1)S(1)}, u32[]{:S(2)}, u32[]{:S(2)}) collective-permute-start(bf16[104,1024]{1,0:T(8,128)(2,1)S(1)} %get-tuple-element.112), channel_id=1, source_target_pairs={{0,16},{8,24},{16,0},{24,8},{1,17},{9,25},{17,1},{25,9},{2,18},{10... | collective-permute-start | bytes 638984 | tf_op jit(solution)/shard_map/ppermute | solution.py:638
  7.7 2.5 maps.1
  10.2 2.5 %collective-permute-done.refs_3_ = bf16[104,1024]{1,0:T(8,128)(2,1)S(1)} collective-permute-done((bf16[104,1024]{1,0:T(8,128)(2,1)S(1)}, bf16[104,1024]{1,0:T(8,128)(2,1)S(1)}, u32[]{:S(2)}, u32[]{:S(2)}) %collective-permute-start) | collective-permute-done | bytes 213024 | tf_op jit(solution)/shard_map/ppermute | solution.py:638
  12.7 9.2 %collective-permute-done.1.refs_4_ = bf16[104,1024]{1,0:T(8,128)(2,1)S(1)} collective-permute-done((bf16[104,1024]{1,0:T(8,128)(2,1)S(1)}, bf16[104,1024]{1,0:T(8,128)(2,1)S(1)}, u32[]{:S(2)}, u32[]{:S(2)}) %collective-permute-start.1) | collective-permute-done | bytes 213024 | tf_op jit(solution)/shard_map/ppermute | solution.py:638
  22.0 4.1 %collective-permute-done.2.refs_5_ = bf16[104,1024]{1,0:T(8,128)(2,1)S(1)} collective-permute-done((bf16[104,1024]{1,0:T(8,128)(2,1)S(1)}, bf16[104,1024]{1,0:T(8,128)(2,1)S(1)}, u32[]{:S(2)}, u32[]{:S(2)}) %collective-permute-start.2) | collective-permute-done | bytes 213024 | tf_op jit(solution)/shard_map/ppermute | solution.py:638
  26.0 1.3 join_span.2
  27.3 2.5 %collective-permute-start.11 = (bf16[400,1024]{1,0:T(8,128)(2,1)S(1)}, bf16[400,1024]{1,0:T(8,128)(2,1)S(1)}, u32[]{:S(2)}, u32[]{:S(2)}) collective-permute-start(bf16[400,1024]{1,0:T(8,128)(2,1)S(1)} %get-tuple-element.125), channel_id=1, source_target_pairs={{0,6},{1,7},{2,4},{3,5},{4,2},{5,3},{6,0},{7,1},{8,14},{9,15},{10,... | collective-permute-start | bytes 2457608 | tf_op jit(solution)/shard_map/ppermute | solution.py:638
  30.9 3.1 %collective-permute-start.4 = (bf16[128,1024]{1,0:T(8,128)(2,1)S(1)}, bf16[128,1024]{1,0:T(8,128)(2,1)S(1)}, u32[]{:S(2)}, u32[]{:S(2)}) collective-permute-start(bf16[128,1024]{1,0:T(8,128)(2,1)S(1)} %get-tuple-element.120), channel_id=1, source_target_pairs={{0,16},{8,24},{16,0},{24,8},{1,17},{9,25},{17,1},{25,9},{2,18},{10... | collective-permute-start | bytes 786440 | tf_op jit(solution)/shard_map/ppermute | solution.py:638
  34.0 6.1 %collective-permute-done.3.refs_1_.refs_2_ = bf16[128,1024]{1,0:T(8,128)(2,1)S(1)} collective-permute-done((bf16[128,1024]{1,0:T(8,128)(2,1)S(1)}, bf16[128,1024]{1,0:T(8,128)(2,1)S(1)}, u32[]{:S(2)}, u32[]{:S(2)}) %collective-permute-start.3) | collective-permute-done | bytes 262176 | tf_op jit(solution)/shard_map/ppermute | solution.py:638
  40.1 1.6 collective-permute-start.5
  41.7 13.4 %collective-permute-done.5.refs_4_.refs_1_ = bf16[128,1024]{1,0:T(8,128)(2,1)S(1)} collective-permute-done((bf16[128,1024]{1,0:T(8,128)(2,1)S(1)}, bf16[128,1024]{1,0:T(8,128)(2,1)S(1)}, u32[]{:S(2)}, u32[]{:S(2)}) %collective-permute-start.5) | collective-permute-done | bytes 262176 | tf_op jit(solution)/shard_map/ppermute | solution.py:638
  55.1 1.7 arrange.1
  56.8 4.5 %crop_block.4 = (bf16[3200,256]{1,0:T(8,128)(2,1)S(1)}, bf16[256,3200]{1,0:T(8,128)(2,1)S(1)}, f32[8,128]{1,0:T(8,128)S(1)}) custom-call(f32[2,8,128]{2,1,0:T(8,128)S(1)} %get-tuple-element.215.box_ref, bf16[2,1024,256]{2,1,0:T(8,128)(2,1)S(1)} %get-tuple-element.122.maps_ref), custom_call_target="tpu_custom_call" | custom-call | flops 40000000000 | bytes 1 | tf_op jit(solution)/shard_map/crop_block/pallas_call | solution.py:190
  61.9 2.7 %collective-permute-done.9.refs_4_ = bf16[400,1024]{1,0:T(8,128)(2,1)S(1)} collective-permute-done((bf16[400,1024]{1,0:T(8,128)(2,1)S(1)}, bf16[400,1024]{1,0:T(8,128)(2,1)S(1)}, u32[]{:S(2)}, u32[]{:S(2)}) %collective-permute-start.9) | collective-permute-done | bytes 819232 | tf_op jit(solution)/shard_map/ppermute | solution.py:638
  67.0 1.2 collective-permute-done.8.refs_3_
  68.1 1.4 gather_pieces.1.weight_ref.refs_0_
  69.6 2.0 multiply.1
  71.5 1.3 collective-permute-start.13
  72.8 6.3 %crop_block.5 = (bf16[3200,256]{1,0:T(8,128)(2,1)S(1)}, f32[256,1024]{1,0:T(8,128)S(1)}, f32[8,128]{1,0:T(8,128)S(1)}) custom-call(f32[2,8,128]{2,1,0:T(8,128)S(1)} %get-tuple-element.213.box_ref, bf16[2,1024,256]{2,1,0:T(8,128)(2,1)S(1)} %get-tuple-element.122.maps_ref, bf16[3200,1024]{1,0:T(8,128)(2,1)S(1)} %gather_pieces.1.weight_ref.refs_0_, ...), custom_call_target="tpu_custom_call" | custom-call | flops 40000000000 | bytes 1 | tf_op jit(solution)/shard_map/crop_block/pallas_call | solution.py:190
  79.8 2.4 collective-permute-start.20
  83.3 4.0 %collective-permute-done.13.refs_2_ = bf16[256,1024]{1,0:T(8,128)(2,1)S(1)} collective-permute-done((bf16[256,1024]{1,0:T(8,128)(2,1)S(1)}, bf16[256,1024]{1,0:T(8,128)(2,1)S(1)}, u32[]{:S(2)}, u32[]{:S(2)}) %collective-permute-start.13) | collective-permute-done | bytes 524320 | tf_op jit(solution)/shard_map/ppermute | solution.py:638
  87.3 1.4 add.19
  88.7 2.4 collective-permute-start.16
  91.1 6.4 %crop_block.6 = (bf16[3200,256]{1,0:T(8,128)(2,1)S(1)}, bf16[256,1024]{1,0:T(8,128)(2,1)S(1)}, f32[8,128]{1,0:T(8,128)S(1)}) custom-call(f32[2,8,128]{2,1,0:T(8,128)S(1)} %get-tuple-element.214.box_ref, bf16[2,1024,256]{2,1,0:T(8,128)(2,1)S(1)} %get-tuple-element.122.maps_ref, bf16[3200,1024]{1,0:T(8,128)(2,1)S(1)} %gather_pieces.1.weight_ref.refs_0_, ...), custom_call_target="tpu_custom_call" | custom-call | flops 40000000000 | bytes 1 | tf_op jit(solution)/shard_map/crop_block/pallas_call | solution.py:190
  97.6 2.3 collective-permute-done.19.refs_3_
  101.2 7.3 %crop_block.7 = (bf16[3200,256]{1,0:T(8,128)(2,1)S(1)}, f32[256,1024]{1,0:T(8,128)S(1)}, f32[8,128]{1,0:T(8,128)}) custom-call(f32[2,8,128]{2,1,0:T(8,128)S(1)} %get-tuple-element.216.box_ref, bf16[2,1024,256]{2,1,0:T(8,128)(2,1)S(1)} %get-tuple-element.122.maps_ref, bf16[3200,1024]{1,0:T(8,128)(2,1)S(1)} %gather_pieces.1.weight_ref.refs_0_, ...), custom_call_target="tpu_custom_call" | custom-call | flops 40000000000 | bytes 1 | tf_op jit(solution)/shard_map/crop_block/pallas_call | solution.py:190
  108.6 1.3 full_small.1
  109.9 3.8 %collective-permute-done.16.one_ref = bf16[256,1024]{1,0:T(8,128)(2,1)} collective-permute-done((bf16[256,1024]{1,0:T(8,128)(2,1)}, bf16[256,1024]{1,0:T(8,128)(2,1)}, u32[]{:S(2)}, u32[]{:S(2)}) %collective-permute-start.16) | collective-permute-done | bytes 524320 | tf_op jit(solution)/shard_map/ppermute | solution.py:638
  113.7 6.2 %collective-permute-done.17.two_ref = bf16[256,1024]{1,0:T(8,128)(2,1)S(1)} collective-permute-done((bf16[256,1024]{1,0:T(8,128)(2,1)S(1)}, bf16[256,1024]{1,0:T(8,128)(2,1)S(1)}, u32[]{:S(2)}, u32[]{:S(2)}) %collective-permute-start.17) | collective-permute-done | bytes 524320 | tf_op jit(solution)/shard_map/ppermute | solution.py:638
  120.0 4.4 %head_block.1 = (f32[81,2,128]{2,1,0:T(2,128)}, f32[2,320,128]{2,1,0:T(8,128)}, bf16[256,1024]{1,0:T(8,128)(2,1)S(1)}, bf16[256,1024]{1,0:T(8,128)(2,1)S(1)}, bf...) custom-call(f32[256,1024]{1,0:T(8,128)S(1)} %get-tuple-element.135.o, ...), custom_call_target="tpu_custom_call" | custom-call | flops 40000000000 | bytes 1 | tf_op jit(solution)/shard_map/head_block/pallas_call | solution.py:517
  124.3 3.4 %collective-permute-start.24 = (bf16[256,1024]{1,0:T(8,128)(2,1)S(1)}, bf16[256,1024]{1,0:T(8,128)(2,1)S(1)}, u32[]{:S(2)}, u32[]{:S(2)}) collective-permute-start(bf16[256,1024]{1,0:T(8,128)(2,1)S(1)} %get-tuple-element.144.grad_ref.refs_3_), channel_id=1, source_target_pairs={{0,16},{8,24},{16,0},{24,8},{1,17},{9,25},{17,1},{25,9},{2,18},{10... | collective-permute-start | bytes 1572872 | tf_op jit(solution)/shard_map/ppermute | solution.py:638
  127.7 2.5 %small_product.1 = (bf16[528,1536]{1,0:T(8,128)(2,1)S(1)}, bf16[528,1536]{1,0:T(8,128)(2,1)S(1)}, f32[8,128]{1,0:T(8,128)S(1)}) custom-call(s32[2]{0:T(128)S(1)} %pad_add_fusion.refs_0_.where_ref, bf16[256,1024]{1,0:T(8,128)(2,1)S(1)} %get-tuple-element.145.first_ref, bf16[256,1024]{1,0:T(8,128)(2,1)S(1)} %get-tuple-element.146.second_grad_ref, ...), custom_call_target="tpu_custom_call" | custom-call | flops 40000000000 | bytes 1 | tf_op jit(solution)/shard_map/small_product/pallas_call | solution.py:372
  130.4 7.1 %spread_block.4 = (bf16[2,1024,256]{2,1,0:T(8,128)(2,1)S(1)}, f32[8,128]{1,0:T(8,128)S(1)}) custom-call(f32[2,8,128]{2,1,0:T(8,128)S(1)} %get-tuple-element.216.box_ref, bf16[256,1024]{1,0:T(8,128)(2,1)S(1)} %get-tuple-element.144.grad_ref.refs_3_, bf16[3200,1024]{1,0:T(8,128)(2,1)S(1)} %gather_pieces.1.weight_ref.refs_0_, ...), custom_call_target="tpu_custom_call" | custom-call | flops 40000000000 | bytes 1 | tf_op jit(solution)/shard_map/spread_block/pallas_call | solution.py:239
  137.5 2.1 quarter_rows.1
  139.6 1.4 collective-permute-start.27
  141.1 1.2 collective-permute-start.28
  143.1 5.2 %collective-permute-done.24.refs_0_ = bf16[256,1024]{1,0:T(8,128)(2,1)S(1)} collective-permute-done((bf16[256,1024]{1,0:T(8,128)(2,1)S(1)}, bf16[256,1024]{1,0:T(8,128)(2,1)S(1)}, u32[]{:S(2)}, u32[]{:S(2)}) %collective-permute-start.24) | collective-permute-done | bytes 524320 | tf_op jit(solution)/shard_map/ppermute | solution.py:638
  148.3 3.3 %collective-permute-start.25 = (bf16[256,1024]{1,0:T(8,128)(2,1)S(1)}, bf16[256,1024]{1,0:T(8,128)(2,1)S(1)}, u32[]{:S(2)}, u32[]{:S(2)}) collective-permute-start(bf16[256,1024]{1,0:T(8,128)(2,1)S(1)} %tie.9.grad_ref.refs_1_), channel_id=1, source_target_pairs={{0,8},{8,0},{16,24},{24,16},{1,9},{9,1},{17,25},{25,17},{2,10},{10... | collective-permute-start | bytes 1572872 | tf_op jit(solution)/shard_map/ppermute | solution.py:638
  151.6 7.3 %spread_block.5 = (bf16[2,1024,256]{2,1,0:T(8,128)(2,1)S(1)}, f32[8,128]{1,0:T(8,128)S(1)}) custom-call(f32[2,8,128]{2,1,0:T(8,128)S(1)} %get-tuple-element.214.box_ref, bf16[256,1024]{1,0:T(8,128)(2,1)S(1)} %collective-permute-done.22.grad_ref.refs_2_, bf16[3200,1024]{1,0:T(8,128)(2,1)S(1)} %gather_pieces.1.weight_ref.refs_0_, ...), custom_call_target="tpu_custom_call" | custom-call | flops 40000000000 | bytes 1 | tf_op jit(solution)/shard_map/spread_block/pallas_call | solution.py:239
  158.9 7.1 %spread_block.6 = (bf16[2,1024,256]{2,1,0:T(8,128)(2,1)S(1)}, f32[8,128]{1,0:T(8,128)S(1)}) custom-call(f32[2,8,128]{2,1,0:T(8,128)S(1)} %get-tuple-element.213.box_ref, bf16[256,1024]{1,0:T(8,128)(2,1)S(1)} %tie.9.grad_ref.refs_1_, bf16[3200,1024]{1,0:T(8,128)(2,1)S(1)} %gather_pieces.1.weight_ref.refs_0_, f32[8,128]{1,0:T(8,128)S(1)} %get-tuple-element.157.refs_0_), custom_call_target="tpu_custom_call" | custom-call | flops 40000000000 | bytes 1 | tf_op jit(solution)/shard_map/spread_block/pallas_call | solution.py:239
  166.0 1.6 piece_product.6
  167.6 2.4 piece_product.7
  170.6 2.7 %piece_product.8 = (bf16[400,1024]{1,0:T(8,128)(2,1)}, f32[8,128]{1,0:T(8,128)S(1)}) custom-call(s32[2]{0:T(128)S(1)} %pad_add_fusion.refs_0_.where_ref, bf16[256,1024]{1,0:T(8,128)(2,1)S(1)} %collective-permute-done.25.refs_0_.grad_ref, bf16[256,1024]{1,0:T(8,128)(2,1)S(1)} %tie.9.grad_ref.refs_1_, ...), custom_call_target="tpu_custom_call" | custom-call | flops 40000000000 | bytes 1 | tf_op jit(solution)/shard_map/piece_product/pallas_call | solution.py:676
  173.3 1.7 halve_rows.2
  175.2 2.9 %collective-permute-start.33 = (bf16[400,1024]{1,0:T(8,128)(2,1)}, bf16[400,1024]{1,0:T(8,128)(2,1)}, u32[]{:S(2)}, u32[]{:S(2)}) collective-permute-start(bf16[400,1024]{1,0:T(8,128)(2,1)} %get-tuple-element.183), channel_id=1, source_target_pairs={{0,6},{1,7},{2,4},{3,5},{4,2},{5,3},{6,0},{7,1},{8,14},{9,15},{10,... | collective-permute-start | bytes 2457608 | tf_op jit(solution)/shard_map/ppermute | solution.py:638
  178.2 3.3 %piece_product.9 = (bf16[400,1024]{1,0:T(8,128)(2,1)}, bf16[400,1024]{1,0:T(8,128)(2,1)}, f32[8,128]{1,0:T(8,128)S(1)}) custom-call(s32[2]{0:T(128)S(1)} %pad_add_fusion.refs_0_.where_ref, bf16[256,1024]{1,0:T(8,128)(2,1)S(1)} %collective-permute-done.25.refs_0_.grad_ref, bf16[256,1024]{1,0:T(8,128)(2,1)S(1)} %tie.9.grad_ref.refs_1_, ...), custom_call_target="tpu_custom_call" | custom-call | flops 40000000000 | bytes 1 | tf_op jit(solution)/shard_map/piece_product/pallas_call | solution.py:676
  181.5 1.5 piece_product.10
  183.1 7.1 %spread_block.7 = (bf16[2,1024,256]{2,1,0:T(8,128)(2,1)S(1)}, f32[8,128]{1,0:T(8,128)S(1)}) custom-call(f32[2,8,128]{2,1,0:T(8,128)S(1)} %copy-done.1, bf16[256,1024]{1,0:T(8,128)(2,1)S(1)} %collective-permute-done.25.refs_0_.grad_ref, bf16[3200,1024]{1,0:T(8,128)(2,1)S(1)} %gather_pieces.1.weight_ref.refs_0_, f32[8,128]{1,0:T(8,128)S(1)} %get-tuple-element.175.refs_0_), custom_call_target="tpu_custom_call" | custom-call | flops 40000000000 | bytes 1 | tf_op jit(solution)/shard_map/spread_block/pallas_call | solution.py:239
  190.9 1.9 collective-permute-start.34
  193.5 1.6 piece_product.11
  195.1 2.2 collective-permute-done.34.refs_2_
  197.3 1.2 small_sum.1
  198.6 1.4 add.20
  200.0 1.7 arrange_back.1
  201.7 1.8 collective-permute-start.35
  204.0 1.3 collective-permute-start.37
  205.7 8.5 %collective-permute-done.38.refs_3_ = bf16[400,1024]{1,0:T(8,128)(2,1)} collective-permute-done((bf16[400,1024]{1,0:T(8,128)(2,1)}, bf16[400,1024]{1,0:T(8,128)(2,1)}, u32[]{:S(2)}, u32[]{:S(2)}) %collective-permute-start.38) | collective-permute-done | bytes 819232 | tf_op jit(solution)/shard_map/ppermute | solution.py:638
  214.4 2.3 return_span.1
  217.3 1.8 collective-permute-start.40
  221.8 16.6 %collective-permute-done.37.refs_4_ = bf16[2,64,1024]{2,1,0:T(8,128)(2,1)S(1)} collective-permute-done((bf16[2,64,1024]{2,1,0:T(8,128)(2,1)S(1)}, bf16[2,64,1024]{2,1,0:T(8,128)(2,1)S(1)}, u32[]{:S(2)}, u32[]{:S(2)}) %collective-permute-start.37) | collective-permute-done | bytes 262176 | tf_op jit(solution)/shard_map/ppermute | solution.py:638
  238.4 4.5 %maps_back.1 = (f32[2,1024,256]{2,1,0:T(8,128)}, f32[8,128]{1,0:T(8,128)S(1)}) custom-call(s32[2]{0:T(128)S(1)} %pad_add_fusion.refs_0_.where_ref, bf16[2,64,1024]{2,1,0:T(8,128)(2,1)S(1)} %get-tuple-element.189.refs_1_, bf16[2,64,1024]{2,1,0:T(8,128)(2,1)S(1)} %collective-permute-done.35.refs_2_, bf16[2,64,1024]{2,1,0:T(8,128)(2,1)S(1)} %collective-permute-done.36.refs_3_, ...), custom_call_target="tpu_custom_call" | custom-call | flops 40000000000 | bytes 1 | tf_op jit(solution)/shard_map/maps_back/pallas_call | solution.py:266
  242.9 3.4 %collective-permute-done.42.refs_5_ = bf16[104,1024]{1,0:T(8,128)(2,1)S(1)} collective-permute-done((bf16[104,1024]{1,0:T(8,128)(2,1)S(1)}, bf16[104,1024]{1,0:T(8,128)(2,1)S(1)}, u32[]{:S(2)}, u32[]{:S(2)}) %collective-permute-start.42) | collective-permute-done | bytes 213024 | tf_op jit(solution)/shard_map/ppermute | solution.py:638
  246.2 2.4 join_span.3
  (128 shorter events, 17.6 us)
Async XLA Ops:
  1.6 1.1 copy-start.3
  2.7 4.9 %copy-start.17 = (bf16[32,320]{1,0:T(8,128)(2,1)S(1)}, bf16[32,320]{1,0:T(8,128)(2,1)}, u32[]{:S(2)}) copy-start(bf16[32,320]{1,0:T(8,128)(2,1)} %param.30) | copy-start | bytes 61444
  2.7 4.9 %copy-start.18 = (bf16[32,81]{1,0:T(8,128)(2,1)S(1)}, bf16[32,81]{1,0:T(8,128)(2,1)}, u32[]{:S(2)}) copy-start(bf16[32,81]{1,0:T(8,128)(2,1)} %param.28) | copy-start | bytes 15556
  2.7 4.9 %copy-start.19 = (f32[320]{0:T(512)S(1)}, f32[320]{0:T(512)}, u32[]{:S(2)}) copy-start(f32[320]{0:T(512)} %param.31) | copy-start | bytes 3844
  2.7 4.9 %copy-start.20 = (f32[81]{0:T(128)S(1)}, f32[81]{0:T(128)}, u32[]{:S(2)}) copy-start(f32[81]{0:T(128)} %param.29) | copy-start | bytes 976
  2.7 4.9 %copy-start.2 = (bf16[1,2,64,16,256]{4,3,2,1,0:T(8,128)(2,1)S(1)}, bf16[1,2,64,16,256]{4,3,2,1,0:T(8,128)(2,1)}, u32[]{:S(2)}) copy-start(bf16[1,2,64,16,256]{4,3,2,1,0:T(8,128)(2,1)} %param.18) | copy-start | bytes 3145732
  2.8 4.9 %copy-start.9 = (bf16[1024,1024]{1,0:T(8,128)(2,1)S(1)}, bf16[1024,1024]{1,0:T(8,128)(2,1)}, u32[]{:S(2)}) copy-start(bf16[1024,1024]{1,0:T(8,128)(2,1)} %constant.28.clone.refs_3_.refs_6_) | copy-start | bytes 6291460
  2.8 4.9 %copy-start.14 = (bf16[4,64,256]{2,1,0:T(8,128)(2,1)S(1)}, bf16[4,64,256]{2,1,0:T(8,128)(2,1)}, u32[]{:S(2)}) copy-start(bf16[4,64,256]{2,1,0:T(8,128)(2,1)} %constant.44.refs_2_.refs_5_) | copy-start | bytes 393220
  4.0 8.7 %collective-permute-start = (bf16[104,1024]{1,0:T(8,128)(2,1)S(1)}, bf16[104,1024]{1,0:T(8,128)(2,1)S(1)}, u32[]{:S(2)}, u32[]{:S(2)}) collective-permute-start(bf16[104,1024]{1,0:T(8,128)(2,1)S(1)} %get-tuple-element.111), channel_id=1, source_target_pairs={{0,8},{8,0},{16,24},{24,16},{1,9},{9,1},{17,25},{25,17},{2,10},{10... | collective-permute-start | bytes 638984 | tf_op jit(solution)/shard_map/ppermute | solution.py:638
  4.1 17.9 %collective-permute-start.1 = (bf16[104,1024]{1,0:T(8,128)(2,1)S(1)}, bf16[104,1024]{1,0:T(8,128)(2,1)S(1)}, u32[]{:S(2)}, u32[]{:S(2)}) collective-permute-start(bf16[104,1024]{1,0:T(8,128)(2,1)S(1)} %get-tuple-element.112), channel_id=1, source_target_pairs={{0,16},{8,24},{16,0},{24,8},{1,17},{9,25},{17,1},{25,9},{2,18},{10... | collective-permute-start | bytes 638984 | tf_op jit(solution)/shard_map/ppermute | solution.py:638
  7.1 18.9 %collective-permute-start.2 = (bf16[104,1024]{1,0:T(8,128)(2,1)S(1)}, bf16[104,1024]{1,0:T(8,128)(2,1)S(1)}, u32[]{:S(2)}, u32[]{:S(2)}) collective-permute-start(bf16[104,1024]{1,0:T(8,128)(2,1)S(1)} %get-tuple-element.113), channel_id=1, source_target_pairs={{0,24},{8,16},{16,8},{24,0},{1,25},{9,17},{17,9},{25,1},{2,26},{10... | collective-permute-start | bytes 638984 | tf_op jit(solution)/shard_map/ppermute | solution.py:638
  7.7 2.5 %copy-start.16 = (bf16[32,1024]{1,0:T(8,128)(2,1)S(1)}, bf16[32,1024]{1,0:T(8,128)(2,1)}, u32[]{:S(2)}) copy-start(bf16[32,1024]{1,0:T(8,128)(2,1)} %param.26) | copy-start | bytes 196612
  7.7 18.3 %copy-start.12 = (bf16[400,416]{1,0:T(8,128)(2,1)S(1)}, bf16[400,416]{1,0:T(8,128)(2,1)}, u32[]{:S(2)}) copy-start(bf16[400,416]{1,0:T(8,128)(2,1)} %constant.26.clone.refs_1_) | copy-start | bytes 998404
  27.3 34.1 %collective-permute-start.11 = (bf16[400,1024]{1,0:T(8,128)(2,1)S(1)}, bf16[400,1024]{1,0:T(8,128)(2,1)S(1)}, u32[]{:S(2)}, u32[]{:S(2)}) collective-permute-start(bf16[400,1024]{1,0:T(8,128)(2,1)S(1)} %get-tuple-element.125), channel_id=1, source_target_pairs={{0,6},{1,7},{2,4},{3,5},{4,2},{5,3},{6,0},{7,1},{8,14},{9,15},{10,... | collective-permute-start | bytes 2457608 | tf_op jit(solution)/shard_map/ppermute | solution.py:638
  29.8 34.9 %collective-permute-start.9 = (bf16[400,1024]{1,0:T(8,128)(2,1)S(1)}, bf16[400,1024]{1,0:T(8,128)(2,1)S(1)}, u32[]{:S(2)}, u32[]{:S(2)}) collective-permute-start(bf16[400,1024]{1,0:T(8,128)(2,1)S(1)} %get-tuple-element.125), channel_id=1, source_target_pairs={{0,4},{1,5},{2,6},{3,7},{4,0},{5,1},{6,2},{7,3},{8,12},{9,13},{10,... | collective-permute-start | bytes 2457608 | tf_op jit(solution)/shard_map/ppermute | solution.py:638
  30.3 34.4 %collective-permute-start.7 = (bf16[400,1024]{1,0:T(8,128)(2,1)S(1)}, bf16[400,1024]{1,0:T(8,128)(2,1)S(1)}, u32[]{:S(2)}, u32[]{:S(2)}) collective-permute-start(bf16[400,1024]{1,0:T(8,128)(2,1)S(1)} %get-tuple-element.125), channel_id=1, source_target_pairs={{0,2},{1,3},{2,0},{3,1},{4,6},{5,7},{6,4},{7,5},{8,10},{9,11},{10,... | collective-permute-start | bytes 2457608 | tf_op jit(solution)/shard_map/ppermute | solution.py:638
  30.8 9.2 %collective-permute-start.3 = (bf16[128,1024]{1,0:T(8,128)(2,1)S(1)}, bf16[128,1024]{1,0:T(8,128)(2,1)S(1)}, u32[]{:S(2)}, u32[]{:S(2)}) collective-permute-start(bf16[128,1024]{1,0:T(8,128)(2,1)S(1)} %get-tuple-element.119), channel_id=1, source_target_pairs={{0,8},{8,0},{16,24},{24,16},{1,9},{9,1},{17,25},{25,17},{2,10},{10... | collective-permute-start | bytes 786440 | tf_op jit(solution)/shard_map/ppermute | solution.py:638
  30.9 24.2 %collective-permute-start.4 = (bf16[128,1024]{1,0:T(8,128)(2,1)S(1)}, bf16[128,1024]{1,0:T(8,128)(2,1)S(1)}, u32[]{:S(2)}, u32[]{:S(2)}) collective-permute-start(bf16[128,1024]{1,0:T(8,128)(2,1)S(1)} %get-tuple-element.120), channel_id=1, source_target_pairs={{0,16},{8,24},{16,0},{24,8},{1,17},{9,25},{17,1},{25,9},{2,18},{10... | collective-permute-start | bytes 786440 | tf_op jit(solution)/shard_map/ppermute | solution.py:638
  40.1 15.0 %collective-permute-start.5 = (bf16[128,1024]{1,0:T(8,128)(2,1)S(1)}, bf16[128,1024]{1,0:T(8,128)(2,1)S(1)}, u32[]{:S(2)}, u32[]{:S(2)}) collective-permute-start(bf16[128,1024]{1,0:T(8,128)(2,1)S(1)} %tie.6), channel_id=1, source_target_pairs={{0,24},{8,16},{16,8},{24,0},{1,25},{9,17},{17,9},{25,1},{2,26},{10... | collective-permute-start | bytes 786440 | tf_op jit(solution)/shard_map/ppermute | solution.py:638
  41.7 15.1 %copy-start = (f32[2,8,128]{2,1,0:T(8,128)}, f32[2,8,128]{2,1,0:T(8,128)S(1)}, u32[]{:S(2)}) copy-start(f32[2,8,128]{2,1,0:T(8,128)S(1)} %get-tuple-element.215.box_ref) | copy-start | bytes 24580
  55.1 10.0 %collective-permute-start.14 = (bf16[48,1024]{1,0:T(8,128)(2,1)S(1)}, bf16[48,1024]{1,0:T(8,128)(2,1)S(1)}, u32[]{:S(2)}, u32[]{:S(2)}) collective-permute-start(bf16[48,1024]{1,0:T(8,128)(2,1)S(1)} %tie.8.refs_1_), channel_id=1, source_target_pairs={{0,8},{8,0},{16,24},{24,16},{1,9},{9,1},{17,25},{25,17},{2,10},{10... | collective-permute-start | bytes 294920 | tf_op jit(solution)/shard_map/ppermute | solution.py:638
  61.3 5.3 %collective-permute-start.6 = (bf16[400,1024]{1,0:T(8,128)(2,1)S(1)}, bf16[400,1024]{1,0:T(8,128)(2,1)S(1)}, u32[]{:S(2)}, u32[]{:S(2)}) collective-permute-start(bf16[400,1024]{1,0:T(8,128)(2,1)S(1)} %tie.7.refs_0_), channel_id=1, source_target_pairs={{0,1},{1,0},{2,3},{3,2},{4,5},{5,4},{6,7},{7,6},{8,9},{9,8},{10,11... | collective-permute-start | bytes 2457608 | tf_op jit(solution)/shard_map/ppermute | solution.py:638
  61.4 5.2 %collective-permute-start.12 = (bf16[400,1024]{1,0:T(8,128)(2,1)S(1)}, bf16[400,1024]{1,0:T(8,128)(2,1)S(1)}, u32[]{:S(2)}, u32[]{:S(2)}) collective-permute-start(bf16[400,1024]{1,0:T(8,128)(2,1)S(1)} %collective-permute-done.11.refs_6_), channel_id=1, source_target_pairs={{0,1},{1,0},{2,3},{3,2},{4,5},{5,4},{6,7},{7,6},{8,9},{9,8},{10,11... | collective-permute-start | bytes 2457608 | tf_op jit(solution)/shard_map/ppermute | solution.py:638
  64.6 2.3 collective-permute-start.10
  64.7 3.4 %collective-permute-start.8 = (bf16[400,1024]{1,0:T(8,128)(2,1)S(1)}, bf16[400,1024]{1,0:T(8,128)(2,1)S(1)}, u32[]{:S(2)}, u32[]{:S(2)}) collective-permute-start(bf16[400,1024]{1,0:T(8,128)(2,1)S(1)} %collective-permute-done.7.refs_2_), channel_id=1, source_target_pairs={{0,1},{1,0},{2,3},{3,2},{4,5},{5,4},{6,7},{7,6},{8,9},{9,8},{10,11... | collective-permute-start | bytes 2457608 | tf_op jit(solution)/shard_map/ppermute | solution.py:638
  66.3 12.9 %collective-permute-start.15 = (bf16[2,48,1024]{2,1,0:T(8,128)(2,1)S(1)}, bf16[2,48,1024]{2,1,0:T(8,128)(2,1)S(1)}, u32[]{:S(2)}, u32[]{:S(2)}) collective-permute-start(bf16[2,48,1024]{2,1,0:T(8,128)(2,1)S(1)} %get-tuple-element.130.refs_1_), channel_id=1, source_target_pairs={{0,16},{8,24},{16,0},{24,8},{1,17},{9,25},{17,1},{25,9},{2,18},{10... | collective-permute-start | bytes 589832 | tf_op jit(solution)/shard_map/ppermute | solution.py:638
  71.5 15.7 %collective-permute-start.13 = (bf16[256,1024]{1,0:T(8,128)(2,1)S(1)}, bf16[256,1024]{1,0:T(8,128)(2,1)S(1)}, u32[]{:S(2)}, u32[]{:S(2)}) collective-permute-start(bf16[256,1024]{1,0:T(8,128)(2,1)S(1)} %get-tuple-element.129), channel_id=1, source_target_pairs={{0,8},{8,0},{16,24},{24,16},{1,9},{9,1},{17,25},{25,17},{2,10},{10... | collective-permute-start | bytes 1572872 | tf_op jit(solution)/shard_map/ppermute | solution.py:638
  79.8 17.9 %collective-permute-start.20 = (bf16[4,48,1024]{2,1,0:T(8,128)(2,1)S(1)}, bf16[4,48,1024]{2,1,0:T(8,128)(2,1)S(1)}, u32[]{:S(2)}, u32[]{:S(2)}) collective-permute-start(bf16[4,48,1024]{2,1,0:T(8,128)(2,1)S(1)} %bitcast.57), channel_id=1, source_target_pairs={{0,6},{1,7},{2,4},{3,5},{4,2},{5,3},{6,0},{7,1},{8,14},{9,15},{10,... | collective-permute-start | bytes 1179656 | tf_op jit(solution)/shard_map/ppermute | solution.py:638
  82.2 17.8 %collective-permute-start.19 = (bf16[4,48,1024]{2,1,0:T(8,128)(2,1)S(1)}, bf16[4,48,1024]{2,1,0:T(8,128)(2,1)S(1)}, u32[]{:S(2)}, u32[]{:S(2)}) collective-permute-start(bf16[4,48,1024]{2,1,0:T(8,128)(2,1)S(1)} %bitcast.58), channel_id=1, source_target_pairs={{0,4},{1,5},{2,6},{3,7},{4,0},{5,1},{6,2},{7,3},{8,12},{9,13},{10,... | collective-permute-start | bytes 1179656 | tf_op jit(solution)/shard_map/ppermute | solution.py:638
  82.8 17.3 %collective-permute-start.18 = (bf16[4,48,1024]{2,1,0:T(8,128)(2,1)S(1)}, bf16[4,48,1024]{2,1,0:T(8,128)(2,1)S(1)}, u32[]{:S(2)}, u32[]{:S(2)}) collective-permute-start(bf16[4,48,1024]{2,1,0:T(8,128)(2,1)S(1)} %bitcast.59), channel_id=1, source_target_pairs={{0,2},{1,3},{2,0},{3,1},{4,6},{5,7},{6,4},{7,5},{8,10},{9,11},{10,... | collective-permute-start | bytes 1179656 | tf_op jit(solution)/shard_map/ppermute | solution.py:638
  88.7 25.0 %collective-permute-start.16 = (bf16[256,1024]{1,0:T(8,128)(2,1)}, bf16[256,1024]{1,0:T(8,128)(2,1)}, u32[]{:S(2)}, u32[]{:S(2)}) collective-permute-start(bf16[256,1024]{1,0:T(8,128)(2,1)} %get-tuple-element.136), channel_id=1, source_target_pairs={{0,16},{8,24},{16,0},{24,8},{1,17},{9,25},{17,1},{25,9},{2,18},{10... | collective-permute-start | bytes 1572872 | tf_op jit(solution)/shard_map/ppermute | solution.py:638
  97.4 22.5 %collective-permute-start.17 = (bf16[256,1024]{1,0:T(8,128)(2,1)S(1)}, bf16[256,1024]{1,0:T(8,128)(2,1)S(1)}, u32[]{:S(2)}, u32[]{:S(2)}) collective-permute-start(bf16[256,1024]{1,0:T(8,128)(2,1)S(1)} %get-tuple-element.137), channel_id=1, source_target_pairs={{0,8},{8,0},{16,24},{24,16},{1,9},{9,1},{17,25},{25,17},{2,10},{10... | collective-permute-start | bytes 1572872 | tf_op jit(solution)/shard_map/ppermute | solution.py:638
  101.2 7.4 %collective-permute-start.21 = (bf16[4,4,48,1024]{3,2,1,0:T(8,128)(2,1)S(1)}, bf16[4,4,48,1024]{3,2,1,0:T(8,128)(2,1)S(1)}, u32[]{:S(2)}, u32[]{:S(2)}) collective-permute-start(bf16[4,4,48,1024]{3,2,1,0:T(8,128)(2,1)S(1)} %get-tuple-element.139.refs_1_), channel_id=1, source_target_pairs={{0,1},{1,0},{2,3},{3,2},{4,5},{5,4},{6,7},{7,6},{8,9},{9,8},{10,11... | collective-permute-start | bytes 4718600 | tf_op jit(solution)/shard_map/ppermute | solution.py:638
  108.6 11.4 %copy-start.4 = (f32[2,128,4]{1,2,0:T(4,128)S(1)}, f32[2,128,4]{1,2,0:T(4,128)}, u32[]{:S(2)}) copy-start(f32[2,128,4]{1,2,0:T(4,128)} %param.23) | copy-start | bytes 12292
  108.6 11.4 %copy-start.5 = (f32[1024]{0:T(1024)S(1)}, f32[1024]{0:T(1024)}, u32[]{:S(2)}) copy-start(f32[1024]{0:T(1024)} %param.25) | copy-start | bytes 12292
  108.6 11.4 %copy-start.6 = (f32[1024]{0:T(1024)S(1)}, f32[1024]{0:T(1024)}, u32[]{:S(2)}) copy-start(f32[1024]{0:T(1024)} %param.27) | copy-start | bytes 12292
  108.6 11.4 %copy-start.7 = (s32[2,128]{1,0:T(2,128)S(1)}, s32[2,128]{1,0:T(2,128)}, u32[]{:S(2)}) copy-start(s32[2,128]{1,0:T(2,128)} %labels_ref.1) | copy-start | bytes 3076
  108.6 11.4 %copy-start.8 = (s32[2,128]{1,0:T(2,128)S(1)}, s32[2,128]{1,0:T(2,128)}, u32[]{:S(2)}) copy-start(s32[2,128]{1,0:T(2,128)} %ignore_ref.1) | copy-start | bytes 3076
  124.3 24.0 %collective-permute-start.24 = (bf16[256,1024]{1,0:T(8,128)(2,1)S(1)}, bf16[256,1024]{1,0:T(8,128)(2,1)S(1)}, u32[]{:S(2)}, u32[]{:S(2)}) collective-permute-start(bf16[256,1024]{1,0:T(8,128)(2,1)S(1)} %get-tuple-element.144.grad_ref.refs_3_), channel_id=1, source_target_pairs={{0,16},{8,24},{16,0},{24,8},{1,17},{9,25},{17,1},{25,9},{2,18},{10... | collective-permute-start | bytes 1572872 | tf_op jit(solution)/shard_map/ppermute | solution.py:638
  127.7 23.9 %collective-permute-start.22 = (bf16[256,1024]{1,0:T(8,128)(2,1)S(1)}, bf16[256,1024]{1,0:T(8,128)(2,1)S(1)}, u32[]{:S(2)}, u32[]{:S(2)}) collective-permute-start(bf16[256,1024]{1,0:T(8,128)(2,1)S(1)} %get-tuple-element.144.grad_ref.refs_3_), channel_id=1, source_target_pairs={{0,8},{8,0},{16,24},{24,16},{1,9},{9,1},{17,25},{25,17},{2,10},{10... | collective-permute-start | bytes 1572872 | tf_op jit(solution)/shard_map/ppermute | solution.py:638
  130.3 7.2 %collective-permute-start.23 = (bf16[528,1536]{1,0:T(8,128)(2,1)S(1)}, bf16[528,1536]{1,0:T(8,128)(2,1)S(1)}, u32[]{:S(2)}, u32[]{:S(2)}) collective-permute-start(bf16[528,1536]{1,0:T(8,128)(2,1)S(1)} %get-tuple-element.153), channel_id=1, source_target_pairs={{0,1},{1,0},{2,3},{3,2},{4,5},{5,4},{6,7},{7,6},{8,9},{9,8},{10,11... | collective-permute-start | bytes 4866056 | tf_op jit(solution)/shard_map/ppermute | solution.py:638
  139.6 33.7 %collective-permute-start.27 = (bf16[144,1536]{1,0:T(8,128)(2,1)}, bf16[144,1536]{1,0:T(8,128)(2,1)}, u32[]{:S(2)}, u32[]{:S(2)}) collective-permute-start(bf16[144,1536]{1,0:T(8,128)(2,1)} %get-tuple-element.167), channel_id=1, source_target_pairs={{0,2},{1,3},{2,0},{3,1},{4,6},{5,7},{6,4},{7,5},{8,10},{9,11},{10,... | collective-permute-start | bytes 1327112 | tf_op jit(solution)/shard_map/ppermute | solution.py:638
  141.1 32.2 %collective-permute-start.28 = (bf16[144,1536]{1,0:T(8,128)(2,1)}, bf16[144,1536]{1,0:T(8,128)(2,1)}, u32[]{:S(2)}, u32[]{:S(2)}) collective-permute-start(bf16[144,1536]{1,0:T(8,128)(2,1)} %get-tuple-element.168), channel_id=1, source_target_pairs={{0,4},{1,5},{2,6},{3,7},{4,0},{5,1},{6,2},{7,3},{8,12},{9,13},{10,... | collective-permute-start | bytes 1327112 | tf_op jit(solution)/shard_map/ppermute | solution.py:638
  142.2 31.1 %collective-permute-start.29 = (bf16[144,1536]{1,0:T(8,128)(2,1)}, bf16[144,1536]{1,0:T(8,128)(2,1)}, u32[]{:S(2)}, u32[]{:S(2)}) collective-permute-start(bf16[144,1536]{1,0:T(8,128)(2,1)} %get-tuple-element.169), channel_id=1, source_target_pairs={{0,6},{1,7},{2,4},{3,5},{4,2},{5,3},{6,0},{7,1},{8,14},{9,15},{10,... | collective-permute-start | bytes 1327112 | tf_op jit(solution)/shard_map/ppermute | solution.py:638
  148.3 17.7 %collective-permute-start.25 = (bf16[256,1024]{1,0:T(8,128)(2,1)S(1)}, bf16[256,1024]{1,0:T(8,128)(2,1)S(1)}, u32[]{:S(2)}, u32[]{:S(2)}) collective-permute-start(bf16[256,1024]{1,0:T(8,128)(2,1)S(1)} %tie.9.grad_ref.refs_1_), channel_id=1, source_target_pairs={{0,8},{8,0},{16,24},{24,16},{1,9},{9,1},{17,25},{25,17},{2,10},{10... | collective-permute-start | bytes 1572872 | tf_op jit(solution)/shard_map/ppermute | solution.py:638
  167.6 3.1 %collective-permute-start.30 = (bf16[1,400,1024]{2,1,0:T(8,128)(2,1)S(1)}, bf16[1,400,1024]{2,1,0:T(8,128)(2,1)S(1)}, u32[]{:S(2)}, u32[]{:S(2)}) collective-permute-start(bf16[1,400,1024]{2,1,0:T(8,128)(2,1)S(1)} %get-tuple-element.170), channel_id=1, source_target_pairs={{0,1},{1,0},{2,3},{3,2},{4,5},{5,4},{6,7},{7,6},{8,9},{9,8},{10,11... | collective-permute-start | bytes 2457608 | tf_op jit(solution)/shard_map/ppermute | solution.py:638
  170.0 8.1 %collective-permute-start.26 = (bf16[2,400,1024]{2,1,0:T(8,128)(2,1)S(1)}, bf16[2,400,1024]{2,1,0:T(8,128)(2,1)S(1)}, u32[]{:S(2)}, u32[]{:S(2)}) collective-permute-start(bf16[2,400,1024]{2,1,0:T(8,128)(2,1)S(1)} %get-tuple-element.165), channel_id=1, source_target_pairs={{0,1},{1,0},{2,3},{3,2},{4,5},{5,4},{6,7},{7,6},{8,9},{9,8},{10,11... | collective-permute-start | bytes 4915208 | tf_op jit(solution)/shard_map/ppermute | solution.py:638
  175.0 15.3 %collective-permute-start.32 = (bf16[80,1536]{1,0:T(8,128)(2,1)S(1)}, bf16[80,1536]{1,0:T(8,128)(2,1)S(1)}, u32[]{:S(2)}, u32[]{:S(2)}) collective-permute-start(bf16[80,1536]{1,0:T(8,128)(2,1)S(1)} %get-tuple-element.179), channel_id=1, source_target_pairs={{0,16},{8,24},{16,0},{24,8},{1,17},{9,25},{17,1},{25,9},{2,18},{10... | collective-permute-start | bytes 737288 | tf_op jit(solution)/shard_map/ppermute | solution.py:638
  175.2 23.3 %collective-permute-start.33 = (bf16[400,1024]{1,0:T(8,128)(2,1)}, bf16[400,1024]{1,0:T(8,128)(2,1)}, u32[]{:S(2)}, u32[]{:S(2)}) collective-permute-start(bf16[400,1024]{1,0:T(8,128)(2,1)} %get-tuple-element.183), channel_id=1, source_target_pairs={{0,6},{1,7},{2,4},{3,5},{4,2},{5,3},{6,0},{7,1},{8,14},{9,15},{10,... | collective-permute-start | bytes 2457608 | tf_op jit(solution)/shard_map/ppermute | solution.py:638
  181.5 1.6 copy-start.1
  183.1 10.5 %collective-permute-start.31 = (bf16[1,400,1024]{2,1,0:T(8,128)(2,1)S(1)}, bf16[1,400,1024]{2,1,0:T(8,128)(2,1)S(1)}, u32[]{:S(2)}, u32[]{:S(2)}) collective-permute-start(bf16[1,400,1024]{2,1,0:T(8,128)(2,1)S(1)} %get-tuple-element.177), channel_id=1, source_target_pairs={{0,1},{1,0},{2,3},{3,2},{4,5},{5,4},{6,7},{7,6},{8,9},{9,8},{10,11... | collective-permute-start | bytes 2457608 | tf_op jit(solution)/shard_map/ppermute | solution.py:638
  190.9 6.4 %collective-permute-start.34 = (bf16[48,1536]{1,0:T(8,128)(2,1)S(1)}, bf16[48,1536]{1,0:T(8,128)(2,1)S(1)}, u32[]{:S(2)}, u32[]{:S(2)}) collective-permute-start(bf16[48,1536]{1,0:T(8,128)(2,1)S(1)} %get-tuple-element.185), channel_id=1, source_target_pairs={{0,8},{8,0},{16,24},{24,16},{1,9},{9,1},{17,25},{25,17},{2,10},{10... | collective-permute-start | bytes 442376 | tf_op jit(solution)/shard_map/ppermute | solution.py:638
  192.8 21.4 %collective-permute-start.38 = (bf16[400,1024]{1,0:T(8,128)(2,1)}, bf16[400,1024]{1,0:T(8,128)(2,1)}, u32[]{:S(2)}, u32[]{:S(2)}) collective-permute-start(bf16[400,1024]{1,0:T(8,128)(2,1)} %get-tuple-element.194), channel_id=1, source_target_pairs={{0,2},{1,3},{2,0},{3,1},{4,6},{5,7},{6,4},{7,5},{8,10},{9,11},{10,... | collective-permute-start | bytes 2457608 | tf_op jit(solution)/shard_map/ppermute | solution.py:638
  193.2 21.2 %collective-permute-start.39 = (bf16[400,1024]{1,0:T(8,128)(2,1)}, bf16[400,1024]{1,0:T(8,128)(2,1)}, u32[]{:S(2)}, u32[]{:S(2)}) collective-permute-start(bf16[400,1024]{1,0:T(8,128)(2,1)} %get-tuple-element.195), channel_id=1, source_target_pairs={{0,4},{1,5},{2,6},{3,7},{4,0},{5,1},{6,2},{7,3},{8,12},{9,13},{10,... | collective-permute-start | bytes 2457608 | tf_op jit(solution)/shard_map/ppermute | solution.py:638
  199.9 14.4 %copy-start.11 = (bf16[416,400]{1,0:T(8,128)(2,1)S(1)}, bf16[416,400]{1,0:T(8,128)(2,1)}, u32[]{:S(2)}) copy-start(bf16[416,400]{1,0:T(8,128)(2,1)} %constant.45.refs_1_) | copy-start | bytes 998404
  201.7 19.0 %collective-permute-start.35 = (bf16[2,64,1024]{2,1,0:T(8,128)(2,1)S(1)}, bf16[2,64,1024]{2,1,0:T(8,128)(2,1)S(1)}, u32[]{:S(2)}, u32[]{:S(2)}) collective-permute-start(bf16[2,64,1024]{2,1,0:T(8,128)(2,1)S(1)} %get-tuple-element.190), channel_id=1, source_target_pairs={{0,8},{8,0},{16,24},{24,16},{1,9},{9,1},{17,25},{25,17},{2,10},{10... | collective-permute-start | bytes 786440 | tf_op jit(solution)/shard_map/ppermute | solution.py:638
  203.5 18.3 %collective-permute-start.36 = (bf16[2,64,1024]{2,1,0:T(8,128)(2,1)S(1)}, bf16[2,64,1024]{2,1,0:T(8,128)(2,1)S(1)}, u32[]{:S(2)}, u32[]{:S(2)}) collective-permute-start(bf16[2,64,1024]{2,1,0:T(8,128)(2,1)S(1)} %get-tuple-element.191), channel_id=1, source_target_pairs={{0,16},{8,24},{16,0},{24,8},{1,17},{9,25},{17,1},{25,9},{2,18},{10... | collective-permute-start | bytes 786440 | tf_op jit(solution)/shard_map/ppermute | solution.py:638
  204.0 34.4 %collective-permute-start.37 = (bf16[2,64,1024]{2,1,0:T(8,128)(2,1)S(1)}, bf16[2,64,1024]{2,1,0:T(8,128)(2,1)S(1)}, u32[]{:S(2)}, u32[]{:S(2)}) collective-permute-start(bf16[2,64,1024]{2,1,0:T(8,128)(2,1)S(1)} %get-tuple-element.192), channel_id=1, source_target_pairs={{0,24},{8,16},{16,8},{24,0},{1,25},{9,17},{17,9},{25,1},{2,26},{10... | collective-permute-start | bytes 786440 | tf_op jit(solution)/shard_map/ppermute | solution.py:638
  214.3 24.0 %copy-start.10 = (bf16[1024,1024]{1,0:T(8,128)(2,1)S(1)}, bf16[1024,1024]{1,0:T(8,128)(2,1)}, u32[]{:S(2)}) copy-start(bf16[1024,1024]{1,0:T(8,128)(2,1)} %constant.28.clone.refs_3_.refs_6_) | copy-start | bytes 6291460
  214.4 24.0 %copy-start.15 = (bf16[4,64,256]{2,1,0:T(8,128)(2,1)S(1)}, bf16[4,64,256]{2,1,0:T(8,128)(2,1)}, u32[]{:S(2)}) copy-start(bf16[4,64,256]{2,1,0:T(8,128)(2,1)} %constant.44.refs_2_.refs_5_) | copy-start | bytes 393220
  217.3 25.5 %collective-permute-start.40 = (bf16[104,1024]{1,0:T(8,128)(2,1)S(1)}, bf16[104,1024]{1,0:T(8,128)(2,1)S(1)}, u32[]{:S(2)}, u32[]{:S(2)}) collective-permute-start(bf16[104,1024]{1,0:T(8,128)(2,1)S(1)} %get-tuple-element.200), channel_id=1, source_target_pairs={{0,8},{8,0},{16,24},{24,16},{1,9},{9,1},{17,25},{25,17},{2,10},{10... | collective-permute-start | bytes 638984 | tf_op jit(solution)/shard_map/ppermute | solution.py:638
  219.1 23.8 %collective-permute-start.41 = (bf16[104,1024]{1,0:T(8,128)(2,1)S(1)}, bf16[104,1024]{1,0:T(8,128)(2,1)S(1)}, u32[]{:S(2)}, u32[]{:S(2)}) collective-permute-start(bf16[104,1024]{1,0:T(8,128)(2,1)S(1)} %get-tuple-element.201), channel_id=1, source_target_pairs={{0,16},{8,24},{16,0},{24,8},{1,17},{9,25},{17,1},{25,9},{2,18},{10... | collective-permute-start | bytes 638984 | tf_op jit(solution)/shard_map/ppermute | solution.py:638
  220.6 25.6 %collective-permute-start.42 = (bf16[104,1024]{1,0:T(8,128)(2,1)S(1)}, bf16[104,1024]{1,0:T(8,128)(2,1)S(1)}, u32[]{:S(2)}, u32[]{:S(2)}) collective-permute-start(bf16[104,1024]{1,0:T(8,128)(2,1)S(1)} %get-tuple-element.202), channel_id=1, source_target_pairs={{0,24},{8,16},{16,8},{24,0},{1,25},{9,17},{17,9},{25,1},{2,26},{10... | collective-permute-start | bytes 638984 | tf_op jit(solution)/shard_map/ppermute | solution.py:638
  238.4 7.8 %copy-start.13 = (bf16[392,416]{1,0:T(8,128)(2,1)S(1)}, bf16[392,416]{1,0:T(8,128)(2,1)}, u32[]{:S(2)}) copy-start(bf16[392,416]{1,0:T(8,128)(2,1)} %constant.46.refs_1_) | copy-start | bytes 978436

commit v5 on v4

--- a/solution.py
+++ b/solution.py
@@ -20,7 +20,7 @@
     SAMPLES * POOL
 )
 SMALL_COST = pl.CostEstimate(flops=10**9, bytes_accessed=1, transcendentals=0)
-LARGE_COST = pl.CostEstimate(flops=4 * 10**10, bytes_accessed=1, transcendentals=0)
+LARGE_COST = pl.CostEstimate(flops=2 * 10**10, bytes_accessed=1, transcendentals=0)
 f32 = jnp.float32
 bf16 = jnp.bfloat16
 FAR = pl.BlockSpec(memory_space=pl.ANY)
@@ -172,7 +172,7 @@
         ).astype(bf16)
 
 
-def crop_block(table, sizes, features, boxes, maps, weight=None, out_type=bf16, earlier=(), kept_in=like):
+def crop_block(table, sizes, features, boxes, maps, weight=None, out_type=bf16, earlier=(), cost=LARGE_COST):
     height, width, part, level_count = sizes
     images = boxes.shape[0]
     product = weight is not None
@@ -185,7 +185,7 @@
         more = [pltpu.VMEM((rows, features), bf16)]
     else:
         out_spec = pl.BlockSpec((LANES, features), lambda n: (n, 0))
-        out_shape = kept_in((rows, features), bf16)
+        out_shape = like((rows, features), bf16)
         more = []
     return pl.pallas_call(
         functools.partial(crop_kernel, table, sizes, product),
@@ -201,7 +201,7 @@
             out_spec,
             pl.BlockSpec((8, LANES), lambda n: (0, 0)),
         ],
-        out_shape=[kept_in((features, rows), bf16), out_shape, SIGN],
+        out_shape=[like((features, rows), bf16), out_shape, SIGN],
         scratch_shapes=[
             pltpu.VMEM((level_count * height, POOL * LANES), bf16),
             pltpu.VMEM((POOL, width, LANES), bf16),
@@ -210,7 +210,7 @@
         ]
         + more,
         compiler_params=pltpu.CompilerParams(vmem_limit_bytes=24 * 2**20),
-        cost_estimate=LARGE_COST,
+        cost_estimate=cost,
         name="crop_block",
     )(*first, *earlier)
 
@@ -254,7 +254,7 @@
     )(boxes, grads, weight, *earlier)
 
 
-def call(kernel, outs, where, arrays, earlier=(), scratch=(), name=None):
+def call(kernel, outs, where, arrays, earlier=(), scratch=(), name=None, cost=LARGE_COST):
     arrays = list(arrays)
 
     def body(*refs):
@@ -270,7 +270,7 @@
         out_shape=[*outs, SIGN],
         scratch_shapes=scratch,
         compiler_params=pltpu.CompilerParams(vmem_limit_bytes=24 * 2**20),
-        cost_estimate=LARGE_COST,
+        cost_estimate=cost,
         name=name,
     )(where, *arrays, *earlier)
 
@@ -429,6 +429,7 @@
         earlier,
         [pltpu.VMEM((count, wide), f32)],
         name="halve_rows",
+        cost=SMALL_COST,
     )
 
 
@@ -842,7 +843,8 @@
     )
 
     ways = (3, 2, 1, 0)
-    crops, signs, came_sums = [], [], []
+    crops = []
+    came_sums = {}
     for turn, way in enumerate(ways):
         if turn == 0:
             crop, turned, sign = crop_block(table, sizes, features, boxes[way], maps)
@@ -856,18 +858,31 @@
             relayed = swap(own, "level", 1)
         else:
             crop, own, sign = crop_block(
-                table, sizes, features, boxes[way], maps, weight, bf16 if way == 1 else f32, signs[-1:]
+                table,
+                sizes,
+                features,
+                boxes[way],
+                maps,
+                weight,
+                bf16 if way == 1 else f32,
+                [sign],
+                SMALL_COST if way == 1 else LARGE_COST,
             )
-        if way == 2 and direct:
-            smalls, sign = pair_up((0, 1), where, smalls, [sign])
-            smalls = smalls.reshape(size, small_rows, units)
-            smalls = [swap(smalls, "img", bit) if bit else smalls for bit in (0, 2, 4, 6)]
+        crops.append(crop)
         if way == 2:
-            own, sign = call(add_kernel, [like(own.shape, bf16)], where, [own, relayed], [sign], name="add")
-        if way in (1, 2):
-            came_sums.append(swap(own, "level", way))
-        crops.append(crop)
-        signs.append(sign)
+            middle = own
+            if direct:
+                smalls, sign = pair_up((0, 1), where, smalls, [sign])
+                smalls = smalls.reshape(size, small_rows, units)
+                smalls = [swap(smalls, "img", bit) if bit else smalls for bit in (0, 2, 4, 6)]
+        if way == 1:
+            came_sums[1] = swap(own, "level", 1)
+            middle, sign = call(
+                add_kernel, [like(middle.shape, bf16)], where, [middle, relayed], [sign], name="add"
+            )
+            came_sums[2] = swap(middle, "level", 2)
+            before = sign
+    came_sums = [came_sums[2], came_sums[1]]
 
     if direct:
         smalls, unused = call(
@@ -875,7 +890,7 @@
             [like((4, size, small_rows, units), bf16)],
             where,
             smalls,
-            signs[2:3],
+            [before],
             name="in_order",
         )
         full_inner, full_heads, sign = call(
@@ -945,14 +960,14 @@
 
         sign = for_other((6,), sign)
         sign = for_other((2, 4), sign)
+        sent, kept, sign = halve_rows((0, 1), 2, count, where, quarters, [sign])
         sign = for_own((6,), sign)
-        sent, kept, sign = halve_rows((0, 1), 2, count, where, quarters, [sign])
         sign = for_own((2, 4), sign)
         sign = for_other((0,), sign)
-        sign = take_up(3, [sign])
         sent, kept, sign = halve_rows(
             (0, 0), 1, count, where, [kept, swap(sent, "level", 2)], [sign]
         )
+        sign = take_up(3, [sign])
         sign = for_own((0,), sign)
         inner_sum, class_sum, delta_sum, bias_total, sign = call(
             small_sum_kernel,
@@ -966,9 +981,7 @@
             [kept, swap(sent, "level", 1)],
             [sign],
             name="small_sum",
-        )
-        half, sign = call(
-            add_kernel, [like(parts[0].shape, f32)], where, [parts[0], parts[6]], [sign], name="add"
+            cost=SMALL_COST,
         )
         *back, sign = call(
             functools.partial(arrange_back_kernel, sizes),
@@ -978,6 +991,10 @@
             [sign],
             name="arrange_back",
         )
+        half, sign = call(
+            add_kernel, [like(parts[0].shape, f32)], where, [parts[0], parts[6]], [sign], name="add", cost=SMALL_COST
+        )
+        back[3] = tie(back[3:], sign)[0]
         *out, sign = call(
             return_span_kernel,
             [like((span, units), bf16)] * size,

time: 253 us -> 242 us (0.957)
  Pallas kernels: 107 us -> 99.8 us
  waiting for transfers between devices: 92.5 us -> 86.3 us
    ppermute x43, waiting for transfers between devices: 92.5 us -> 86.3 us  [swap(): return lax.ppermute(array, axis, [(at, at ^ bit) for at in range(size)])]
    pallas_call x17, Pallas kernels: 28 us -> 25.1 us  [call(): pl.pallas_call(body, in_specs=[SCALAR] + [WHOLE for one in arrays] + [FAR...]
  transfers between devices with their start and end apart: 43 -> 43, of which waited for: 21 -> 20; matrix products, arithmetic and copies ran while one was open for 1% -> 1% of each run, Pallas kernels for 39% -> 38%
where the time goes in v5:
time: 242 us; the launch traced here: 238 us
  Pallas kernels  99.8 us (41%)
  waiting for transfers between devices  86.3 us (36%)
  starting transfers between devices  46.8 us (19%)
  local copies, waits for them, and re-layouts  3.1 us (1%)
    ppermute x43, waiting for transfers between devices, swap(): return lax.ppermute(array, axis, [(at, at ^ bit) for at in range(size)])  86.3 us
    ppermute x43, starting transfers between devices, swap(): return lax.ppermute(array, axis, [(at, at ^ bit) for at in range(size)])  46.8 us
    pallas_call x4, Pallas kernels, spread_block(): pl.pallas_call(functools.partial(spread_kernel, table, sizes), in_specs=[...  28.6 us
    pallas_call x17, Pallas kernels, call(): pl.pallas_call(body, in_specs=[SCALAR] + [WHOLE for one in arrays] + [FAR...  25.1 us
    pallas_call x4, Pallas kernels, crop_block(): pl.pallas_call(functools.partial(crop_kernel, table, sizes, product), gri...  24.4 us
    pallas_call x6, Pallas kernels, piece_product(): pl.pallas_call(functools.partial(product_kernel, bits, len(grads), with_s...  11.1 us
  transfers between devices with their start and end apart: 43, of which 20 were waited for; matrix products, arithmetic and copies ran while one was open for 1% of the time, Pallas kernels for 38%

profile of v5, /device:TPU:8, one launch (start us, length us, event | category | flops | bytes accessed | tf_op | source)
XLA Modules:
  0.0 238.5 jit_solution(6865642766379061551)
XLA Ops:
  2.8 1.2 split_span.1
  4.1 3.0 %collective-permute-start.1 = (bf16[104,1024]{1,0:T(8,128)(2,1)S(1)}, bf16[104,1024]{1,0:T(8,128)(2,1)S(1)}, u32[]{:S(2)}, u32[]{:S(2)}) collective-permute-start(bf16[104,1024]{1,0:T(8,128)(2,1)S(1)} %get-tuple-element.112), channel_id=1, source_target_pairs={{0,16},{8,24},{16,0},{24,8},{1,17},{9,25},{17,1},{25,9},{2,18},{10... | collective-permute-start | bytes 638984 | tf_op jit(solution)/shard_map/ppermute | solution.py:639
  7.7 2.5 %maps.1 = (bf16[128,1024]{1,0:T(8,128)(2,1)S(1)}, bf16[128,1024]{1,0:T(8,128)(2,1)S(1)}, bf16[128,1024]{1,0:T(8,128)(2,1)S(1)}, bf16[128,1024]{1,0:T(8,128)(2,1)S(1)}, f32[8,128]{1,0:T(8,128)}) custom-call(s32[2]{0:T(128)S(1)} %pad_add_fusion.refs_0_.where_ref, bf16[2,1024,256]{2,1,0:T(8,128)(2,1)S(1)} %bitcast.56, bf16[4,64,256]{2,1,0:T(8,128)(2,1)S(1)} %copy-done.16, ...), custom_call_target="tpu_custom_call" | custom-call | flops 20000000000 | bytes 1 | tf_op jit(solution)/shard_map/maps/pallas_call | solution.py:266
  10.2 2.5 %collective-permute-done.refs_3_ = bf16[104,1024]{1,0:T(8,128)(2,1)S(1)} collective-permute-done((bf16[104,1024]{1,0:T(8,128)(2,1)S(1)}, bf16[104,1024]{1,0:T(8,128)(2,1)S(1)}, u32[]{:S(2)}, u32[]{:S(2)}) %collective-permute-start) | collective-permute-done | bytes 213024 | tf_op jit(solution)/shard_map/ppermute | solution.py:639
  12.7 9.2 %collective-permute-done.1.refs_4_ = bf16[104,1024]{1,0:T(8,128)(2,1)S(1)} collective-permute-done((bf16[104,1024]{1,0:T(8,128)(2,1)S(1)}, bf16[104,1024]{1,0:T(8,128)(2,1)S(1)}, u32[]{:S(2)}, u32[]{:S(2)}) %collective-permute-start.1) | collective-permute-done | bytes 213024 | tf_op jit(solution)/shard_map/ppermute | solution.py:639
  22.0 4.1 %collective-permute-done.2.refs_5_ = bf16[104,1024]{1,0:T(8,128)(2,1)S(1)} collective-permute-done((bf16[104,1024]{1,0:T(8,128)(2,1)S(1)}, bf16[104,1024]{1,0:T(8,128)(2,1)S(1)}, u32[]{:S(2)}, u32[]{:S(2)}) %collective-permute-start.2) | collective-permute-done | bytes 213024 | tf_op jit(solution)/shard_map/ppermute | solution.py:639
  26.0 1.3 join_span.2
  27.3 2.5 %collective-permute-start.11 = (bf16[400,1024]{1,0:T(8,128)(2,1)S(1)}, bf16[400,1024]{1,0:T(8,128)(2,1)S(1)}, u32[]{:S(2)}, u32[]{:S(2)}) collective-permute-start(bf16[400,1024]{1,0:T(8,128)(2,1)S(1)} %get-tuple-element.125), channel_id=1, source_target_pairs={{0,6},{1,7},{2,4},{3,5},{4,2},{5,3},{6,0},{7,1},{8,14},{9,15},{10,... | collective-permute-start | bytes 2457608 | tf_op jit(solution)/shard_map/ppermute | solution.py:639
  30.9 3.1 %collective-permute-start.4 = (bf16[128,1024]{1,0:T(8,128)(2,1)S(1)}, bf16[128,1024]{1,0:T(8,128)(2,1)S(1)}, u32[]{:S(2)}, u32[]{:S(2)}) collective-permute-start(bf16[128,1024]{1,0:T(8,128)(2,1)S(1)} %get-tuple-element.120), channel_id=1, source_target_pairs={{0,16},{8,24},{16,0},{24,8},{1,17},{9,25},{17,1},{25,9},{2,18},{10... | collective-permute-start | bytes 786440 | tf_op jit(solution)/shard_map/ppermute | solution.py:639
  34.0 6.1 %collective-permute-done.3.refs_1_.refs_2_ = bf16[128,1024]{1,0:T(8,128)(2,1)S(1)} collective-permute-done((bf16[128,1024]{1,0:T(8,128)(2,1)S(1)}, bf16[128,1024]{1,0:T(8,128)(2,1)S(1)}, u32[]{:S(2)}, u32[]{:S(2)}) %collective-permute-start.3) | collective-permute-done | bytes 262176 | tf_op jit(solution)/shard_map/ppermute | solution.py:639
  40.1 1.6 collective-permute-start.5
  41.7 13.4 %collective-permute-done.5.refs_4_.refs_1_ = bf16[128,1024]{1,0:T(8,128)(2,1)S(1)} collective-permute-done((bf16[128,1024]{1,0:T(8,128)(2,1)S(1)}, bf16[128,1024]{1,0:T(8,128)(2,1)S(1)}, u32[]{:S(2)}, u32[]{:S(2)}) %collective-permute-start.5) | collective-permute-done | bytes 262176 | tf_op jit(solution)/shard_map/ppermute | solution.py:639
  55.1 1.7 arrange.1
  56.8 4.5 %crop_block.4 = (bf16[3200,256]{1,0:T(8,128)(2,1)S(1)}, bf16[256,3200]{1,0:T(8,128)(2,1)S(1)}, f32[8,128]{1,0:T(8,128)S(1)}) custom-call(f32[2,8,128]{2,1,0:T(8,128)S(1)} %get-tuple-element.215.box_ref, bf16[2,1024,256]{2,1,0:T(8,128)(2,1)S(1)} %get-tuple-element.122.maps_ref), custom_call_target="tpu_custom_call" | custom-call | flops 20000000000 | bytes 1 | tf_op jit(solution)/shard_map/crop_block/pallas_call | solution.py:190
  61.9 2.8 %collective-permute-done.9.refs_4_ = bf16[400,1024]{1,0:T(8,128)(2,1)S(1)} collective-permute-done((bf16[400,1024]{1,0:T(8,128)(2,1)S(1)}, bf16[400,1024]{1,0:T(8,128)(2,1)S(1)}, u32[]{:S(2)}, u32[]{:S(2)}) %collective-permute-start.9) | collective-permute-done | bytes 819232 | tf_op jit(solution)/shard_map/ppermute | solution.py:639
  67.0 1.2 collective-permute-done.8.refs_3_
  68.1 1.4 gather_pieces.1.weight_ref.refs_0_
  69.6 2.0 multiply.1
  71.6 1.3 collective-permute-start.13
  72.8 6.3 %crop_block.5 = (bf16[3200,256]{1,0:T(8,128)(2,1)S(1)}, f32[256,1024]{1,0:T(8,128)S(1)}, f32[8,128]{1,0:T(8,128)S(1)}) custom-call(f32[2,8,128]{2,1,0:T(8,128)S(1)} %get-tuple-element.214.box_ref, bf16[2,1024,256]{2,1,0:T(8,128)(2,1)S(1)} %get-tuple-element.122.maps_ref, bf16[3200,1024]{1,0:T(8,128)(2,1)S(1)} %gather_pieces.1.weight_ref.refs_0_, ...), custom_call_target="tpu_custom_call" | custom-call | flops 20000000000 | bytes 1 | tf_op jit(solution)/shard_map/crop_block/pallas_call | solution.py:190
  79.7 2.4 collective-permute-start.20
  83.3 6.3 %crop_block.6 = (bf16[3200,256]{1,0:T(8,128)(2,1)S(1)}, bf16[256,1024]{1,0:T(8,128)(2,1)S(1)}, f32[8,128]{1,0:T(8,128)S(1)}) custom-call(f32[2,8,128]{2,1,0:T(8,128)S(1)} %get-tuple-element.213.box_ref, bf16[2,1024,256]{2,1,0:T(8,128)(2,1)S(1)} %get-tuple-element.122.maps_ref, bf16[3200,1024]{1,0:T(8,128)(2,1)S(1)} %gather_pieces.1.weight_ref.refs_0_, ...), custom_call_target="tpu_custom_call" | custom-call | flops 1000000000 | bytes 1 | tf_op jit(solution)/shard_map/crop_block/pallas_call | solution.py:190
  91.2 2.1 collective-permute-start.16
  93.3 6.6 %collective-permute-done.19.refs_3_ = bf16[4,48,1024]{2,1,0:T(8,128)(2,1)S(1)} collective-permute-done((bf16[4,48,1024]{2,1,0:T(8,128)(2,1)S(1)}, bf16[4,48,1024]{2,1,0:T(8,128)(2,1)S(1)}, u32[]{:S(2)}, u32[]{:S(2)}) %collective-permute-start.19) | collective-permute-done | bytes 393248 | tf_op jit(solution)/shard_map/ppermute | solution.py:639
  101.1 7.3 %crop_block.7 = (bf16[3200,256]{1,0:T(8,128)(2,1)S(1)}, f32[256,1024]{1,0:T(8,128)S(1)}, f32[8,128]{1,0:T(8,128)}) custom-call(f32[2,8,128]{2,1,0:T(8,128)S(1)} %get-tuple-element.216.box_ref, bf16[2,1024,256]{2,1,0:T(8,128)(2,1)S(1)} %get-tuple-element.122.maps_ref, bf16[3200,1024]{1,0:T(8,128)(2,1)S(1)} %gather_pieces.1.weight_ref.refs_0_, ...), custom_call_target="tpu_custom_call" | custom-call | flops 20000000000 | bytes 1 | tf_op jit(solution)/shard_map/crop_block/pallas_call | solution.py:190
  108.4 1.3 full_small.1
  109.7 1.5 collective-permute-done.17.two_ref
  111.2 3.5 %collective-permute-done.16.one_ref = bf16[256,1024]{1,0:T(8,128)(2,1)S(1)} collective-permute-done((bf16[256,1024]{1,0:T(8,128)(2,1)S(1)}, bf16[256,1024]{1,0:T(8,128)(2,1)S(1)}, u32[]{:S(2)}, u32[]{:S(2)}) %collective-permute-start.16) | collective-permute-done | bytes 524320 | tf_op jit(solution)/shard_map/ppermute | solution.py:639
  114.8 3.5 %head_block.1 = (f32[81,2,128]{2,1,0:T(2,128)}, f32[2,320,128]{2,1,0:T(8,128)}, bf16[256,1024]{1,0:T(8,128)(2,1)S(1)}, bf16[256,1024]{1,0:T(8,128)(2,1)S(1)}, bf...) custom-call(f32[256,1024]{1,0:T(8,128)S(1)} %get-tuple-element.135.o, ...), custom_call_target="tpu_custom_call" | custom-call | flops 20000000000 | bytes 1 | tf_op jit(solution)/shard_map/head_block/pallas_call | solution.py:518
  118.3 3.3 %collective-permute-start.24 = (bf16[256,1024]{1,0:T(8,128)(2,1)S(1)}, bf16[256,1024]{1,0:T(8,128)(2,1)S(1)}, u32[]{:S(2)}, u32[]{:S(2)}) collective-permute-start(bf16[256,1024]{1,0:T(8,128)(2,1)S(1)} %get-tuple-element.144.grad_ref.refs_3_), channel_id=1, source_target_pairs={{0,16},{8,24},{16,0},{24,8},{1,17},{9,25},{17,1},{25,9},{2,18},{10... | collective-permute-start | bytes 1572872 | tf_op jit(solution)/shard_map/ppermute | solution.py:639
  121.6 2.5 %small_product.1 = (bf16[528,1536]{1,0:T(8,128)(2,1)S(1)}, bf16[528,1536]{1,0:T(8,128)(2,1)S(1)}, f32[8,128]{1,0:T(8,128)S(1)}) custom-call(s32[2]{0:T(128)S(1)} %pad_add_fusion.refs_0_.where_ref, bf16[256,1024]{1,0:T(8,128)(2,1)S(1)} %get-tuple-element.145.first_ref, bf16[256,1024]{1,0:T(8,128)(2,1)S(1)} %get-tuple-element.146.second_grad_ref, ...), custom_call_target="tpu_custom_call" | custom-call | flops 20000000000 | bytes 1 | tf_op jit(solution)/shard_map/small_product/pallas_call | solution.py:372
  124.3 7.1 %spread_block.4 = (bf16[2,1024,256]{2,1,0:T(8,128)(2,1)S(1)}, f32[8,128]{1,0:T(8,128)S(1)}) custom-call(f32[2,8,128]{2,1,0:T(8,128)S(1)} %get-tuple-element.216.box_ref, bf16[256,1024]{1,0:T(8,128)(2,1)S(1)} %get-tuple-element.144.grad_ref.refs_3_, bf16[3200,1024]{1,0:T(8,128)(2,1)S(1)} %gather_pieces.1.weight_ref.refs_0_, ...), custom_call_target="tpu_custom_call" | custom-call | flops 20000000000 | bytes 1 | tf_op jit(solution)/shard_map/spread_block/pallas_call | solution.py:239
  131.4 1.2 quarter_rows.1
  132.6 1.5 collective-permute-start.26
  134.2 1.5 collective-permute-start.27
  136.2 3.1 %collective-permute-done.24.refs_0_ = bf16[256,1024]{1,0:T(8,128)(2,1)S(1)} collective-permute-done((bf16[256,1024]{1,0:T(8,128)(2,1)S(1)}, bf16[256,1024]{1,0:T(8,128)(2,1)S(1)}, u32[]{:S(2)}, u32[]{:S(2)}) %collective-permute-start.24) | collective-permute-done | bytes 524320 | tf_op jit(solution)/shard_map/ppermute | solution.py:639
  139.3 2.2 collective-permute-start.25
  141.5 7.3 %spread_block.5 = (bf16[2,1024,256]{2,1,0:T(8,128)(2,1)S(1)}, f32[8,128]{1,0:T(8,128)S(1)}) custom-call(f32[2,8,128]{2,1,0:T(8,128)S(1)} %get-tuple-element.213.box_ref, bf16[256,1024]{1,0:T(8,128)(2,1)S(1)} %collective-permute-done.22.grad_ref.refs_2_, bf16[3200,1024]{1,0:T(8,128)(2,1)S(1)} %gather_pieces.1.weight_ref.refs_0_, ...), custom_call_target="tpu_custom_call" | custom-call | flops 20000000000 | bytes 1 | tf_op jit(solution)/shard_map/spread_block/pallas_call | solution.py:239
  148.8 7.1 %spread_block.6 = (bf16[2,1024,256]{2,1,0:T(8,128)(2,1)S(1)}, f32[8,128]{1,0:T(8,128)S(1)}) custom-call(f32[2,8,128]{2,1,0:T(8,128)S(1)} %copy-done.3, bf16[256,1024]{1,0:T(8,128)(2,1)S(1)} %tie.10.grad_ref.refs_1_, bf16[3200,1024]{1,0:T(8,128)(2,1)S(1)} %gather_pieces.1.weight_ref.refs_0_, f32[8,128]{1,0:T(8,128)S(1)} %get-tuple-element.157.refs_0_), custom_call_target="tpu_custom_call" | custom-call | flops 20000000000 | bytes 1 | tf_op jit(solution)/shard_map/spread_block/pallas_call | solution.py:239
  156.0 1.6 piece_product.6
  157.6 2.4 %piece_product.7 = (bf16[2,400,1024]{2,1,0:T(8,128)(2,1)S(1)}, f32[8,128]{1,0:T(8,128)S(1)}) custom-call(s32[2]{0:T(128)S(1)} %pad_add_fusion.refs_0_.where_ref, bf16[256,1024]{1,0:T(8,128)(2,1)S(1)} %collective-permute-done.25.refs_0_.grad_ref, bf16[256,1024]{1,0:T(8,128)(2,1)S(1)} %tie.10.grad_ref.refs_1_, ...), custom_call_target="tpu_custom_call" | custom-call | flops 20000000000 | bytes 1 | tf_op jit(solution)/shard_map/piece_product/pallas_call | solution.py:677
  160.1 1.1 halve_rows.2
  161.2 1.5 collective-permute-start.29
  162.9 1.6 piece_product.8
  164.5 2.4 collective-permute-start.36
  166.9 2.4 %piece_product.9 = (bf16[400,1024]{1,0:T(8,128)(2,1)S(1)}, bf16[400,1024]{1,0:T(8,128)(2,1)S(1)}, f32[8,128]{1,0:T(8,128)S(1)}) custom-call(s32[2]{0:T(128)S(1)} %pad_add_fusion.refs_0_.where_ref, bf16[256,1024]{1,0:T(8,128)(2,1)S(1)} %collective-permute-done.25.refs_0_.grad_ref, bf16[256,1024]{1,0:T(8,128)(2,1)S(1)} %tie.10.grad_ref.refs_1_, ...), custom_call_target="tpu_custom_call" | custom-call | flops 20000000000 | bytes 1 | tf_op jit(solution)/shard_map/piece_product/pallas_call | solution.py:677
  169.3 1.6 piece_product.10
  170.9 3.0 %collective-permute-done.29.refs_2_ = bf16[80,1536]{1,0:T(8,128)(2,1)S(1)} collective-permute-done((bf16[80,1536]{1,0:T(8,128)(2,1)S(1)}, bf16[80,1536]{1,0:T(8,128)(2,1)S(1)}, u32[]{:S(2)}, u32[]{:S(2)}) %collective-permute-start.29) | collective-permute-done | bytes 245792 | tf_op jit(solution)/shard_map/ppermute | solution.py:639
  174.5 2.5 %collective-permute-start.32 = (bf16[48,1536]{1,0:T(8,128)(2,1)S(1)}, bf16[48,1536]{1,0:T(8,128)(2,1)S(1)}, u32[]{:S(2)}, u32[]{:S(2)}) collective-permute-start(bf16[48,1536]{1,0:T(8,128)(2,1)S(1)} %get-tuple-element.181), channel_id=1, source_target_pairs={{0,8},{8,0},{16,24},{24,16},{1,9},{9,1},{17,25},{25,17},{2,10},{10... | collective-permute-start | bytes 442376 | tf_op jit(solution)/shard_map/ppermute | solution.py:639
  177.0 1.5 collective-permute-start.38
  178.5 1.5 collective-permute-start.39
  180.0 7.1 %spread_block.7 = (bf16[2,1024,256]{2,1,0:T(8,128)(2,1)S(1)}, f32[8,128]{1,0:T(8,128)S(1)}) custom-call(f32[2,8,128]{2,1,0:T(8,128)S(1)} %copy-done.1, bf16[256,1024]{1,0:T(8,128)(2,1)S(1)} %collective-permute-done.25.refs_0_.grad_ref, bf16[3200,1024]{1,0:T(8,128)(2,1)S(1)} %gather_pieces.1.weight_ref.refs_0_, f32[8,128]{1,0:T(8,128)S(1)} %get-tuple-element.178.refs_0_), custom_call_target="tpu_custom_call" | custom-call | flops 20000000000 | bytes 1 | tf_op jit(solution)/shard_map/spread_block/pallas_call | solution.py:239
  187.2 1.6 piece_product.11
  188.7 1.2 small_sum.1
  190.0 1.8 arrange_back.1
  192.5 1.4 collective-permute-start.37
  196.5 7.1 %collective-permute-done.38.refs_3_ = bf16[400,1024]{1,0:T(8,128)(2,1)S(1)} collective-permute-done((bf16[400,1024]{1,0:T(8,128)(2,1)S(1)}, bf16[400,1024]{1,0:T(8,128)(2,1)S(1)}, u32[]{:S(2)}, u32[]{:S(2)}) %collective-permute-start.38) | collective-permute-done | bytes 819232 | tf_op jit(solution)/shard_map/ppermute | solution.py:639
  203.6 1.3 return_span.1
  205.5 1.7 collective-permute-start.40
  207.9 1.7 collective-permute-start.42
  209.6 16.5 %collective-permute-done.35.refs_3_ = bf16[2,64,1024]{2,1,0:T(8,128)(2,1)S(1)} collective-permute-done((bf16[2,64,1024]{2,1,0:T(8,128)(2,1)S(1)}, bf16[2,64,1024]{2,1,0:T(8,128)(2,1)S(1)}, u32[]{:S(2)}, u32[]{:S(2)}) %collective-permute-start.35) | collective-permute-done | bytes 262176 | tf_op jit(solution)/shard_map/ppermute | solution.py:639
  226.1 4.5 %maps_back.1 = (f32[2,1024,256]{2,1,0:T(8,128)}, f32[8,128]{1,0:T(8,128)S(1)}) custom-call(s32[2]{0:T(128)S(1)} %pad_add_fusion.refs_0_.where_ref, bf16[2,64,1024]{2,1,0:T(8,128)(2,1)S(1)} %get-tuple-element.186.refs_1_, bf16[2,64,1024]{2,1,0:T(8,128)(2,1)S(1)} %collective-permute-done.34.refs_2_, bf16[2,64,1024]{2,1,0:T(8,128)(2,1)S(1)} %collective-permute-done.35.refs_3_, ...), custom_call_target="tpu_custom_call" | custom-call | flops 20000000000 | bytes 1 | tf_op jit(solution)/shard_map/maps_back/pallas_call | solution.py:266
  230.6 5.2 %collective-permute-done.42.refs_5_ = bf16[104,1024]{1,0:T(8,128)(2,1)S(1)} collective-permute-done((bf16[104,1024]{1,0:T(8,128)(2,1)S(1)}, bf16[104,1024]{1,0:T(8,128)(2,1)S(1)}, u32[]{:S(2)}, u32[]{:S(2)}) %collective-permute-start.42) | collective-permute-done | bytes 213024 | tf_op jit(solution)/shard_map/ppermute | solution.py:639
  235.9 2.4 %join_span.3 = (f32[392,1024]{1,0:T(8,128)}, f32[8,128]{1,0:T(8,128)}) custom-call(s32[2]{0:T(128)S(1)} %pad_add_fusion.refs_0_.where_ref, bf16[392,416]{1,0:T(8,128)(2,1)S(1)} %copy-done.15, bf16[104,1024]{1,0:T(8,128)(2,1)S(1)} %get-tuple-element.199.refs_2_, bf16[104,1024]{1,0:T(8,128)(2,1)S(1)} %collective-permute-done.40.refs_3_, ...), custom_call_target="tpu_custom_call" | custom-call | flops 20000000000 | bytes 1 | tf_op jit(solution)/shard_map/join_span/pallas_call | solution.py:266
  (133 shorter events, 17.7 us)
Async XLA Ops:
  2.7 4.9 %copy-start.19 = (bf16[32,320]{1,0:T(8,128)(2,1)S(1)}, bf16[32,320]{1,0:T(8,128)(2,1)}, u32[]{:S(2)}) copy-start(bf16[32,320]{1,0:T(8,128)(2,1)} %param.30) | copy-start | bytes 61444
  2.7 4.9 %copy-start.20 = (bf16[32,81]{1,0:T(8,128)(2,1)S(1)}, bf16[32,81]{1,0:T(8,128)(2,1)}, u32[]{:S(2)}) copy-start(bf16[32,81]{1,0:T(8,128)(2,1)} %param.28) | copy-start | bytes 15556
  2.7 4.9 %copy-start.21 = (f32[320]{0:T(512)S(1)}, f32[320]{0:T(512)}, u32[]{:S(2)}) copy-start(f32[320]{0:T(512)} %param.31) | copy-start | bytes 3844
  2.7 4.9 %copy-start.22 = (f32[81]{0:T(128)S(1)}, f32[81]{0:T(128)}, u32[]{:S(2)}) copy-start(f32[81]{0:T(128)} %param.29) | copy-start | bytes 976
  2.7 4.9 %copy-start.4 = (bf16[1,2,64,16,256]{4,3,2,1,0:T(8,128)(2,1)S(1)}, bf16[1,2,64,16,256]{4,3,2,1,0:T(8,128)(2,1)}, u32[]{:S(2)}) copy-start(bf16[1,2,64,16,256]{4,3,2,1,0:T(8,128)(2,1)} %param.18) | copy-start | bytes 3145732
  2.8 4.9 %copy-start.11 = (bf16[1024,1024]{1,0:T(8,128)(2,1)S(1)}, bf16[1024,1024]{1,0:T(8,128)(2,1)}, u32[]{:S(2)}) copy-start(bf16[1024,1024]{1,0:T(8,128)(2,1)} %constant.28.clone.refs_3_.refs_6_) | copy-start | bytes 6291460
  2.8 4.9 %copy-start.16 = (bf16[4,64,256]{2,1,0:T(8,128)(2,1)S(1)}, bf16[4,64,256]{2,1,0:T(8,128)(2,1)}, u32[]{:S(2)}) copy-start(bf16[4,64,256]{2,1,0:T(8,128)(2,1)} %constant.44.refs_2_.refs_5_) | copy-start | bytes 393220
  4.0 8.7 %collective-permute-start = (bf16[104,1024]{1,0:T(8,128)(2,1)S(1)}, bf16[104,1024]{1,0:T(8,128)(2,1)S(1)}, u32[]{:S(2)}, u32[]{:S(2)}) collective-permute-start(bf16[104,1024]{1,0:T(8,128)(2,1)S(1)} %get-tuple-element.111), channel_id=1, source_target_pairs={{0,8},{8,0},{16,24},{24,16},{1,9},{9,1},{17,25},{25,17},{2,10},{10... | collective-permute-start | bytes 638984 | tf_op jit(solution)/shard_map/ppermute | solution.py:639
  4.1 17.9 %collective-permute-start.1 = (bf16[104,1024]{1,0:T(8,128)(2,1)S(1)}, bf16[104,1024]{1,0:T(8,128)(2,1)S(1)}, u32[]{:S(2)}, u32[]{:S(2)}) collective-permute-start(bf16[104,1024]{1,0:T(8,128)(2,1)S(1)} %get-tuple-element.112), channel_id=1, source_target_pairs={{0,16},{8,24},{16,0},{24,8},{1,17},{9,25},{17,1},{25,9},{2,18},{10... | collective-permute-start | bytes 638984 | tf_op jit(solution)/shard_map/ppermute | solution.py:639
  7.1 18.9 %collective-permute-start.2 = (bf16[104,1024]{1,0:T(8,128)(2,1)S(1)}, bf16[104,1024]{1,0:T(8,128)(2,1)S(1)}, u32[]{:S(2)}, u32[]{:S(2)}) collective-permute-start(bf16[104,1024]{1,0:T(8,128)(2,1)S(1)} %get-tuple-element.113), channel_id=1, source_target_pairs={{0,24},{8,16},{16,8},{24,0},{1,25},{9,17},{17,9},{25,1},{2,26},{10... | collective-permute-start | bytes 638984 | tf_op jit(solution)/shard_map/ppermute | solution.py:639
  7.7 18.3 %copy-start.14 = (bf16[400,416]{1,0:T(8,128)(2,1)S(1)}, bf16[400,416]{1,0:T(8,128)(2,1)}, u32[]{:S(2)}) copy-start(bf16[400,416]{1,0:T(8,128)(2,1)} %constant.26.clone.refs_1_) | copy-start | bytes 998404
  27.3 34.1 %collective-permute-start.11 = (bf16[400,1024]{1,0:T(8,128)(2,1)S(1)}, bf16[400,1024]{1,0:T(8,128)(2,1)S(1)}, u32[]{:S(2)}, u32[]{:S(2)}) collective-permute-start(bf16[400,1024]{1,0:T(8,128)(2,1)S(1)} %get-tuple-element.125), channel_id=1, source_target_pairs={{0,6},{1,7},{2,4},{3,5},{4,2},{5,3},{6,0},{7,1},{8,14},{9,15},{10,... | collective-permute-start | bytes 2457608 | tf_op jit(solution)/shard_map/ppermute | solution.py:639
  29.8 34.9 %collective-permute-start.9 = (bf16[400,1024]{1,0:T(8,128)(2,1)S(1)}, bf16[400,1024]{1,0:T(8,128)(2,1)S(1)}, u32[]{:S(2)}, u32[]{:S(2)}) collective-permute-start(bf16[400,1024]{1,0:T(8,128)(2,1)S(1)} %get-tuple-element.125), channel_id=1, source_target_pairs={{0,4},{1,5},{2,6},{3,7},{4,0},{5,1},{6,2},{7,3},{8,12},{9,13},{10,... | collective-permute-start | bytes 2457608 | tf_op jit(solution)/shard_map/ppermute | solution.py:639
  30.3 34.4 %collective-permute-start.7 = (bf16[400,1024]{1,0:T(8,128)(2,1)S(1)}, bf16[400,1024]{1,0:T(8,128)(2,1)S(1)}, u32[]{:S(2)}, u32[]{:S(2)}) collective-permute-start(bf16[400,1024]{1,0:T(8,128)(2,1)S(1)} %get-tuple-element.125), channel_id=1, source_target_pairs={{0,2},{1,3},{2,0},{3,1},{4,6},{5,7},{6,4},{7,5},{8,10},{9,11},{10,... | collective-permute-start | bytes 2457608 | tf_op jit(solution)/shard_map/ppermute | solution.py:639
  30.8 9.2 %collective-permute-start.3 = (bf16[128,1024]{1,0:T(8,128)(2,1)S(1)}, bf16[128,1024]{1,0:T(8,128)(2,1)S(1)}, u32[]{:S(2)}, u32[]{:S(2)}) collective-permute-start(bf16[128,1024]{1,0:T(8,128)(2,1)S(1)} %get-tuple-element.119), channel_id=1, source_target_pairs={{0,8},{8,0},{16,24},{24,16},{1,9},{9,1},{17,25},{25,17},{2,10},{10... | collective-permute-start | bytes 786440 | tf_op jit(solution)/shard_map/ppermute | solution.py:639
  30.9 24.2 %collective-permute-start.4 = (bf16[128,1024]{1,0:T(8,128)(2,1)S(1)}, bf16[128,1024]{1,0:T(8,128)(2,1)S(1)}, u32[]{:S(2)}, u32[]{:S(2)}) collective-permute-start(bf16[128,1024]{1,0:T(8,128)(2,1)S(1)} %get-tuple-element.120), channel_id=1, source_target_pairs={{0,16},{8,24},{16,0},{24,8},{1,17},{9,25},{17,1},{25,9},{2,18},{10... | collective-permute-start | bytes 786440 | tf_op jit(solution)/shard_map/ppermute | solution.py:639
  40.1 15.0 %collective-permute-start.5 = (bf16[128,1024]{1,0:T(8,128)(2,1)S(1)}, bf16[128,1024]{1,0:T(8,128)(2,1)S(1)}, u32[]{:S(2)}, u32[]{:S(2)}) collective-permute-start(bf16[128,1024]{1,0:T(8,128)(2,1)S(1)} %tie.7), channel_id=1, source_target_pairs={{0,24},{8,16},{16,8},{24,0},{1,25},{9,17},{17,9},{25,1},{2,26},{10... | collective-permute-start | bytes 786440 | tf_op jit(solution)/shard_map/ppermute | solution.py:639
  41.7 15.1 %copy-start = (f32[2,8,128]{2,1,0:T(8,128)}, f32[2,8,128]{2,1,0:T(8,128)S(1)}, u32[]{:S(2)}) copy-start(f32[2,8,128]{2,1,0:T(8,128)S(1)} %get-tuple-element.215.box_ref) | copy-start | bytes 24580
  41.7 31.1 %copy-start.2 = (f32[2,8,128]{2,1,0:T(8,128)}, f32[2,8,128]{2,1,0:T(8,128)S(1)}, u32[]{:S(2)}) copy-start(f32[2,8,128]{2,1,0:T(8,128)S(1)} %get-tuple-element.214.box_ref) | copy-start | bytes 24580
  55.1 10.0 %collective-permute-start.14 = (bf16[48,1024]{1,0:T(8,128)(2,1)S(1)}, bf16[48,1024]{1,0:T(8,128)(2,1)S(1)}, u32[]{:S(2)}, u32[]{:S(2)}) collective-permute-start(bf16[48,1024]{1,0:T(8,128)(2,1)S(1)} %tie.9.refs_1_), channel_id=1, source_target_pairs={{0,8},{8,0},{16,24},{24,16},{1,9},{9,1},{17,25},{25,17},{2,10},{10... | collective-permute-start | bytes 294920 | tf_op jit(solution)/shard_map/ppermute | solution.py:639
  61.3 5.3 %collective-permute-start.6 = (bf16[400,1024]{1,0:T(8,128)(2,1)S(1)}, bf16[400,1024]{1,0:T(8,128)(2,1)S(1)}, u32[]{:S(2)}, u32[]{:S(2)}) collective-permute-start(bf16[400,1024]{1,0:T(8,128)(2,1)S(1)} %tie.8.refs_0_), channel_id=1, source_target_pairs={{0,1},{1,0},{2,3},{3,2},{4,5},{5,4},{6,7},{7,6},{8,9},{9,8},{10,11... | collective-permute-start | bytes 2457608 | tf_op jit(solution)/shard_map/ppermute | solution.py:639
  61.4 5.2 %collective-permute-start.12 = (bf16[400,1024]{1,0:T(8,128)(2,1)S(1)}, bf16[400,1024]{1,0:T(8,128)(2,1)S(1)}, u32[]{:S(2)}, u32[]{:S(2)}) collective-permute-start(bf16[400,1024]{1,0:T(8,128)(2,1)S(1)} %collective-permute-done.11.refs_6_), channel_id=1, source_target_pairs={{0,1},{1,0},{2,3},{3,2},{4,5},{5,4},{6,7},{7,6},{8,9},{9,8},{10,11... | collective-permute-start | bytes 2457608 | tf_op jit(solution)/shard_map/ppermute | solution.py:639
  64.6 2.3 collective-permute-start.10
  64.7 3.4 %collective-permute-start.8 = (bf16[400,1024]{1,0:T(8,128)(2,1)S(1)}, bf16[400,1024]{1,0:T(8,128)(2,1)S(1)}, u32[]{:S(2)}, u32[]{:S(2)}) collective-permute-start(bf16[400,1024]{1,0:T(8,128)(2,1)S(1)} %collective-permute-done.7.refs_2_), channel_id=1, source_target_pairs={{0,1},{1,0},{2,3},{3,2},{4,5},{5,4},{6,7},{7,6},{8,9},{9,8},{10,11... | collective-permute-start | bytes 2457608 | tf_op jit(solution)/shard_map/ppermute | solution.py:639
  66.3 12.8 %collective-permute-start.15 = (bf16[2,48,1024]{2,1,0:T(8,128)(2,1)S(1)}, bf16[2,48,1024]{2,1,0:T(8,128)(2,1)S(1)}, u32[]{:S(2)}, u32[]{:S(2)}) collective-permute-start(bf16[2,48,1024]{2,1,0:T(8,128)(2,1)S(1)} %get-tuple-element.130.refs_1_), channel_id=1, source_target_pairs={{0,16},{8,24},{16,0},{24,8},{1,17},{9,25},{17,1},{25,9},{2,18},{10... | collective-permute-start | bytes 589832 | tf_op jit(solution)/shard_map/ppermute | solution.py:639
  71.6 18.9 %collective-permute-start.13 = (bf16[256,1024]{1,0:T(8,128)(2,1)S(1)}, bf16[256,1024]{1,0:T(8,128)(2,1)S(1)}, u32[]{:S(2)}, u32[]{:S(2)}) collective-permute-start(bf16[256,1024]{1,0:T(8,128)(2,1)S(1)} %get-tuple-element.129), channel_id=1, source_target_pairs={{0,8},{8,0},{16,24},{24,16},{1,9},{9,1},{17,25},{25,17},{2,10},{10... | collective-permute-start | bytes 1572872 | tf_op jit(solution)/shard_map/ppermute | solution.py:639
  79.7 13.6 %collective-permute-start.20 = (bf16[4,48,1024]{2,1,0:T(8,128)(2,1)S(1)}, bf16[4,48,1024]{2,1,0:T(8,128)(2,1)S(1)}, u32[]{:S(2)}, u32[]{:S(2)}) collective-permute-start(bf16[4,48,1024]{2,1,0:T(8,128)(2,1)S(1)} %bitcast.57), channel_id=1, source_target_pairs={{0,6},{1,7},{2,4},{3,5},{4,2},{5,3},{6,0},{7,1},{8,14},{9,15},{10,... | collective-permute-start | bytes 1179656 | tf_op jit(solution)/shard_map/ppermute | solution.py:639
  82.1 17.8 %collective-permute-start.19 = (bf16[4,48,1024]{2,1,0:T(8,128)(2,1)S(1)}, bf16[4,48,1024]{2,1,0:T(8,128)(2,1)S(1)}, u32[]{:S(2)}, u32[]{:S(2)}) collective-permute-start(bf16[4,48,1024]{2,1,0:T(8,128)(2,1)S(1)} %bitcast.58), channel_id=1, source_target_pairs={{0,4},{1,5},{2,6},{3,7},{4,0},{5,1},{6,2},{7,3},{8,12},{9,13},{10,... | collective-permute-start | bytes 1179656 | tf_op jit(solution)/shard_map/ppermute | solution.py:639
  82.7 17.2 %collective-permute-start.18 = (bf16[4,48,1024]{2,1,0:T(8,128)(2,1)S(1)}, bf16[4,48,1024]{2,1,0:T(8,128)(2,1)S(1)}, u32[]{:S(2)}, u32[]{:S(2)}) collective-permute-start(bf16[4,48,1024]{2,1,0:T(8,128)(2,1)S(1)} %bitcast.59), channel_id=1, source_target_pairs={{0,2},{1,3},{2,0},{3,1},{4,6},{5,7},{6,4},{7,5},{8,10},{9,11},{10,... | collective-permute-start | bytes 1179656 | tf_op jit(solution)/shard_map/ppermute | solution.py:639
  89.6 21.6 %collective-permute-start.17 = (bf16[256,1024]{1,0:T(8,128)(2,1)S(1)}, bf16[256,1024]{1,0:T(8,128)(2,1)S(1)}, u32[]{:S(2)}, u32[]{:S(2)}) collective-permute-start(bf16[256,1024]{1,0:T(8,128)(2,1)S(1)} %get-tuple-element.137), channel_id=1, source_target_pairs={{0,8},{8,0},{16,24},{24,16},{1,9},{9,1},{17,25},{25,17},{2,10},{10... | collective-permute-start | bytes 1572872 | tf_op jit(solution)/shard_map/ppermute | solution.py:639
  91.2 23.6 %collective-permute-start.16 = (bf16[256,1024]{1,0:T(8,128)(2,1)S(1)}, bf16[256,1024]{1,0:T(8,128)(2,1)S(1)}, u32[]{:S(2)}, u32[]{:S(2)}) collective-permute-start(bf16[256,1024]{1,0:T(8,128)(2,1)S(1)} %get-tuple-element.136), channel_id=1, source_target_pairs={{0,16},{8,24},{16,0},{24,8},{1,17},{9,25},{17,1},{25,9},{2,18},{10... | collective-permute-start | bytes 1572872 | tf_op jit(solution)/shard_map/ppermute | solution.py:639
  101.1 7.3 %collective-permute-start.21 = (bf16[4,4,48,1024]{3,2,1,0:T(8,128)(2,1)S(1)}, bf16[4,4,48,1024]{3,2,1,0:T(8,128)(2,1)S(1)}, u32[]{:S(2)}, u32[]{:S(2)}) collective-permute-start(bf16[4,4,48,1024]{3,2,1,0:T(8,128)(2,1)S(1)} %get-tuple-element.139.refs_1_), channel_id=1, source_target_pairs={{0,1},{1,0},{2,3},{3,2},{4,5},{5,4},{6,7},{7,6},{8,9},{9,8},{10,11... | collective-permute-start | bytes 4718600 | tf_op jit(solution)/shard_map/ppermute | solution.py:639
  108.4 6.3 %copy-start.6 = (f32[2,128,4]{1,2,0:T(4,128)S(1)}, f32[2,128,4]{1,2,0:T(4,128)}, u32[]{:S(2)}) copy-start(f32[2,128,4]{1,2,0:T(4,128)} %param.23) | copy-start | bytes 12292
  108.4 6.3 %copy-start.7 = (f32[1024]{0:T(1024)S(1)}, f32[1024]{0:T(1024)}, u32[]{:S(2)}) copy-start(f32[1024]{0:T(1024)} %param.25) | copy-start | bytes 12292
  108.4 6.3 %copy-start.8 = (f32[1024]{0:T(1024)S(1)}, f32[1024]{0:T(1024)}, u32[]{:S(2)}) copy-start(f32[1024]{0:T(1024)} %param.27) | copy-start | bytes 12292
  108.4 6.3 %copy-start.9 = (s32[2,128]{1,0:T(2,128)S(1)}, s32[2,128]{1,0:T(2,128)}, u32[]{:S(2)}) copy-start(s32[2,128]{1,0:T(2,128)} %labels_ref.1) | copy-start | bytes 3076
  108.4 6.3 %copy-start.10 = (s32[2,128]{1,0:T(2,128)S(1)}, s32[2,128]{1,0:T(2,128)}, u32[]{:S(2)}) copy-start(s32[2,128]{1,0:T(2,128)} %ignore_ref.1) | copy-start | bytes 3076
  118.3 21.0 %collective-permute-start.24 = (bf16[256,1024]{1,0:T(8,128)(2,1)S(1)}, bf16[256,1024]{1,0:T(8,128)(2,1)S(1)}, u32[]{:S(2)}, u32[]{:S(2)}) collective-permute-start(bf16[256,1024]{1,0:T(8,128)(2,1)S(1)} %get-tuple-element.144.grad_ref.refs_3_), channel_id=1, source_target_pairs={{0,16},{8,24},{16,0},{24,8},{1,17},{9,25},{17,1},{25,9},{2,18},{10... | collective-permute-start | bytes 1572872 | tf_op jit(solution)/shard_map/ppermute | solution.py:639
  121.6 19.9 %collective-permute-start.22 = (bf16[256,1024]{1,0:T(8,128)(2,1)S(1)}, bf16[256,1024]{1,0:T(8,128)(2,1)S(1)}, u32[]{:S(2)}, u32[]{:S(2)}) collective-permute-start(bf16[256,1024]{1,0:T(8,128)(2,1)S(1)} %get-tuple-element.144.grad_ref.refs_3_), channel_id=1, source_target_pairs={{0,8},{8,0},{16,24},{24,16},{1,9},{9,1},{17,25},{25,17},{2,10},{10... | collective-permute-start | bytes 1572872 | tf_op jit(solution)/shard_map/ppermute | solution.py:639
  124.2 7.2 %collective-permute-start.23 = (bf16[528,1536]{1,0:T(8,128)(2,1)S(1)}, bf16[528,1536]{1,0:T(8,128)(2,1)S(1)}, u32[]{:S(2)}, u32[]{:S(2)}) collective-permute-start(bf16[528,1536]{1,0:T(8,128)(2,1)S(1)} %get-tuple-element.153), channel_id=1, source_target_pairs={{0,1},{1,0},{2,3},{3,2},{4,5},{5,4},{6,7},{7,6},{8,9},{9,8},{10,11... | collective-permute-start | bytes 4866056 | tf_op jit(solution)/shard_map/ppermute | solution.py:639
  132.6 27.4 %collective-permute-start.26 = (bf16[144,1536]{1,0:T(8,128)(2,1)S(1)}, bf16[144,1536]{1,0:T(8,128)(2,1)S(1)}, u32[]{:S(2)}, u32[]{:S(2)}) collective-permute-start(bf16[144,1536]{1,0:T(8,128)(2,1)S(1)} %get-tuple-element.160), channel_id=1, source_target_pairs={{0,2},{1,3},{2,0},{3,1},{4,6},{5,7},{6,4},{7,5},{8,10},{9,11},{10,... | collective-permute-start | bytes 1327112 | tf_op jit(solution)/shard_map/ppermute | solution.py:639
  134.2 25.9 %collective-permute-start.27 = (bf16[144,1536]{1,0:T(8,128)(2,1)S(1)}, bf16[144,1536]{1,0:T(8,128)(2,1)S(1)}, u32[]{:S(2)}, u32[]{:S(2)}) collective-permute-start(bf16[144,1536]{1,0:T(8,128)(2,1)S(1)} %get-tuple-element.161), channel_id=1, source_target_pairs={{0,4},{1,5},{2,6},{3,7},{4,0},{5,1},{6,2},{7,3},{8,12},{9,13},{10,... | collective-permute-start | bytes 1327112 | tf_op jit(solution)/shard_map/ppermute | solution.py:639
  135.7 24.4 %collective-permute-start.28 = (bf16[144,1536]{1,0:T(8,128)(2,1)S(1)}, bf16[144,1536]{1,0:T(8,128)(2,1)S(1)}, u32[]{:S(2)}, u32[]{:S(2)}) collective-permute-start(bf16[144,1536]{1,0:T(8,128)(2,1)S(1)} %get-tuple-element.162), channel_id=1, source_target_pairs={{0,6},{1,7},{2,4},{3,5},{4,2},{5,3},{6,0},{7,1},{8,14},{9,15},{10,... | collective-permute-start | bytes 1327112 | tf_op jit(solution)/shard_map/ppermute | solution.py:639
  139.3 9.6 %copy-start.3 = (f32[2,8,128]{2,1,0:T(8,128)S(1)}, f32[2,8,128]{2,1,0:T(8,128)}, u32[]{:S(2)}) copy-start(f32[2,8,128]{2,1,0:T(8,128)} %copy-done.2) | copy-start | bytes 24580
  139.3 16.7 %collective-permute-start.25 = (bf16[256,1024]{1,0:T(8,128)(2,1)S(1)}, bf16[256,1024]{1,0:T(8,128)(2,1)S(1)}, u32[]{:S(2)}, u32[]{:S(2)}) collective-permute-start(bf16[256,1024]{1,0:T(8,128)(2,1)S(1)} %tie.10.grad_ref.refs_1_), channel_id=1, source_target_pairs={{0,8},{8,0},{16,24},{24,16},{1,9},{9,1},{17,25},{25,17},{2,10},{10... | collective-permute-start | bytes 1572872 | tf_op jit(solution)/shard_map/ppermute | solution.py:639
  157.5 5.4 %collective-permute-start.31 = (bf16[1,400,1024]{2,1,0:T(8,128)(2,1)S(1)}, bf16[1,400,1024]{2,1,0:T(8,128)(2,1)S(1)}, u32[]{:S(2)}, u32[]{:S(2)}) collective-permute-start(bf16[1,400,1024]{2,1,0:T(8,128)(2,1)S(1)} %get-tuple-element.173), channel_id=1, source_target_pairs={{0,1},{1,0},{2,3},{3,2},{4,5},{5,4},{6,7},{7,6},{8,9},{9,8},{10,11... | collective-permute-start | bytes 2457608 | tf_op jit(solution)/shard_map/ppermute | solution.py:639
  161.2 12.7 %collective-permute-start.29 = (bf16[80,1536]{1,0:T(8,128)(2,1)S(1)}, bf16[80,1536]{1,0:T(8,128)(2,1)S(1)}, u32[]{:S(2)}, u32[]{:S(2)}) collective-permute-start(bf16[80,1536]{1,0:T(8,128)(2,1)S(1)} %get-tuple-element.171), channel_id=1, source_target_pairs={{0,16},{8,24},{16,0},{24,8},{1,17},{9,25},{17,1},{25,9},{2,18},{10... | collective-permute-start | bytes 737288 | tf_op jit(solution)/shard_map/ppermute | solution.py:639
  162.7 4.1 %collective-permute-start.30 = (bf16[2,400,1024]{2,1,0:T(8,128)(2,1)S(1)}, bf16[2,400,1024]{2,1,0:T(8,128)(2,1)S(1)}, u32[]{:S(2)}, u32[]{:S(2)}) collective-permute-start(bf16[2,400,1024]{2,1,0:T(8,128)(2,1)S(1)} %get-tuple-element.172), channel_id=1, source_target_pairs={{0,1},{1,0},{2,3},{3,2},{4,5},{5,4},{6,7},{7,6},{8,9},{9,8},{10,11... | collective-permute-start | bytes 4915208 | tf_op jit(solution)/shard_map/ppermute | solution.py:639
  164.5 27.2 %collective-permute-start.36 = (bf16[400,1024]{1,0:T(8,128)(2,1)S(1)}, bf16[400,1024]{1,0:T(8,128)(2,1)S(1)}, u32[]{:S(2)}, u32[]{:S(2)}) collective-permute-start(bf16[400,1024]{1,0:T(8,128)(2,1)S(1)} %get-tuple-element.191), channel_id=1, source_target_pairs={{0,6},{1,7},{2,4},{3,5},{4,2},{5,3},{6,0},{7,1},{8,14},{9,15},{10,... | collective-permute-start | bytes 2457608 | tf_op jit(solution)/shard_map/ppermute | solution.py:639
  173.9 6.2 %copy-start.1 = (f32[2,8,128]{2,1,0:T(8,128)S(1)}, f32[2,8,128]{2,1,0:T(8,128)}, u32[]{:S(2)}) copy-start(f32[2,8,128]{2,1,0:T(8,128)} %copy-done) | copy-start | bytes 24580
  174.5 14.2 %collective-permute-start.32 = (bf16[48,1536]{1,0:T(8,128)(2,1)S(1)}, bf16[48,1536]{1,0:T(8,128)(2,1)S(1)}, u32[]{:S(2)}, u32[]{:S(2)}) collective-permute-start(bf16[48,1536]{1,0:T(8,128)(2,1)S(1)} %get-tuple-element.181), channel_id=1, source_target_pairs={{0,8},{8,0},{16,24},{24,16},{1,9},{9,1},{17,25},{25,17},{2,10},{10... | collective-permute-start | bytes 442376 | tf_op jit(solution)/shard_map/ppermute | solution.py:639
  177.0 10.1 %collective-permute-start.33 = (bf16[1,400,1024]{2,1,0:T(8,128)(2,1)S(1)}, bf16[1,400,1024]{2,1,0:T(8,128)(2,1)S(1)}, u32[]{:S(2)}, u32[]{:S(2)}) collective-permute-start(bf16[1,400,1024]{2,1,0:T(8,128)(2,1)S(1)} %get-tuple-element.182), channel_id=1, source_target_pairs={{0,1},{1,0},{2,3},{3,2},{4,5},{5,4},{6,7},{7,6},{8,9},{9,8},{10,11... | collective-permute-start | bytes 2457608 | tf_op jit(solution)/shard_map/ppermute | solution.py:639
  177.0 26.5 %collective-permute-start.38 = (bf16[400,1024]{1,0:T(8,128)(2,1)S(1)}, bf16[400,1024]{1,0:T(8,128)(2,1)S(1)}, u32[]{:S(2)}, u32[]{:S(2)}) collective-permute-start(bf16[400,1024]{1,0:T(8,128)(2,1)S(1)} %get-tuple-element.195), channel_id=1, source_target_pairs={{0,2},{1,3},{2,0},{3,1},{4,6},{5,7},{6,4},{7,5},{8,10},{9,11},{10,... | collective-permute-start | bytes 2457608 | tf_op jit(solution)/shard_map/ppermute | solution.py:639
  178.5 25.1 %collective-permute-start.39 = (bf16[400,1024]{1,0:T(8,128)(2,1)S(1)}, bf16[400,1024]{1,0:T(8,128)(2,1)S(1)}, u32[]{:S(2)}, u32[]{:S(2)}) collective-permute-start(bf16[400,1024]{1,0:T(8,128)(2,1)S(1)} %get-tuple-element.196), channel_id=1, source_target_pairs={{0,4},{1,5},{2,6},{3,7},{4,0},{5,1},{6,2},{7,3},{8,12},{9,13},{10,... | collective-permute-start | bytes 2457608 | tf_op jit(solution)/shard_map/ppermute | solution.py:639
  192.4 11.2 %copy-start.13 = (bf16[416,400]{1,0:T(8,128)(2,1)S(1)}, bf16[416,400]{1,0:T(8,128)(2,1)}, u32[]{:S(2)}) copy-start(bf16[416,400]{1,0:T(8,128)(2,1)} %constant.45.refs_1_) | copy-start | bytes 998404
  192.5 15.5 %collective-permute-start.37 = (bf16[2,64,1024]{2,1,0:T(8,128)(2,1)S(1)}, bf16[2,64,1024]{2,1,0:T(8,128)(2,1)S(1)}, u32[]{:S(2)}, u32[]{:S(2)}) collective-permute-start(bf16[2,64,1024]{2,1,0:T(8,128)(2,1)S(1)} %tie.11), channel_id=1, source_target_pairs={{0,24},{8,16},{16,8},{24,0},{1,25},{9,17},{17,9},{25,1},{2,26},{10... | collective-permute-start | bytes 786440 | tf_op jit(solution)/shard_map/ppermute | solution.py:639
  193.9 15.7 %collective-permute-start.34 = (bf16[2,64,1024]{2,1,0:T(8,128)(2,1)S(1)}, bf16[2,64,1024]{2,1,0:T(8,128)(2,1)S(1)}, u32[]{:S(2)}, u32[]{:S(2)}) collective-permute-start(bf16[2,64,1024]{2,1,0:T(8,128)(2,1)S(1)} %get-tuple-element.187), channel_id=1, source_target_pairs={{0,8},{8,0},{16,24},{24,16},{1,9},{9,1},{17,25},{25,17},{2,10},{10... | collective-permute-start | bytes 786440 | tf_op jit(solution)/shard_map/ppermute | solution.py:639
  194.9 31.1 %collective-permute-start.35 = (bf16[2,64,1024]{2,1,0:T(8,128)(2,1)S(1)}, bf16[2,64,1024]{2,1,0:T(8,128)(2,1)S(1)}, u32[]{:S(2)}, u32[]{:S(2)}) collective-permute-start(bf16[2,64,1024]{2,1,0:T(8,128)(2,1)S(1)} %get-tuple-element.188), channel_id=1, source_target_pairs={{0,16},{8,24},{16,0},{24,8},{1,17},{9,25},{17,1},{25,9},{2,18},{10... | collective-permute-start | bytes 786440 | tf_op jit(solution)/shard_map/ppermute | solution.py:639
  203.6 22.5 %copy-start.12 = (bf16[1024,1024]{1,0:T(8,128)(2,1)S(1)}, bf16[1024,1024]{1,0:T(8,128)(2,1)}, u32[]{:S(2)}) copy-start(bf16[1024,1024]{1,0:T(8,128)(2,1)} %constant.28.clone.refs_3_.refs_6_) | copy-start | bytes 6291460
  203.6 22.5 %copy-start.17 = (bf16[4,64,256]{2,1,0:T(8,128)(2,1)S(1)}, bf16[4,64,256]{2,1,0:T(8,128)(2,1)}, u32[]{:S(2)}) copy-start(bf16[4,64,256]{2,1,0:T(8,128)(2,1)} %constant.44.refs_2_.refs_5_) | copy-start | bytes 393220
  205.5 25.0 %collective-permute-start.40 = (bf16[104,1024]{1,0:T(8,128)(2,1)S(1)}, bf16[104,1024]{1,0:T(8,128)(2,1)S(1)}, u32[]{:S(2)}, u32[]{:S(2)}) collective-permute-start(bf16[104,1024]{1,0:T(8,128)(2,1)S(1)} %get-tuple-element.200), channel_id=1, source_target_pairs={{0,8},{8,0},{16,24},{24,16},{1,9},{9,1},{17,25},{25,17},{2,10},{10... | collective-permute-start | bytes 638984 | tf_op jit(solution)/shard_map/ppermute | solution.py:639
  207.2 23.4 %collective-permute-start.41 = (bf16[104,1024]{1,0:T(8,128)(2,1)S(1)}, bf16[104,1024]{1,0:T(8,128)(2,1)S(1)}, u32[]{:S(2)}, u32[]{:S(2)}) collective-permute-start(bf16[104,1024]{1,0:T(8,128)(2,1)S(1)} %get-tuple-element.201), channel_id=1, source_target_pairs={{0,16},{8,24},{16,0},{24,8},{1,17},{9,25},{17,1},{25,9},{2,18},{10... | collective-permute-start | bytes 638984 | tf_op jit(solution)/shard_map/ppermute | solution.py:639
  207.9 27.9 %collective-permute-start.42 = (bf16[104,1024]{1,0:T(8,128)(2,1)S(1)}, bf16[104,1024]{1,0:T(8,128)(2,1)S(1)}, u32[]{:S(2)}, u32[]{:S(2)}) collective-permute-start(bf16[104,1024]{1,0:T(8,128)(2,1)S(1)} %get-tuple-element.202), channel_id=1, source_target_pairs={{0,24},{8,16},{16,8},{24,0},{1,25},{9,17},{17,9},{25,1},{2,26},{10... | collective-permute-start | bytes 638984 | tf_op jit(solution)/shard_map/ppermute | solution.py:639
  226.1 9.8 %copy-start.15 = (bf16[392,416]{1,0:T(8,128)(2,1)S(1)}, bf16[392,416]{1,0:T(8,128)(2,1)}, u32[]{:S(2)}) copy-start(bf16[392,416]{1,0:T(8,128)(2,1)} %constant.46.refs_1_) | copy-start | bytes 978436
  (2 other events, 3.7 us)

commit v6 on v5

--- a/solution.py
+++ b/solution.py
@@ -20,7 +20,7 @@
     SAMPLES * POOL
 )
 SMALL_COST = pl.CostEstimate(flops=10**9, bytes_accessed=1, transcendentals=0)
-LARGE_COST = pl.CostEstimate(flops=2 * 10**10, bytes_accessed=1, transcendentals=0)
+LARGE_COST = pl.CostEstimate(flops=3 * 10**10, bytes_accessed=1, transcendentals=0)
 f32 = jnp.float32
 bf16 = jnp.bfloat16
 FAR = pl.BlockSpec(memory_space=pl.ANY)
@@ -40,7 +40,7 @@
     x0, y0, x1, y1, level = [box_ref[k : k + 1, :] for k in range(5)]
     centres = lax.broadcasted_iota(jnp.int32, (width, LANES), 0).astype(f32)
     for q in range(POOL):
-        across_ref[q] = bin_weights(x0, x1 - x0, centres, q)
+        across_ref[q] = bin_weights(x0, x1 - x0, centres, q).astype(across_ref.dtype)
     centres = lax.broadcasted_iota(jnp.int32, (height, LANES), 0).astype(f32)
     for p in range(POOL):
         weights = bin_weights(y0, y1 - y0, centres, p).astype(f32)
@@ -113,7 +113,9 @@
     for first, end in gaps_of(table, rows_ref.shape[0]):
         rows_ref[first:end, :] = jnp.zeros((end - first, LANES), f32)
     fill_weights(box_ref, down_ref, across_ref, height, width, level_count)
-    sums_ref[...] = jnp.dot(maps_ref[...], down_ref[...], preferred_element_type=f32).astype(bf16)
+    sums_ref[...] = jnp.dot(maps_ref[...], down_ref[...], preferred_element_type=f32).astype(
+        sums_ref.dtype
+    )
     for p in range(POOL):
         lanes = slice(p * LANES, (p + 1) * LANES)
         for start in range(0, POOL, 2):
@@ -172,7 +174,7 @@
         ).astype(bf16)
 
 
-def crop_block(table, sizes, features, boxes, maps, weight=None, out_type=bf16, earlier=(), cost=LARGE_COST):
+def crop_block(table, sizes, features, boxes, maps, weight=None, out_type=bf16, earlier=(), cost=LARGE_COST, sum_type=bf16):
     height, width, part, level_count = sizes
     images = boxes.shape[0]
     product = weight is not None
@@ -204,8 +206,8 @@
         out_shape=[like((features, rows), bf16), out_shape, SIGN],
         scratch_shapes=[
             pltpu.VMEM((level_count * height, POOL * LANES), bf16),
-            pltpu.VMEM((POOL, width, LANES), bf16),
-            pltpu.VMEM((width * part, POOL * LANES), bf16),
+            pltpu.VMEM((POOL, width, LANES), sum_type),
+            pltpu.VMEM((width * part, POOL * LANES), sum_type),
             pltpu.VMEM((features, LANES), f32),
         ]
         + more,
@@ -867,6 +869,7 @@
                 bf16 if way == 1 else f32,
                 [sign],
                 SMALL_COST if way == 1 else LARGE_COST,
+                bf16 if way else f32,
             )
         crops.append(crop)
         if way == 2:
@@ -959,16 +962,22 @@
             return sign
 
         sign = for_other((6,), sign)
-        sign = for_other((2, 4), sign)
+        sign = for_other((2, 4, 0), sign)
+        sign = for_own((6,), sign)
         sent, kept, sign = halve_rows((0, 1), 2, count, where, quarters, [sign])
-        sign = for_own((6,), sign)
-        sign = for_own((2, 4), sign)
-        sign = for_other((0,), sign)
+        sign = for_own((2, 4, 0), sign)
+        sign = take_up(3, [sign])
         sent, kept, sign = halve_rows(
             (0, 0), 1, count, where, [kept, swap(sent, "level", 2)], [sign]
         )
-        sign = take_up(3, [sign])
-        sign = for_own((0,), sign)
+        *back, sign = call(
+            functools.partial(arrange_back_kernel, sizes),
+            [like((images, part, spots), bf16)] * size,
+            where,
+            shares,
+            [sign],
+            name="arrange_back",
+        )
         inner_sum, class_sum, delta_sum, bias_total, sign = call(
             small_sum_kernel,
             [
@@ -983,18 +992,11 @@
             name="small_sum",
             cost=SMALL_COST,
         )
-        *back, sign = call(
-            functools.partial(arrange_back_kernel, sizes),
-            [like((images, part, spots), bf16)] * size,
-            where,
-            shares,
-            [sign],
-            name="arrange_back",
-        )
+        back[3] = tie(back[3:], sign)[0]
         half, sign = call(
             add_kernel, [like(parts[0].shape, f32)], where, [parts[0], parts[6]], [sign], name="add", cost=SMALL_COST
         )
-        back[3] = tie(back[3:], sign)[0]
+        back[1] = tie(back[1:2], sign)[0]
         *out, sign = call(
             return_span_kernel,
             [like((span, units), bf16)] * size,

time: 242 us -> 235 us (0.971)
  waiting for transfers between devices: 86.3 us -> 79.9 us
  starting transfers between devices: 46.8 us -> 43.8 us
    ppermute x43 -> x42, waiting for transfers between devices: 86.3 us -> 79.9 us  [swap(): return lax.ppermute(array, axis, [(at, at ^ bit) for at in range(size)])]
    ppermute x43 -> x42, starting transfers between devices: 46.8 us -> 43.8 us  [swap(): return lax.ppermute(array, axis, [(at, at ^ bit) for at in range(size)])]
    pallas_call x6 -> x4, Pallas kernels: 11.1 us -> 9.88 us  [piece_product(): pl.pallas_call(functools.partial(product_kernel, bits, len(grads), with_s...]
  transfers between devices with their start and end apart: 43 -> 42, of which waited for: 20 -> 18; matrix products, arithmetic and copies ran while one was open for 1% -> 1% of each run, Pallas kernels for 38% -> 41%
where the time goes in v6:
time: 235 us; the launch traced here: 232 us
  Pallas kernels  102 us (43%)
  waiting for transfers between devices  79.9 us (34%)
  starting transfers between devices  43.8 us (19%)
  local copies, waits for them, and re-layouts  3.11 us (1%)
    ppermute x42, waiting for transfers between devices, swap(): return lax.ppermute(array, axis, [(at, at ^ bit) for at in range(size)])  79.9 us
    ppermute x42, starting transfers between devices, swap(): return lax.ppermute(array, axis, [(at, at ^ bit) for at in range(size)])  43.8 us
    pallas_call x4, Pallas kernels, spread_block(): pl.pallas_call(functools.partial(spread_kernel, table, sizes), in_specs=[...  28.6 us
    pallas_call x4, Pallas kernels, crop_block(): pl.pallas_call(functools.partial(crop_kernel, table, sizes, product), gri...  26.7 us
    pallas_call x17, Pallas kernels, call(): pl.pallas_call(body, in_specs=[SCALAR] + [WHOLE for one in arrays] + [FAR...  25.6 us
    pallas_call x4, Pallas kernels, piece_product(): pl.pallas_call(functools.partial(product_kernel, bits, len(grads), with_s...  9.88 us
  transfers between devices with their start and end apart: 42, of which 18 were waited for; matrix products, arithmetic and copies ran while one was open for 1% of the time, Pallas kernels for 41%

profile of v6, /device:TPU:8, one launch (start us, length us, event | category | flops | bytes accessed | tf_op | source)
XLA Modules:
  0.0 231.6 jit_solution(17070030726681722162)
XLA Ops:
  1.6 1.1 copy-done.7
  2.8 1.2 split_span.1
  4.1 3.0 %collective-permute-start.1 = (bf16[104,1024]{1,0:T(8,128)(2,1)S(1)}, bf16[104,1024]{1,0:T(8,128)(2,1)S(1)}, u32[]{:S(2)}, u32[]{:S(2)}) collective-permute-start(bf16[104,1024]{1,0:T(8,128)(2,1)S(1)} %get-tuple-element.109), channel_id=1, source_target_pairs={{0,16},{8,24},{16,0},{24,8},{1,17},{9,25},{17,1},{25,9},{2,18},{10... | collective-permute-start | bytes 638984 | tf_op jit(solution)/shard_map/ppermute | solution.py:641
  7.7 2.5 %maps.1 = (bf16[128,1024]{1,0:T(8,128)(2,1)S(1)}, bf16[128,1024]{1,0:T(8,128)(2,1)S(1)}, bf16[128,1024]{1,0:T(8,128)(2,1)S(1)}, bf16[128,1024]{1,0:T(8,128)(2,1)S(1)}, f32[8,128]{1,0:T(8,128)}) custom-call(s32[2]{0:T(128)S(1)} %pad_add_fusion.refs_0_.where_ref, bf16[2,1024,256]{2,1,0:T(8,128)(2,1)S(1)} %bitcast.56, bf16[4,64,256]{2,1,0:T(8,128)(2,1)S(1)} %copy-done.18, ...), custom_call_target="tpu_custom_call" | custom-call | flops 30000001024 | bytes 1 | tf_op jit(solution)/shard_map/maps/pallas_call | solution.py:268
  10.2 2.5 %collective-permute-done.refs_3_ = bf16[104,1024]{1,0:T(8,128)(2,1)S(1)} collective-permute-done((bf16[104,1024]{1,0:T(8,128)(2,1)S(1)}, bf16[104,1024]{1,0:T(8,128)(2,1)S(1)}, u32[]{:S(2)}, u32[]{:S(2)}) %collective-permute-start) | collective-permute-done | bytes 213024 | tf_op jit(solution)/shard_map/ppermute | solution.py:641
  12.7 9.2 %collective-permute-done.1.refs_4_ = bf16[104,1024]{1,0:T(8,128)(2,1)S(1)} collective-permute-done((bf16[104,1024]{1,0:T(8,128)(2,1)S(1)}, bf16[104,1024]{1,0:T(8,128)(2,1)S(1)}, u32[]{:S(2)}, u32[]{:S(2)}) %collective-permute-start.1) | collective-permute-done | bytes 213024 | tf_op jit(solution)/shard_map/ppermute | solution.py:641
  22.0 4.1 %collective-permute-done.2.refs_5_ = bf16[104,1024]{1,0:T(8,128)(2,1)S(1)} collective-permute-done((bf16[104,1024]{1,0:T(8,128)(2,1)S(1)}, bf16[104,1024]{1,0:T(8,128)(2,1)S(1)}, u32[]{:S(2)}, u32[]{:S(2)}) %collective-permute-start.2) | collective-permute-done | bytes 213024 | tf_op jit(solution)/shard_map/ppermute | solution.py:641
  26.0 1.3 join_span.2
  27.3 2.5 %collective-permute-start.11 = (bf16[400,1024]{1,0:T(8,128)(2,1)S(1)}, bf16[400,1024]{1,0:T(8,128)(2,1)S(1)}, u32[]{:S(2)}, u32[]{:S(2)}) collective-permute-start(bf16[400,1024]{1,0:T(8,128)(2,1)S(1)} %get-tuple-element.122), channel_id=1, source_target_pairs={{0,6},{1,7},{2,4},{3,5},{4,2},{5,3},{6,0},{7,1},{8,14},{9,15},{10,... | collective-permute-start | bytes 2457608 | tf_op jit(solution)/shard_map/ppermute | solution.py:641
  30.9 3.1 %collective-permute-start.4 = (bf16[128,1024]{1,0:T(8,128)(2,1)S(1)}, bf16[128,1024]{1,0:T(8,128)(2,1)S(1)}, u32[]{:S(2)}, u32[]{:S(2)}) collective-permute-start(bf16[128,1024]{1,0:T(8,128)(2,1)S(1)} %get-tuple-element.117), channel_id=1, source_target_pairs={{0,16},{8,24},{16,0},{24,8},{1,17},{9,25},{17,1},{25,9},{2,18},{10... | collective-permute-start | bytes 786440 | tf_op jit(solution)/shard_map/ppermute | solution.py:641
  34.0 6.1 %collective-permute-done.3.refs_1_.refs_2_ = bf16[128,1024]{1,0:T(8,128)(2,1)S(1)} collective-permute-done((bf16[128,1024]{1,0:T(8,128)(2,1)S(1)}, bf16[128,1024]{1,0:T(8,128)(2,1)S(1)}, u32[]{:S(2)}, u32[]{:S(2)}) %collective-permute-start.3) | collective-permute-done | bytes 262176 | tf_op jit(solution)/shard_map/ppermute | solution.py:641
  40.1 1.6 collective-permute-start.5
  41.8 13.4 %collective-permute-done.5.refs_4_.refs_1_ = bf16[128,1024]{1,0:T(8,128)(2,1)S(1)} collective-permute-done((bf16[128,1024]{1,0:T(8,128)(2,1)S(1)}, bf16[128,1024]{1,0:T(8,128)(2,1)S(1)}, u32[]{:S(2)}, u32[]{:S(2)}) %collective-permute-start.5) | collective-permute-done | bytes 262176 | tf_op jit(solution)/shard_map/ppermute | solution.py:641
  55.1 1.7 arrange.1
  56.8 4.5 %crop_block.4 = (bf16[3200,256]{1,0:T(8,128)(2,1)S(1)}, bf16[256,3200]{1,0:T(8,128)(2,1)S(1)}, f32[8,128]{1,0:T(8,128)S(1)}) custom-call(f32[2,8,128]{2,1,0:T(8,128)S(1)} %get-tuple-element.209.box_ref, bf16[2,1024,256]{2,1,0:T(8,128)(2,1)S(1)} %get-tuple-element.119.maps_ref), custom_call_target="tpu_custom_call" | custom-call | flops 30000001024 | bytes 1 | tf_op jit(solution)/shard_map/crop_block/pallas_call | solution.py:192
  61.9 2.8 %collective-permute-done.9.refs_4_ = bf16[400,1024]{1,0:T(8,128)(2,1)S(1)} collective-permute-done((bf16[400,1024]{1,0:T(8,128)(2,1)S(1)}, bf16[400,1024]{1,0:T(8,128)(2,1)S(1)}, u32[]{:S(2)}, u32[]{:S(2)}) %collective-permute-start.9) | collective-permute-done | bytes 819232 | tf_op jit(solution)/shard_map/ppermute | solution.py:641
  65.2 1.1 pair_up.2
  67.0 1.2 collective-permute-done.8.refs_3_
  68.1 1.4 gather_pieces.1.weight_ref.refs_0_
  69.6 1.9 multiply.1
  71.5 1.3 collective-permute-start.13
  72.8 6.3 %crop_block.5 = (bf16[3200,256]{1,0:T(8,128)(2,1)S(1)}, f32[256,1024]{1,0:T(8,128)S(1)}, f32[8,128]{1,0:T(8,128)S(1)}) custom-call(f32[2,8,128]{2,1,0:T(8,128)S(1)} %get-tuple-element.208.box_ref, bf16[2,1024,256]{2,1,0:T(8,128)(2,1)S(1)} %get-tuple-element.119.maps_ref, bf16[3200,1024]{1,0:T(8,128)(2,1)S(1)} %gather_pieces.1.weight_ref.refs_0_, ...), custom_call_target="tpu_custom_call" | custom-call | flops 30000001024 | bytes 1 | tf_op jit(solution)/shard_map/crop_block/pallas_call | solution.py:192
  79.7 2.4 %collective-permute-start.20 = (bf16[4,48,1024]{2,1,0:T(8,128)(2,1)S(1)}, bf16[4,48,1024]{2,1,0:T(8,128)(2,1)S(1)}, u32[]{:S(2)}, u32[]{:S(2)}) collective-permute-start(bf16[4,48,1024]{2,1,0:T(8,128)(2,1)S(1)} %bitcast.57), channel_id=1, source_target_pairs={{0,6},{1,7},{2,4},{3,5},{4,2},{5,3},{6,0},{7,1},{8,14},{9,15},{10,... | collective-permute-start | bytes 1179656 | tf_op jit(solution)/shard_map/ppermute | solution.py:641
  83.2 6.3 %crop_block.6 = (bf16[3200,256]{1,0:T(8,128)(2,1)S(1)}, bf16[256,1024]{1,0:T(8,128)(2,1)S(1)}, f32[8,128]{1,0:T(8,128)S(1)}) custom-call(f32[2,8,128]{2,1,0:T(8,128)S(1)} %get-tuple-element.207.box_ref, bf16[2,1024,256]{2,1,0:T(8,128)(2,1)S(1)} %get-tuple-element.119.maps_ref, bf16[3200,1024]{1,0:T(8,128)(2,1)S(1)} %gather_pieces.1.weight_ref.refs_0_, ...), custom_call_target="tpu_custom_call" | custom-call | flops 1000000000 | bytes 1 | tf_op jit(solution)/shard_map/crop_block/pallas_call | solution.py:192
  91.1 2.1 collective-permute-start.16
  93.3 6.5 %collective-permute-done.19.refs_3_ = bf16[4,48,1024]{2,1,0:T(8,128)(2,1)S(1)} collective-permute-done((bf16[4,48,1024]{2,1,0:T(8,128)(2,1)S(1)}, bf16[4,48,1024]{2,1,0:T(8,128)(2,1)S(1)}, u32[]{:S(2)}, u32[]{:S(2)}) %collective-permute-start.19) | collective-permute-done | bytes 393248 | tf_op jit(solution)/shard_map/ppermute | solution.py:641
  99.9 1.1 in_order.1
  101.0 9.6 %crop_block.7 = (bf16[3200,256]{1,0:T(8,128)(2,1)S(1)}, f32[256,1024]{1,0:T(8,128)S(1)}, f32[8,128]{1,0:T(8,128)}) custom-call(f32[2,8,128]{2,1,0:T(8,128)S(1)} %get-tuple-element.210.box_ref, bf16[2,1024,256]{2,1,0:T(8,128)(2,1)S(1)} %get-tuple-element.119.maps_ref, bf16[3200,1024]{1,0:T(8,128)(2,1)S(1)} %gather_pieces.1.weight_ref.refs_0_, ...), custom_call_target="tpu_custom_call" | custom-call | flops 30000001024 | bytes 1 | tf_op jit(solution)/shard_map/crop_block/pallas_call | solution.py:192
  110.6 1.3 full_small.1
  111.9 2.7 %collective-permute-done.16.one_ref = bf16[256,1024]{1,0:T(8,128)(2,1)S(1)} collective-permute-done((bf16[256,1024]{1,0:T(8,128)(2,1)S(1)}, bf16[256,1024]{1,0:T(8,128)(2,1)S(1)}, u32[]{:S(2)}, u32[]{:S(2)}) %collective-permute-start.16) | collective-permute-done | bytes 524320 | tf_op jit(solution)/shard_map/ppermute | solution.py:641
  114.7 3.5 %head_block.1 = (f32[81,2,128]{2,1,0:T(2,128)}, f32[2,320,128]{2,1,0:T(8,128)}, bf16[256,1024]{1,0:T(8,128)(2,1)S(1)}, bf16[256,1024]{1,0:T(8,128)(2,1)S(1)}, bf...) custom-call(f32[256,1024]{1,0:T(8,128)S(1)} %get-tuple-element.132.o, ...), custom_call_target="tpu_custom_call" | custom-call | flops 30000001024 | bytes 1 | tf_op jit(solution)/shard_map/head_block/pallas_call | solution.py:520
  118.2 3.3 %collective-permute-start.24 = (bf16[256,1024]{1,0:T(8,128)(2,1)S(1)}, bf16[256,1024]{1,0:T(8,128)(2,1)S(1)}, u32[]{:S(2)}, u32[]{:S(2)}) collective-permute-start(bf16[256,1024]{1,0:T(8,128)(2,1)S(1)} %get-tuple-element.141.grad_ref.refs_3_), channel_id=1, source_target_pairs={{0,16},{8,24},{16,0},{24,8},{1,17},{9,25},{17,1},{25,9},{2,18},{10... | collective-permute-start | bytes 1572872 | tf_op jit(solution)/shard_map/ppermute | solution.py:641
  121.5 2.6 %small_product.1 = (bf16[528,1536]{1,0:T(8,128)(2,1)S(1)}, bf16[528,1536]{1,0:T(8,128)(2,1)S(1)}, f32[8,128]{1,0:T(8,128)S(1)}) custom-call(s32[2]{0:T(128)S(1)} %pad_add_fusion.refs_0_.where_ref, bf16[256,1024]{1,0:T(8,128)(2,1)S(1)} %get-tuple-element.142.first_ref, bf16[256,1024]{1,0:T(8,128)(2,1)S(1)} %get-tuple-element.143.second_grad_ref, ...), custom_call_target="tpu_custom_call" | custom-call | flops 30000001024 | bytes 1 | tf_op jit(solution)/shard_map/small_product/pallas_call | solution.py:374
  124.2 7.1 %spread_block.4 = (bf16[2,1024,256]{2,1,0:T(8,128)(2,1)S(1)}, f32[8,128]{1,0:T(8,128)S(1)}) custom-call(f32[2,8,128]{2,1,0:T(8,128)S(1)} %get-tuple-element.210.box_ref, bf16[256,1024]{1,0:T(8,128)(2,1)S(1)} %get-tuple-element.141.grad_ref.refs_3_, bf16[3200,1024]{1,0:T(8,128)(2,1)S(1)} %gather_pieces.1.weight_ref.refs_0_, ...), custom_call_target="tpu_custom_call" | custom-call | flops 30000001024 | bytes 1 | tf_op jit(solution)/shard_map/spread_block/pallas_call | solution.py:241
  131.3 2.1 quarter_rows.1
  133.4 1.5 collective-permute-start.27
  134.9 1.5 collective-permute-start.28
  136.9 3.6 %collective-permute-done.24.refs_0_ = bf16[256,1024]{1,0:T(8,128)(2,1)S(1)} collective-permute-done((bf16[256,1024]{1,0:T(8,128)(2,1)S(1)}, bf16[256,1024]{1,0:T(8,128)(2,1)S(1)}, u32[]{:S(2)}, u32[]{:S(2)}) %collective-permute-start.24) | collective-permute-done | bytes 524320 | tf_op jit(solution)/shard_map/ppermute | solution.py:641
  140.5 2.4 %collective-permute-start.25 = (bf16[256,1024]{1,0:T(8,128)(2,1)S(1)}, bf16[256,1024]{1,0:T(8,128)(2,1)S(1)}, u32[]{:S(2)}, u32[]{:S(2)}) collective-permute-start(bf16[256,1024]{1,0:T(8,128)(2,1)S(1)} %tie.11.grad_ref.refs_1_), channel_id=1, source_target_pairs={{0,8},{8,0},{16,24},{24,16},{1,9},{9,1},{17,25},{25,17},{2,10},{10... | collective-permute-start | bytes 1572872 | tf_op jit(solution)/shard_map/ppermute | solution.py:641
  143.0 7.3 %spread_block.5 = (bf16[2,1024,256]{2,1,0:T(8,128)(2,1)S(1)}, f32[8,128]{1,0:T(8,128)S(1)}) custom-call(f32[2,8,128]{2,1,0:T(8,128)S(1)} %copy-done.1, bf16[256,1024]{1,0:T(8,128)(2,1)S(1)} %collective-permute-done.22.grad_ref.refs_2_, bf16[3200,1024]{1,0:T(8,128)(2,1)S(1)} %gather_pieces.1.weight_ref.refs_0_, f32[8,128]{1,0:T(8,128)S(1)} %get-tuple-element.152.refs_0_.refs_1_), custom_call_target="tpu_custom_call" | custom-call | flops 30000001024 | bytes 1 | tf_op jit(solution)/shard_map/spread_block/pallas_call | solution.py:241
  150.3 7.1 %spread_block.6 = (bf16[2,1024,256]{2,1,0:T(8,128)(2,1)S(1)}, f32[8,128]{1,0:T(8,128)S(1)}) custom-call(f32[2,8,128]{2,1,0:T(8,128)S(1)} %copy-done.5, bf16[256,1024]{1,0:T(8,128)(2,1)S(1)} %tie.11.grad_ref.refs_1_, bf16[3200,1024]{1,0:T(8,128)(2,1)S(1)} %gather_pieces.1.weight_ref.refs_0_, f32[8,128]{1,0:T(8,128)S(1)} %get-tuple-element.154.refs_0_), custom_call_target="tpu_custom_call" | custom-call | flops 30000001024 | bytes 1 | tf_op jit(solution)/shard_map/spread_block/pallas_call | solution.py:241
  157.4 1.6 piece_product.4
  159.1 3.5 %piece_product.5 = (bf16[3,400,1024]{2,1,0:T(8,128)(2,1)S(1)}, f32[8,128]{1,0:T(8,128)S(1)}) custom-call(s32[2]{0:T(128)S(1)} %pad_add_fusion.refs_0_.where_ref, bf16[256,1024]{1,0:T(8,128)(2,1)S(1)} %collective-permute-done.25.refs_0_.grad_ref, bf16[256,1024]{1,0:T(8,128)(2,1)S(1)} %tie.11.grad_ref.refs_1_, ...), custom_call_target="tpu_custom_call" | custom-call | flops 30000001024 | bytes 1 | tf_op jit(solution)/shard_map/piece_product/pallas_call | solution.py:679
  163.1 1.6 piece_product.6
  164.7 1.7 halve_rows.2
  166.4 1.7 collective-permute-start.31
  168.1 1.7 collective-permute-start.32
  169.8 3.3 %piece_product.7 = (bf16[400,1024]{1,0:T(8,128)(2,1)S(1)}, bf16[400,1024]{1,0:T(8,128)(2,1)S(1)}, bf16[400,1024]{1,0:T(8,128)(2,1)S(1)}, f32[8,128]{1,0:T(8,128)S(1)}) custom-call(s32[2]{0:T(128)S(1)} %pad_add_fusion.refs_0_.where_ref, bf16[256,1024]{1,0:T(8,128)(2,1)S(1)} %collective-permute-done.25.refs_0_.grad_ref, ...), custom_call_target="tpu_custom_call" | custom-call | flops 30000001024 | bytes 1 | tf_op jit(solution)/shard_map/piece_product/pallas_call | solution.py:679
  173.1 7.1 %spread_block.7 = (bf16[2,1024,256]{2,1,0:T(8,128)(2,1)S(1)}, f32[8,128]{1,0:T(8,128)S(1)}) custom-call(f32[2,8,128]{2,1,0:T(8,128)S(1)} %copy-done.3, bf16[256,1024]{1,0:T(8,128)(2,1)S(1)} %collective-permute-done.25.refs_0_.grad_ref, bf16[3200,1024]{1,0:T(8,128)(2,1)S(1)} %gather_pieces.1.weight_ref.refs_0_, f32[8,128]{1,0:T(8,128)S(1)} %get-tuple-element.171.refs_0_), custom_call_target="tpu_custom_call" | custom-call | flops 30000001024 | bytes 1 | tf_op jit(solution)/shard_map/spread_block/pallas_call | solution.py:241
  180.9 1.4 collective-permute-start.33
  182.3 1.8 arrange_back.1
  184.7 1.4 collective-permute-start.37
  186.0 0.9 collective-permute-start.38
  187.0 1.2 small_sum.1
  188.2 1.9 collective-permute-done.32.refs_2_
  190.8 1.4 collective-permute-start.34
  194.2 12.2 %collective-permute-done.37.refs_3_ = bf16[400,1024]{1,0:T(8,128)(2,1)S(1)} collective-permute-done((bf16[400,1024]{1,0:T(8,128)(2,1)S(1)}, bf16[400,1024]{1,0:T(8,128)(2,1)S(1)}, u32[]{:S(2)}, u32[]{:S(2)}) %collective-permute-start.37) | collective-permute-done | bytes 819232 | tf_op jit(solution)/shard_map/ppermute | solution.py:641
  206.4 1.4 return_span.1
  207.8 1.5 collective-permute-start.39
  210.0 1.4 collective-permute-start.41
  211.4 4.5 %maps_back.1 = (f32[2,1024,256]{2,1,0:T(8,128)}, f32[8,128]{1,0:T(8,128)S(1)}) custom-call(s32[2]{0:T(128)S(1)} %pad_add_fusion.refs_0_.where_ref, bf16[2,64,1024]{2,1,0:T(8,128)(2,1)S(1)} %get-tuple-element.177.refs_1_, bf16[2,64,1024]{2,1,0:T(8,128)(2,1)S(1)} %collective-permute-done.34.refs_2_, bf16[2,64,1024]{2,1,0:T(8,128)(2,1)S(1)} %collective-permute-done.35.refs_3_, ...), custom_call_target="tpu_custom_call" | custom-call | flops 30000001024 | bytes 1 | tf_op jit(solution)/shard_map/maps_back/pallas_call | solution.py:268
  216.5 8.0 %collective-permute-done.40.refs_4_ = bf16[104,1024]{1,0:T(8,128)(2,1)S(1)} collective-permute-done((bf16[104,1024]{1,0:T(8,128)(2,1)S(1)}, bf16[104,1024]{1,0:T(8,128)(2,1)S(1)}, u32[]{:S(2)}, u32[]{:S(2)}) %collective-permute-start.40) | collective-permute-done | bytes 213024 | tf_op jit(solution)/shard_map/ppermute | solution.py:641
  224.5 4.5 %collective-permute-done.41.refs_5_ = bf16[104,1024]{1,0:T(8,128)(2,1)S(1)} collective-permute-done((bf16[104,1024]{1,0:T(8,128)(2,1)S(1)}, bf16[104,1024]{1,0:T(8,128)(2,1)S(1)}, u32[]{:S(2)}, u32[]{:S(2)}) %collective-permute-start.41) | collective-permute-done | bytes 213024 | tf_op jit(solution)/shard_map/ppermute | solution.py:641
  228.9 2.4 %join_span.3 = (f32[392,1024]{1,0:T(8,128)}, f32[8,128]{1,0:T(8,128)}) custom-call(s32[2]{0:T(128)S(1)} %pad_add_fusion.refs_0_.where_ref, bf16[392,416]{1,0:T(8,128)(2,1)S(1)} %copy-done.17, bf16[104,1024]{1,0:T(8,128)(2,1)S(1)} %get-tuple-element.193.refs_2_, bf16[104,1024]{1,0:T(8,128)(2,1)S(1)} %collective-permute-done.39.refs_3_, ...), custom_call_target="tpu_custom_call" | custom-call | flops 30000001024 | bytes 1 | tf_op jit(solution)/shard_map/join_span/pallas_call | solution.py:268
  (134 shorter events, 14.5 us)
Async XLA Ops:
  2.7 4.9 %copy-start.21 = (bf16[32,320]{1,0:T(8,128)(2,1)S(1)}, bf16[32,320]{1,0:T(8,128)(2,1)}, u32[]{:S(2)}) copy-start(bf16[32,320]{1,0:T(8,128)(2,1)} %param.30) | copy-start | bytes 61444
  2.7 4.9 %copy-start.22 = (bf16[32,81]{1,0:T(8,128)(2,1)S(1)}, bf16[32,81]{1,0:T(8,128)(2,1)}, u32[]{:S(2)}) copy-start(bf16[32,81]{1,0:T(8,128)(2,1)} %param.28) | copy-start | bytes 15556
  2.7 4.9 %copy-start.23 = (f32[320]{0:T(512)S(1)}, f32[320]{0:T(512)}, u32[]{:S(2)}) copy-start(f32[320]{0:T(512)} %param.31) | copy-start | bytes 3844
  2.7 4.9 %copy-start.24 = (f32[81]{0:T(128)S(1)}, f32[81]{0:T(128)}, u32[]{:S(2)}) copy-start(f32[81]{0:T(128)} %param.29) | copy-start | bytes 976
  2.7 4.9 %copy-start.6 = (bf16[1,2,64,16,256]{4,3,2,1,0:T(8,128)(2,1)S(1)}, bf16[1,2,64,16,256]{4,3,2,1,0:T(8,128)(2,1)}, u32[]{:S(2)}) copy-start(bf16[1,2,64,16,256]{4,3,2,1,0:T(8,128)(2,1)} %param.18) | copy-start | bytes 3145732
  2.8 4.9 %copy-start.13 = (bf16[1024,1024]{1,0:T(8,128)(2,1)S(1)}, bf16[1024,1024]{1,0:T(8,128)(2,1)}, u32[]{:S(2)}) copy-start(bf16[1024,1024]{1,0:T(8,128)(2,1)} %constant.28.clone.refs_3_.refs_6_) | copy-start | bytes 6291460
  2.8 4.9 %copy-start.18 = (bf16[4,64,256]{2,1,0:T(8,128)(2,1)S(1)}, bf16[4,64,256]{2,1,0:T(8,128)(2,1)}, u32[]{:S(2)}) copy-start(bf16[4,64,256]{2,1,0:T(8,128)(2,1)} %constant.44.refs_2_.refs_5_) | copy-start | bytes 393220
  4.0 8.7 %collective-permute-start = (bf16[104,1024]{1,0:T(8,128)(2,1)S(1)}, bf16[104,1024]{1,0:T(8,128)(2,1)S(1)}, u32[]{:S(2)}, u32[]{:S(2)}) collective-permute-start(bf16[104,1024]{1,0:T(8,128)(2,1)S(1)} %get-tuple-element.108), channel_id=1, source_target_pairs={{0,8},{8,0},{16,24},{24,16},{1,9},{9,1},{17,25},{25,17},{2,10},{10... | collective-permute-start | bytes 638984 | tf_op jit(solution)/shard_map/ppermute | solution.py:641
  4.1 17.9 %collective-permute-start.1 = (bf16[104,1024]{1,0:T(8,128)(2,1)S(1)}, bf16[104,1024]{1,0:T(8,128)(2,1)S(1)}, u32[]{:S(2)}, u32[]{:S(2)}) collective-permute-start(bf16[104,1024]{1,0:T(8,128)(2,1)S(1)} %get-tuple-element.109), channel_id=1, source_target_pairs={{0,16},{8,24},{16,0},{24,8},{1,17},{9,25},{17,1},{25,9},{2,18},{10... | collective-permute-start | bytes 638984 | tf_op jit(solution)/shard_map/ppermute | solution.py:641
  7.1 18.9 %collective-permute-start.2 = (bf16[104,1024]{1,0:T(8,128)(2,1)S(1)}, bf16[104,1024]{1,0:T(8,128)(2,1)S(1)}, u32[]{:S(2)}, u32[]{:S(2)}) collective-permute-start(bf16[104,1024]{1,0:T(8,128)(2,1)S(1)} %get-tuple-element.110), channel_id=1, source_target_pairs={{0,24},{8,16},{16,8},{24,0},{1,25},{9,17},{17,9},{25,1},{2,26},{10... | collective-permute-start | bytes 638984 | tf_op jit(solution)/shard_map/ppermute | solution.py:641
  7.7 18.3 %copy-start.16 = (bf16[400,416]{1,0:T(8,128)(2,1)S(1)}, bf16[400,416]{1,0:T(8,128)(2,1)}, u32[]{:S(2)}) copy-start(bf16[400,416]{1,0:T(8,128)(2,1)} %constant.26.clone.refs_1_) | copy-start | bytes 998404
  27.3 34.1 %collective-permute-start.11 = (bf16[400,1024]{1,0:T(8,128)(2,1)S(1)}, bf16[400,1024]{1,0:T(8,128)(2,1)S(1)}, u32[]{:S(2)}, u32[]{:S(2)}) collective-permute-start(bf16[400,1024]{1,0:T(8,128)(2,1)S(1)} %get-tuple-element.122), channel_id=1, source_target_pairs={{0,6},{1,7},{2,4},{3,5},{4,2},{5,3},{6,0},{7,1},{8,14},{9,15},{10,... | collective-permute-start | bytes 2457608 | tf_op jit(solution)/shard_map/ppermute | solution.py:641
  29.8 34.9 %collective-permute-start.9 = (bf16[400,1024]{1,0:T(8,128)(2,1)S(1)}, bf16[400,1024]{1,0:T(8,128)(2,1)S(1)}, u32[]{:S(2)}, u32[]{:S(2)}) collective-permute-start(bf16[400,1024]{1,0:T(8,128)(2,1)S(1)} %get-tuple-element.122), channel_id=1, source_target_pairs={{0,4},{1,5},{2,6},{3,7},{4,0},{5,1},{6,2},{7,3},{8,12},{9,13},{10,... | collective-permute-start | bytes 2457608 | tf_op jit(solution)/shard_map/ppermute | solution.py:641
  30.3 34.4 %collective-permute-start.7 = (bf16[400,1024]{1,0:T(8,128)(2,1)S(1)}, bf16[400,1024]{1,0:T(8,128)(2,1)S(1)}, u32[]{:S(2)}, u32[]{:S(2)}) collective-permute-start(bf16[400,1024]{1,0:T(8,128)(2,1)S(1)} %get-tuple-element.122), channel_id=1, source_target_pairs={{0,2},{1,3},{2,0},{3,1},{4,6},{5,7},{6,4},{7,5},{8,10},{9,11},{10,... | collective-permute-start | bytes 2457608 | tf_op jit(solution)/shard_map/ppermute | solution.py:641
  30.8 9.2 %collective-permute-start.3 = (bf16[128,1024]{1,0:T(8,128)(2,1)S(1)}, bf16[128,1024]{1,0:T(8,128)(2,1)S(1)}, u32[]{:S(2)}, u32[]{:S(2)}) collective-permute-start(bf16[128,1024]{1,0:T(8,128)(2,1)S(1)} %get-tuple-element.116), channel_id=1, source_target_pairs={{0,8},{8,0},{16,24},{24,16},{1,9},{9,1},{17,25},{25,17},{2,10},{10... | collective-permute-start | bytes 786440 | tf_op jit(solution)/shard_map/ppermute | solution.py:641
  30.9 24.2 %collective-permute-start.4 = (bf16[128,1024]{1,0:T(8,128)(2,1)S(1)}, bf16[128,1024]{1,0:T(8,128)(2,1)S(1)}, u32[]{:S(2)}, u32[]{:S(2)}) collective-permute-start(bf16[128,1024]{1,0:T(8,128)(2,1)S(1)} %get-tuple-element.117), channel_id=1, source_target_pairs={{0,16},{8,24},{16,0},{24,8},{1,17},{9,25},{17,1},{25,9},{2,18},{10... | collective-permute-start | bytes 786440 | tf_op jit(solution)/shard_map/ppermute | solution.py:641
  40.1 15.0 %collective-permute-start.5 = (bf16[128,1024]{1,0:T(8,128)(2,1)S(1)}, bf16[128,1024]{1,0:T(8,128)(2,1)S(1)}, u32[]{:S(2)}, u32[]{:S(2)}) collective-permute-start(bf16[128,1024]{1,0:T(8,128)(2,1)S(1)} %tie.8), channel_id=1, source_target_pairs={{0,24},{8,16},{16,8},{24,0},{1,25},{9,17},{17,9},{25,1},{2,26},{10... | collective-permute-start | bytes 786440 | tf_op jit(solution)/shard_map/ppermute | solution.py:641
  41.7 15.1 %copy-start.2 = (f32[2,8,128]{2,1,0:T(8,128)}, f32[2,8,128]{2,1,0:T(8,128)S(1)}, u32[]{:S(2)}) copy-start(f32[2,8,128]{2,1,0:T(8,128)S(1)} %get-tuple-element.209.box_ref) | copy-start | bytes 24580
  41.7 31.0 %copy-start.4 = (f32[2,8,128]{2,1,0:T(8,128)}, f32[2,8,128]{2,1,0:T(8,128)S(1)}, u32[]{:S(2)}) copy-start(f32[2,8,128]{2,1,0:T(8,128)S(1)} %get-tuple-element.208.box_ref) | copy-start | bytes 24580
  41.7 41.5 %copy-start = (f32[2,8,128]{2,1,0:T(8,128)}, f32[2,8,128]{2,1,0:T(8,128)S(1)}, u32[]{:S(2)}) copy-start(f32[2,8,128]{2,1,0:T(8,128)S(1)} %get-tuple-element.207.box_ref) | copy-start | bytes 24580
  55.1 10.0 %collective-permute-start.14 = (bf16[48,1024]{1,0:T(8,128)(2,1)S(1)}, bf16[48,1024]{1,0:T(8,128)(2,1)S(1)}, u32[]{:S(2)}, u32[]{:S(2)}) collective-permute-start(bf16[48,1024]{1,0:T(8,128)(2,1)S(1)} %tie.10.refs_1_), channel_id=1, source_target_pairs={{0,8},{8,0},{16,24},{24,16},{1,9},{9,1},{17,25},{25,17},{2,10},{10... | collective-permute-start | bytes 294920 | tf_op jit(solution)/shard_map/ppermute | solution.py:641
  61.3 5.3 %collective-permute-start.6 = (bf16[400,1024]{1,0:T(8,128)(2,1)S(1)}, bf16[400,1024]{1,0:T(8,128)(2,1)S(1)}, u32[]{:S(2)}, u32[]{:S(2)}) collective-permute-start(bf16[400,1024]{1,0:T(8,128)(2,1)S(1)} %tie.9.refs_0_), channel_id=1, source_target_pairs={{0,1},{1,0},{2,3},{3,2},{4,5},{5,4},{6,7},{7,6},{8,9},{9,8},{10,11... | collective-permute-start | bytes 2457608 | tf_op jit(solution)/shard_map/ppermute | solution.py:641
  61.4 5.2 %collective-permute-start.12 = (bf16[400,1024]{1,0:T(8,128)(2,1)S(1)}, bf16[400,1024]{1,0:T(8,128)(2,1)S(1)}, u32[]{:S(2)}, u32[]{:S(2)}) collective-permute-start(bf16[400,1024]{1,0:T(8,128)(2,1)S(1)} %collective-permute-done.11.refs_6_), channel_id=1, source_target_pairs={{0,1},{1,0},{2,3},{3,2},{4,5},{5,4},{6,7},{7,6},{8,9},{9,8},{10,11... | collective-permute-start | bytes 2457608 | tf_op jit(solution)/shard_map/ppermute | solution.py:641
  64.6 2.3 %collective-permute-start.10 = (bf16[400,1024]{1,0:T(8,128)(2,1)S(1)}, bf16[400,1024]{1,0:T(8,128)(2,1)S(1)}, u32[]{:S(2)}, u32[]{:S(2)}) collective-permute-start(bf16[400,1024]{1,0:T(8,128)(2,1)S(1)} %collective-permute-done.9.refs_4_), channel_id=1, source_target_pairs={{0,1},{1,0},{2,3},{3,2},{4,5},{5,4},{6,7},{7,6},{8,9},{9,8},{10,11... | collective-permute-start | bytes 2457608 | tf_op jit(solution)/shard_map/ppermute | solution.py:641
  64.7 3.4 %collective-permute-start.8 = (bf16[400,1024]{1,0:T(8,128)(2,1)S(1)}, bf16[400,1024]{1,0:T(8,128)(2,1)S(1)}, u32[]{:S(2)}, u32[]{:S(2)}) collective-permute-start(bf16[400,1024]{1,0:T(8,128)(2,1)S(1)} %collective-permute-done.7.refs_2_), channel_id=1, source_target_pairs={{0,1},{1,0},{2,3},{3,2},{4,5},{5,4},{6,7},{7,6},{8,9},{9,8},{10,11... | collective-permute-start | bytes 2457608 | tf_op jit(solution)/shard_map/ppermute | solution.py:641
  66.3 12.8 %collective-permute-start.15 = (bf16[2,48,1024]{2,1,0:T(8,128)(2,1)S(1)}, bf16[2,48,1024]{2,1,0:T(8,128)(2,1)S(1)}, u32[]{:S(2)}, u32[]{:S(2)}) collective-permute-start(bf16[2,48,1024]{2,1,0:T(8,128)(2,1)S(1)} %get-tuple-element.127.refs_1_), channel_id=1, source_target_pairs={{0,16},{8,24},{16,0},{24,8},{1,17},{9,25},{17,1},{25,9},{2,18},{10... | collective-permute-start | bytes 589832 | tf_op jit(solution)/shard_map/ppermute | solution.py:641
  71.5 18.9 %collective-permute-start.13 = (bf16[256,1024]{1,0:T(8,128)(2,1)S(1)}, bf16[256,1024]{1,0:T(8,128)(2,1)S(1)}, u32[]{:S(2)}, u32[]{:S(2)}) collective-permute-start(bf16[256,1024]{1,0:T(8,128)(2,1)S(1)} %get-tuple-element.126), channel_id=1, source_target_pairs={{0,8},{8,0},{16,24},{24,16},{1,9},{9,1},{17,25},{25,17},{2,10},{10... | collective-permute-start | bytes 1572872 | tf_op jit(solution)/shard_map/ppermute | solution.py:641
  79.7 13.6 %collective-permute-start.20 = (bf16[4,48,1024]{2,1,0:T(8,128)(2,1)S(1)}, bf16[4,48,1024]{2,1,0:T(8,128)(2,1)S(1)}, u32[]{:S(2)}, u32[]{:S(2)}) collective-permute-start(bf16[4,48,1024]{2,1,0:T(8,128)(2,1)S(1)} %bitcast.57), channel_id=1, source_target_pairs={{0,6},{1,7},{2,4},{3,5},{4,2},{5,3},{6,0},{7,1},{8,14},{9,15},{10,... | collective-permute-start | bytes 1179656 | tf_op jit(solution)/shard_map/ppermute | solution.py:641
  82.0 17.8 %collective-permute-start.19 = (bf16[4,48,1024]{2,1,0:T(8,128)(2,1)S(1)}, bf16[4,48,1024]{2,1,0:T(8,128)(2,1)S(1)}, u32[]{:S(2)}, u32[]{:S(2)}) collective-permute-start(bf16[4,48,1024]{2,1,0:T(8,128)(2,1)S(1)} %bitcast.58), channel_id=1, source_target_pairs={{0,4},{1,5},{2,6},{3,7},{4,0},{5,1},{6,2},{7,3},{8,12},{9,13},{10,... | collective-permute-start | bytes 1179656 | tf_op jit(solution)/shard_map/ppermute | solution.py:641
  82.7 17.2 %collective-permute-start.18 = (bf16[4,48,1024]{2,1,0:T(8,128)(2,1)S(1)}, bf16[4,48,1024]{2,1,0:T(8,128)(2,1)S(1)}, u32[]{:S(2)}, u32[]{:S(2)}) collective-permute-start(bf16[4,48,1024]{2,1,0:T(8,128)(2,1)S(1)} %bitcast.59), channel_id=1, source_target_pairs={{0,2},{1,3},{2,0},{3,1},{4,6},{5,7},{6,4},{7,5},{8,10},{9,11},{10,... | collective-permute-start | bytes 1179656 | tf_op jit(solution)/shard_map/ppermute | solution.py:641
  89.5 22.4 %collective-permute-start.17 = (bf16[256,1024]{1,0:T(8,128)(2,1)S(1)}, bf16[256,1024]{1,0:T(8,128)(2,1)S(1)}, u32[]{:S(2)}, u32[]{:S(2)}) collective-permute-start(bf16[256,1024]{1,0:T(8,128)(2,1)S(1)} %get-tuple-element.134), channel_id=1, source_target_pairs={{0,8},{8,0},{16,24},{24,16},{1,9},{9,1},{17,25},{25,17},{2,10},{10... | collective-permute-start | bytes 1572872 | tf_op jit(solution)/shard_map/ppermute | solution.py:641
  91.1 23.5 %collective-permute-start.16 = (bf16[256,1024]{1,0:T(8,128)(2,1)S(1)}, bf16[256,1024]{1,0:T(8,128)(2,1)S(1)}, u32[]{:S(2)}, u32[]{:S(2)}) collective-permute-start(bf16[256,1024]{1,0:T(8,128)(2,1)S(1)} %get-tuple-element.133), channel_id=1, source_target_pairs={{0,16},{8,24},{16,0},{24,8},{1,17},{9,25},{17,1},{25,9},{2,18},{10... | collective-permute-start | bytes 1572872 | tf_op jit(solution)/shard_map/ppermute | solution.py:641
  101.0 9.6 %collective-permute-start.21 = (bf16[4,4,48,1024]{3,2,1,0:T(8,128)(2,1)S(1)}, bf16[4,4,48,1024]{3,2,1,0:T(8,128)(2,1)S(1)}, u32[]{:S(2)}, u32[]{:S(2)}) collective-permute-start(bf16[4,4,48,1024]{3,2,1,0:T(8,128)(2,1)S(1)} %get-tuple-element.136.refs_1_), channel_id=1, source_target_pairs={{0,1},{1,0},{2,3},{3,2},{4,5},{5,4},{6,7},{7,6},{8,9},{9,8},{10,11... | collective-permute-start | bytes 4718600 | tf_op jit(solution)/shard_map/ppermute | solution.py:641
  110.6 4.0 %copy-start.8 = (f32[2,128,4]{1,2,0:T(4,128)S(1)}, f32[2,128,4]{1,2,0:T(4,128)}, u32[]{:S(2)}) copy-start(f32[2,128,4]{1,2,0:T(4,128)} %param.23) | copy-start | bytes 12292
  110.6 4.0 %copy-start.9 = (f32[1024]{0:T(1024)S(1)}, f32[1024]{0:T(1024)}, u32[]{:S(2)}) copy-start(f32[1024]{0:T(1024)} %param.25) | copy-start | bytes 12292
  110.6 4.0 %copy-start.10 = (f32[1024]{0:T(1024)S(1)}, f32[1024]{0:T(1024)}, u32[]{:S(2)}) copy-start(f32[1024]{0:T(1024)} %param.27) | copy-start | bytes 12292
  110.6 4.0 %copy-start.11 = (s32[2,128]{1,0:T(2,128)S(1)}, s32[2,128]{1,0:T(2,128)}, u32[]{:S(2)}) copy-start(s32[2,128]{1,0:T(2,128)} %labels_ref.1) | copy-start | bytes 3076
  110.6 4.1 %copy-start.12 = (s32[2,128]{1,0:T(2,128)S(1)}, s32[2,128]{1,0:T(2,128)}, u32[]{:S(2)}) copy-start(s32[2,128]{1,0:T(2,128)} %ignore_ref.1) | copy-start | bytes 3076
  118.2 22.4 %collective-permute-start.24 = (bf16[256,1024]{1,0:T(8,128)(2,1)S(1)}, bf16[256,1024]{1,0:T(8,128)(2,1)S(1)}, u32[]{:S(2)}, u32[]{:S(2)}) collective-permute-start(bf16[256,1024]{1,0:T(8,128)(2,1)S(1)} %get-tuple-element.141.grad_ref.refs_3_), channel_id=1, source_target_pairs={{0,16},{8,24},{16,0},{24,8},{1,17},{9,25},{17,1},{25,9},{2,18},{10... | collective-permute-start | bytes 1572872 | tf_op jit(solution)/shard_map/ppermute | solution.py:641
  121.5 21.5 %collective-permute-start.22 = (bf16[256,1024]{1,0:T(8,128)(2,1)S(1)}, bf16[256,1024]{1,0:T(8,128)(2,1)S(1)}, u32[]{:S(2)}, u32[]{:S(2)}) collective-permute-start(bf16[256,1024]{1,0:T(8,128)(2,1)S(1)} %get-tuple-element.141.grad_ref.refs_3_), channel_id=1, source_target_pairs={{0,8},{8,0},{16,24},{24,16},{1,9},{9,1},{17,25},{25,17},{2,10},{10... | collective-permute-start | bytes 1572872 | tf_op jit(solution)/shard_map/ppermute | solution.py:641
  124.1 7.2 %collective-permute-start.23 = (bf16[528,1536]{1,0:T(8,128)(2,1)S(1)}, bf16[528,1536]{1,0:T(8,128)(2,1)S(1)}, u32[]{:S(2)}, u32[]{:S(2)}) collective-permute-start(bf16[528,1536]{1,0:T(8,128)(2,1)S(1)} %get-tuple-element.150), channel_id=1, source_target_pairs={{0,1},{1,0},{2,3},{3,2},{4,5},{5,4},{6,7},{7,6},{8,9},{9,8},{10,11... | collective-permute-start | bytes 4866056 | tf_op jit(solution)/shard_map/ppermute | solution.py:641
  133.4 31.2 %collective-permute-start.27 = (bf16[144,1536]{1,0:T(8,128)(2,1)}, bf16[144,1536]{1,0:T(8,128)(2,1)}, u32[]{:S(2)}, u32[]{:S(2)}) collective-permute-start(bf16[144,1536]{1,0:T(8,128)(2,1)} %get-tuple-element.164), channel_id=1, source_target_pairs={{0,2},{1,3},{2,0},{3,1},{4,6},{5,7},{6,4},{7,5},{8,10},{9,11},{10,... | collective-permute-start | bytes 1327112 | tf_op jit(solution)/shard_map/ppermute | solution.py:641
  134.9 29.7 %collective-permute-start.28 = (bf16[144,1536]{1,0:T(8,128)(2,1)}, bf16[144,1536]{1,0:T(8,128)(2,1)}, u32[]{:S(2)}, u32[]{:S(2)}) collective-permute-start(bf16[144,1536]{1,0:T(8,128)(2,1)} %get-tuple-element.165), channel_id=1, source_target_pairs={{0,4},{1,5},{2,6},{3,7},{4,0},{5,1},{6,2},{7,3},{8,12},{9,13},{10,... | collective-permute-start | bytes 1327112 | tf_op jit(solution)/shard_map/ppermute | solution.py:641
  136.4 28.2 %collective-permute-start.29 = (bf16[144,1536]{1,0:T(8,128)(2,1)}, bf16[144,1536]{1,0:T(8,128)(2,1)}, u32[]{:S(2)}, u32[]{:S(2)}) collective-permute-start(bf16[144,1536]{1,0:T(8,128)(2,1)} %get-tuple-element.166), channel_id=1, source_target_pairs={{0,6},{1,7},{2,4},{3,5},{4,2},{5,3},{6,0},{7,1},{8,14},{9,15},{10,... | collective-permute-start | bytes 1327112 | tf_op jit(solution)/shard_map/ppermute | solution.py:641
  140.5 9.7 %copy-start.5 = (f32[2,8,128]{2,1,0:T(8,128)S(1)}, f32[2,8,128]{2,1,0:T(8,128)}, u32[]{:S(2)}) copy-start(f32[2,8,128]{2,1,0:T(8,128)} %copy-done.4) | copy-start | bytes 24580
  140.5 16.9 %collective-permute-start.25 = (bf16[256,1024]{1,0:T(8,128)(2,1)S(1)}, bf16[256,1024]{1,0:T(8,128)(2,1)S(1)}, u32[]{:S(2)}, u32[]{:S(2)}) collective-permute-start(bf16[256,1024]{1,0:T(8,128)(2,1)S(1)} %tie.11.grad_ref.refs_1_), channel_id=1, source_target_pairs={{0,8},{8,0},{16,24},{24,16},{1,9},{9,1},{17,25},{25,17},{2,10},{10... | collective-permute-start | bytes 1572872 | tf_op jit(solution)/shard_map/ppermute | solution.py:641
  159.0 4.1 %collective-permute-start.30 = (bf16[1,400,1024]{2,1,0:T(8,128)(2,1)S(1)}, bf16[1,400,1024]{2,1,0:T(8,128)(2,1)S(1)}, u32[]{:S(2)}, u32[]{:S(2)}) collective-permute-start(bf16[1,400,1024]{2,1,0:T(8,128)(2,1)S(1)} %get-tuple-element.167), channel_id=1, source_target_pairs={{0,1},{1,0},{2,3},{3,2},{4,5},{5,4},{6,7},{7,6},{8,9},{9,8},{10,11... | collective-permute-start | bytes 2457608 | tf_op jit(solution)/shard_map/ppermute | solution.py:641
  162.5 7.3 %collective-permute-start.26 = (bf16[3,400,1024]{2,1,0:T(8,128)(2,1)S(1)}, bf16[3,400,1024]{2,1,0:T(8,128)(2,1)S(1)}, u32[]{:S(2)}, u32[]{:S(2)}) collective-permute-start(bf16[3,400,1024]{2,1,0:T(8,128)(2,1)S(1)} %get-tuple-element.162), channel_id=1, source_target_pairs={{0,1},{1,0},{2,3},{3,2},{4,5},{5,4},{6,7},{7,6},{8,9},{9,8},{10,11... | collective-permute-start | bytes 7372808 | tf_op jit(solution)/shard_map/ppermute | solution.py:641
  166.4 13.9 %collective-permute-start.31 = (bf16[80,1536]{1,0:T(8,128)(2,1)S(1)}, bf16[80,1536]{1,0:T(8,128)(2,1)S(1)}, u32[]{:S(2)}, u32[]{:S(2)}) collective-permute-start(bf16[80,1536]{1,0:T(8,128)(2,1)S(1)} %get-tuple-element.174), channel_id=1, source_target_pairs={{0,16},{8,24},{16,0},{24,8},{1,17},{9,25},{17,1},{25,9},{2,18},{10... | collective-permute-start | bytes 737288 | tf_op jit(solution)/shard_map/ppermute | solution.py:641
  168.1 22.0 %collective-permute-start.32 = (bf16[400,1024]{1,0:T(8,128)(2,1)S(1)}, bf16[400,1024]{1,0:T(8,128)(2,1)S(1)}, u32[]{:S(2)}, u32[]{:S(2)}) collective-permute-start(bf16[400,1024]{1,0:T(8,128)(2,1)S(1)} %get-tuple-element.180), channel_id=1, source_target_pairs={{0,6},{1,7},{2,4},{3,5},{4,2},{5,3},{6,0},{7,1},{8,14},{9,15},{10,... | collective-permute-start | bytes 2457608 | tf_op jit(solution)/shard_map/ppermute | solution.py:641
  169.8 3.3 %copy-start.3 = (f32[2,8,128]{2,1,0:T(8,128)S(1)}, f32[2,8,128]{2,1,0:T(8,128)}, u32[]{:S(2)}) copy-start(f32[2,8,128]{2,1,0:T(8,128)} %copy-done.2) | copy-start | bytes 24580
  180.9 6.1 %collective-permute-start.33 = (bf16[48,1536]{1,0:T(8,128)(2,1)S(1)}, bf16[48,1536]{1,0:T(8,128)(2,1)S(1)}, u32[]{:S(2)}, u32[]{:S(2)}) collective-permute-start(bf16[48,1536]{1,0:T(8,128)(2,1)S(1)} %get-tuple-element.182), channel_id=1, source_target_pairs={{0,8},{8,0},{16,24},{24,16},{1,9},{9,1},{17,25},{25,17},{2,10},{10... | collective-permute-start | bytes 442376 | tf_op jit(solution)/shard_map/ppermute | solution.py:641
  184.1 25.9 %collective-permute-start.35 = (bf16[2,64,1024]{2,1,0:T(8,128)(2,1)S(1)}, bf16[2,64,1024]{2,1,0:T(8,128)(2,1)S(1)}, u32[]{:S(2)}, u32[]{:S(2)}) collective-permute-start(bf16[2,64,1024]{2,1,0:T(8,128)(2,1)S(1)} %get-tuple-element.186), channel_id=1, source_target_pairs={{0,16},{8,24},{16,0},{24,8},{1,17},{9,25},{17,1},{25,9},{2,18},{10... | collective-permute-start | bytes 786440 | tf_op jit(solution)/shard_map/ppermute | solution.py:641
  184.7 21.7 %collective-permute-start.37 = (bf16[400,1024]{1,0:T(8,128)(2,1)S(1)}, bf16[400,1024]{1,0:T(8,128)(2,1)S(1)}, u32[]{:S(2)}, u32[]{:S(2)}) collective-permute-start(bf16[400,1024]{1,0:T(8,128)(2,1)S(1)} %get-tuple-element.189), channel_id=1, source_target_pairs={{0,2},{1,3},{2,0},{3,1},{4,6},{5,7},{6,4},{7,5},{8,10},{9,11},{10,... | collective-permute-start | bytes 2457608 | tf_op jit(solution)/shard_map/ppermute | solution.py:641
  186.0 20.4 %collective-permute-start.38 = (bf16[400,1024]{1,0:T(8,128)(2,1)S(1)}, bf16[400,1024]{1,0:T(8,128)(2,1)S(1)}, u32[]{:S(2)}, u32[]{:S(2)}) collective-permute-start(bf16[400,1024]{1,0:T(8,128)(2,1)S(1)} %get-tuple-element.190), channel_id=1, source_target_pairs={{0,4},{1,5},{2,6},{3,7},{4,0},{5,1},{6,2},{7,3},{8,12},{9,13},{10,... | collective-permute-start | bytes 2457608 | tf_op jit(solution)/shard_map/ppermute | solution.py:641
  190.8 20.5 %collective-permute-start.34 = (bf16[2,64,1024]{2,1,0:T(8,128)(2,1)S(1)}, bf16[2,64,1024]{2,1,0:T(8,128)(2,1)S(1)}, u32[]{:S(2)}, u32[]{:S(2)}) collective-permute-start(bf16[2,64,1024]{2,1,0:T(8,128)(2,1)S(1)} %tie.12), channel_id=1, source_target_pairs={{0,8},{8,0},{16,24},{24,16},{1,9},{9,1},{17,25},{25,17},{2,10},{10... | collective-permute-start | bytes 786440 | tf_op jit(solution)/shard_map/ppermute | solution.py:641
  192.2 14.2 %copy-start.15 = (bf16[416,400]{1,0:T(8,128)(2,1)S(1)}, bf16[416,400]{1,0:T(8,128)(2,1)}, u32[]{:S(2)}) copy-start(bf16[416,400]{1,0:T(8,128)(2,1)} %constant.45.refs_1_) | copy-start | bytes 998404
  192.2 19.1 %collective-permute-start.36 = (bf16[2,64,1024]{2,1,0:T(8,128)(2,1)S(1)}, bf16[2,64,1024]{2,1,0:T(8,128)(2,1)S(1)}, u32[]{:S(2)}, u32[]{:S(2)}) collective-permute-start(bf16[2,64,1024]{2,1,0:T(8,128)(2,1)S(1)} %tie.13), channel_id=1, source_target_pairs={{0,24},{8,16},{16,8},{24,0},{1,25},{9,17},{17,9},{25,1},{2,26},{10... | collective-permute-start | bytes 786440 | tf_op jit(solution)/shard_map/ppermute | solution.py:641
  206.4 4.9 %copy-start.14 = (bf16[1024,1024]{1,0:T(8,128)(2,1)S(1)}, bf16[1024,1024]{1,0:T(8,128)(2,1)}, u32[]{:S(2)}) copy-start(bf16[1024,1024]{1,0:T(8,128)(2,1)} %constant.28.clone.refs_3_.refs_6_) | copy-start | bytes 6291460
  206.4 4.9 %copy-start.19 = (bf16[4,64,256]{2,1,0:T(8,128)(2,1)S(1)}, bf16[4,64,256]{2,1,0:T(8,128)(2,1)}, u32[]{:S(2)}) copy-start(bf16[4,64,256]{2,1,0:T(8,128)(2,1)} %constant.44.refs_2_.refs_5_) | copy-start | bytes 393220
  207.8 8.7 %collective-permute-start.39 = (bf16[104,1024]{1,0:T(8,128)(2,1)S(1)}, bf16[104,1024]{1,0:T(8,128)(2,1)S(1)}, u32[]{:S(2)}, u32[]{:S(2)}) collective-permute-start(bf16[104,1024]{1,0:T(8,128)(2,1)S(1)} %get-tuple-element.194), channel_id=1, source_target_pairs={{0,8},{8,0},{16,24},{24,16},{1,9},{9,1},{17,25},{25,17},{2,10},{10... | collective-permute-start | bytes 638984 | tf_op jit(solution)/shard_map/ppermute | solution.py:641
  209.2 15.2 %collective-permute-start.40 = (bf16[104,1024]{1,0:T(8,128)(2,1)S(1)}, bf16[104,1024]{1,0:T(8,128)(2,1)S(1)}, u32[]{:S(2)}, u32[]{:S(2)}) collective-permute-start(bf16[104,1024]{1,0:T(8,128)(2,1)S(1)} %get-tuple-element.195), channel_id=1, source_target_pairs={{0,16},{8,24},{16,0},{24,8},{1,17},{9,25},{17,1},{25,9},{2,18},{10... | collective-permute-start | bytes 638984 | tf_op jit(solution)/shard_map/ppermute | solution.py:641
  210.0 19.0 %collective-permute-start.41 = (bf16[104,1024]{1,0:T(8,128)(2,1)S(1)}, bf16[104,1024]{1,0:T(8,128)(2,1)S(1)}, u32[]{:S(2)}, u32[]{:S(2)}) collective-permute-start(bf16[104,1024]{1,0:T(8,128)(2,1)S(1)} %get-tuple-element.196), channel_id=1, source_target_pairs={{0,24},{8,16},{16,8},{24,0},{1,25},{9,17},{17,9},{25,1},{2,26},{10... | collective-permute-start | bytes 638984 | tf_op jit(solution)/shard_map/ppermute | solution.py:641
  211.4 17.6 %copy-start.17 = (bf16[392,416]{1,0:T(8,128)(2,1)S(1)}, bf16[392,416]{1,0:T(8,128)(2,1)}, u32[]{:S(2)}) copy-start(bf16[392,416]{1,0:T(8,128)(2,1)} %constant.46.refs_1_) | copy-start | bytes 978436
  (3 other events, 6.1 us)

commit v7 on v6

--- a/solution.py
+++ b/solution.py
@@ -20,6 +20,7 @@
     SAMPLES * POOL
 )
 SMALL_COST = pl.CostEstimate(flops=10**9, bytes_accessed=1, transcendentals=0)
+TINY_COST = pl.CostEstimate(flops=1, bytes_accessed=1, transcendentals=0)
 LARGE_COST = pl.CostEstimate(flops=3 * 10**10, bytes_accessed=1, transcendentals=0)
 f32 = jnp.float32
 bf16 = jnp.bfloat16
@@ -289,7 +290,7 @@
         out_shape=[like(one.shape, one.dtype) for one in arrays],
         input_output_aliases={k: k for k in range(len(arrays))},
         compiler_params=pltpu.CompilerParams(vmem_limit_bytes=2**20),
-        cost_estimate=SMALL_COST,
+        cost_estimate=TINY_COST,
         name="tie",
     )(*arrays, *earlier)
 
@@ -339,12 +340,10 @@
 
 
 def put_biases(biases, refs):
-    high = biases.astype(bf16)
-    low = (biases - high.astype(f32)).astype(bf16)
+    high = biases.astype(bf16).astype(f32)
+    both = jnp.concatenate([high, biases - high], axis=0).astype(bf16)
     for ref in refs:
-        end = ref.shape[0]
-        ref[end - 16 : end - 8, : high.shape[1]] = high
-        ref[end - 8 : end, : high.shape[1]] = low
+        ref[ref.shape[0] - 16 :, : both.shape[1]] = both
 
 
 def get_biases(ref, units):
@@ -353,7 +352,7 @@
     return last[:8] + last[8:]
 
 
-def small_product_kernel(rows, where_ref, first_ref, second_grad_ref, second_ref, slopes_ref, bias_ref, sent_ref, kept_ref, sign_ref, total_ref):
+def small_product_kernel(rows, where_ref, first_ref, second_grad_ref, second_ref, slopes_ref, first_grad_ref, sent_ref, kept_ref, sign_ref, total_ref, bias_ref):
     turned = (((0,), (0,)), ((), ()))
     units = first_ref.shape[1]
     total_ref[:, :units] = lax.dot_general(
@@ -363,11 +362,12 @@
         second_ref[...], slopes_ref[...], turned, preferred_element_type=f32
     )
     split_rows(where_ref[1] & 1, 1, total_ref, rows, sent_ref, kept_ref)
+    sum_rows([first_grad_ref, second_grad_ref, slopes_ref], bias_ref)
     put_biases(bias_ref[...], [sent_ref, kept_ref])
     sign_ref[...] = jnp.zeros_like(sign_ref)
 
 
-def small_product(where, rows, first_act, second_grad, second_act, slopes, biases):
+def small_product(where, rows, first_act, second_grad, second_act, slopes, first_grad):
     units = first_act.shape[1]
     wide = units + slopes.shape[1]
     half = like((units // 2 + 16, wide), bf16)
@@ -376,11 +376,11 @@
         in_specs=[SCALAR] + [WHOLE] * 5,
         out_specs=[WHOLE] * 3,
         out_shape=[half, half, SIGN],
-        scratch_shapes=[pltpu.VMEM((units, wide), f32)],
+        scratch_shapes=[pltpu.VMEM((units, wide), f32), pltpu.VMEM((8, units), f32)],
         compiler_params=pltpu.CompilerParams(vmem_limit_bytes=24 * 2**20),
         cost_estimate=LARGE_COST,
         name="small_product",
-    )(where, first_act, second_grad, second_act, slopes, biases)
+    )(where, first_act, second_grad, second_act, slopes, first_grad)
 
 
 def quarter_kernel(rows, where_ref, kept_ref, come_ref, *refs):
@@ -452,7 +452,7 @@
 
 def head_kernel(
     own_ref, one_ref, two_ref, labels_ref, ignore_ref, targets_ref, hidden_bias_ref, inner_ref, inner_bias_ref, heads_ref, heads_bias_ref,
-    logits_ref, deltas_ref, first_act_ref, second_act_ref, slopes_ref, second_grad_ref, first_grad_ref, bias_ref, first_slope_ref, second_slope_ref,
+    heads_out_ref, first_act_ref, second_act_ref, slopes_ref, second_grad_ref, first_grad_ref, first_slope_ref, second_slope_ref,
 ):
     first_pre = own_ref[...] + hidden_bias_ref[...]
     for come_ref in (one_ref, two_ref):
@@ -467,12 +467,10 @@
     act = act.astype(bf16)
     second_act_ref[...] = act
     heads = jnp.dot(act, heads_ref[...], preferred_element_type=f32) + heads_bias_ref[...]
+    heads_out_ref[...] = heads
     logits, deltas = heads[:, :LANES], heads[:, LANES:]
     facts = []
     for n in range(labels_ref.shape[0]):
-        rows = slice(n * LANES, (n + 1) * LANES)
-        logits_ref[:, n, :] = logits[rows].T[:CLS]
-        deltas_ref[n] = deltas[rows].T[:BOX]
         fact = [labels_ref[n : n + 1, :].astype(f32), ignore_ref[n : n + 1, :].astype(f32)]
         fact += [targets_ref[n], jnp.zeros((2, LANES), f32)]
         facts.append(jnp.concatenate(fact, axis=0).T)
@@ -506,30 +504,38 @@
     act_grad = lax.dot_general(second_grad, inner_ref[...], turned, preferred_element_type=f32)
     first_grad = (act_grad * first_slope_ref[...]).astype(bf16)
     first_grad_ref[...] = first_grad
-    units = first_grad.shape[1]
-    bias_ref[...] = jnp.zeros_like(bias_ref)
-    bias_ref[0:1, :] = jnp.sum(first_grad.astype(f32), axis=0, keepdims=True)
-    bias_ref[1:2, :] = jnp.sum(second_grad.astype(f32), axis=0, keepdims=True)
-    bias_ref[2:3, : slopes.shape[1]] = jnp.sum(slopes.astype(f32), axis=0, keepdims=True)
+
+
+def sum_rows(refs, out_ref):
+    out_ref[...] = jnp.zeros_like(out_ref)
+    for k, ref in enumerate(refs):
+        out_ref[k : k + 1, : ref.shape[1]] = jnp.sum(ref[...].astype(f32), axis=0, keepdims=True)
+
+
+def row_outputs_kernel(where, arrays, outs):
+    heads_ref, first_grad_ref, second_grad_ref, slopes_ref = arrays
+    logits_ref, deltas_ref, bias_ref = outs
+    for n in range(deltas_ref.shape[0]):
+        rows = slice(n * LANES, (n + 1) * LANES)
+        logits_ref[:, n, :] = heads_ref[rows, :LANES].T[:CLS]
+        deltas_ref[n] = heads_ref[rows, LANES:].T[:BOX]
+    sum_rows([first_grad_ref, second_grad_ref, slopes_ref], bias_ref)
 
 
 def head_block(own, come, labels, ignore, targets, hidden_bias, inner, inner_bias, heads, heads_bias):
     count, units = own.shape
     wide = heads.shape[1]
-    images = labels.shape[0]
     return pl.pallas_call(
         head_kernel,
         in_specs=[pl.BlockSpec(memory_space=pltpu.VMEM)] * 11,
-        out_specs=[pl.BlockSpec(memory_space=pltpu.VMEM)] * 8,
+        out_specs=[pl.BlockSpec(memory_space=pltpu.VMEM)] * 6,
         out_shape=[
-            like((CLS, images, LANES), f32),
-            like((images, BOX, LANES), f32),
+            like((count, wide), f32),
             like((count, units), bf16),
             like((count, units), bf16),
             like((count, wide), bf16),
             like((count, units), bf16),
             like((count, units), bf16),
-            like((8, units), f32),
         ],
         scratch_shapes=[pltpu.VMEM((count, units), f32)] * 2,
         compiler_params=pltpu.CompilerParams(vmem_limit_bytes=24 * 2**20),
@@ -907,7 +913,7 @@
         smalls = lax.all_gather(small, AXES, axis=0, tiled=True)
         full_inner, full_heads = smalls[:, :units], smalls[:, units:]
 
-    logits, deltas, first_act, second_act, slopes, second_grad, first_grad, bias_sums = head_block(
+    head_rows, first_act, second_act, slopes, second_grad, first_grad = head_block(
         own,
         came_sums,
         labels,
@@ -934,7 +940,7 @@
     if direct:
         count = small.shape[0]
         sent, kept, sign = small_product(
-            where, count, first_act, second_grad, second_act, slopes, bias_sums
+            where, count, first_act, second_grad, second_act, slopes, first_grad
         )
         sign = take_up(0, [sign])
         *quarters, sign = quarter_rows(count, where, kept, swap(sent, "img", 1), [sign])
@@ -990,11 +996,11 @@
             [kept, swap(sent, "level", 1)],
             [sign],
             name="small_sum",
-            cost=SMALL_COST,
+            cost=TINY_COST,
         )
         back[3] = tie(back[3:], sign)[0]
         half, sign = call(
-            add_kernel, [like(parts[0].shape, f32)], where, [parts[0], parts[6]], [sign], name="add", cost=SMALL_COST
+            add_kernel, [like(parts[0].shape, f32)], where, [parts[0], parts[6]], [sign], name="add", cost=TINY_COST
         )
         back[1] = tie(back[1:2], sign)[0]
         *out, sign = call(
@@ -1017,7 +1023,6 @@
             shares,
             name="arrange_back",
         )
-        bias_total = butterfly(bias_sums)
         small_sum = jnp.concatenate(
             [contract_rows(first_act, second_grad), contract_rows(second_act, slopes)], axis=1
         )
@@ -1047,6 +1052,18 @@
         name="maps_back",
     )
     map_grads = map_grads.reshape(1, images, height, width, channels)
+    logits, deltas, bias_sums, unused = call(
+        row_outputs_kernel,
+        [
+            like((CLS, images, LANES), f32),
+            like((images, BOX, LANES), f32),
+            like((8, units), f32),
+        ],
+        where,
+        [head_rows, first_grad, second_grad, slopes],
+        [sign],
+        name="row_outputs",
+    )
     if direct:
         hidden_sum = call(
             join_span_kernel,
@@ -1058,6 +1075,8 @@
             name="join_span",
         )[0]
 
+    if not direct:
+        bias_total = butterfly(bias_sums)
     head_bias = bias_total[2, : class_room + delta_room]
     return (
         jnp.transpose(logits, (1, 2, 0)),

time: 235 us -> 235 us (level)
    pallas_call x17 -> x18, Pallas kernels: 25.6 us -> 27 us  [call(): pl.pallas_call(body, in_specs=[SCALAR] + [WHOLE for one in arrays] + [FAR...]
where the time goes in v7:
time: 235 us; the launch traced here: 231 us
  Pallas kernels  103 us (44%)
  waiting for transfers between devices  78.4 us (33%)
  starting transfers between devices  44.3 us (19%)
  local copies, waits for them, and re-layouts  3.14 us (1%)
    ppermute x42, waiting for transfers between devices, swap(): return lax.ppermute(array, axis, [(at, at ^ bit) for at in range(size)])  78.4 us
    ppermute x42, starting transfers between devices, swap(): return lax.ppermute(array, axis, [(at, at ^ bit) for at in range(size)])  44.3 us
    pallas_call x4, Pallas kernels, spread_block(): pl.pallas_call(functools.partial(spread_kernel, table, sizes), in_specs=[...  28.7 us
    pallas_call x18, Pallas kernels, call(): pl.pallas_call(body, in_specs=[SCALAR] + [WHOLE for one in arrays] + [FAR...  27 us
    pallas_call x4, Pallas kernels, crop_block(): pl.pallas_call(functools.partial(crop_kernel, table, sizes, product), gri...  26.7 us
    pallas_call x4, Pallas kernels, piece_product(): pl.pallas_call(functools.partial(product_kernel, bits, len(grads), with_s...  9.87 us
  transfers between devices with their start and end apart: 42, of which 18 were waited for; matrix products, arithmetic and copies ran while one was open for 1% of the time, Pallas kernels for 41%

profile of v7, /device:TPU:8, one launch (start us, length us, event | category | flops | bytes accessed | tf_op | source)
XLA Modules:
  0.0 231.4 jit_solution(13532814226685014968)
XLA Ops:
  1.6 1.1 copy-done.7
  2.8 1.2 split_span.1
  4.1 3.0 %collective-permute-start.1 = (bf16[104,1024]{1,0:T(8,128)(2,1)S(1)}, bf16[104,1024]{1,0:T(8,128)(2,1)S(1)}, u32[]{:S(2)}, u32[]{:S(2)}) collective-permute-start(bf16[104,1024]{1,0:T(8,128)(2,1)S(1)} %get-tuple-element.109), channel_id=1, source_target_pairs={{0,16},{8,24},{16,0},{24,8},{1,17},{9,25},{17,1},{25,9},{2,18},{10... | collective-permute-start | bytes 638984 | tf_op jit(solution)/shard_map/ppermute | solution.py:647
  7.7 2.5 %maps.1 = (bf16[128,1024]{1,0:T(8,128)(2,1)S(1)}, bf16[128,1024]{1,0:T(8,128)(2,1)S(1)}, bf16[128,1024]{1,0:T(8,128)(2,1)S(1)}, bf16[128,1024]{1,0:T(8,128)(2,1)S(1)}, f32[8,128]{1,0:T(8,128)}) custom-call(s32[2]{0:T(128)S(1)} %pad_add_fusion.refs_0_.where_ref, bf16[2,1024,256]{2,1,0:T(8,128)(2,1)S(1)} %bitcast.56, bf16[4,64,256]{2,1,0:T(8,128)(2,1)S(1)} %copy-done.18, ...), custom_call_target="tpu_custom_call" | custom-call | flops 30000001024 | bytes 1 | tf_op jit(solution)/shard_map/maps/pallas_call | solution.py:269
  10.2 2.5 %collective-permute-done.refs_3_ = bf16[104,1024]{1,0:T(8,128)(2,1)S(1)} collective-permute-done((bf16[104,1024]{1,0:T(8,128)(2,1)S(1)}, bf16[104,1024]{1,0:T(8,128)(2,1)S(1)}, u32[]{:S(2)}, u32[]{:S(2)}) %collective-permute-start) | collective-permute-done | bytes 213024 | tf_op jit(solution)/shard_map/ppermute | solution.py:647
  12.7 9.2 %collective-permute-done.1.refs_4_ = bf16[104,1024]{1,0:T(8,128)(2,1)S(1)} collective-permute-done((bf16[104,1024]{1,0:T(8,128)(2,1)S(1)}, bf16[104,1024]{1,0:T(8,128)(2,1)S(1)}, u32[]{:S(2)}, u32[]{:S(2)}) %collective-permute-start.1) | collective-permute-done | bytes 213024 | tf_op jit(solution)/shard_map/ppermute | solution.py:647
  22.0 4.1 %collective-permute-done.2.refs_5_ = bf16[104,1024]{1,0:T(8,128)(2,1)S(1)} collective-permute-done((bf16[104,1024]{1,0:T(8,128)(2,1)S(1)}, bf16[104,1024]{1,0:T(8,128)(2,1)S(1)}, u32[]{:S(2)}, u32[]{:S(2)}) %collective-permute-start.2) | collective-permute-done | bytes 213024 | tf_op jit(solution)/shard_map/ppermute | solution.py:647
  26.0 1.2 join_span.2
  27.3 2.5 %collective-permute-start.11 = (bf16[400,1024]{1,0:T(8,128)(2,1)S(1)}, bf16[400,1024]{1,0:T(8,128)(2,1)S(1)}, u32[]{:S(2)}, u32[]{:S(2)}) collective-permute-start(bf16[400,1024]{1,0:T(8,128)(2,1)S(1)} %get-tuple-element.122), channel_id=1, source_target_pairs={{0,6},{1,7},{2,4},{3,5},{4,2},{5,3},{6,0},{7,1},{8,14},{9,15},{10,... | collective-permute-start | bytes 2457608 | tf_op jit(solution)/shard_map/ppermute | solution.py:647
  30.9 3.1 %collective-permute-start.4 = (bf16[128,1024]{1,0:T(8,128)(2,1)S(1)}, bf16[128,1024]{1,0:T(8,128)(2,1)S(1)}, u32[]{:S(2)}, u32[]{:S(2)}) collective-permute-start(bf16[128,1024]{1,0:T(8,128)(2,1)S(1)} %get-tuple-element.117), channel_id=1, source_target_pairs={{0,16},{8,24},{16,0},{24,8},{1,17},{9,25},{17,1},{25,9},{2,18},{10... | collective-permute-start | bytes 786440 | tf_op jit(solution)/shard_map/ppermute | solution.py:647
  34.0 6.1 %collective-permute-done.3.refs_1_.refs_2_ = bf16[128,1024]{1,0:T(8,128)(2,1)S(1)} collective-permute-done((bf16[128,1024]{1,0:T(8,128)(2,1)S(1)}, bf16[128,1024]{1,0:T(8,128)(2,1)S(1)}, u32[]{:S(2)}, u32[]{:S(2)}) %collective-permute-start.3) | collective-permute-done | bytes 262176 | tf_op jit(solution)/shard_map/ppermute | solution.py:647
  40.1 1.6 collective-permute-start.5
  41.7 13.4 %collective-permute-done.5.refs_4_.refs_1_ = bf16[128,1024]{1,0:T(8,128)(2,1)S(1)} collective-permute-done((bf16[128,1024]{1,0:T(8,128)(2,1)S(1)}, bf16[128,1024]{1,0:T(8,128)(2,1)S(1)}, u32[]{:S(2)}, u32[]{:S(2)}) %collective-permute-start.5) | collective-permute-done | bytes 262176 | tf_op jit(solution)/shard_map/ppermute | solution.py:647
  55.1 1.7 arrange.1
  56.8 4.5 %crop_block.4 = (bf16[3200,256]{1,0:T(8,128)(2,1)S(1)}, bf16[256,3200]{1,0:T(8,128)(2,1)S(1)}, f32[8,128]{1,0:T(8,128)S(1)}) custom-call(f32[2,8,128]{2,1,0:T(8,128)S(1)} %get-tuple-element.209.box_ref, bf16[2,1024,256]{2,1,0:T(8,128)(2,1)S(1)} %get-tuple-element.119.maps_ref), custom_call_target="tpu_custom_call" | custom-call | flops 30000001024 | bytes 1 | tf_op jit(solution)/shard_map/crop_block/pallas_call | solution.py:193
  61.9 2.8 %collective-permute-done.9.refs_4_ = bf16[400,1024]{1,0:T(8,128)(2,1)S(1)} collective-permute-done((bf16[400,1024]{1,0:T(8,128)(2,1)S(1)}, bf16[400,1024]{1,0:T(8,128)(2,1)S(1)}, u32[]{:S(2)}, u32[]{:S(2)}) %collective-permute-start.9) | collective-permute-done | bytes 819232 | tf_op jit(solution)/shard_map/ppermute | solution.py:647
  65.1 1.1 pair_up.2
  67.0 1.2 collective-permute-done.8.refs_3_
  68.1 1.4 gather_pieces.1.weight_ref.refs_0_
  69.6 2.0 multiply.1
  71.5 1.3 collective-permute-start.13
  72.8 6.3 %crop_block.5 = (bf16[3200,256]{1,0:T(8,128)(2,1)S(1)}, f32[256,1024]{1,0:T(8,128)S(1)}, f32[8,128]{1,0:T(8,128)S(1)}) custom-call(f32[2,8,128]{2,1,0:T(8,128)S(1)} %get-tuple-element.208.box_ref, bf16[2,1024,256]{2,1,0:T(8,128)(2,1)S(1)} %get-tuple-element.119.maps_ref, bf16[3200,1024]{1,0:T(8,128)(2,1)S(1)} %gather_pieces.1.weight_ref.refs_0_, ...), custom_call_target="tpu_custom_call" | custom-call | flops 30000001024 | bytes 1 | tf_op jit(solution)/shard_map/crop_block/pallas_call | solution.py:193
  79.7 2.4 %collective-permute-start.20 = (bf16[4,48,1024]{2,1,0:T(8,128)(2,1)S(1)}, bf16[4,48,1024]{2,1,0:T(8,128)(2,1)S(1)}, u32[]{:S(2)}, u32[]{:S(2)}) collective-permute-start(bf16[4,48,1024]{2,1,0:T(8,128)(2,1)S(1)} %bitcast.57), channel_id=1, source_target_pairs={{0,6},{1,7},{2,4},{3,5},{4,2},{5,3},{6,0},{7,1},{8,14},{9,15},{10,... | collective-permute-start | bytes 1179656 | tf_op jit(solution)/shard_map/ppermute | solution.py:647
  83.3 6.3 %crop_block.6 = (bf16[3200,256]{1,0:T(8,128)(2,1)S(1)}, bf16[256,1024]{1,0:T(8,128)(2,1)S(1)}, f32[8,128]{1,0:T(8,128)S(1)}) custom-call(f32[2,8,128]{2,1,0:T(8,128)S(1)} %get-tuple-element.207.box_ref, bf16[2,1024,256]{2,1,0:T(8,128)(2,1)S(1)} %get-tuple-element.119.maps_ref, bf16[3200,1024]{1,0:T(8,128)(2,1)S(1)} %gather_pieces.1.weight_ref.refs_0_, ...), custom_call_target="tpu_custom_call" | custom-call | flops 1000000000 | bytes 1 | tf_op jit(solution)/shard_map/crop_block/pallas_call | solution.py:193
  91.1 2.1 collective-permute-start.16
  93.2 6.6 %collective-permute-done.19.refs_3_ = bf16[4,48,1024]{2,1,0:T(8,128)(2,1)S(1)} collective-permute-done((bf16[4,48,1024]{2,1,0:T(8,128)(2,1)S(1)}, bf16[4,48,1024]{2,1,0:T(8,128)(2,1)S(1)}, u32[]{:S(2)}, u32[]{:S(2)}) %collective-permute-start.19) | collective-permute-done | bytes 393248 | tf_op jit(solution)/shard_map/ppermute | solution.py:647
  99.9 1.1 in_order.1
  101.1 9.6 %crop_block.7 = (bf16[3200,256]{1,0:T(8,128)(2,1)S(1)}, f32[256,1024]{1,0:T(8,128)S(1)}, f32[8,128]{1,0:T(8,128)}) custom-call(f32[2,8,128]{2,1,0:T(8,128)S(1)} %get-tuple-element.210.box_ref, bf16[2,1024,256]{2,1,0:T(8,128)(2,1)S(1)} %get-tuple-element.119.maps_ref, bf16[3200,1024]{1,0:T(8,128)(2,1)S(1)} %gather_pieces.1.weight_ref.refs_0_, ...), custom_call_target="tpu_custom_call" | custom-call | flops 30000001024 | bytes 1 | tf_op jit(solution)/shard_map/crop_block/pallas_call | solution.py:193
  110.7 1.3 full_small.1
  112.0 2.7 %collective-permute-done.16.one_ref = bf16[256,1024]{1,0:T(8,128)(2,1)S(1)} collective-permute-done((bf16[256,1024]{1,0:T(8,128)(2,1)S(1)}, bf16[256,1024]{1,0:T(8,128)(2,1)S(1)}, u32[]{:S(2)}, u32[]{:S(2)}) %collective-permute-start.16) | collective-permute-done | bytes 524320 | tf_op jit(solution)/shard_map/ppermute | solution.py:647
  114.7 2.6 %head_block.1 = (f32[256,512]{1,0:T(8,128)S(1)}, bf16[256,1024]{1,0:T(8,128)(2,1)S(1)}, bf16[256,1024]{1,0:T(8,128)(2,1)S(1)}, bf16[256,512]{1,0:T(8,128)(2,1)S(...) custom-call(f32[256,1024]{1,0:T(8,128)S(1)} %get-tuple-element.132.own_ref, ...), custom_call_target="tpu_custom_call" | custom-call | flops 30000001024 | bytes 1 | tf_op jit(solution)/shard_map/head_block/pallas_call | solution.py:528
  117.3 3.3 %collective-permute-start.24 = (bf16[256,1024]{1,0:T(8,128)(2,1)S(1)}, bf16[256,1024]{1,0:T(8,128)(2,1)S(1)}, u32[]{:S(2)}, u32[]{:S(2)}) collective-permute-start(bf16[256,1024]{1,0:T(8,128)(2,1)S(1)} %get-tuple-element.140.first_grad_ref.grad_ref.refs_3_.refs_2_), channel_id=1, source_target_pairs={{0,16},{8,24},{16,0},{24,8},{1,17},{9,25},{17,1},{25,9},{2,18},{10... | collective-permute-start | bytes 1572872 | tf_op jit(solution)/shard_map/ppermute | solution.py:647
  120.7 2.8 %small_product.1 = (bf16[528,1536]{1,0:T(8,128)(2,1)S(1)}, bf16[528,1536]{1,0:T(8,128)(2,1)S(1)}, f32[8,128]{1,0:T(8,128)S(1)}) custom-call(s32[2]{0:T(128)S(1)} %pad_add_fusion.refs_0_.where_ref, bf16[256,1024]{1,0:T(8,128)(2,1)S(1)} %get-tuple-element.143.first_ref, bf16[256,1024]{1,0:T(8,128)(2,1)S(1)} %get-tuple-element.141.second_grad_ref.refs_3_, ...), custom_call_target="tpu_custom_call" | custom-call | flops 30000001024 | bytes 1 | tf_op jit(solution)/shard_map/small_product/pallas_call | solution.py:374
  123.5 7.1 %spread_block.4 = (bf16[2,1024,256]{2,1,0:T(8,128)(2,1)S(1)}, f32[8,128]{1,0:T(8,128)S(1)}) custom-call(f32[2,8,128]{2,1,0:T(8,128)S(1)} %get-tuple-element.210.box_ref, bf16[256,1024]{1,0:T(8,128)(2,1)S(1)} %get-tuple-element.140.first_grad_ref.grad_ref.refs_3_.refs_2_, bf16[3200,1024]{1,0:T(8,128)(2,1)S(1)} %gather_pieces.1.weight_ref.refs_0_, ...), custom_call_target="tpu_custom_call" | custom-call | flops 30000001024 | bytes 1 | tf_op jit(solution)/shard_map/spread_block/pallas_call | solution.py:242
  130.7 2.2 quarter_rows.1
  132.8 1.5 collective-permute-start.27
  134.3 1.5 collective-permute-start.28
  136.3 3.4 %collective-permute-done.24.refs_0_ = bf16[256,1024]{1,0:T(8,128)(2,1)S(1)} collective-permute-done((bf16[256,1024]{1,0:T(8,128)(2,1)S(1)}, bf16[256,1024]{1,0:T(8,128)(2,1)S(1)}, u32[]{:S(2)}, u32[]{:S(2)}) %collective-permute-start.24) | collective-permute-done | bytes 524320 | tf_op jit(solution)/shard_map/ppermute | solution.py:647
  139.7 2.4 %collective-permute-start.25 = (bf16[256,1024]{1,0:T(8,128)(2,1)S(1)}, bf16[256,1024]{1,0:T(8,128)(2,1)S(1)}, u32[]{:S(2)}, u32[]{:S(2)}) collective-permute-start(bf16[256,1024]{1,0:T(8,128)(2,1)S(1)} %tie.11.grad_ref.refs_1_), channel_id=1, source_target_pairs={{0,8},{8,0},{16,24},{24,16},{1,9},{9,1},{17,25},{25,17},{2,10},{10... | collective-permute-start | bytes 1572872 | tf_op jit(solution)/shard_map/ppermute | solution.py:647
  142.2 7.3 %spread_block.5 = (bf16[2,1024,256]{2,1,0:T(8,128)(2,1)S(1)}, f32[8,128]{1,0:T(8,128)S(1)}) custom-call(f32[2,8,128]{2,1,0:T(8,128)S(1)} %copy-done.1, bf16[256,1024]{1,0:T(8,128)(2,1)S(1)} %collective-permute-done.22.grad_ref.refs_2_, bf16[3200,1024]{1,0:T(8,128)(2,1)S(1)} %gather_pieces.1.weight_ref.refs_0_, f32[8,128]{1,0:T(8,128)S(1)} %get-tuple-element.150.refs_0_.refs_1_), custom_call_target="tpu_custom_call" | custom-call | flops 30000001024 | bytes 1 | tf_op jit(solution)/shard_map/spread_block/pallas_call | solution.py:242
  149.5 7.1 %spread_block.6 = (bf16[2,1024,256]{2,1,0:T(8,128)(2,1)S(1)}, f32[8,128]{1,0:T(8,128)S(1)}) custom-call(f32[2,8,128]{2,1,0:T(8,128)S(1)} %copy-done.5, bf16[256,1024]{1,0:T(8,128)(2,1)S(1)} %tie.11.grad_ref.refs_1_, bf16[3200,1024]{1,0:T(8,128)(2,1)S(1)} %gather_pieces.1.weight_ref.refs_0_, f32[8,128]{1,0:T(8,128)S(1)} %get-tuple-element.152.refs_0_), custom_call_target="tpu_custom_call" | custom-call | flops 30000001024 | bytes 1 | tf_op jit(solution)/shard_map/spread_block/pallas_call | solution.py:242
  156.6 1.6 piece_product.4
  158.3 3.5 %piece_product.5 = (bf16[3,400,1024]{2,1,0:T(8,128)(2,1)S(1)}, f32[8,128]{1,0:T(8,128)S(1)}) custom-call(s32[2]{0:T(128)S(1)} %pad_add_fusion.refs_0_.where_ref, bf16[256,1024]{1,0:T(8,128)(2,1)S(1)} %collective-permute-done.25.refs_0_.grad_ref, bf16[256,1024]{1,0:T(8,128)(2,1)S(1)} %tie.11.grad_ref.refs_1_, ...), custom_call_target="tpu_custom_call" | custom-call | flops 30000001024 | bytes 1 | tf_op jit(solution)/shard_map/piece_product/pallas_call | solution.py:685
  162.3 1.6 piece_product.6
  163.9 1.7 halve_rows.2
  165.6 1.0 collective-permute-start.31
  166.6 1.8 collective-permute-start.32
  168.4 3.3 %piece_product.7 = (bf16[400,1024]{1,0:T(8,128)(2,1)S(1)}, bf16[400,1024]{1,0:T(8,128)(2,1)S(1)}, bf16[400,1024]{1,0:T(8,128)(2,1)S(1)}, f32[8,128]{1,0:T(8,128)S(1)}) custom-call(s32[2]{0:T(128)S(1)} %pad_add_fusion.refs_0_.where_ref, bf16[256,1024]{1,0:T(8,128)(2,1)S(1)} %collective-permute-done.25.refs_0_.grad_ref, ...), custom_call_target="tpu_custom_call" | custom-call | flops 30000001024 | bytes 1 | tf_op jit(solution)/shard_map/piece_product/pallas_call | solution.py:685
  171.7 7.1 %spread_block.7 = (bf16[2,1024,256]{2,1,0:T(8,128)(2,1)S(1)}, f32[8,128]{1,0:T(8,128)S(1)}) custom-call(f32[2,8,128]{2,1,0:T(8,128)S(1)} %copy-done.3, bf16[256,1024]{1,0:T(8,128)(2,1)S(1)} %collective-permute-done.25.refs_0_.grad_ref, bf16[3200,1024]{1,0:T(8,128)(2,1)S(1)} %gather_pieces.1.weight_ref.refs_0_, f32[8,128]{1,0:T(8,128)S(1)} %get-tuple-element.169.refs_0_), custom_call_target="tpu_custom_call" | custom-call | flops 30000001024 | bytes 1 | tf_op jit(solution)/shard_map/spread_block/pallas_call | solution.py:242
  179.5 2.0 collective-permute-start.33
  181.5 1.1 collective-permute-start.37
  183.2 1.7 arrange_back.1
  185.6 1.2 small_sum.1
  186.8 1.9 collective-permute-done.32.refs_2_
  189.5 2.1 collective-permute-start.34
  193.7 11.2 %collective-permute-done.37.refs_3_ = bf16[400,1024]{1,0:T(8,128)(2,1)S(1)} collective-permute-done((bf16[400,1024]{1,0:T(8,128)(2,1)S(1)}, bf16[400,1024]{1,0:T(8,128)(2,1)S(1)}, u32[]{:S(2)}, u32[]{:S(2)}) %collective-permute-start.37) | collective-permute-done | bytes 819232 | tf_op jit(solution)/shard_map/ppermute | solution.py:647
  205.0 1.3 return_span.1
  206.3 2.1 collective-permute-start.39
  208.7 1.2 collective-permute-start.41
  209.9 4.5 %maps_back.1 = (f32[2,1024,256]{2,1,0:T(8,128)}, f32[8,128]{1,0:T(8,128)S(1)}) custom-call(s32[2]{0:T(128)S(1)} %pad_add_fusion.refs_0_.where_ref, bf16[2,64,1024]{2,1,0:T(8,128)(2,1)S(1)} %get-tuple-element.175.refs_1_, bf16[2,64,1024]{2,1,0:T(8,128)(2,1)S(1)} %collective-permute-done.34.refs_2_, bf16[2,64,1024]{2,1,0:T(8,128)(2,1)S(1)} %collective-permute-done.35.refs_3_, ...), custom_call_target="tpu_custom_call" | custom-call | flops 30000001024 | bytes 1 | tf_op jit(solution)/shard_map/maps_back/pallas_call | solution.py:269
  214.4 1.5 row_outputs.1
  216.5 7.1 %collective-permute-done.40.refs_4_ = bf16[104,1024]{1,0:T(8,128)(2,1)S(1)} collective-permute-done((bf16[104,1024]{1,0:T(8,128)(2,1)S(1)}, bf16[104,1024]{1,0:T(8,128)(2,1)S(1)}, u32[]{:S(2)}, u32[]{:S(2)}) %collective-permute-start.40) | collective-permute-done | bytes 213024 | tf_op jit(solution)/shard_map/ppermute | solution.py:647
  223.5 5.2 %collective-permute-done.41.refs_5_ = bf16[104,1024]{1,0:T(8,128)(2,1)S(1)} collective-permute-done((bf16[104,1024]{1,0:T(8,128)(2,1)S(1)}, bf16[104,1024]{1,0:T(8,128)(2,1)S(1)}, u32[]{:S(2)}, u32[]{:S(2)}) %collective-permute-start.41) | collective-permute-done | bytes 213024 | tf_op jit(solution)/shard_map/ppermute | solution.py:647
  228.8 2.4 %join_span.3 = (f32[392,1024]{1,0:T(8,128)}, f32[8,128]{1,0:T(8,128)}) custom-call(s32[2]{0:T(128)S(1)} %pad_add_fusion.refs_0_.where_ref, bf16[392,416]{1,0:T(8,128)(2,1)S(1)} %copy-done.17, bf16[104,1024]{1,0:T(8,128)(2,1)S(1)} %get-tuple-element.194.refs_2_, bf16[104,1024]{1,0:T(8,128)(2,1)S(1)} %collective-permute-done.39.refs_3_, ...), custom_call_target="tpu_custom_call" | custom-call | flops 30000001024 | bytes 1 | tf_op jit(solution)/shard_map/join_span/pallas_call | solution.py:269
  (143 shorter events, 14.9 us)
Async XLA Ops:
  2.7 4.9 %copy-start.25 = (bf16[32,320]{1,0:T(8,128)(2,1)S(1)}, bf16[32,320]{1,0:T(8,128)(2,1)}, u32[]{:S(2)}) copy-start(bf16[32,320]{1,0:T(8,128)(2,1)} %param.30) | copy-start | bytes 61444
  2.7 4.9 %copy-start.26 = (bf16[32,81]{1,0:T(8,128)(2,1)S(1)}, bf16[32,81]{1,0:T(8,128)(2,1)}, u32[]{:S(2)}) copy-start(bf16[32,81]{1,0:T(8,128)(2,1)} %param.28) | copy-start | bytes 15556
  2.7 4.9 %copy-start.27 = (f32[320]{0:T(512)S(1)}, f32[320]{0:T(512)}, u32[]{:S(2)}) copy-start(f32[320]{0:T(512)} %param.31) | copy-start | bytes 3844
  2.7 4.9 %copy-start.28 = (f32[81]{0:T(128)S(1)}, f32[81]{0:T(128)}, u32[]{:S(2)}) copy-start(f32[81]{0:T(128)} %param.29) | copy-start | bytes 976
  2.7 4.9 %copy-start.6 = (bf16[1,2,64,16,256]{4,3,2,1,0:T(8,128)(2,1)S(1)}, bf16[1,2,64,16,256]{4,3,2,1,0:T(8,128)(2,1)}, u32[]{:S(2)}) copy-start(bf16[1,2,64,16,256]{4,3,2,1,0:T(8,128)(2,1)} %param.18) | copy-start | bytes 3145732
  2.8 4.9 %copy-start.13 = (bf16[1024,1024]{1,0:T(8,128)(2,1)S(1)}, bf16[1024,1024]{1,0:T(8,128)(2,1)}, u32[]{:S(2)}) copy-start(bf16[1024,1024]{1,0:T(8,128)(2,1)} %constant.28.clone.refs_3_.refs_6_) | copy-start | bytes 6291460
  2.8 4.9 %copy-start.18 = (bf16[4,64,256]{2,1,0:T(8,128)(2,1)S(1)}, bf16[4,64,256]{2,1,0:T(8,128)(2,1)}, u32[]{:S(2)}) copy-start(bf16[4,64,256]{2,1,0:T(8,128)(2,1)} %constant.44.refs_2_.refs_5_) | copy-start | bytes 393220
  4.0 8.7 %collective-permute-start = (bf16[104,1024]{1,0:T(8,128)(2,1)S(1)}, bf16[104,1024]{1,0:T(8,128)(2,1)S(1)}, u32[]{:S(2)}, u32[]{:S(2)}) collective-permute-start(bf16[104,1024]{1,0:T(8,128)(2,1)S(1)} %get-tuple-element.108), channel_id=1, source_target_pairs={{0,8},{8,0},{16,24},{24,16},{1,9},{9,1},{17,25},{25,17},{2,10},{10... | collective-permute-start | bytes 638984 | tf_op jit(solution)/shard_map/ppermute | solution.py:647
  4.1 17.9 %collective-permute-start.1 = (bf16[104,1024]{1,0:T(8,128)(2,1)S(1)}, bf16[104,1024]{1,0:T(8,128)(2,1)S(1)}, u32[]{:S(2)}, u32[]{:S(2)}) collective-permute-start(bf16[104,1024]{1,0:T(8,128)(2,1)S(1)} %get-tuple-element.109), channel_id=1, source_target_pairs={{0,16},{8,24},{16,0},{24,8},{1,17},{9,25},{17,1},{25,9},{2,18},{10... | collective-permute-start | bytes 638984 | tf_op jit(solution)/shard_map/ppermute | solution.py:647
  7.1 18.9 %collective-permute-start.2 = (bf16[104,1024]{1,0:T(8,128)(2,1)S(1)}, bf16[104,1024]{1,0:T(8,128)(2,1)S(1)}, u32[]{:S(2)}, u32[]{:S(2)}) collective-permute-start(bf16[104,1024]{1,0:T(8,128)(2,1)S(1)} %get-tuple-element.110), channel_id=1, source_target_pairs={{0,24},{8,16},{16,8},{24,0},{1,25},{9,17},{17,9},{25,1},{2,26},{10... | collective-permute-start | bytes 638984 | tf_op jit(solution)/shard_map/ppermute | solution.py:647
  7.7 18.3 %copy-start.16 = (bf16[400,416]{1,0:T(8,128)(2,1)S(1)}, bf16[400,416]{1,0:T(8,128)(2,1)}, u32[]{:S(2)}) copy-start(bf16[400,416]{1,0:T(8,128)(2,1)} %constant.26.clone.refs_1_) | copy-start | bytes 998404
  27.3 34.1 %collective-permute-start.11 = (bf16[400,1024]{1,0:T(8,128)(2,1)S(1)}, bf16[400,1024]{1,0:T(8,128)(2,1)S(1)}, u32[]{:S(2)}, u32[]{:S(2)}) collective-permute-start(bf16[400,1024]{1,0:T(8,128)(2,1)S(1)} %get-tuple-element.122), channel_id=1, source_target_pairs={{0,6},{1,7},{2,4},{3,5},{4,2},{5,3},{6,0},{7,1},{8,14},{9,15},{10,... | collective-permute-start | bytes 2457608 | tf_op jit(solution)/shard_map/ppermute | solution.py:647
  29.8 34.9 %collective-permute-start.9 = (bf16[400,1024]{1,0:T(8,128)(2,1)S(1)}, bf16[400,1024]{1,0:T(8,128)(2,1)S(1)}, u32[]{:S(2)}, u32[]{:S(2)}) collective-permute-start(bf16[400,1024]{1,0:T(8,128)(2,1)S(1)} %get-tuple-element.122), channel_id=1, source_target_pairs={{0,4},{1,5},{2,6},{3,7},{4,0},{5,1},{6,2},{7,3},{8,12},{9,13},{10,... | collective-permute-start | bytes 2457608 | tf_op jit(solution)/shard_map/ppermute | solution.py:647
  30.3 34.4 %collective-permute-start.7 = (bf16[400,1024]{1,0:T(8,128)(2,1)S(1)}, bf16[400,1024]{1,0:T(8,128)(2,1)S(1)}, u32[]{:S(2)}, u32[]{:S(2)}) collective-permute-start(bf16[400,1024]{1,0:T(8,128)(2,1)S(1)} %get-tuple-element.122), channel_id=1, source_target_pairs={{0,2},{1,3},{2,0},{3,1},{4,6},{5,7},{6,4},{7,5},{8,10},{9,11},{10,... | collective-permute-start | bytes 2457608 | tf_op jit(solution)/shard_map/ppermute | solution.py:647
  30.8 9.2 %collective-permute-start.3 = (bf16[128,1024]{1,0:T(8,128)(2,1)S(1)}, bf16[128,1024]{1,0:T(8,128)(2,1)S(1)}, u32[]{:S(2)}, u32[]{:S(2)}) collective-permute-start(bf16[128,1024]{1,0:T(8,128)(2,1)S(1)} %get-tuple-element.116), channel_id=1, source_target_pairs={{0,8},{8,0},{16,24},{24,16},{1,9},{9,1},{17,25},{25,17},{2,10},{10... | collective-permute-start | bytes 786440 | tf_op jit(solution)/shard_map/ppermute | solution.py:647
  30.9 24.2 %collective-permute-start.4 = (bf16[128,1024]{1,0:T(8,128)(2,1)S(1)}, bf16[128,1024]{1,0:T(8,128)(2,1)S(1)}, u32[]{:S(2)}, u32[]{:S(2)}) collective-permute-start(bf16[128,1024]{1,0:T(8,128)(2,1)S(1)} %get-tuple-element.117), channel_id=1, source_target_pairs={{0,16},{8,24},{16,0},{24,8},{1,17},{9,25},{17,1},{25,9},{2,18},{10... | collective-permute-start | bytes 786440 | tf_op jit(solution)/shard_map/ppermute | solution.py:647
  40.1 15.0 %collective-permute-start.5 = (bf16[128,1024]{1,0:T(8,128)(2,1)S(1)}, bf16[128,1024]{1,0:T(8,128)(2,1)S(1)}, u32[]{:S(2)}, u32[]{:S(2)}) collective-permute-start(bf16[128,1024]{1,0:T(8,128)(2,1)S(1)} %tie.8), channel_id=1, source_target_pairs={{0,24},{8,16},{16,8},{24,0},{1,25},{9,17},{17,9},{25,1},{2,26},{10... | collective-permute-start | bytes 786440 | tf_op jit(solution)/shard_map/ppermute | solution.py:647
  41.7 15.1 %copy-start.2 = (f32[2,8,128]{2,1,0:T(8,128)}, f32[2,8,128]{2,1,0:T(8,128)S(1)}, u32[]{:S(2)}) copy-start(f32[2,8,128]{2,1,0:T(8,128)S(1)} %get-tuple-element.209.box_ref) | copy-start | bytes 24580
  41.7 31.1 %copy-start.4 = (f32[2,8,128]{2,1,0:T(8,128)}, f32[2,8,128]{2,1,0:T(8,128)S(1)}, u32[]{:S(2)}) copy-start(f32[2,8,128]{2,1,0:T(8,128)S(1)} %get-tuple-element.208.box_ref) | copy-start | bytes 24580
  41.7 41.5 %copy-start = (f32[2,8,128]{2,1,0:T(8,128)}, f32[2,8,128]{2,1,0:T(8,128)S(1)}, u32[]{:S(2)}) copy-start(f32[2,8,128]{2,1,0:T(8,128)S(1)} %get-tuple-element.207.box_ref) | copy-start | bytes 24580
  55.1 10.0 %collective-permute-start.14 = (bf16[48,1024]{1,0:T(8,128)(2,1)S(1)}, bf16[48,1024]{1,0:T(8,128)(2,1)S(1)}, u32[]{:S(2)}, u32[]{:S(2)}) collective-permute-start(bf16[48,1024]{1,0:T(8,128)(2,1)S(1)} %tie.10.refs_1_), channel_id=1, source_target_pairs={{0,8},{8,0},{16,24},{24,16},{1,9},{9,1},{17,25},{25,17},{2,10},{10... | collective-permute-start | bytes 294920 | tf_op jit(solution)/shard_map/ppermute | solution.py:647
  61.3 5.3 %collective-permute-start.6 = (bf16[400,1024]{1,0:T(8,128)(2,1)S(1)}, bf16[400,1024]{1,0:T(8,128)(2,1)S(1)}, u32[]{:S(2)}, u32[]{:S(2)}) collective-permute-start(bf16[400,1024]{1,0:T(8,128)(2,1)S(1)} %tie.9.refs_0_), channel_id=1, source_target_pairs={{0,1},{1,0},{2,3},{3,2},{4,5},{5,4},{6,7},{7,6},{8,9},{9,8},{10,11... | collective-permute-start | bytes 2457608 | tf_op jit(solution)/shard_map/ppermute | solution.py:647
  61.4 5.2 %collective-permute-start.12 = (bf16[400,1024]{1,0:T(8,128)(2,1)S(1)}, bf16[400,1024]{1,0:T(8,128)(2,1)S(1)}, u32[]{:S(2)}, u32[]{:S(2)}) collective-permute-start(bf16[400,1024]{1,0:T(8,128)(2,1)S(1)} %collective-permute-done.11.refs_6_), channel_id=1, source_target_pairs={{0,1},{1,0},{2,3},{3,2},{4,5},{5,4},{6,7},{7,6},{8,9},{9,8},{10,11... | collective-permute-start | bytes 2457608 | tf_op jit(solution)/shard_map/ppermute | solution.py:647
  64.6 2.3 %collective-permute-start.10 = (bf16[400,1024]{1,0:T(8,128)(2,1)S(1)}, bf16[400,1024]{1,0:T(8,128)(2,1)S(1)}, u32[]{:S(2)}, u32[]{:S(2)}) collective-permute-start(bf16[400,1024]{1,0:T(8,128)(2,1)S(1)} %collective-permute-done.9.refs_4_), channel_id=1, source_target_pairs={{0,1},{1,0},{2,3},{3,2},{4,5},{5,4},{6,7},{7,6},{8,9},{9,8},{10,11... | collective-permute-start | bytes 2457608 | tf_op jit(solution)/shard_map/ppermute | solution.py:647
  64.7 3.4 %collective-permute-start.8 = (bf16[400,1024]{1,0:T(8,128)(2,1)S(1)}, bf16[400,1024]{1,0:T(8,128)(2,1)S(1)}, u32[]{:S(2)}, u32[]{:S(2)}) collective-permute-start(bf16[400,1024]{1,0:T(8,128)(2,1)S(1)} %collective-permute-done.7.refs_2_), channel_id=1, source_target_pairs={{0,1},{1,0},{2,3},{3,2},{4,5},{5,4},{6,7},{7,6},{8,9},{9,8},{10,11... | collective-permute-start | bytes 2457608 | tf_op jit(solution)/shard_map/ppermute | solution.py:647
  66.3 12.8 %collective-permute-start.15 = (bf16[2,48,1024]{2,1,0:T(8,128)(2,1)S(1)}, bf16[2,48,1024]{2,1,0:T(8,128)(2,1)S(1)}, u32[]{:S(2)}, u32[]{:S(2)}) collective-permute-start(bf16[2,48,1024]{2,1,0:T(8,128)(2,1)S(1)} %get-tuple-element.127.refs_1_), channel_id=1, source_target_pairs={{0,16},{8,24},{16,0},{24,8},{1,17},{9,25},{17,1},{25,9},{2,18},{10... | collective-permute-start | bytes 589832 | tf_op jit(solution)/shard_map/ppermute | solution.py:647
  71.5 18.9 %collective-permute-start.13 = (bf16[256,1024]{1,0:T(8,128)(2,1)S(1)}, bf16[256,1024]{1,0:T(8,128)(2,1)S(1)}, u32[]{:S(2)}, u32[]{:S(2)}) collective-permute-start(bf16[256,1024]{1,0:T(8,128)(2,1)S(1)} %get-tuple-element.126), channel_id=1, source_target_pairs={{0,8},{8,0},{16,24},{24,16},{1,9},{9,1},{17,25},{25,17},{2,10},{10... | collective-permute-start | bytes 1572872 | tf_op jit(solution)/shard_map/ppermute | solution.py:647
  79.7 13.5 %collective-permute-start.20 = (bf16[4,48,1024]{2,1,0:T(8,128)(2,1)S(1)}, bf16[4,48,1024]{2,1,0:T(8,128)(2,1)S(1)}, u32[]{:S(2)}, u32[]{:S(2)}) collective-permute-start(bf16[4,48,1024]{2,1,0:T(8,128)(2,1)S(1)} %bitcast.57), channel_id=1, source_target_pairs={{0,6},{1,7},{2,4},{3,5},{4,2},{5,3},{6,0},{7,1},{8,14},{9,15},{10,... | collective-permute-start | bytes 1179656 | tf_op jit(solution)/shard_map/ppermute | solution.py:647
  82.1 17.8 %collective-permute-start.19 = (bf16[4,48,1024]{2,1,0:T(8,128)(2,1)S(1)}, bf16[4,48,1024]{2,1,0:T(8,128)(2,1)S(1)}, u32[]{:S(2)}, u32[]{:S(2)}) collective-permute-start(bf16[4,48,1024]{2,1,0:T(8,128)(2,1)S(1)} %bitcast.58), channel_id=1, source_target_pairs={{0,4},{1,5},{2,6},{3,7},{4,0},{5,1},{6,2},{7,3},{8,12},{9,13},{10,... | collective-permute-start | bytes 1179656 | tf_op jit(solution)/shard_map/ppermute | solution.py:647
  82.7 17.2 %collective-permute-start.18 = (bf16[4,48,1024]{2,1,0:T(8,128)(2,1)S(1)}, bf16[4,48,1024]{2,1,0:T(8,128)(2,1)S(1)}, u32[]{:S(2)}, u32[]{:S(2)}) collective-permute-start(bf16[4,48,1024]{2,1,0:T(8,128)(2,1)S(1)} %bitcast.59), channel_id=1, source_target_pairs={{0,2},{1,3},{2,0},{3,1},{4,6},{5,7},{6,4},{7,5},{8,10},{9,11},{10,... | collective-permute-start | bytes 1179656 | tf_op jit(solution)/shard_map/ppermute | solution.py:647
  89.6 22.4 %collective-permute-start.17 = (bf16[256,1024]{1,0:T(8,128)(2,1)S(1)}, bf16[256,1024]{1,0:T(8,128)(2,1)S(1)}, u32[]{:S(2)}, u32[]{:S(2)}) collective-permute-start(bf16[256,1024]{1,0:T(8,128)(2,1)S(1)} %get-tuple-element.134), channel_id=1, source_target_pairs={{0,8},{8,0},{16,24},{24,16},{1,9},{9,1},{17,25},{25,17},{2,10},{10... | collective-permute-start | bytes 1572872 | tf_op jit(solution)/shard_map/ppermute | solution.py:647
  91.1 23.6 %collective-permute-start.16 = (bf16[256,1024]{1,0:T(8,128)(2,1)S(1)}, bf16[256,1024]{1,0:T(8,128)(2,1)S(1)}, u32[]{:S(2)}, u32[]{:S(2)}) collective-permute-start(bf16[256,1024]{1,0:T(8,128)(2,1)S(1)} %get-tuple-element.133), channel_id=1, source_target_pairs={{0,16},{8,24},{16,0},{24,8},{1,17},{9,25},{17,1},{25,9},{2,18},{10... | collective-permute-start | bytes 1572872 | tf_op jit(solution)/shard_map/ppermute | solution.py:647
  101.1 9.6 %collective-permute-start.21 = (bf16[4,4,48,1024]{3,2,1,0:T(8,128)(2,1)S(1)}, bf16[4,4,48,1024]{3,2,1,0:T(8,128)(2,1)S(1)}, u32[]{:S(2)}, u32[]{:S(2)}) collective-permute-start(bf16[4,4,48,1024]{3,2,1,0:T(8,128)(2,1)S(1)} %get-tuple-element.136.refs_1_), channel_id=1, source_target_pairs={{0,1},{1,0},{2,3},{3,2},{4,5},{5,4},{6,7},{7,6},{8,9},{9,8},{10,11... | collective-permute-start | bytes 4718600 | tf_op jit(solution)/shard_map/ppermute | solution.py:647
  110.7 4.0 %copy-start.12 = (s32[2,128]{1,0:T(2,128)S(1)}, s32[2,128]{1,0:T(2,128)}, u32[]{:S(2)}) copy-start(s32[2,128]{1,0:T(2,128)} %ignore_ref.1) | copy-start | bytes 3076
  117.3 6.1 %copy-start.20 = (bf16[256,1024]{1,0:T(8,128)(2,1)}, bf16[256,1024]{1,0:T(8,128)(2,1)S(1)}, u32[]{:S(2)}) copy-start(bf16[256,1024]{1,0:T(8,128)(2,1)S(1)} %get-tuple-element.141.second_grad_ref.refs_3_) | copy-start | bytes 1572868
  117.3 6.1 %copy-start.22 = (bf16[256,512]{1,0:T(8,128)(2,1)}, bf16[256,512]{1,0:T(8,128)(2,1)S(1)}, u32[]{:S(2)}) copy-start(bf16[256,512]{1,0:T(8,128)(2,1)S(1)} %get-tuple-element.142.slopes_ref.refs_4_) | copy-start | bytes 786436
  117.3 22.4 %collective-permute-start.24 = (bf16[256,1024]{1,0:T(8,128)(2,1)S(1)}, bf16[256,1024]{1,0:T(8,128)(2,1)S(1)}, u32[]{:S(2)}, u32[]{:S(2)}) collective-permute-start(bf16[256,1024]{1,0:T(8,128)(2,1)S(1)} %get-tuple-element.140.first_grad_ref.grad_ref.refs_3_.refs_2_), channel_id=1, source_target_pairs={{0,16},{8,24},{16,0},{24,8},{1,17},{9,25},{17,1},{25,9},{2,18},{10... | collective-permute-start | bytes 1572872 | tf_op jit(solution)/shard_map/ppermute | solution.py:647
  120.7 21.5 %collective-permute-start.22 = (bf16[256,1024]{1,0:T(8,128)(2,1)S(1)}, bf16[256,1024]{1,0:T(8,128)(2,1)S(1)}, u32[]{:S(2)}, u32[]{:S(2)}) collective-permute-start(bf16[256,1024]{1,0:T(8,128)(2,1)S(1)} %get-tuple-element.140.first_grad_ref.grad_ref.refs_3_.refs_2_), channel_id=1, source_target_pairs={{0,8},{8,0},{16,24},{24,16},{1,9},{9,1},{17,25},{25,17},{2,10},{10... | collective-permute-start | bytes 1572872 | tf_op jit(solution)/shard_map/ppermute | solution.py:647
  123.5 7.2 %collective-permute-start.23 = (bf16[528,1536]{1,0:T(8,128)(2,1)S(1)}, bf16[528,1536]{1,0:T(8,128)(2,1)S(1)}, u32[]{:S(2)}, u32[]{:S(2)}) collective-permute-start(bf16[528,1536]{1,0:T(8,128)(2,1)S(1)} %get-tuple-element.148), channel_id=1, source_target_pairs={{0,1},{1,0},{2,3},{3,2},{4,5},{5,4},{6,7},{7,6},{8,9},{9,8},{10,11... | collective-permute-start | bytes 4866056 | tf_op jit(solution)/shard_map/ppermute | solution.py:647
  130.7 11.5 %copy-start.1 = (f32[2,8,128]{2,1,0:T(8,128)S(1)}, f32[2,8,128]{2,1,0:T(8,128)}, u32[]{:S(2)}) copy-start(f32[2,8,128]{2,1,0:T(8,128)} %copy-done) | copy-start | bytes 24580
  132.8 31.0 %collective-permute-start.27 = (bf16[144,1536]{1,0:T(8,128)(2,1)}, bf16[144,1536]{1,0:T(8,128)(2,1)}, u32[]{:S(2)}, u32[]{:S(2)}) collective-permute-start(bf16[144,1536]{1,0:T(8,128)(2,1)} %get-tuple-element.162), channel_id=1, source_target_pairs={{0,2},{1,3},{2,0},{3,1},{4,6},{5,7},{6,4},{7,5},{8,10},{9,11},{10,... | collective-permute-start | bytes 1327112 | tf_op jit(solution)/shard_map/ppermute | solution.py:647
  134.3 29.6 %collective-permute-start.28 = (bf16[144,1536]{1,0:T(8,128)(2,1)}, bf16[144,1536]{1,0:T(8,128)(2,1)}, u32[]{:S(2)}, u32[]{:S(2)}) collective-permute-start(bf16[144,1536]{1,0:T(8,128)(2,1)} %get-tuple-element.163), channel_id=1, source_target_pairs={{0,4},{1,5},{2,6},{3,7},{4,0},{5,1},{6,2},{7,3},{8,12},{9,13},{10,... | collective-permute-start | bytes 1327112 | tf_op jit(solution)/shard_map/ppermute | solution.py:647
  135.9 28.0 %collective-permute-start.29 = (bf16[144,1536]{1,0:T(8,128)(2,1)}, bf16[144,1536]{1,0:T(8,128)(2,1)}, u32[]{:S(2)}, u32[]{:S(2)}) collective-permute-start(bf16[144,1536]{1,0:T(8,128)(2,1)} %get-tuple-element.164), channel_id=1, source_target_pairs={{0,6},{1,7},{2,4},{3,5},{4,2},{5,3},{6,0},{7,1},{8,14},{9,15},{10,... | collective-permute-start | bytes 1327112 | tf_op jit(solution)/shard_map/ppermute | solution.py:647
  139.7 9.7 %copy-start.5 = (f32[2,8,128]{2,1,0:T(8,128)S(1)}, f32[2,8,128]{2,1,0:T(8,128)}, u32[]{:S(2)}) copy-start(f32[2,8,128]{2,1,0:T(8,128)} %copy-done.4) | copy-start | bytes 24580
  139.7 16.9 %collective-permute-start.25 = (bf16[256,1024]{1,0:T(8,128)(2,1)S(1)}, bf16[256,1024]{1,0:T(8,128)(2,1)S(1)}, u32[]{:S(2)}, u32[]{:S(2)}) collective-permute-start(bf16[256,1024]{1,0:T(8,128)(2,1)S(1)} %tie.11.grad_ref.refs_1_), channel_id=1, source_target_pairs={{0,8},{8,0},{16,24},{24,16},{1,9},{9,1},{17,25},{25,17},{2,10},{10... | collective-permute-start | bytes 1572872 | tf_op jit(solution)/shard_map/ppermute | solution.py:647
  158.2 4.1 %collective-permute-start.30 = (bf16[1,400,1024]{2,1,0:T(8,128)(2,1)S(1)}, bf16[1,400,1024]{2,1,0:T(8,128)(2,1)S(1)}, u32[]{:S(2)}, u32[]{:S(2)}) collective-permute-start(bf16[1,400,1024]{2,1,0:T(8,128)(2,1)S(1)} %get-tuple-element.165), channel_id=1, source_target_pairs={{0,1},{1,0},{2,3},{3,2},{4,5},{5,4},{6,7},{7,6},{8,9},{9,8},{10,11... | collective-permute-start | bytes 2457608 | tf_op jit(solution)/shard_map/ppermute | solution.py:647
  161.7 6.7 %collective-permute-start.26 = (bf16[3,400,1024]{2,1,0:T(8,128)(2,1)S(1)}, bf16[3,400,1024]{2,1,0:T(8,128)(2,1)S(1)}, u32[]{:S(2)}, u32[]{:S(2)}) collective-permute-start(bf16[3,400,1024]{2,1,0:T(8,128)(2,1)S(1)} %get-tuple-element.160), channel_id=1, source_target_pairs={{0,1},{1,0},{2,3},{3,2},{4,5},{5,4},{6,7},{7,6},{8,9},{9,8},{10,11... | collective-permute-start | bytes 7372808 | tf_op jit(solution)/shard_map/ppermute | solution.py:647
  165.6 13.3 %collective-permute-start.31 = (bf16[80,1536]{1,0:T(8,128)(2,1)S(1)}, bf16[80,1536]{1,0:T(8,128)(2,1)S(1)}, u32[]{:S(2)}, u32[]{:S(2)}) collective-permute-start(bf16[80,1536]{1,0:T(8,128)(2,1)S(1)} %get-tuple-element.172), channel_id=1, source_target_pairs={{0,16},{8,24},{16,0},{24,8},{1,17},{9,25},{17,1},{25,9},{2,18},{10... | collective-permute-start | bytes 737288 | tf_op jit(solution)/shard_map/ppermute | solution.py:647
  166.6 22.1 %collective-permute-start.32 = (bf16[400,1024]{1,0:T(8,128)(2,1)S(1)}, bf16[400,1024]{1,0:T(8,128)(2,1)S(1)}, u32[]{:S(2)}, u32[]{:S(2)}) collective-permute-start(bf16[400,1024]{1,0:T(8,128)(2,1)S(1)} %get-tuple-element.178), channel_id=1, source_target_pairs={{0,6},{1,7},{2,4},{3,5},{4,2},{5,3},{6,0},{7,1},{8,14},{9,15},{10,... | collective-permute-start | bytes 2457608 | tf_op jit(solution)/shard_map/ppermute | solution.py:647
  179.5 6.1 %collective-permute-start.33 = (bf16[48,1536]{1,0:T(8,128)(2,1)S(1)}, bf16[48,1536]{1,0:T(8,128)(2,1)S(1)}, u32[]{:S(2)}, u32[]{:S(2)}) collective-permute-start(bf16[48,1536]{1,0:T(8,128)(2,1)S(1)} %get-tuple-element.180), channel_id=1, source_target_pairs={{0,8},{8,0},{16,24},{24,16},{1,9},{9,1},{17,25},{25,17},{2,10},{10... | collective-permute-start | bytes 442376 | tf_op jit(solution)/shard_map/ppermute | solution.py:647
  181.5 23.5 %collective-permute-start.37 = (bf16[400,1024]{1,0:T(8,128)(2,1)S(1)}, bf16[400,1024]{1,0:T(8,128)(2,1)S(1)}, u32[]{:S(2)}, u32[]{:S(2)}) collective-permute-start(bf16[400,1024]{1,0:T(8,128)(2,1)S(1)} %get-tuple-element.187), channel_id=1, source_target_pairs={{0,2},{1,3},{2,0},{3,1},{4,6},{5,7},{6,4},{7,5},{8,10},{9,11},{10,... | collective-permute-start | bytes 2457608 | tf_op jit(solution)/shard_map/ppermute | solution.py:647
  182.6 22.3 %collective-permute-start.38 = (bf16[400,1024]{1,0:T(8,128)(2,1)S(1)}, bf16[400,1024]{1,0:T(8,128)(2,1)S(1)}, u32[]{:S(2)}, u32[]{:S(2)}) collective-permute-start(bf16[400,1024]{1,0:T(8,128)(2,1)S(1)} %get-tuple-element.188), channel_id=1, source_target_pairs={{0,4},{1,5},{2,6},{3,7},{4,0},{5,1},{6,2},{7,3},{8,12},{9,13},{10,... | collective-permute-start | bytes 2457608 | tf_op jit(solution)/shard_map/ppermute | solution.py:647
  185.0 20.0 %copy-start.15 = (bf16[416,400]{1,0:T(8,128)(2,1)S(1)}, bf16[416,400]{1,0:T(8,128)(2,1)}, u32[]{:S(2)}) copy-start(bf16[416,400]{1,0:T(8,128)(2,1)} %constant.45.refs_1_) | copy-start | bytes 998404
  185.0 23.7 %collective-permute-start.35 = (bf16[2,64,1024]{2,1,0:T(8,128)(2,1)S(1)}, bf16[2,64,1024]{2,1,0:T(8,128)(2,1)S(1)}, u32[]{:S(2)}, u32[]{:S(2)}) collective-permute-start(bf16[2,64,1024]{2,1,0:T(8,128)(2,1)S(1)} %get-tuple-element.184), channel_id=1, source_target_pairs={{0,16},{8,24},{16,0},{24,8},{1,17},{9,25},{17,1},{25,9},{2,18},{10... | collective-permute-start | bytes 786440 | tf_op jit(solution)/shard_map/ppermute | solution.py:647
  189.5 20.4 %collective-permute-start.34 = (bf16[2,64,1024]{2,1,0:T(8,128)(2,1)S(1)}, bf16[2,64,1024]{2,1,0:T(8,128)(2,1)S(1)}, u32[]{:S(2)}, u32[]{:S(2)}) collective-permute-start(bf16[2,64,1024]{2,1,0:T(8,128)(2,1)S(1)} %tie.12), channel_id=1, source_target_pairs={{0,8},{8,0},{16,24},{24,16},{1,9},{9,1},{17,25},{25,17},{2,10},{10... | collective-permute-start | bytes 786440 | tf_op jit(solution)/shard_map/ppermute | solution.py:647
  191.5 18.4 %collective-permute-start.36 = (bf16[2,64,1024]{2,1,0:T(8,128)(2,1)S(1)}, bf16[2,64,1024]{2,1,0:T(8,128)(2,1)S(1)}, u32[]{:S(2)}, u32[]{:S(2)}) collective-permute-start(bf16[2,64,1024]{2,1,0:T(8,128)(2,1)S(1)} %tie.13), channel_id=1, source_target_pairs={{0,24},{8,16},{16,8},{24,0},{1,25},{9,17},{17,9},{25,1},{2,26},{10... | collective-permute-start | bytes 786440 | tf_op jit(solution)/shard_map/ppermute | solution.py:647
  205.0 4.9 %copy-start.14 = (bf16[1024,1024]{1,0:T(8,128)(2,1)S(1)}, bf16[1024,1024]{1,0:T(8,128)(2,1)}, u32[]{:S(2)}) copy-start(bf16[1024,1024]{1,0:T(8,128)(2,1)} %constant.28.clone.refs_3_.refs_6_) | copy-start | bytes 6291460
  205.0 4.9 %copy-start.19 = (bf16[4,64,256]{2,1,0:T(8,128)(2,1)S(1)}, bf16[4,64,256]{2,1,0:T(8,128)(2,1)}, u32[]{:S(2)}) copy-start(bf16[4,64,256]{2,1,0:T(8,128)(2,1)} %constant.44.refs_2_.refs_5_) | copy-start | bytes 393220
  206.3 10.2 %collective-permute-start.39 = (bf16[104,1024]{1,0:T(8,128)(2,1)S(1)}, bf16[104,1024]{1,0:T(8,128)(2,1)S(1)}, u32[]{:S(2)}, u32[]{:S(2)}) collective-permute-start(bf16[104,1024]{1,0:T(8,128)(2,1)S(1)} %get-tuple-element.195), channel_id=1, source_target_pairs={{0,8},{8,0},{16,24},{24,16},{1,9},{9,1},{17,25},{25,17},{2,10},{10... | collective-permute-start | bytes 638984 | tf_op jit(solution)/shard_map/ppermute | solution.py:647
  208.4 15.2 %collective-permute-start.40 = (bf16[104,1024]{1,0:T(8,128)(2,1)S(1)}, bf16[104,1024]{1,0:T(8,128)(2,1)S(1)}, u32[]{:S(2)}, u32[]{:S(2)}) collective-permute-start(bf16[104,1024]{1,0:T(8,128)(2,1)S(1)} %get-tuple-element.196), channel_id=1, source_target_pairs={{0,16},{8,24},{16,0},{24,8},{1,17},{9,25},{17,1},{25,9},{2,18},{10... | collective-permute-start | bytes 638984 | tf_op jit(solution)/shard_map/ppermute | solution.py:647
  208.7 20.0 %collective-permute-start.41 = (bf16[104,1024]{1,0:T(8,128)(2,1)S(1)}, bf16[104,1024]{1,0:T(8,128)(2,1)S(1)}, u32[]{:S(2)}, u32[]{:S(2)}) collective-permute-start(bf16[104,1024]{1,0:T(8,128)(2,1)S(1)} %get-tuple-element.197), channel_id=1, source_target_pairs={{0,24},{8,16},{16,8},{24,0},{1,25},{9,17},{17,9},{25,1},{2,26},{10... | collective-permute-start | bytes 638984 | tf_op jit(solution)/shard_map/ppermute | solution.py:647
  209.9 4.5 %copy-start.21 = (bf16[256,1024]{1,0:T(8,128)(2,1)S(1)}, bf16[256,1024]{1,0:T(8,128)(2,1)}, u32[]{:S(2)}) copy-start(bf16[256,1024]{1,0:T(8,128)(2,1)} %copy-done.20) | copy-start | bytes 1572868
  209.9 4.5 %copy-start.23 = (bf16[256,512]{1,0:T(8,128)(2,1)S(1)}, bf16[256,512]{1,0:T(8,128)(2,1)}, u32[]{:S(2)}) copy-start(bf16[256,512]{1,0:T(8,128)(2,1)} %copy-done.22) | copy-start | bytes 786436
  214.4 14.4 %copy-start.17 = (bf16[392,416]{1,0:T(8,128)(2,1)S(1)}, bf16[392,416]{1,0:T(8,128)(2,1)}, u32[]{:S(2)}) copy-start(bf16[392,416]{1,0:T(8,128)(2,1)} %constant.46.refs_1_) | copy-start | bytes 978436
  (7 other events, 23.1 us)

commit v8 on v7

--- a/solution.py
+++ b/solution.py
@@ -970,11 +970,11 @@
         sign = for_other((6,), sign)
         sign = for_other((2, 4, 0), sign)
         sign = for_own((6,), sign)
-        sent, kept, sign = halve_rows((0, 1), 2, count, where, quarters, [sign])
+        sent, kept, sign = halve_rows((0, 0), 1, count, where, quarters, [sign])
         sign = for_own((2, 4, 0), sign)
         sign = take_up(3, [sign])
         sent, kept, sign = halve_rows(
-            (0, 0), 1, count, where, [kept, swap(sent, "level", 2)], [sign]
+            (0, 1), 1, count, where, [kept, swap(sent, "level", 1)], [sign]
         )
         *back, sign = call(
             functools.partial(arrange_back_kernel, sizes),
@@ -993,7 +993,7 @@
                 like((8, units), f32),
             ],
             where,
-            [kept, swap(sent, "level", 1)],
+            [kept, swap(sent, "level", 2)],
             [sign],
             name="small_sum",
             cost=TINY_COST,

time: 235 us -> 235 us (level)
  transfers between devices with their start and end apart: 42 -> 42, of which waited for: 18 -> 20; matrix products, arithmetic and copies ran while one was open for 1% -> 1% of each run, Pallas kernels for 41% -> 41%
where the time goes in v8:
time: 235 us; the launch traced here: 232 us
  Pallas kernels  103 us (44%)
  waiting for transfers between devices  78 us (33%)
  starting transfers between devices  45.1 us (19%)
  local copies, waits for them, and re-layouts  3.13 us (1%)
    ppermute x42, waiting for transfers between devices, swap(): return lax.ppermute(array, axis, [(at, at ^ bit) for at in range(size)])  78 us
    ppermute x42, starting transfers between devices, swap(): return lax.ppermute(array, axis, [(at, at ^ bit) for at in range(size)])  45.1 us
    pallas_call x4, Pallas kernels, spread_block(): pl.pallas_call(functools.partial(spread_kernel, table, sizes), in_specs=[...  28.7 us
    pallas_call x18, Pallas kernels, call(): pl.pallas_call(body, in_specs=[SCALAR] + [WHOLE for one in arrays] + [FAR...  27 us
    pallas_call x4, Pallas kernels, crop_block(): pl.pallas_call(functools.partial(crop_kernel, table, sizes, product), gri...  26.7 us
    pallas_call x4, Pallas kernels, piece_product(): pl.pallas_call(functools.partial(product_kernel, bits, len(grads), with_s...  9.87 us
  transfers between devices with their start and end apart: 42, of which 20 were waited for; matrix products, arithmetic and copies ran while one was open for 1% of the time, Pallas kernels for 41%

profile of v8, /device:TPU:8, one launch (start us, length us, event | category | flops | bytes accessed | tf_op | source)
XLA Modules:
  0.0 231.8 jit_solution(7004687951212830090)
XLA Ops:
  1.6 1.1 copy-done.7
  2.8 1.2 split_span.1
  4.1 3.0 %collective-permute-start.1 = (bf16[104,1024]{1,0:T(8,128)(2,1)S(1)}, bf16[104,1024]{1,0:T(8,128)(2,1)S(1)}, u32[]{:S(2)}, u32[]{:S(2)}) collective-permute-start(bf16[104,1024]{1,0:T(8,128)(2,1)S(1)} %get-tuple-element.109), channel_id=1, source_target_pairs={{0,16},{8,24},{16,0},{24,8},{1,17},{9,25},{17,1},{25,9},{2,18},{10... | collective-permute-start | bytes 638984 | tf_op jit(solution)/shard_map/ppermute | solution.py:647
  7.7 2.5 %maps.1 = (bf16[128,1024]{1,0:T(8,128)(2,1)S(1)}, bf16[128,1024]{1,0:T(8,128)(2,1)S(1)}, bf16[128,1024]{1,0:T(8,128)(2,1)S(1)}, bf16[128,1024]{1,0:T(8,128)(2,1)S(1)}, f32[8,128]{1,0:T(8,128)}) custom-call(s32[2]{0:T(128)S(1)} %pad_add_fusion.refs_0_.where_ref, bf16[2,1024,256]{2,1,0:T(8,128)(2,1)S(1)} %bitcast.56, bf16[4,64,256]{2,1,0:T(8,128)(2,1)S(1)} %copy-done.18, ...), custom_call_target="tpu_custom_call" | custom-call | flops 30000001024 | bytes 1 | tf_op jit(solution)/shard_map/maps/pallas_call | solution.py:269
  10.2 2.5 %collective-permute-done.refs_3_ = bf16[104,1024]{1,0:T(8,128)(2,1)S(1)} collective-permute-done((bf16[104,1024]{1,0:T(8,128)(2,1)S(1)}, bf16[104,1024]{1,0:T(8,128)(2,1)S(1)}, u32[]{:S(2)}, u32[]{:S(2)}) %collective-permute-start) | collective-permute-done | bytes 213024 | tf_op jit(solution)/shard_map/ppermute | solution.py:647
  12.7 9.2 %collective-permute-done.1.refs_4_ = bf16[104,1024]{1,0:T(8,128)(2,1)S(1)} collective-permute-done((bf16[104,1024]{1,0:T(8,128)(2,1)S(1)}, bf16[104,1024]{1,0:T(8,128)(2,1)S(1)}, u32[]{:S(2)}, u32[]{:S(2)}) %collective-permute-start.1) | collective-permute-done | bytes 213024 | tf_op jit(solution)/shard_map/ppermute | solution.py:647
  22.0 4.1 %collective-permute-done.2.refs_5_ = bf16[104,1024]{1,0:T(8,128)(2,1)S(1)} collective-permute-done((bf16[104,1024]{1,0:T(8,128)(2,1)S(1)}, bf16[104,1024]{1,0:T(8,128)(2,1)S(1)}, u32[]{:S(2)}, u32[]{:S(2)}) %collective-permute-start.2) | collective-permute-done | bytes 213024 | tf_op jit(solution)/shard_map/ppermute | solution.py:647
  26.0 1.2 join_span.2
  27.3 2.5 %collective-permute-start.11 = (bf16[400,1024]{1,0:T(8,128)(2,1)S(1)}, bf16[400,1024]{1,0:T(8,128)(2,1)S(1)}, u32[]{:S(2)}, u32[]{:S(2)}) collective-permute-start(bf16[400,1024]{1,0:T(8,128)(2,1)S(1)} %get-tuple-element.122), channel_id=1, source_target_pairs={{0,6},{1,7},{2,4},{3,5},{4,2},{5,3},{6,0},{7,1},{8,14},{9,15},{10,... | collective-permute-start | bytes 2457608 | tf_op jit(solution)/shard_map/ppermute | solution.py:647
  30.9 3.1 %collective-permute-start.4 = (bf16[128,1024]{1,0:T(8,128)(2,1)S(1)}, bf16[128,1024]{1,0:T(8,128)(2,1)S(1)}, u32[]{:S(2)}, u32[]{:S(2)}) collective-permute-start(bf16[128,1024]{1,0:T(8,128)(2,1)S(1)} %get-tuple-element.117), channel_id=1, source_target_pairs={{0,16},{8,24},{16,0},{24,8},{1,17},{9,25},{17,1},{25,9},{2,18},{10... | collective-permute-start | bytes 786440 | tf_op jit(solution)/shard_map/ppermute | solution.py:647
  34.0 6.1 %collective-permute-done.3.refs_1_.refs_2_ = bf16[128,1024]{1,0:T(8,128)(2,1)S(1)} collective-permute-done((bf16[128,1024]{1,0:T(8,128)(2,1)S(1)}, bf16[128,1024]{1,0:T(8,128)(2,1)S(1)}, u32[]{:S(2)}, u32[]{:S(2)}) %collective-permute-start.3) | collective-permute-done | bytes 262176 | tf_op jit(solution)/shard_map/ppermute | solution.py:647
  40.1 1.6 collective-permute-start.5
  41.7 13.4 %collective-permute-done.5.refs_4_.refs_1_ = bf16[128,1024]{1,0:T(8,128)(2,1)S(1)} collective-permute-done((bf16[128,1024]{1,0:T(8,128)(2,1)S(1)}, bf16[128,1024]{1,0:T(8,128)(2,1)S(1)}, u32[]{:S(2)}, u32[]{:S(2)}) %collective-permute-start.5) | collective-permute-done | bytes 262176 | tf_op jit(solution)/shard_map/ppermute | solution.py:647
  55.1 1.7 arrange.1
  56.8 4.5 %crop_block.4 = (bf16[3200,256]{1,0:T(8,128)(2,1)S(1)}, bf16[256,3200]{1,0:T(8,128)(2,1)S(1)}, f32[8,128]{1,0:T(8,128)S(1)}) custom-call(f32[2,8,128]{2,1,0:T(8,128)S(1)} %get-tuple-element.209.box_ref, bf16[2,1024,256]{2,1,0:T(8,128)(2,1)S(1)} %get-tuple-element.119.maps_ref), custom_call_target="tpu_custom_call" | custom-call | flops 30000001024 | bytes 1 | tf_op jit(solution)/shard_map/crop_block/pallas_call | solution.py:193
  61.9 2.8 %collective-permute-done.9.refs_4_ = bf16[400,1024]{1,0:T(8,128)(2,1)S(1)} collective-permute-done((bf16[400,1024]{1,0:T(8,128)(2,1)S(1)}, bf16[400,1024]{1,0:T(8,128)(2,1)S(1)}, u32[]{:S(2)}, u32[]{:S(2)}) %collective-permute-start.9) | collective-permute-done | bytes 819232 | tf_op jit(solution)/shard_map/ppermute | solution.py:647
  67.0 1.2 collective-permute-done.8.refs_3_
  68.1 1.4 gather_pieces.1.weight_ref.refs_0_
  69.6 2.0 multiply.1
  71.5 1.3 collective-permute-start.13
  72.8 6.3 %crop_block.5 = (bf16[3200,256]{1,0:T(8,128)(2,1)S(1)}, f32[256,1024]{1,0:T(8,128)S(1)}, f32[8,128]{1,0:T(8,128)S(1)}) custom-call(f32[2,8,128]{2,1,0:T(8,128)S(1)} %get-tuple-element.208.box_ref, bf16[2,1024,256]{2,1,0:T(8,128)(2,1)S(1)} %get-tuple-element.119.maps_ref, bf16[3200,1024]{1,0:T(8,128)(2,1)S(1)} %gather_pieces.1.weight_ref.refs_0_, ...), custom_call_target="tpu_custom_call" | custom-call | flops 30000001024 | bytes 1 | tf_op jit(solution)/shard_map/crop_block/pallas_call | solution.py:193
  79.7 2.4 %collective-permute-start.20 = (bf16[4,48,1024]{2,1,0:T(8,128)(2,1)S(1)}, bf16[4,48,1024]{2,1,0:T(8,128)(2,1)S(1)}, u32[]{:S(2)}, u32[]{:S(2)}) collective-permute-start(bf16[4,48,1024]{2,1,0:T(8,128)(2,1)S(1)} %bitcast.57), channel_id=1, source_target_pairs={{0,6},{1,7},{2,4},{3,5},{4,2},{5,3},{6,0},{7,1},{8,14},{9,15},{10,... | collective-permute-start | bytes 1179656 | tf_op jit(solution)/shard_map/ppermute | solution.py:647
  83.3 6.3 %crop_block.6 = (bf16[3200,256]{1,0:T(8,128)(2,1)S(1)}, bf16[256,1024]{1,0:T(8,128)(2,1)S(1)}, f32[8,128]{1,0:T(8,128)S(1)}) custom-call(f32[2,8,128]{2,1,0:T(8,128)S(1)} %get-tuple-element.207.box_ref, bf16[2,1024,256]{2,1,0:T(8,128)(2,1)S(1)} %get-tuple-element.119.maps_ref, bf16[3200,1024]{1,0:T(8,128)(2,1)S(1)} %gather_pieces.1.weight_ref.refs_0_, ...), custom_call_target="tpu_custom_call" | custom-call | flops 1000000000 | bytes 1 | tf_op jit(solution)/shard_map/crop_block/pallas_call | solution.py:193
  91.1 2.1 collective-permute-start.16
  93.2 6.6 %collective-permute-done.19.refs_3_ = bf16[4,48,1024]{2,1,0:T(8,128)(2,1)S(1)} collective-permute-done((bf16[4,48,1024]{2,1,0:T(8,128)(2,1)S(1)}, bf16[4,48,1024]{2,1,0:T(8,128)(2,1)S(1)}, u32[]{:S(2)}, u32[]{:S(2)}) %collective-permute-start.19) | collective-permute-done | bytes 393248 | tf_op jit(solution)/shard_map/ppermute | solution.py:647
  101.1 9.6 %crop_block.7 = (bf16[3200,256]{1,0:T(8,128)(2,1)S(1)}, f32[256,1024]{1,0:T(8,128)S(1)}, f32[8,128]{1,0:T(8,128)}) custom-call(f32[2,8,128]{2,1,0:T(8,128)S(1)} %get-tuple-element.210.box_ref, bf16[2,1024,256]{2,1,0:T(8,128)(2,1)S(1)} %get-tuple-element.119.maps_ref, bf16[3200,1024]{1,0:T(8,128)(2,1)S(1)} %gather_pieces.1.weight_ref.refs_0_, ...), custom_call_target="tpu_custom_call" | custom-call | flops 30000001024 | bytes 1 | tf_op jit(solution)/shard_map/crop_block/pallas_call | solution.py:193
  110.7 1.3 full_small.1
  112.0 2.7 %collective-permute-done.16.one_ref = bf16[256,1024]{1,0:T(8,128)(2,1)S(1)} collective-permute-done((bf16[256,1024]{1,0:T(8,128)(2,1)S(1)}, bf16[256,1024]{1,0:T(8,128)(2,1)S(1)}, u32[]{:S(2)}, u32[]{:S(2)}) %collective-permute-start.16) | collective-permute-done | bytes 524320 | tf_op jit(solution)/shard_map/ppermute | solution.py:647
  114.7 2.6 %head_block.1 = (f32[256,512]{1,0:T(8,128)S(1)}, bf16[256,1024]{1,0:T(8,128)(2,1)S(1)}, bf16[256,1024]{1,0:T(8,128)(2,1)S(1)}, bf16[256,512]{1,0:T(8,128)(2,1)S(...) custom-call(f32[256,1024]{1,0:T(8,128)S(1)} %get-tuple-element.132.own_ref, ...), custom_call_target="tpu_custom_call" | custom-call | flops 30000001024 | bytes 1 | tf_op jit(solution)/shard_map/head_block/pallas_call | solution.py:528
  117.3 3.3 %collective-permute-start.24 = (bf16[256,1024]{1,0:T(8,128)(2,1)S(1)}, bf16[256,1024]{1,0:T(8,128)(2,1)S(1)}, u32[]{:S(2)}, u32[]{:S(2)}) collective-permute-start(bf16[256,1024]{1,0:T(8,128)(2,1)S(1)} %get-tuple-element.140.first_grad_ref.grad_ref.refs_3_.refs_2_), channel_id=1, source_target_pairs={{0,16},{8,24},{16,0},{24,8},{1,17},{9,25},{17,1},{25,9},{2,18},{10... | collective-permute-start | bytes 1572872 | tf_op jit(solution)/shard_map/ppermute | solution.py:647
  120.7 2.8 %small_product.1 = (bf16[528,1536]{1,0:T(8,128)(2,1)S(1)}, bf16[528,1536]{1,0:T(8,128)(2,1)S(1)}, f32[8,128]{1,0:T(8,128)S(1)}) custom-call(s32[2]{0:T(128)S(1)} %pad_add_fusion.refs_0_.where_ref, bf16[256,1024]{1,0:T(8,128)(2,1)S(1)} %get-tuple-element.143.first_ref, bf16[256,1024]{1,0:T(8,128)(2,1)S(1)} %get-tuple-element.141.second_grad_ref.refs_3_, ...), custom_call_target="tpu_custom_call" | custom-call | flops 30000001024 | bytes 1 | tf_op jit(solution)/shard_map/small_product/pallas_call | solution.py:374
  123.5 7.1 %spread_block.4 = (bf16[2,1024,256]{2,1,0:T(8,128)(2,1)S(1)}, f32[8,128]{1,0:T(8,128)S(1)}) custom-call(f32[2,8,128]{2,1,0:T(8,128)S(1)} %get-tuple-element.210.box_ref, bf16[256,1024]{1,0:T(8,128)(2,1)S(1)} %get-tuple-element.140.first_grad_ref.grad_ref.refs_3_.refs_2_, bf16[3200,1024]{1,0:T(8,128)(2,1)S(1)} %gather_pieces.1.weight_ref.refs_0_, ...), custom_call_target="tpu_custom_call" | custom-call | flops 30000001024 | bytes 1 | tf_op jit(solution)/shard_map/spread_block/pallas_call | solution.py:242
  130.7 2.2 quarter_rows.1
  132.8 1.5 collective-permute-start.27
  134.3 1.5 collective-permute-start.28
  136.3 3.4 %collective-permute-done.24.refs_0_ = bf16[256,1024]{1,0:T(8,128)(2,1)S(1)} collective-permute-done((bf16[256,1024]{1,0:T(8,128)(2,1)S(1)}, bf16[256,1024]{1,0:T(8,128)(2,1)S(1)}, u32[]{:S(2)}, u32[]{:S(2)}) %collective-permute-start.24) | collective-permute-done | bytes 524320 | tf_op jit(solution)/shard_map/ppermute | solution.py:647
  139.7 2.4 %collective-permute-start.25 = (bf16[256,1024]{1,0:T(8,128)(2,1)S(1)}, bf16[256,1024]{1,0:T(8,128)(2,1)S(1)}, u32[]{:S(2)}, u32[]{:S(2)}) collective-permute-start(bf16[256,1024]{1,0:T(8,128)(2,1)S(1)} %tie.11.grad_ref.refs_1_), channel_id=1, source_target_pairs={{0,8},{8,0},{16,24},{24,16},{1,9},{9,1},{17,25},{25,17},{2,10},{10... | collective-permute-start | bytes 1572872 | tf_op jit(solution)/shard_map/ppermute | solution.py:647
  142.2 7.3 %spread_block.5 = (bf16[2,1024,256]{2,1,0:T(8,128)(2,1)S(1)}, f32[8,128]{1,0:T(8,128)S(1)}) custom-call(f32[2,8,128]{2,1,0:T(8,128)S(1)} %copy-done.1, bf16[256,1024]{1,0:T(8,128)(2,1)S(1)} %collective-permute-done.22.grad_ref.refs_2_, bf16[3200,1024]{1,0:T(8,128)(2,1)S(1)} %gather_pieces.1.weight_ref.refs_0_, f32[8,128]{1,0:T(8,128)S(1)} %get-tuple-element.150.refs_0_.refs_1_), custom_call_target="tpu_custom_call" | custom-call | flops 30000001024 | bytes 1 | tf_op jit(solution)/shard_map/spread_block/pallas_call | solution.py:242
  149.5 7.1 %spread_block.6 = (bf16[2,1024,256]{2,1,0:T(8,128)(2,1)S(1)}, f32[8,128]{1,0:T(8,128)S(1)}) custom-call(f32[2,8,128]{2,1,0:T(8,128)S(1)} %copy-done.5, bf16[256,1024]{1,0:T(8,128)(2,1)S(1)} %tie.11.grad_ref.refs_1_, bf16[3200,1024]{1,0:T(8,128)(2,1)S(1)} %gather_pieces.1.weight_ref.refs_0_, f32[8,128]{1,0:T(8,128)S(1)} %get-tuple-element.152.refs_0_), custom_call_target="tpu_custom_call" | custom-call | flops 30000001024 | bytes 1 | tf_op jit(solution)/shard_map/spread_block/pallas_call | solution.py:242
  156.6 1.6 piece_product.4
  158.3 3.5 %piece_product.5 = (bf16[3,400,1024]{2,1,0:T(8,128)(2,1)S(1)}, f32[8,128]{1,0:T(8,128)S(1)}) custom-call(s32[2]{0:T(128)S(1)} %pad_add_fusion.refs_0_.where_ref, bf16[256,1024]{1,0:T(8,128)(2,1)S(1)} %collective-permute-done.25.refs_0_.grad_ref, bf16[256,1024]{1,0:T(8,128)(2,1)S(1)} %tie.11.grad_ref.refs_1_, ...), custom_call_target="tpu_custom_call" | custom-call | flops 30000001024 | bytes 1 | tf_op jit(solution)/shard_map/piece_product/pallas_call | solution.py:685
  162.3 1.6 piece_product.6
  163.9 1.7 halve_rows.2
  165.6 1.7 collective-permute-start.32
  167.3 3.3 %piece_product.7 = (bf16[400,1024]{1,0:T(8,128)(2,1)S(1)}, bf16[400,1024]{1,0:T(8,128)(2,1)S(1)}, bf16[400,1024]{1,0:T(8,128)(2,1)S(1)}, f32[8,128]{1,0:T(8,128)S(1)}) custom-call(s32[2]{0:T(128)S(1)} %pad_add_fusion.refs_0_.where_ref, bf16[256,1024]{1,0:T(8,128)(2,1)S(1)} %collective-permute-done.25.refs_0_.grad_ref, ...), custom_call_target="tpu_custom_call" | custom-call | flops 30000001024 | bytes 1 | tf_op jit(solution)/shard_map/piece_product/pallas_call | solution.py:685
  170.6 7.1 %spread_block.7 = (bf16[2,1024,256]{2,1,0:T(8,128)(2,1)S(1)}, f32[8,128]{1,0:T(8,128)S(1)}) custom-call(f32[2,8,128]{2,1,0:T(8,128)S(1)} %copy-done.3, bf16[256,1024]{1,0:T(8,128)(2,1)S(1)} %collective-permute-done.25.refs_0_.grad_ref, bf16[3200,1024]{1,0:T(8,128)(2,1)S(1)} %gather_pieces.1.weight_ref.refs_0_, f32[8,128]{1,0:T(8,128)S(1)} %get-tuple-element.169.refs_0_), custom_call_target="tpu_custom_call" | custom-call | flops 30000001024 | bytes 1 | tf_op jit(solution)/shard_map/spread_block/pallas_call | solution.py:242
  178.4 3.1 %collective-permute-start.33 = (bf16[48,1536]{1,0:T(8,128)(2,1)S(1)}, bf16[48,1536]{1,0:T(8,128)(2,1)S(1)}, u32[]{:S(2)}, u32[]{:S(2)}) collective-permute-start(bf16[48,1536]{1,0:T(8,128)(2,1)S(1)} %get-tuple-element.180), channel_id=1, source_target_pairs={{0,16},{8,24},{16,0},{24,8},{1,17},{9,25},{17,1},{25,9},{2,18},{10... | collective-permute-start | bytes 442376 | tf_op jit(solution)/shard_map/ppermute | solution.py:647
  181.5 1.1 collective-permute-start.37
  183.2 1.7 arrange_back.1
  185.1 7.8 %collective-permute-done.33.refs_2_ = bf16[48,1536]{1,0:T(8,128)(2,1)S(1)} collective-permute-done((bf16[48,1536]{1,0:T(8,128)(2,1)S(1)}, bf16[48,1536]{1,0:T(8,128)(2,1)S(1)}, u32[]{:S(2)}, u32[]{:S(2)}) %collective-permute-start.33) | collective-permute-done | bytes 147488 | tf_op jit(solution)/shard_map/ppermute | solution.py:647
  193.0 1.2 small_sum.1
  194.9 2.5 %collective-permute-start.34 = (bf16[2,64,1024]{2,1,0:T(8,128)(2,1)S(1)}, bf16[2,64,1024]{2,1,0:T(8,128)(2,1)S(1)}, u32[]{:S(2)}, u32[]{:S(2)}) collective-permute-start(bf16[2,64,1024]{2,1,0:T(8,128)(2,1)S(1)} %tie.12), channel_id=1, source_target_pairs={{0,8},{8,0},{16,24},{24,16},{1,9},{9,1},{17,25},{25,17},{2,10},{10... | collective-permute-start | bytes 786440 | tf_op jit(solution)/shard_map/ppermute | solution.py:647
  197.4 1.5 collective-permute-start.36
  200.7 3.6 %collective-permute-done.37.refs_3_ = bf16[400,1024]{1,0:T(8,128)(2,1)S(1)} collective-permute-done((bf16[400,1024]{1,0:T(8,128)(2,1)S(1)}, bf16[400,1024]{1,0:T(8,128)(2,1)S(1)}, u32[]{:S(2)}, u32[]{:S(2)}) %collective-permute-start.37) | collective-permute-done | bytes 819232 | tf_op jit(solution)/shard_map/ppermute | solution.py:647
  204.4 1.3 return_span.1
  205.6 1.7 collective-permute-start.39
  207.4 1.3 collective-permute-start.40
  209.2 2.0 collective-permute-done.36.refs_4_
  211.2 4.5 %maps_back.1 = (f32[2,1024,256]{2,1,0:T(8,128)}, f32[8,128]{1,0:T(8,128)S(1)}) custom-call(s32[2]{0:T(128)S(1)} %pad_add_fusion.refs_0_.where_ref, bf16[2,64,1024]{2,1,0:T(8,128)(2,1)S(1)} %get-tuple-element.175.refs_1_, bf16[2,64,1024]{2,1,0:T(8,128)(2,1)S(1)} %collective-permute-done.34.refs_2_, bf16[2,64,1024]{2,1,0:T(8,128)(2,1)S(1)} %collective-permute-done.35.refs_3_, ...), custom_call_target="tpu_custom_call" | custom-call | flops 30000001024 | bytes 1 | tf_op jit(solution)/shard_map/maps_back/pallas_call | solution.py:269
  215.7 1.5 row_outputs.1
  217.2 1.6 collective-permute-done.39.refs_3_
  218.8 5.9 %collective-permute-done.40.refs_4_ = bf16[104,1024]{1,0:T(8,128)(2,1)S(1)} collective-permute-done((bf16[104,1024]{1,0:T(8,128)(2,1)S(1)}, bf16[104,1024]{1,0:T(8,128)(2,1)S(1)}, u32[]{:S(2)}, u32[]{:S(2)}) %collective-permute-start.40) | collective-permute-done | bytes 213024 | tf_op jit(solution)/shard_map/ppermute | solution.py:647
  224.6 4.5 %collective-permute-done.41.refs_5_ = bf16[104,1024]{1,0:T(8,128)(2,1)S(1)} collective-permute-done((bf16[104,1024]{1,0:T(8,128)(2,1)S(1)}, bf16[104,1024]{1,0:T(8,128)(2,1)S(1)}, u32[]{:S(2)}, u32[]{:S(2)}) %collective-permute-start.41) | collective-permute-done | bytes 213024 | tf_op jit(solution)/shard_map/ppermute | solution.py:647
  229.1 2.4 %join_span.3 = (f32[392,1024]{1,0:T(8,128)}, f32[8,128]{1,0:T(8,128)}) custom-call(s32[2]{0:T(128)S(1)} %pad_add_fusion.refs_0_.where_ref, bf16[392,416]{1,0:T(8,128)(2,1)S(1)} %copy-done.17, bf16[104,1024]{1,0:T(8,128)(2,1)S(1)} %get-tuple-element.194.refs_2_, bf16[104,1024]{1,0:T(8,128)(2,1)S(1)} %collective-permute-done.39.refs_3_, ...), custom_call_target="tpu_custom_call" | custom-call | flops 30000001024 | bytes 1 | tf_op jit(solution)/shard_map/join_span/pallas_call | solution.py:269
  (143 shorter events, 15.9 us)
Async XLA Ops:
  2.7 4.9 %copy-start.25 = (bf16[32,320]{1,0:T(8,128)(2,1)S(1)}, bf16[32,320]{1,0:T(8,128)(2,1)}, u32[]{:S(2)}) copy-start(bf16[32,320]{1,0:T(8,128)(2,1)} %param.30) | copy-start | bytes 61444
  2.7 4.9 %copy-start.26 = (bf16[32,81]{1,0:T(8,128)(2,1)S(1)}, bf16[32,81]{1,0:T(8,128)(2,1)}, u32[]{:S(2)}) copy-start(bf16[32,81]{1,0:T(8,128)(2,1)} %param.28) | copy-start | bytes 15556
  2.7 4.9 %copy-start.27 = (f32[320]{0:T(512)S(1)}, f32[320]{0:T(512)}, u32[]{:S(2)}) copy-start(f32[320]{0:T(512)} %param.31) | copy-start | bytes 3844
  2.7 4.9 %copy-start.28 = (f32[81]{0:T(128)S(1)}, f32[81]{0:T(128)}, u32[]{:S(2)}) copy-start(f32[81]{0:T(128)} %param.29) | copy-start | bytes 976
  2.7 4.9 %copy-start.6 = (bf16[1,2,64,16,256]{4,3,2,1,0:T(8,128)(2,1)S(1)}, bf16[1,2,64,16,256]{4,3,2,1,0:T(8,128)(2,1)}, u32[]{:S(2)}) copy-start(bf16[1,2,64,16,256]{4,3,2,1,0:T(8,128)(2,1)} %param.18) | copy-start | bytes 3145732
  2.8 4.9 %copy-start.13 = (bf16[1024,1024]{1,0:T(8,128)(2,1)S(1)}, bf16[1024,1024]{1,0:T(8,128)(2,1)}, u32[]{:S(2)}) copy-start(bf16[1024,1024]{1,0:T(8,128)(2,1)} %constant.28.clone.refs_3_.refs_6_) | copy-start | bytes 6291460
  2.8 4.9 %copy-start.18 = (bf16[4,64,256]{2,1,0:T(8,128)(2,1)S(1)}, bf16[4,64,256]{2,1,0:T(8,128)(2,1)}, u32[]{:S(2)}) copy-start(bf16[4,64,256]{2,1,0:T(8,128)(2,1)} %constant.44.refs_2_.refs_5_) | copy-start | bytes 393220
  4.0 8.7 %collective-permute-start = (bf16[104,1024]{1,0:T(8,128)(2,1)S(1)}, bf16[104,1024]{1,0:T(8,128)(2,1)S(1)}, u32[]{:S(2)}, u32[]{:S(2)}) collective-permute-start(bf16[104,1024]{1,0:T(8,128)(2,1)S(1)} %get-tuple-element.108), channel_id=1, source_target_pairs={{0,8},{8,0},{16,24},{24,16},{1,9},{9,1},{17,25},{25,17},{2,10},{10... | collective-permute-start | bytes 638984 | tf_op jit(solution)/shard_map/ppermute | solution.py:647
  4.1 17.9 %collective-permute-start.1 = (bf16[104,1024]{1,0:T(8,128)(2,1)S(1)}, bf16[104,1024]{1,0:T(8,128)(2,1)S(1)}, u32[]{:S(2)}, u32[]{:S(2)}) collective-permute-start(bf16[104,1024]{1,0:T(8,128)(2,1)S(1)} %get-tuple-element.109), channel_id=1, source_target_pairs={{0,16},{8,24},{16,0},{24,8},{1,17},{9,25},{17,1},{25,9},{2,18},{10... | collective-permute-start | bytes 638984 | tf_op jit(solution)/shard_map/ppermute | solution.py:647
  7.1 18.9 %collective-permute-start.2 = (bf16[104,1024]{1,0:T(8,128)(2,1)S(1)}, bf16[104,1024]{1,0:T(8,128)(2,1)S(1)}, u32[]{:S(2)}, u32[]{:S(2)}) collective-permute-start(bf16[104,1024]{1,0:T(8,128)(2,1)S(1)} %get-tuple-element.110), channel_id=1, source_target_pairs={{0,24},{8,16},{16,8},{24,0},{1,25},{9,17},{17,9},{25,1},{2,26},{10... | collective-permute-start | bytes 638984 | tf_op jit(solution)/shard_map/ppermute | solution.py:647
  7.7 18.3 %copy-start.16 = (bf16[400,416]{1,0:T(8,128)(2,1)S(1)}, bf16[400,416]{1,0:T(8,128)(2,1)}, u32[]{:S(2)}) copy-start(bf16[400,416]{1,0:T(8,128)(2,1)} %constant.26.clone.refs_1_) | copy-start | bytes 998404
  27.3 34.1 %collective-permute-start.11 = (bf16[400,1024]{1,0:T(8,128)(2,1)S(1)}, bf16[400,1024]{1,0:T(8,128)(2,1)S(1)}, u32[]{:S(2)}, u32[]{:S(2)}) collective-permute-start(bf16[400,1024]{1,0:T(8,128)(2,1)S(1)} %get-tuple-element.122), channel_id=1, source_target_pairs={{0,6},{1,7},{2,4},{3,5},{4,2},{5,3},{6,0},{7,1},{8,14},{9,15},{10,... | collective-permute-start | bytes 2457608 | tf_op jit(solution)/shard_map/ppermute | solution.py:647
  29.8 34.9 %collective-permute-start.9 = (bf16[400,1024]{1,0:T(8,128)(2,1)S(1)}, bf16[400,1024]{1,0:T(8,128)(2,1)S(1)}, u32[]{:S(2)}, u32[]{:S(2)}) collective-permute-start(bf16[400,1024]{1,0:T(8,128)(2,1)S(1)} %get-tuple-element.122), channel_id=1, source_target_pairs={{0,4},{1,5},{2,6},{3,7},{4,0},{5,1},{6,2},{7,3},{8,12},{9,13},{10,... | collective-permute-start | bytes 2457608 | tf_op jit(solution)/shard_map/ppermute | solution.py:647
  30.3 34.4 %collective-permute-start.7 = (bf16[400,1024]{1,0:T(8,128)(2,1)S(1)}, bf16[400,1024]{1,0:T(8,128)(2,1)S(1)}, u32[]{:S(2)}, u32[]{:S(2)}) collective-permute-start(bf16[400,1024]{1,0:T(8,128)(2,1)S(1)} %get-tuple-element.122), channel_id=1, source_target_pairs={{0,2},{1,3},{2,0},{3,1},{4,6},{5,7},{6,4},{7,5},{8,10},{9,11},{10,... | collective-permute-start | bytes 2457608 | tf_op jit(solution)/shard_map/ppermute | solution.py:647
  30.8 9.2 %collective-permute-start.3 = (bf16[128,1024]{1,0:T(8,128)(2,1)S(1)}, bf16[128,1024]{1,0:T(8,128)(2,1)S(1)}, u32[]{:S(2)}, u32[]{:S(2)}) collective-permute-start(bf16[128,1024]{1,0:T(8,128)(2,1)S(1)} %get-tuple-element.116), channel_id=1, source_target_pairs={{0,8},{8,0},{16,24},{24,16},{1,9},{9,1},{17,25},{25,17},{2,10},{10... | collective-permute-start | bytes 786440 | tf_op jit(solution)/shard_map/ppermute | solution.py:647
  30.9 24.2 %collective-permute-start.4 = (bf16[128,1024]{1,0:T(8,128)(2,1)S(1)}, bf16[128,1024]{1,0:T(8,128)(2,1)S(1)}, u32[]{:S(2)}, u32[]{:S(2)}) collective-permute-start(bf16[128,1024]{1,0:T(8,128)(2,1)S(1)} %get-tuple-element.117), channel_id=1, source_target_pairs={{0,16},{8,24},{16,0},{24,8},{1,17},{9,25},{17,1},{25,9},{2,18},{10... | collective-permute-start | bytes 786440 | tf_op jit(solution)/shard_map/ppermute | solution.py:647
  40.1 15.0 %collective-permute-start.5 = (bf16[128,1024]{1,0:T(8,128)(2,1)S(1)}, bf16[128,1024]{1,0:T(8,128)(2,1)S(1)}, u32[]{:S(2)}, u32[]{:S(2)}) collective-permute-start(bf16[128,1024]{1,0:T(8,128)(2,1)S(1)} %tie.8), channel_id=1, source_target_pairs={{0,24},{8,16},{16,8},{24,0},{1,25},{9,17},{17,9},{25,1},{2,26},{10... | collective-permute-start | bytes 786440 | tf_op jit(solution)/shard_map/ppermute | solution.py:647
  41.7 15.1 %copy-start.2 = (f32[2,8,128]{2,1,0:T(8,128)}, f32[2,8,128]{2,1,0:T(8,128)S(1)}, u32[]{:S(2)}) copy-start(f32[2,8,128]{2,1,0:T(8,128)S(1)} %get-tuple-element.209.box_ref) | copy-start | bytes 24580
  41.7 31.1 %copy-start.4 = (f32[2,8,128]{2,1,0:T(8,128)}, f32[2,8,128]{2,1,0:T(8,128)S(1)}, u32[]{:S(2)}) copy-start(f32[2,8,128]{2,1,0:T(8,128)S(1)} %get-tuple-element.208.box_ref) | copy-start | bytes 24580
  41.7 41.5 %copy-start = (f32[2,8,128]{2,1,0:T(8,128)}, f32[2,8,128]{2,1,0:T(8,128)S(1)}, u32[]{:S(2)}) copy-start(f32[2,8,128]{2,1,0:T(8,128)S(1)} %get-tuple-element.207.box_ref) | copy-start | bytes 24580
  55.1 10.0 %collective-permute-start.14 = (bf16[48,1024]{1,0:T(8,128)(2,1)S(1)}, bf16[48,1024]{1,0:T(8,128)(2,1)S(1)}, u32[]{:S(2)}, u32[]{:S(2)}) collective-permute-start(bf16[48,1024]{1,0:T(8,128)(2,1)S(1)} %tie.10.refs_1_), channel_id=1, source_target_pairs={{0,8},{8,0},{16,24},{24,16},{1,9},{9,1},{17,25},{25,17},{2,10},{10... | collective-permute-start | bytes 294920 | tf_op jit(solution)/shard_map/ppermute | solution.py:647
  61.3 5.3 %collective-permute-start.6 = (bf16[400,1024]{1,0:T(8,128)(2,1)S(1)}, bf16[400,1024]{1,0:T(8,128)(2,1)S(1)}, u32[]{:S(2)}, u32[]{:S(2)}) collective-permute-start(bf16[400,1024]{1,0:T(8,128)(2,1)S(1)} %tie.9.refs_0_), channel_id=1, source_target_pairs={{0,1},{1,0},{2,3},{3,2},{4,5},{5,4},{6,7},{7,6},{8,9},{9,8},{10,11... | collective-permute-start | bytes 2457608 | tf_op jit(solution)/shard_map/ppermute | solution.py:647
  61.4 5.2 %collective-permute-start.12 = (bf16[400,1024]{1,0:T(8,128)(2,1)S(1)}, bf16[400,1024]{1,0:T(8,128)(2,1)S(1)}, u32[]{:S(2)}, u32[]{:S(2)}) collective-permute-start(bf16[400,1024]{1,0:T(8,128)(2,1)S(1)} %collective-permute-done.11.refs_6_), channel_id=1, source_target_pairs={{0,1},{1,0},{2,3},{3,2},{4,5},{5,4},{6,7},{7,6},{8,9},{9,8},{10,11... | collective-permute-start | bytes 2457608 | tf_op jit(solution)/shard_map/ppermute | solution.py:647
  64.6 2.3 %collective-permute-start.10 = (bf16[400,1024]{1,0:T(8,128)(2,1)S(1)}, bf16[400,1024]{1,0:T(8,128)(2,1)S(1)}, u32[]{:S(2)}, u32[]{:S(2)}) collective-permute-start(bf16[400,1024]{1,0:T(8,128)(2,1)S(1)} %collective-permute-done.9.refs_4_), channel_id=1, source_target_pairs={{0,1},{1,0},{2,3},{3,2},{4,5},{5,4},{6,7},{7,6},{8,9},{9,8},{10,11... | collective-permute-start | bytes 2457608 | tf_op jit(solution)/shard_map/ppermute | solution.py:647
  64.7 3.4 %collective-permute-start.8 = (bf16[400,1024]{1,0:T(8,128)(2,1)S(1)}, bf16[400,1024]{1,0:T(8,128)(2,1)S(1)}, u32[]{:S(2)}, u32[]{:S(2)}) collective-permute-start(bf16[400,1024]{1,0:T(8,128)(2,1)S(1)} %collective-permute-done.7.refs_2_), channel_id=1, source_target_pairs={{0,1},{1,0},{2,3},{3,2},{4,5},{5,4},{6,7},{7,6},{8,9},{9,8},{10,11... | collective-permute-start | bytes 2457608 | tf_op jit(solution)/shard_map/ppermute | solution.py:647
  66.3 12.8 %collective-permute-start.15 = (bf16[2,48,1024]{2,1,0:T(8,128)(2,1)S(1)}, bf16[2,48,1024]{2,1,0:T(8,128)(2,1)S(1)}, u32[]{:S(2)}, u32[]{:S(2)}) collective-permute-start(bf16[2,48,1024]{2,1,0:T(8,128)(2,1)S(1)} %get-tuple-element.127.refs_1_), channel_id=1, source_target_pairs={{0,16},{8,24},{16,0},{24,8},{1,17},{9,25},{17,1},{25,9},{2,18},{10... | collective-permute-start | bytes 589832 | tf_op jit(solution)/shard_map/ppermute | solution.py:647
  71.5 18.9 %collective-permute-start.13 = (bf16[256,1024]{1,0:T(8,128)(2,1)S(1)}, bf16[256,1024]{1,0:T(8,128)(2,1)S(1)}, u32[]{:S(2)}, u32[]{:S(2)}) collective-permute-start(bf16[256,1024]{1,0:T(8,128)(2,1)S(1)} %get-tuple-element.126), channel_id=1, source_target_pairs={{0,8},{8,0},{16,24},{24,16},{1,9},{9,1},{17,25},{25,17},{2,10},{10... | collective-permute-start | bytes 1572872 | tf_op jit(solution)/shard_map/ppermute | solution.py:647
  79.7 13.5 %collective-permute-start.20 = (bf16[4,48,1024]{2,1,0:T(8,128)(2,1)S(1)}, bf16[4,48,1024]{2,1,0:T(8,128)(2,1)S(1)}, u32[]{:S(2)}, u32[]{:S(2)}) collective-permute-start(bf16[4,48,1024]{2,1,0:T(8,128)(2,1)S(1)} %bitcast.57), channel_id=1, source_target_pairs={{0,6},{1,7},{2,4},{3,5},{4,2},{5,3},{6,0},{7,1},{8,14},{9,15},{10,... | collective-permute-start | bytes 1179656 | tf_op jit(solution)/shard_map/ppermute | solution.py:647
  82.1 17.8 %collective-permute-start.19 = (bf16[4,48,1024]{2,1,0:T(8,128)(2,1)S(1)}, bf16[4,48,1024]{2,1,0:T(8,128)(2,1)S(1)}, u32[]{:S(2)}, u32[]{:S(2)}) collective-permute-start(bf16[4,48,1024]{2,1,0:T(8,128)(2,1)S(1)} %bitcast.58), channel_id=1, source_target_pairs={{0,4},{1,5},{2,6},{3,7},{4,0},{5,1},{6,2},{7,3},{8,12},{9,13},{10,... | collective-permute-start | bytes 1179656 | tf_op jit(solution)/shard_map/ppermute | solution.py:647
  82.7 17.2 %collective-permute-start.18 = (bf16[4,48,1024]{2,1,0:T(8,128)(2,1)S(1)}, bf16[4,48,1024]{2,1,0:T(8,128)(2,1)S(1)}, u32[]{:S(2)}, u32[]{:S(2)}) collective-permute-start(bf16[4,48,1024]{2,1,0:T(8,128)(2,1)S(1)} %bitcast.59), channel_id=1, source_target_pairs={{0,2},{1,3},{2,0},{3,1},{4,6},{5,7},{6,4},{7,5},{8,10},{9,11},{10,... | collective-permute-start | bytes 1179656 | tf_op jit(solution)/shard_map/ppermute | solution.py:647
  89.6 22.4 %collective-permute-start.17 = (bf16[256,1024]{1,0:T(8,128)(2,1)S(1)}, bf16[256,1024]{1,0:T(8,128)(2,1)S(1)}, u32[]{:S(2)}, u32[]{:S(2)}) collective-permute-start(bf16[256,1024]{1,0:T(8,128)(2,1)S(1)} %get-tuple-element.134), channel_id=1, source_target_pairs={{0,8},{8,0},{16,24},{24,16},{1,9},{9,1},{17,25},{25,17},{2,10},{10... | collective-permute-start | bytes 1572872 | tf_op jit(solution)/shard_map/ppermute | solution.py:647
  91.1 23.6 %collective-permute-start.16 = (bf16[256,1024]{1,0:T(8,128)(2,1)S(1)}, bf16[256,1024]{1,0:T(8,128)(2,1)S(1)}, u32[]{:S(2)}, u32[]{:S(2)}) collective-permute-start(bf16[256,1024]{1,0:T(8,128)(2,1)S(1)} %get-tuple-element.133), channel_id=1, source_target_pairs={{0,16},{8,24},{16,0},{24,8},{1,17},{9,25},{17,1},{25,9},{2,18},{10... | collective-permute-start | bytes 1572872 | tf_op jit(solution)/shard_map/ppermute | solution.py:647
  101.1 9.6 %collective-permute-start.21 = (bf16[4,4,48,1024]{3,2,1,0:T(8,128)(2,1)S(1)}, bf16[4,4,48,1024]{3,2,1,0:T(8,128)(2,1)S(1)}, u32[]{:S(2)}, u32[]{:S(2)}) collective-permute-start(bf16[4,4,48,1024]{3,2,1,0:T(8,128)(2,1)S(1)} %get-tuple-element.136.refs_1_), channel_id=1, source_target_pairs={{0,1},{1,0},{2,3},{3,2},{4,5},{5,4},{6,7},{7,6},{8,9},{9,8},{10,11... | collective-permute-start | bytes 4718600 | tf_op jit(solution)/shard_map/ppermute | solution.py:647
  110.7 4.0 %copy-start.12 = (s32[2,128]{1,0:T(2,128)S(1)}, s32[2,128]{1,0:T(2,128)}, u32[]{:S(2)}) copy-start(s32[2,128]{1,0:T(2,128)} %ignore_ref.1) | copy-start | bytes 3076
  117.3 6.1 %copy-start.20 = (bf16[256,1024]{1,0:T(8,128)(2,1)}, bf16[256,1024]{1,0:T(8,128)(2,1)S(1)}, u32[]{:S(2)}) copy-start(bf16[256,1024]{1,0:T(8,128)(2,1)S(1)} %get-tuple-element.141.second_grad_ref.refs_3_) | copy-start | bytes 1572868
  117.3 6.1 %copy-start.22 = (bf16[256,512]{1,0:T(8,128)(2,1)}, bf16[256,512]{1,0:T(8,128)(2,1)S(1)}, u32[]{:S(2)}) copy-start(bf16[256,512]{1,0:T(8,128)(2,1)S(1)} %get-tuple-element.142.slopes_ref.refs_4_) | copy-start | bytes 786436
  117.3 22.4 %collective-permute-start.24 = (bf16[256,1024]{1,0:T(8,128)(2,1)S(1)}, bf16[256,1024]{1,0:T(8,128)(2,1)S(1)}, u32[]{:S(2)}, u32[]{:S(2)}) collective-permute-start(bf16[256,1024]{1,0:T(8,128)(2,1)S(1)} %get-tuple-element.140.first_grad_ref.grad_ref.refs_3_.refs_2_), channel_id=1, source_target_pairs={{0,16},{8,24},{16,0},{24,8},{1,17},{9,25},{17,1},{25,9},{2,18},{10... | collective-permute-start | bytes 1572872 | tf_op jit(solution)/shard_map/ppermute | solution.py:647
  120.7 21.5 %collective-permute-start.22 = (bf16[256,1024]{1,0:T(8,128)(2,1)S(1)}, bf16[256,1024]{1,0:T(8,128)(2,1)S(1)}, u32[]{:S(2)}, u32[]{:S(2)}) collective-permute-start(bf16[256,1024]{1,0:T(8,128)(2,1)S(1)} %get-tuple-element.140.first_grad_ref.grad_ref.refs_3_.refs_2_), channel_id=1, source_target_pairs={{0,8},{8,0},{16,24},{24,16},{1,9},{9,1},{17,25},{25,17},{2,10},{10... | collective-permute-start | bytes 1572872 | tf_op jit(solution)/shard_map/ppermute | solution.py:647
  123.5 7.2 %collective-permute-start.23 = (bf16[528,1536]{1,0:T(8,128)(2,1)S(1)}, bf16[528,1536]{1,0:T(8,128)(2,1)S(1)}, u32[]{:S(2)}, u32[]{:S(2)}) collective-permute-start(bf16[528,1536]{1,0:T(8,128)(2,1)S(1)} %get-tuple-element.148), channel_id=1, source_target_pairs={{0,1},{1,0},{2,3},{3,2},{4,5},{5,4},{6,7},{7,6},{8,9},{9,8},{10,11... | collective-permute-start | bytes 4866056 | tf_op jit(solution)/shard_map/ppermute | solution.py:647
  130.7 11.5 %copy-start.1 = (f32[2,8,128]{2,1,0:T(8,128)S(1)}, f32[2,8,128]{2,1,0:T(8,128)}, u32[]{:S(2)}) copy-start(f32[2,8,128]{2,1,0:T(8,128)} %copy-done) | copy-start | bytes 24580
  132.8 31.0 %collective-permute-start.27 = (bf16[144,1536]{1,0:T(8,128)(2,1)}, bf16[144,1536]{1,0:T(8,128)(2,1)}, u32[]{:S(2)}, u32[]{:S(2)}) collective-permute-start(bf16[144,1536]{1,0:T(8,128)(2,1)} %get-tuple-element.162), channel_id=1, source_target_pairs={{0,2},{1,3},{2,0},{3,1},{4,6},{5,7},{6,4},{7,5},{8,10},{9,11},{10,... | collective-permute-start | bytes 1327112 | tf_op jit(solution)/shard_map/ppermute | solution.py:647
  134.3 29.6 %collective-permute-start.28 = (bf16[144,1536]{1,0:T(8,128)(2,1)}, bf16[144,1536]{1,0:T(8,128)(2,1)}, u32[]{:S(2)}, u32[]{:S(2)}) collective-permute-start(bf16[144,1536]{1,0:T(8,128)(2,1)} %get-tuple-element.163), channel_id=1, source_target_pairs={{0,4},{1,5},{2,6},{3,7},{4,0},{5,1},{6,2},{7,3},{8,12},{9,13},{10,... | collective-permute-start | bytes 1327112 | tf_op jit(solution)/shard_map/ppermute | solution.py:647
  135.9 28.0 %collective-permute-start.29 = (bf16[144,1536]{1,0:T(8,128)(2,1)}, bf16[144,1536]{1,0:T(8,128)(2,1)}, u32[]{:S(2)}, u32[]{:S(2)}) collective-permute-start(bf16[144,1536]{1,0:T(8,128)(2,1)} %get-tuple-element.164), channel_id=1, source_target_pairs={{0,6},{1,7},{2,4},{3,5},{4,2},{5,3},{6,0},{7,1},{8,14},{9,15},{10,... | collective-permute-start | bytes 1327112 | tf_op jit(solution)/shard_map/ppermute | solution.py:647
  139.7 9.7 %copy-start.5 = (f32[2,8,128]{2,1,0:T(8,128)S(1)}, f32[2,8,128]{2,1,0:T(8,128)}, u32[]{:S(2)}) copy-start(f32[2,8,128]{2,1,0:T(8,128)} %copy-done.4) | copy-start | bytes 24580
  139.7 16.9 %collective-permute-start.25 = (bf16[256,1024]{1,0:T(8,128)(2,1)S(1)}, bf16[256,1024]{1,0:T(8,128)(2,1)S(1)}, u32[]{:S(2)}, u32[]{:S(2)}) collective-permute-start(bf16[256,1024]{1,0:T(8,128)(2,1)S(1)} %tie.11.grad_ref.refs_1_), channel_id=1, source_target_pairs={{0,8},{8,0},{16,24},{24,16},{1,9},{9,1},{17,25},{25,17},{2,10},{10... | collective-permute-start | bytes 1572872 | tf_op jit(solution)/shard_map/ppermute | solution.py:647
  158.2 4.1 %collective-permute-start.30 = (bf16[1,400,1024]{2,1,0:T(8,128)(2,1)S(1)}, bf16[1,400,1024]{2,1,0:T(8,128)(2,1)S(1)}, u32[]{:S(2)}, u32[]{:S(2)}) collective-permute-start(bf16[1,400,1024]{2,1,0:T(8,128)(2,1)S(1)} %get-tuple-element.165), channel_id=1, source_target_pairs={{0,1},{1,0},{2,3},{3,2},{4,5},{5,4},{6,7},{7,6},{8,9},{9,8},{10,11... | collective-permute-start | bytes 2457608 | tf_op jit(solution)/shard_map/ppermute | solution.py:647
  161.7 5.6 %collective-permute-start.26 = (bf16[3,400,1024]{2,1,0:T(8,128)(2,1)S(1)}, bf16[3,400,1024]{2,1,0:T(8,128)(2,1)S(1)}, u32[]{:S(2)}, u32[]{:S(2)}) collective-permute-start(bf16[3,400,1024]{2,1,0:T(8,128)(2,1)S(1)} %get-tuple-element.160), channel_id=1, source_target_pairs={{0,1},{1,0},{2,3},{3,2},{4,5},{5,4},{6,7},{7,6},{8,9},{9,8},{10,11... | collective-permute-start | bytes 7372808 | tf_op jit(solution)/shard_map/ppermute | solution.py:647
  165.6 12.2 %collective-permute-start.31 = (bf16[80,1536]{1,0:T(8,128)(2,1)S(1)}, bf16[80,1536]{1,0:T(8,128)(2,1)S(1)}, u32[]{:S(2)}, u32[]{:S(2)}) collective-permute-start(bf16[80,1536]{1,0:T(8,128)(2,1)S(1)} %get-tuple-element.172), channel_id=1, source_target_pairs={{0,8},{8,0},{16,24},{24,16},{1,9},{9,1},{17,25},{25,17},{2,10},{10... | collective-permute-start | bytes 737288 | tf_op jit(solution)/shard_map/ppermute | solution.py:647
  165.6 28.5 %collective-permute-start.32 = (bf16[400,1024]{1,0:T(8,128)(2,1)S(1)}, bf16[400,1024]{1,0:T(8,128)(2,1)S(1)}, u32[]{:S(2)}, u32[]{:S(2)}) collective-permute-start(bf16[400,1024]{1,0:T(8,128)(2,1)S(1)} %get-tuple-element.178), channel_id=1, source_target_pairs={{0,6},{1,7},{2,4},{3,5},{4,2},{5,3},{6,0},{7,1},{8,14},{9,15},{10,... | collective-permute-start | bytes 2457608 | tf_op jit(solution)/shard_map/ppermute | solution.py:647
  178.4 14.6 %collective-permute-start.33 = (bf16[48,1536]{1,0:T(8,128)(2,1)S(1)}, bf16[48,1536]{1,0:T(8,128)(2,1)S(1)}, u32[]{:S(2)}, u32[]{:S(2)}) collective-permute-start(bf16[48,1536]{1,0:T(8,128)(2,1)S(1)} %get-tuple-element.180), channel_id=1, source_target_pairs={{0,16},{8,24},{16,0},{24,8},{1,17},{9,25},{17,1},{25,9},{2,18},{10... | collective-permute-start | bytes 442376 | tf_op jit(solution)/shard_map/ppermute | solution.py:647
  181.5 22.8 %collective-permute-start.37 = (bf16[400,1024]{1,0:T(8,128)(2,1)S(1)}, bf16[400,1024]{1,0:T(8,128)(2,1)S(1)}, u32[]{:S(2)}, u32[]{:S(2)}) collective-permute-start(bf16[400,1024]{1,0:T(8,128)(2,1)S(1)} %get-tuple-element.187), channel_id=1, source_target_pairs={{0,2},{1,3},{2,0},{3,1},{4,6},{5,7},{6,4},{7,5},{8,10},{9,11},{10,... | collective-permute-start | bytes 2457608 | tf_op jit(solution)/shard_map/ppermute | solution.py:647
  182.6 21.7 %collective-permute-start.38 = (bf16[400,1024]{1,0:T(8,128)(2,1)S(1)}, bf16[400,1024]{1,0:T(8,128)(2,1)S(1)}, u32[]{:S(2)}, u32[]{:S(2)}) collective-permute-start(bf16[400,1024]{1,0:T(8,128)(2,1)S(1)} %get-tuple-element.188), channel_id=1, source_target_pairs={{0,4},{1,5},{2,6},{3,7},{4,0},{5,1},{6,2},{7,3},{8,12},{9,13},{10,... | collective-permute-start | bytes 2457608 | tf_op jit(solution)/shard_map/ppermute | solution.py:647
  185.0 19.4 %copy-start.15 = (bf16[416,400]{1,0:T(8,128)(2,1)S(1)}, bf16[416,400]{1,0:T(8,128)(2,1)}, u32[]{:S(2)}) copy-start(bf16[416,400]{1,0:T(8,128)(2,1)} %constant.45.refs_1_) | copy-start | bytes 998404
  185.0 23.7 %collective-permute-start.35 = (bf16[2,64,1024]{2,1,0:T(8,128)(2,1)S(1)}, bf16[2,64,1024]{2,1,0:T(8,128)(2,1)S(1)}, u32[]{:S(2)}, u32[]{:S(2)}) collective-permute-start(bf16[2,64,1024]{2,1,0:T(8,128)(2,1)S(1)} %get-tuple-element.184), channel_id=1, source_target_pairs={{0,16},{8,24},{16,0},{24,8},{1,17},{9,25},{17,1},{25,9},{2,18},{10... | collective-permute-start | bytes 786440 | tf_op jit(solution)/shard_map/ppermute | solution.py:647
  194.9 14.3 %collective-permute-start.34 = (bf16[2,64,1024]{2,1,0:T(8,128)(2,1)S(1)}, bf16[2,64,1024]{2,1,0:T(8,128)(2,1)S(1)}, u32[]{:S(2)}, u32[]{:S(2)}) collective-permute-start(bf16[2,64,1024]{2,1,0:T(8,128)(2,1)S(1)} %tie.12), channel_id=1, source_target_pairs={{0,8},{8,0},{16,24},{24,16},{1,9},{9,1},{17,25},{25,17},{2,10},{10... | collective-permute-start | bytes 786440 | tf_op jit(solution)/shard_map/ppermute | solution.py:647
  197.4 13.8 %collective-permute-start.36 = (bf16[2,64,1024]{2,1,0:T(8,128)(2,1)S(1)}, bf16[2,64,1024]{2,1,0:T(8,128)(2,1)S(1)}, u32[]{:S(2)}, u32[]{:S(2)}) collective-permute-start(bf16[2,64,1024]{2,1,0:T(8,128)(2,1)S(1)} %tie.13), channel_id=1, source_target_pairs={{0,24},{8,16},{16,8},{24,0},{1,25},{9,17},{17,9},{25,1},{2,26},{10... | collective-permute-start | bytes 786440 | tf_op jit(solution)/shard_map/ppermute | solution.py:647
  204.4 6.9 %copy-start.14 = (bf16[1024,1024]{1,0:T(8,128)(2,1)S(1)}, bf16[1024,1024]{1,0:T(8,128)(2,1)}, u32[]{:S(2)}) copy-start(bf16[1024,1024]{1,0:T(8,128)(2,1)} %constant.28.clone.refs_3_.refs_6_) | copy-start | bytes 6291460
  204.4 6.9 %copy-start.19 = (bf16[4,64,256]{2,1,0:T(8,128)(2,1)S(1)}, bf16[4,64,256]{2,1,0:T(8,128)(2,1)}, u32[]{:S(2)}) copy-start(bf16[4,64,256]{2,1,0:T(8,128)(2,1)} %constant.44.refs_2_.refs_5_) | copy-start | bytes 393220
  205.6 13.1 %collective-permute-start.39 = (bf16[104,1024]{1,0:T(8,128)(2,1)S(1)}, bf16[104,1024]{1,0:T(8,128)(2,1)S(1)}, u32[]{:S(2)}, u32[]{:S(2)}) collective-permute-start(bf16[104,1024]{1,0:T(8,128)(2,1)S(1)} %get-tuple-element.195), channel_id=1, source_target_pairs={{0,8},{8,0},{16,24},{24,16},{1,9},{9,1},{17,25},{25,17},{2,10},{10... | collective-permute-start | bytes 638984 | tf_op jit(solution)/shard_map/ppermute | solution.py:647
  207.4 17.3 %collective-permute-start.40 = (bf16[104,1024]{1,0:T(8,128)(2,1)S(1)}, bf16[104,1024]{1,0:T(8,128)(2,1)S(1)}, u32[]{:S(2)}, u32[]{:S(2)}) collective-permute-start(bf16[104,1024]{1,0:T(8,128)(2,1)S(1)} %get-tuple-element.196), channel_id=1, source_target_pairs={{0,16},{8,24},{16,0},{24,8},{1,17},{9,25},{17,1},{25,9},{2,18},{10... | collective-permute-start | bytes 638984 | tf_op jit(solution)/shard_map/ppermute | solution.py:647
  208.7 20.4 %collective-permute-start.41 = (bf16[104,1024]{1,0:T(8,128)(2,1)S(1)}, bf16[104,1024]{1,0:T(8,128)(2,1)S(1)}, u32[]{:S(2)}, u32[]{:S(2)}) collective-permute-start(bf16[104,1024]{1,0:T(8,128)(2,1)S(1)} %get-tuple-element.197), channel_id=1, source_target_pairs={{0,24},{8,16},{16,8},{24,0},{1,25},{9,17},{17,9},{25,1},{2,26},{10... | collective-permute-start | bytes 638984 | tf_op jit(solution)/shard_map/ppermute | solution.py:647
  211.2 4.5 %copy-start.21 = (bf16[256,1024]{1,0:T(8,128)(2,1)S(1)}, bf16[256,1024]{1,0:T(8,128)(2,1)}, u32[]{:S(2)}) copy-start(bf16[256,1024]{1,0:T(8,128)(2,1)} %copy-done.20) | copy-start | bytes 1572868
  211.2 4.5 %copy-start.23 = (bf16[256,512]{1,0:T(8,128)(2,1)S(1)}, bf16[256,512]{1,0:T(8,128)(2,1)}, u32[]{:S(2)}) copy-start(bf16[256,512]{1,0:T(8,128)(2,1)} %copy-done.22) | copy-start | bytes 786436
  215.7 13.5 %copy-start.17 = (bf16[392,416]{1,0:T(8,128)(2,1)S(1)}, bf16[392,416]{1,0:T(8,128)(2,1)}, u32[]{:S(2)}) copy-start(bf16[392,416]{1,0:T(8,128)(2,1)} %constant.46.refs_1_) | copy-start | bytes 978436
  (7 other events, 23.1 us)
